TPU v7x, 32 devices: a whole 2x2x4 slice. The times are simulated.
32 devices in a mesh: freq: 4 (over y, x), ga: 4 (over z), band: 2 (over core).
Axes of the slice: x: 2, y: 2, z: 4, core: 2. Of those that a mesh axis runs over, the one named last changes fastest.
Arguments:
- pair_matrix: bfloat16 [16, 768, 2048], P('band', 'freq', 'ga'), may hold values from -0.29882812 to 0.29882812
- screened: bfloat16 [8, 2048, 2048], P('freq', None, 'ga'), may hold values from -0.125 to 0.125
- imag_freq: float32 [8], P('freq'), may hold values from 0.1 to 20
- quad_weight: float32 [8], P('freq'), may hold values from 0.05 to 2
- band_energy: float32 [256], replicated, may hold values from -12 to 12
- band_index: int32 [768], P('freq'), may hold values from 0 to 255
Outputs:
- sigma: float32 [16, 256], P('band')
All inputs are finite; a program needn't handle non-finite values.
Results may differ from a plain program's by a relative error of at most 0.0003.
Values may be sent and summed in bfloat16 or wider, within the bound.
No kernel may reach another device: no remote copies, remote signals or barrier semaphores. Data moves between devices by JAX's collectives and lax.ppermute only.
A program may use at most 128 MiB of HBM per device.

v0:
```python
import math

import jax
import jax.numpy as jnp
from jax import lax
from jax.sharding import PartitionSpec as P

NW = 256


omega_low = -10.0
omega_span = 20.0


def from_behind(block, axis, distance):
    devices = range(lax.axis_size(axis))
    route = [((i - distance) % len(devices), i) for i in devices]
    return lax.ppermute(block, axis, route)


def make_grid(count):
    return omega_low + omega_span * jnp.arange(count, dtype=jnp.float32) / (count - 1)


def lookup(indices, table):
    onehot = (indices[:, None] == jnp.arange(table.shape[0], dtype=jnp.int32)[None, :]).astype(
        jnp.float32
    )
    return jnp.dot(onehot, table, precision=lax.Precision.HIGHEST)


def contribute(full_rows, panel_rows, w_mat, nu_val, weight_val, energies, omega_grid, n_dev):
    product = jnp.dot(full_rows, w_mat, preferred_element_type=jnp.float32)
    contract = jnp.sum(product * panel_rows.astype(jnp.float32), axis=-1).reshape(n_dev, -1)
    offsets = omega_grid[None, :] - energies[:, None]
    kernel = offsets / (offsets * offsets + nu_val * nu_val)
    return -weight_val / math.pi * jnp.dot(contract, kernel, precision=lax.Precision.HIGHEST)


def on_device(pair_matrix, screened, imag_freq, quad_weight, band_energy, band_index):
    n_dev, m_dev, g_panel = pair_matrix.shape
    f_dev = screened.shape[0]
    cycle_size = lax.axis_size("freq")
    cycle_pos = lax.axis_index("freq")
    full_pairs = lax.all_gather(pair_matrix, "ga", axis=2, tiled=True)
    g_all = full_pairs.shape[2]
    omega_grid = make_grid(NW)
    sigma_part = jnp.zeros((n_dev, NW), jnp.float32)
    panel_rows = pair_matrix.reshape(n_dev * m_dev, g_panel)
    full_rows = full_pairs.reshape(n_dev * m_dev, g_all)
    energies = lookup(band_index, band_energy)
    nu_all, weight_all = (
        lax.all_gather(imag_freq, "freq", axis=0, tiled=True),
        lax.all_gather(quad_weight, "freq", axis=0, tiled=True),
    )
    w_slab = screened
    for turn_index in range(cycle_size):
        source = jnp.mod(cycle_pos - turn_index, cycle_size)
        nu_vals = lax.dynamic_slice_in_dim(nu_all, source * f_dev, f_dev)
        weight_vals = lax.dynamic_slice_in_dim(weight_all, source * f_dev, f_dev)
        for slot_index in range(f_dev):
            sigma_part = sigma_part + contribute(
                full_rows,
                panel_rows,
                w_slab[slot_index],
                nu_vals[slot_index],
                weight_vals[slot_index],
                energies,
                omega_grid,
                n_dev,
            )
        if turn_index + 1 < cycle_size:
            w_slab = from_behind(w_slab, "freq", 1)
    sigma = lax.psum(sigma_part, ("freq", "ga"))
    return sigma


def solution(mesh):
    placed = (P("band", "freq", "ga"), P("freq", None, "ga"), P("freq"), P("freq"), P(), P("freq"))
    return jax.shard_map(
        on_device, mesh=mesh, in_specs=placed, out_specs=P("band", None), check_vma=False
    )
```

profile of v0, /device:TPU:0, one launch (start us, length us, event | category | flops | bytes accessed | tf_op | source)
XLA Modules:
  0.0 378.4 jit_solution(4580515740433021303)
XLA Ops:
  6.5 0.0 copy-start
  6.5 0.0 all-gather.2.cloned.1.call-start
  6.5 0.7 all-gather.2.cloned.1.call-update
  7.3 3.0 collective-permute-start
  10.2 91.8 %collective-permute-done = bf16[2,2048,512]{2,1,0:T(8,128)(2,1)} collective-permute-done((bf16[2,2048,512]{2,1,0:T(8,128)(2,1)}, bf16[2,2048,512]{2,1,0:T(8,128)(2,1)}, u32[]{:S(2)}, u32[]{:S(2)}) %collective-permute-start) | collective-permute-done | bytes 4194336 | tf_op jit(solution)/shard_map/ppermute | solution.py:18
  102.1 0.8 collective-permute-start.1
  102.9 1.2 dynamic-slice
  104.8 0.9 dynamic-update-slice.1
  105.6 0.8 dynamic-update-slice
  106.5 90.8 %all-reduce.2 = (f32[8]{0:T(128)S(1)}, f32[8]{0:T(128)S(1)}) all-reduce(f32[8]{0:T(128)S(1)} %dynamic-update-slice.1, f32[8]{0:T(128)S(1)} %dynamic-update-slice), channel_id=1, replica_groups=mesh['freq'=4,'ga'=4,'band'=2] {'freq'}, use_global_device_ids=true, to_apply=%add.1 | all-reduce | flops 16 | bytes 128
  197.3 1.8 bitcast_convert_fusion
  199.1 0.0 copy-start.4
  199.1 2.4 copy.8
  201.5 0.1 fusion.59
  201.6 0.6 fusion.66
  203.5 0.6 fusion.65
  206.7 0.6 fusion.64
  208.8 0.7 fusion.63
  212.0 0.6 fusion.62
  214.1 0.7 fusion.61
  217.3 0.6 fusion.58
  219.4 0.7 fusion.57
  222.6 0.0 copy-done
  222.6 0.0 copy-done.4
  222.6 0.2 fusion.31
  222.9 0.0 collective-permute-done.1
  222.9 1.6 collective-permute-start.2
  224.5 0.0 all-gather.2.cloned.1.call-done
  224.5 0.0 copy-start.1
  224.5 0.0 copy-start.2
  224.5 0.0 copy-start.3
  224.5 8.0 %fusion.4 = f32[1536]{0:T(1024)S(1)} fusion(f32[1536,512]{0,1:T(8,128)} %copy.8, bf16[1536,2048]{1,0:T(8,128)(2,1)} %bitcast.81, bf16[2,2048,512]{2,1,0:T(8,128)(2,1)} %param.7), kind=kOutput, calls=%fused_computation.19 | convolution fusion | flops 3222796800 | bytes 11540480 | tf_op jit(solution)/shard_map/dot_general | solution.py:33
  232.5 0.0 copy-done.1
  232.5 0.0 copy-done.2
  232.5 0.3 copy-done.3
  232.8 3.8 fusion.7
  236.5 0.1 reshape.70
  236.6 0.1 reshape.71
  236.7 7.0 %fusion.10 = f32[1536]{0:T(1024)S(1)} fusion(f32[1536,512]{0,1:T(8,128)S(1)} %copy-done.1, bf16[1536,2048]{1,0:T(8,128)(2,1)} %bitcast.82, bf16[2,2048,512]{2,1,0:T(8,128)(2,1)} %collective-permute-done), kind=kOutput, calls=%fused_computation.21 | convolution fusion | flops 3222796800 | bytes 11540480 | tf_op jit(solution)/shard_map/dot_general | solution.py:33
  243.7 0.1 reshape.72
  243.8 7.2 %fusion.11 = f32[1536]{0:T(1024)S(1)} fusion(f32[1536,512]{0,1:T(8,128)S(1)} %copy-done.1, bf16[1536,2048]{1,0:T(8,128)(2,1)} %bitcast.83, bf16[2,2048,512]{2,1,0:T(8,128)(2,1)} %collective-permute-done), kind=kOutput, calls=%fused_computation.22 | convolution fusion | flops 3222796800 | bytes 11540480 | tf_op jit(solution)/shard_map/dot_general | solution.py:33
  251.0 0.1 reshape.73
  251.1 7.0 %fusion.12 = f32[1536]{0:T(1024)S(1)} fusion(f32[1536,512]{0,1:T(8,128)S(1)} %copy-done.1, bf16[1536,2048]{1,0:T(8,128)(2,1)} %bitcast.84, bf16[2,2048,512]{2,1,0:T(8,128)(2,1)} %collective-permute-done.1), kind=kOutput, calls=%fused_computation.23 | convolution fusion | flops 3222796800 | bytes 11540480 | tf_op jit(solution)/shard_map/dot_general | solution.py:33
  258.1 0.1 reshape.74
  258.2 7.0 %fusion.13 = f32[1536]{0:T(1024)S(1)} fusion(f32[1536,512]{0,1:T(8,128)S(1)} %copy-done.1, bf16[1536,2048]{1,0:T(8,128)(2,1)} %bitcast.85, bf16[2,2048,512]{2,1,0:T(8,128)(2,1)} %collective-permute-done.1), kind=kOutput, calls=%fused_computation.24 | convolution fusion | flops 3222796800 | bytes 11540480 | tf_op jit(solution)/shard_map/dot_general | solution.py:33
  265.2 0.1 reshape.75
  265.2 0.3 convolution_multiply_fusion.15
  265.5 0.3 fusion.22
  265.8 0.3 fusion.21
  266.1 0.3 fusion.20
  266.4 0.3 fusion.19
  266.7 0.3 fusion.18
  267.0 47.3 %collective-permute-done.2 = bf16[2,2048,512]{2,1,0:T(8,128)(2,1)} collective-permute-done((bf16[2,2048,512]{2,1,0:T(8,128)(2,1)}, bf16[2,2048,512]{2,1,0:T(8,128)(2,1)}, u32[]{:S(2)}, u32[]{:S(2)}) %collective-permute-start.2) | collective-permute-done | bytes 4194336 | tf_op jit(solution)/shard_map/ppermute | solution.py:18
  314.3 7.3 %fusion.14 = f32[1536]{0:T(1024)S(1)} fusion(f32[1536,512]{0,1:T(8,128)S(1)} %copy-done.1, bf16[1536,2048]{1,0:T(8,128)(2,1)} %bitcast.86, bf16[2,2048,512]{2,1,0:T(8,128)(2,1)} %collective-permute-done.2), kind=kOutput, calls=%fused_computation.25 | convolution fusion | flops 3222796800 | bytes 11540480 | tf_op jit(solution)/shard_map/dot_general | solution.py:33
  321.6 0.1 reshape.76
  321.7 7.0 %fusion.15 = f32[1536]{0:T(1024)S(1)} fusion(f32[1536,512]{0,1:T(8,128)S(1)} %copy-done.1, bf16[1536,2048]{1,0:T(8,128)(2,1)} %bitcast.87, bf16[2,2048,512]{2,1,0:T(8,128)(2,1)} %collective-permute-done.2), kind=kOutput, calls=%fused_computation.26 | convolution fusion | flops 3222796800 | bytes 11540480 | tf_op jit(solution)/shard_map/dot_general | solution.py:33
  328.7 0.1 reshape.77
  328.8 0.3 fusion.17
  329.0 0.3 fusion.16
  329.3 42.2 %psum.7 = f32[8,256]{1,0:T(8,128)} all-reduce(f32[8,256]{1,0:T(8,128)S(1)} %fusion.16), channel_id=1, replica_groups=mesh['freq'=4,'ga'=4,'band'=2] {'freq','ga'}, use_global_device_ids=true, to_apply=%region_8.9 | all-reduce | flops 2048 | bytes 16384 | tf_op jit(solution)/shard_map/psum | solution.py:74
  (3 shorter events, 0.0 us)
Async XLA Ops:
  6.5 216.1 %copy-start = (f32[256]{0:T(256)S(1)}, f32[256]{0:T(256)}, u32[]{:S(2)}) copy-start(f32[256]{0:T(256)} %param.10) | copy-start | bytes 3076
  6.5 218.0 %all-gather.2.cloned.1.call-start = ((), (), s32[]{:S(2)}) async-start(), calls=%async_computation | async-start | bytes 7864320 | tf_op jit(solution)/shard_map/all_gather | solution.py:45
  7.3 94.8 %collective-permute-start = (bf16[2,2048,512]{2,1,0:T(8,128)(2,1)}, bf16[2,2048,512]{2,1,0:T(8,128)(2,1)}, u32[]{:S(2)}, u32[]{:S(2)}) collective-permute-start(bf16[2,2048,512]{2,1,0:T(8,128)(2,1)} %param.7), channel_id=1, source_target_pairs={{24,0},{0,8},{8,16},{16,24},{25,1},{1,9},{9,17},{17,25},{26,2},{2,... | collective-permute-start | bytes 12582920 | tf_op jit(solution)/shard_map/ppermute | solution.py:18
  102.1 120.8 %collective-permute-start.1 = (bf16[2,2048,512]{2,1,0:T(8,128)(2,1)}, bf16[2,2048,512]{2,1,0:T(8,128)(2,1)}, u32[]{:S(2)}, u32[]{:S(2)}) collective-permute-start(bf16[2,2048,512]{2,1,0:T(8,128)(2,1)} %collective-permute-done), channel_id=1, source_target_pairs={{24,0},{0,8},{8,16},{16,24},{25,1},{1,9},{9,17},{17,25},{26,2},{2,... | collective-permute-start | bytes 12582920 | tf_op jit(solution)/shard_map/ppermute | solution.py:18
  199.1 23.5 %copy-start.4 = (s32[192]{0:T(256)S(1)}, s32[192]{0:T(256)}, u32[]{:S(2)}) copy-start(s32[192]{0:T(256)} %param.11) | copy-start | bytes 2308
  222.9 91.5 %collective-permute-start.2 = (bf16[2,2048,512]{2,1,0:T(8,128)(2,1)}, bf16[2,2048,512]{2,1,0:T(8,128)(2,1)}, u32[]{:S(2)}, u32[]{:S(2)}) collective-permute-start(bf16[2,2048,512]{2,1,0:T(8,128)(2,1)} %collective-permute-done.1), channel_id=1, source_target_pairs={{24,0},{0,8},{8,16},{16,24},{25,1},{1,9},{9,17},{17,25},{26,2},{2,... | collective-permute-start | bytes 12582920 | tf_op jit(solution)/shard_map/ppermute | solution.py:18
  224.5 8.0 %copy-start.1 = (f32[1536,512]{0,1:T(8,128)S(1)}, f32[1536,512]{0,1:T(8,128)}, u32[]{:S(2)}) copy-start(f32[1536,512]{0,1:T(8,128)} %copy.8) | copy-start | bytes 9437188
  224.5 8.0 %copy-start.2 = (bf16[8,192,2048]{2,1,0:T(8,128)(2,1)S(1)}, bf16[8,192,2048]{2,1,0:T(8,128)(2,1)}, u32[]{:S(2)}) copy-start(bf16[8,192,2048]{2,1,0:T(8,128)(2,1)} %all-gather.2.cloned.1.call-done) | copy-start | bytes 18874372
  224.5 8.2 %copy-start.3 = (bf16[2,2048,512]{2,1,0:T(8,128)(2,1)S(1)}, bf16[2,2048,512]{2,1,0:T(8,128)(2,1)}, u32[]{:S(2)}) copy-start(bf16[2,2048,512]{2,1,0:T(8,128)(2,1)} %param.7) | copy-start | bytes 12582916
Sparse Core Ops, SparseCore 0:
  8.9 118.0 all-gather.1
where the time goes:
time: 379 us; the launch traced here: 378 us
  waiting for transfers between devices  140 us (37%)
  blocking collectives  133 us (35%)
  matrix products  56.8 us (15%)
  between operations  30 us (8%)
  local copies, waits for them, and re-layouts  11.4 us (3%)
  starting transfers between devices  5.41 us (1%)
    ppermute x3, waiting for transfers between devices, from_behind(): return lax.ppermute(block, axis, route)  139 us
    unnamed x1, blocking collectives  90.8 us
    dot_general x8, matrix products, contribute(): product = jnp.dot(full_rows, w_mat, preferred_element_type=jnp.float32)  54.3 us
    psum x1, blocking collectives, on_device(): sigma = lax.psum(sigma_part, ('freq', 'ga'))  42.2 us
  transfers between devices with their start and end apart: 4, of which 2 were waited for; matrix products, arithmetic and copies ran while one was open for 14% of the time, Pallas kernels for 0%

commit v1 on v0

v1 whole, which is shorter than its diff:
```python
import functools
import math

import jax
import jax.numpy as jnp
from jax import lax
from jax.experimental import pallas as pl
from jax.experimental.pallas import tpu as pltpu
from jax.sharding import PartitionSpec as P

NW = 256

omega_low = -10.0
omega_span = 20.0


def make_grid(count):
    return omega_low + omega_span * jnp.arange(count, dtype=jnp.float32) / (count - 1)


def lookup(indices, table):
    hit = indices[:, None] == jnp.arange(table.shape[0], dtype=jnp.int32)[None, :]
    return jnp.sum(jnp.where(hit, table[None, :], 0.0), axis=1)


def from_behind(block, axis, distance):
    devices = range(lax.axis_size(axis))
    route = [((i - distance) % len(devices), i) for i in devices]
    return lax.ppermute(block, axis, route)


def flip(block, axis, bits):
    return lax.ppermute(block, axis, [(i, i ^ bits) for i in range(lax.axis_size(axis))])


def contribute(full_rows, panel_rows, w_mat, nu_val, weight_val, energies, omega_grid, n_dev):
    product = jnp.dot(full_rows, w_mat, preferred_element_type=jnp.float32)
    contract = jnp.sum(product * panel_rows.astype(jnp.float32), axis=-1).reshape(n_dev, -1)
    offsets = omega_grid[None, :] - energies[:, None]
    kernel = offsets / (offsets * offsets + nu_val * nu_val)
    return -weight_val / math.pi * jnp.dot(contract, kernel, precision=lax.Precision.HIGHEST)


def general(pair_matrix, screened, imag_freq, quad_weight, band_energy, band_index):
    n_dev, m_dev, g_panel = pair_matrix.shape
    f_dev = screened.shape[0]
    cycle_size = lax.axis_size("freq")
    cycle_pos = lax.axis_index("freq")
    full_pairs = lax.all_gather(pair_matrix, "ga", axis=2, tiled=True)
    g_all = full_pairs.shape[2]
    omega_grid = make_grid(NW)
    sigma_part = jnp.zeros((n_dev, NW), jnp.float32)
    panel_rows = pair_matrix.reshape(n_dev * m_dev, g_panel)
    full_rows = full_pairs.reshape(n_dev * m_dev, g_all)
    energies = lookup(band_index, band_energy)
    nu_all = lax.all_gather(imag_freq, "freq", axis=0, tiled=True)
    weight_all = lax.all_gather(quad_weight, "freq", axis=0, tiled=True)
    w_slab = screened
    for turn_index in range(cycle_size):
        source = jnp.mod(cycle_pos - turn_index, cycle_size)
        nu_vals = lax.dynamic_slice_in_dim(nu_all, source * f_dev, f_dev)
        weight_vals = lax.dynamic_slice_in_dim(weight_all, source * f_dev, f_dev)
        for slot in range(f_dev):
            sigma_part = sigma_part + contribute(
                full_rows, panel_rows, w_slab[slot], nu_vals[slot], weight_vals[slot],
                energies, omega_grid, n_dev,
            )
        if turn_index + 1 < cycle_size:
            w_slab = from_behind(w_slab, "freq", 1)
    return lax.psum(sigma_part, ("freq", "ga"))


def accumulate(contract, weight_ref, slot, out_ref, first, m_dev):
    for k in range(contract.shape[0] // m_dev):
        rows = contract[k * m_dev : (k + 1) * m_dev]
        term = rows * weight_ref[slot]
        out_ref[first + k] += jnp.sum(term.reshape(m_dev // 8, 8, NW), axis=0)


def near_kernel(n_slots, n_tile, m_dev, panel, where_ref, k_ref, own_ref, a_ref, b_ref, *rest):
    w_refs, (out_ref, left, own, w_all, k_all, sems, w_sems) = rest[:-7], rest[-7:]
    end, low = where_ref[0], where_ref[1]
    here = pl.multiple_of((1 - low) * panel, panel)
    there = pl.multiple_of(low * panel, panel)
    copies = [
        pltpu.make_async_copy(own_ref, own, sems.at[0]),
        pltpu.make_async_copy(own_ref, left.at[:, pl.ds(here, panel)], sems.at[1]),
    ]
    for c in copies:
        c.start()
    from_a = pltpu.make_async_copy(a_ref, left.at[:, pl.ds(there, panel)], sems.at[2])
    from_b = pltpu.make_async_copy(b_ref, left.at[:, pl.ds(there, panel)], sems.at[2])

    @pl.when(end == 1)
    def _():
        from_a.start()

    @pl.when(end == 0)
    def _():
        from_b.start()

    k_copy = pltpu.make_async_copy(k_ref, k_all, sems.at[3])
    k_copy.start()
    start_slots(where_ref, w_refs, w_all, w_sems, 2)
    out_ref[...] = jnp.zeros_like(out_ref)
    for c in copies:
        c.wait()
    from_a.wait()
    k_copy.wait()
    rows = n_tile * m_dev

    def one(slot, carry):
        pltpu.make_async_copy(w_all.at[slot], w_all.at[slot], w_sems.at[slot]).wait()
        for t in range(own.shape[0] // rows):
            at = slice(t * rows, (t + 1) * rows)
            y = jnp.dot(left[at], w_all[slot], preferred_element_type=jnp.float32)
            c = jnp.sum(y * own[at].astype(jnp.float32), axis=1, keepdims=True)
            accumulate(c, k_all, slot, out_ref, t * n_tile, m_dev)
        return carry

    lax.fori_loop(0, n_slots, one, 0)


def far_kernel(n_slots, n_tile, m_dev, panel, where_ref, k_ref, own_ref, a_ref, c_ref, d_ref, *rest):
    w_refs, (out_ref, own, far, other, left, w_all, k_all, sems, w_sems) = rest[:-9], rest[-9:]
    end = where_ref[0]
    copies = [
        pltpu.make_async_copy(own_ref, own, sems.at[0]),
        pltpu.make_async_copy(a_ref, other, sems.at[1]),
    ]
    for c in copies:
        c.start()
    far_c = pltpu.make_async_copy(c_ref, far, sems.at[2])
    far_d = pltpu.make_async_copy(d_ref, far, sems.at[2])
    left_own = pltpu.make_async_copy(own_ref, left, sems.at[3])
    left_far = pltpu.make_async_copy(d_ref, left, sems.at[3])

    @pl.when(end == 1)
    def _():
        far_c.start()
        left_own.start()

    @pl.when(end == 0)
    def _():
        far_d.start()
        left_far.start()

    k_copy = pltpu.make_async_copy(k_ref, k_all, sems.at[4])
    k_copy.start()
    start_slots(where_ref, w_refs, w_all, w_sems, 3)
    out_ref[...] = jnp.zeros_like(out_ref)
    for c in copies:
        c.wait()
    far_c.wait()
    left_own.wait()
    k_copy.wait()
    rows = n_tile * m_dev

    def one(slot, carry):
        pltpu.make_async_copy(w_all.at[slot], w_all.at[slot], w_sems.at[slot]).wait()
        for t in range(own.shape[0] // rows):
            at = slice(t * rows, (t + 1) * rows)
            y = jnp.dot(far[at], w_all[slot, :panel], preferred_element_type=jnp.float32)
            x = jnp.dot(left[at], w_all[slot, panel:], preferred_element_type=jnp.float32)
            z = y * own[at].astype(jnp.float32) + x * other[at].astype(jnp.float32)
            c = jnp.sum(z, axis=1, keepdims=True)
            accumulate(c, k_all, slot, out_ref, t * n_tile, m_dev)
        return carry

    lax.fori_loop(0, n_slots, one, 0)


def start_slots(where_ref, w_refs, w_all, w_sems, row_entry):
    slot, filled = 0, 0
    depth = w_all.shape[1]
    for ref in w_refs:
        if len(ref.shape) == 3:
            count = min(depth - filled, depth // 2 if row_entry == 3 else depth)
            begin = pl.multiple_of(where_ref[row_entry], 512)
            src = ref.at[where_ref[4], pl.ds(begin, count), :]
        else:
            count = ref.shape[0]
            src = ref
        dst = w_all.at[slot, filled : filled + count, :]
        pltpu.make_async_copy(src, dst, w_sems.at[slot]).start()
        filled += count
        if filled == depth:
            slot, filled = slot + 1, 0
    assert filled == 0


def run_kernel(body, where, k_part, mats, n_rows, slots, m_dev, n_lefts, left_width):
    panel = mats[0].shape[1]
    n_slots = k_part.shape[0]
    n_states = n_rows // m_dev
    n_tile = 2 if n_states % 2 == 0 else 1
    arrays = [w for slot in slots for w in slot]
    depth = 2 * panel
    scratch = [pltpu.VMEM((n_rows, left_width), jnp.bfloat16)]
    scratch += [pltpu.VMEM((n_rows, panel), jnp.bfloat16)] * (n_lefts - 1)
    scratch += [
        pltpu.VMEM((n_slots, depth, panel), jnp.bfloat16),
        pltpu.VMEM(k_part.shape, jnp.float32),
        pltpu.SemaphoreType.DMA((5,)),
        pltpu.SemaphoreType.DMA((n_slots,)),
    ]
    flops = 2 * n_rows * depth * panel * n_slots
    return pl.pallas_call(
        functools.partial(body, n_slots, n_tile, m_dev, panel),
        out_shape=jax.ShapeDtypeStruct((n_states, 8, NW), jnp.float32),
        in_specs=[pl.BlockSpec(memory_space=pltpu.SMEM)]
        + [pl.BlockSpec(memory_space=pl.ANY)] * (1 + len(mats) + len(arrays)),
        out_specs=pl.BlockSpec(memory_space=pltpu.VMEM),
        scratch_shapes=scratch,
        cost_estimate=pl.CostEstimate(flops=flops, bytes_accessed=n_slots * depth * panel * 2, transcendentals=0),
        compiler_params=pltpu.CompilerParams(vmem_limit_bytes=48 * 2**20),
    )(where, k_part, *mats, *arrays)


def square_line(pair_matrix, screened, imag_freq, quad_weight, band_energy, band_index):
    n_dev, m_dev, panel = pair_matrix.shape
    ga = lax.axis_index("ga")
    core = lax.axis_index("band")
    rows = n_dev * m_dev
    own = pair_matrix.reshape(rows, panel)
    end = (ga == 0) | (ga == 3)
    low = ga < 2
    near_at = jnp.where(ga == 0, 0, jnp.where(ga == 3, 2, 1)) * panel
    far_at = (ga + 2) % 4 * panel
    give_at = jnp.where(ga % 2 == 0, 3, 0) * panel
    where = jnp.stack([end, low, near_at, far_at, 1 - core]).astype(jnp.int32)

    outer = [(0, 1), (1, 0), (2, 3), (3, 2)]
    inner = [(1, 2), (2, 1)]
    outward = [(1, 0), (2, 3)]

    nodes = jnp.stack([imag_freq, quad_weight])
    node_sets = [nodes] + [flip(nodes, "freq", r) for r in (1, 2, 3)]

    def piece(start, count):
        return lax.dynamic_slice(screened, (core, start, 0), (1, count, panel))[0]

    given = lax.ppermute(piece(give_at, panel), "ga", outer)
    near_w = piece(near_at, 2 * panel)
    x1 = flip(near_w, "freq", 1)
    y1 = flip(near_w, "freq", 2)
    a_rows = lax.ppermute(own, "ga", outer)
    b_rows = lax.ppermute(own, "ga", inner)
    far_w = jnp.concatenate([piece(far_at, panel), given])
    x2 = flip(far_w, "freq", 1)
    y2 = flip(far_w, "freq", 2)
    d1a = flip(y1[:panel], "freq", 1)
    d1b = flip(x1[panel:], "freq", 2)
    d2a = flip(y2[:panel], "freq", 1)
    d2b = flip(x2[panel:], "freq", 2)
    given_o, x1_o, y1_o, x2_o, y2_o, d1a_o, d1b_o, d2a_o, d2b_o = (
        flip(w, "band", 1) for w in (given, x1, y1, x2, y2, d1a, d1b, d2a, d2b)
    )
    half = rows // 2
    cuts = [slice(0, half), slice(half, rows)]
    c_rows = [lax.ppermute(b_rows[cut], "ga", outward) for cut in cuts]
    d_rows = [lax.ppermute(a_rows[cut], "ga", inner) for cut in cuts]

    energies = lookup(band_index, band_energy)
    offsets = make_grid(NW)[None, :] - energies[:, None]
    ordered = [jnp.where(core == 0, s, s[:, ::-1]) for s in node_sets]
    nu = jnp.concatenate([s[0] for s in ordered])[:, None, None]
    weight = jnp.concatenate([s[1] for s in ordered])[:, None, None]
    k_all = (-weight / math.pi) * (offsets / (offsets * offsets + nu * nu))

    near = functools.partial(run_kernel, near_kernel, where, n_lefts=2, left_width=2 * panel, m_dev=m_dev, n_rows=rows, mats=(own, a_rows, b_rows))
    s1 = near(k_part=k_all[:6], slots=[[near_w], [screened], [x1], [x1_o], [y1], [y1_o]])
    s2 = near(k_part=k_all[6:], slots=[[d1a, d1b], [d1a_o, d1b_o]])
    first = [[far_w], [screened, given_o], [x2], [x2_o], [y2], [y2_o]]
    second = [[d2a, d2b], [d2a_o, d2b_o]]
    parts = []
    for i, cut in enumerate(cuts):
        mats = (own[cut], a_rows[cut], c_rows[i], d_rows[i])
        if i == 0:
            parts.append(
                run_kernel(far_kernel, where, k_all[:6], mats, half, first, m_dev, 4, panel)
                + run_kernel(far_kernel, where, k_all[6:], mats, half, second, m_dev, 4, panel)
            )
        else:
            parts.append(run_kernel(far_kernel, where, k_all, mats, half, first + second, m_dev, 4, panel))
    sigma = jnp.sum(s1 + s2 + jnp.concatenate(parts), axis=1)
    for axis in ("freq", "ga"):
        t1, t2, t3 = (flip(sigma, axis, r) for r in (1, 2, 3))
        sigma = (sigma + t1) + (t2 + t3)
    return sigma


def solution(mesh):
    placed = (P("band", "freq", "ga"), P("freq", None, "ga"), P("freq"), P("freq"), P(), P("freq"))
    fits = mesh.shape["freq"] == 4 and mesh.shape["ga"] == 4 and mesh.shape["band"] == 2
    return jax.shard_map(
        square_line if fits else general,
        mesh=mesh, in_specs=placed, out_specs=P("band", None), check_vma=False,
    )
```

time: 379 us -> 198 us (0.52)
  blocking collectives: 133 us -> 0 us
  matrix products: 56.8 us -> 0 us
  waiting for transfers between devices: 140 us -> 86.2 us
  Pallas kernels: 0 us -> 49.5 us
  between operations: 30 us -> 0.55 us
  starting transfers between devices: 5.41 us -> 33.4 us
  local copies, waits for them, and re-layouts: 11.4 us -> 22.2 us
    unnamed x1 -> x0, blocking collectives: 90.8 us -> none
    dot_general x17 -> x0, matrix products: 56.8 us -> none  [the longest x8 54.3 us: contribute(): product = jnp.dot(full_rows, w_mat, preferred_element_type=jnp.float32)]
    ppermute x3 -> x33, waiting for transfers between devices: 139 us -> 86.2 us  [the longest x26 64.7 us: flip(): lax.ppermute(block, axis, [(i, i ^ bits) for i in range(lax.axis_size(axi...]
    pallas_call x0 -> x5, Pallas kernels: none -> 49.5 us  [run_kernel(): pl.pallas_call(functools.partial(body, n_slots, n_tile, m_dev, panel), ou...]
    psum x1 -> x0, blocking collectives: 42.2 us -> none  [on_device(): sigma = lax.psum(sigma_part, ('freq', 'ga'))]
    ppermute x3 -> x33, starting transfers between devices: 5.41 us -> 33.4 us  [the longest x26 25.8 us: flip(): lax.ppermute(block, axis, [(i, i ^ bits) for i in range(lax.axis_size(axi...]
    squeeze x0 -> x2, local copies, waits for them, and re-layouts: none -> 4.58 us  [piece(): return lax.dynamic_slice(screened, (core, start, 0), (1, count, panel))[0]]
    slice x8 -> x9, local copies, waits for them, and re-layouts: 5.18 us -> 9.27 us  [the longest x1 1.89 us: square_line(): d1a = flip(y1[:panel], 'freq', 1)]
  transfers between devices with their start and end apart: 4 -> 33, of which waited for: 2 -> 14; matrix products, arithmetic and copies ran while one was open for 14% -> 10% of each run, Pallas kernels for 0% -> 18%
where the time goes in v1:
time: 198 us; the launch traced here: 197 us
  waiting for transfers between devices  86.2 us (44%)
  Pallas kernels  49.5 us (25%)
  starting transfers between devices  33.4 us (17%)
  local copies, waits for them, and re-layouts  22.2 us (11%)
  other arithmetic  5.38 us (3%)
    ppermute x26, waiting for transfers between devices, flip(): lax.ppermute(block, axis, [(i, i ^ bits) for i in range(lax.axis_size(axi...  64.7 us
    pallas_call x5, Pallas kernels, run_kernel(): pl.pallas_call(functools.partial(body, n_slots, n_tile, m_dev, panel), ou...  49.5 us
    ppermute x26, starting transfers between devices, flip(): lax.ppermute(block, axis, [(i, i ^ bits) for i in range(lax.axis_size(axi...  25.8 us
    ppermute x2, waiting for transfers between devices, square_line(): c_rows = [lax.ppermute(b_rows[cut], 'ga', outward) for cut in cuts]  11.2 us
    ppermute x1, waiting for transfers between devices, square_line(): given = lax.ppermute(piece(give_at, panel), 'ga', outer)  10.3 us
    unnamed x70, local copies, waits for them, and re-layouts  5.09 us
    squeeze x2, local copies, waits for them, and re-layouts, piece(): return lax.dynamic_slice(screened, (core, start, 0), (1, count, panel))[0]  4.58 us
  transfers between devices with their start and end apart: 33, of which 14 were waited for; matrix products, arithmetic and copies ran while one was open for 10% of the time, Pallas kernels for 18%

profile of v1, /device:TPU:0, one launch (start us, length us, event | category | flops | bytes accessed | tf_op | source)
XLA Modules:
  0.0 197.2 jit_solution(15191833492606530229)
XLA Ops:
  0.0 2.3 %dynamic-slice_bitcast_fusion.rest_0_ = bf16[1024,512]{1,0:T(8,128)(2,1)} fusion(bf16[2,2048,512]{2,1,0:T(8,128)(2,1)} %rest_1_.5, s32[]{:T(128)S(6)} %select_n.69, s32[]{:T(128)S(6)} %select_n.70), kind=kLoop, calls=%fused_computation.2 | loop fusion | bytes 2097160 | tf_op jit(solution)/shard_map/squeeze | solution.py:241
  2.4 3.0 %collective-permute-start.5 = (bf16[1024,512]{1,0:T(8,128)(2,1)}, bf16[1024,512]{1,0:T(8,128)(2,1)}, u32[]{:S(2)}, u32[]{:S(2)}) collective-permute-start(bf16[1024,512]{1,0:T(8,128)(2,1)} %dynamic-slice_bitcast_fusion.rest_0_), channel_id=1, source_target_pairs={{0,8},{8,0},{16,24},{24,16},{1,9},{9,1},{17,25},{25,17},{2,10},{10... | collective-permute-start | bytes 3145736 | tf_op jit(solution)/shard_map/ppermute | solution.py:33
  5.4 1.5 collective-permute-start.7
  6.9 2.2 %dynamic-slice_bitcast_fusion.2 = (bf16[512,512]{1,0:T(8,128)(2,1)}, bf16[512,512]{1,0:T(8,128)(2,1)}) fusion(bf16[2,2048,512]{2,1,0:T(8,128)(2,1)} %rest_1_.5, s32[]{:T(128)S(6)} %select_n.69, s32[]{:T(128)S(6)} %select_n.71, s32[]{:T(128)S(6)} %select_n.74), kind=kLoop, calls=%fused_computation.4 | loop fusion | bytes 2097164 | tf_op jit(solution)/shard_map/squeeze | solution.py:241
  9.1 1.6 collective-permute-start.15
  10.7 0.5 collective-permute-start.2
  11.5 1.2 fusion.5
  12.8 0.5 multiply_add_fusion
  13.3 0.7 rev.12
  14.1 10.3 %collective-permute-done.15 = bf16[512,512]{1,0:T(8,128)(2,1)} collective-permute-done((bf16[512,512]{1,0:T(8,128)(2,1)}, bf16[512,512]{1,0:T(8,128)(2,1)}, u32[]{:S(2)}, u32[]{:S(2)}) %collective-permute-start.15) | collective-permute-done | bytes 524320 | tf_op jit(solution)/shard_map/ppermute | solution.py:243
  24.3 2.2 %pad_maximum_fusion.rest_0_ = bf16[1024,512]{1,0:T(8,128)(2,1)} fusion(bf16[512,512]{1,0:T(8,128)(2,1)} %collective-permute-done.15, bf16[512,512]{1,0:T(8,128)(2,1)} %get-tuple-element.5), kind=kLoop, calls=%fused_computation.1 | loop fusion | flops 2097152 | bytes 2097152 | tf_op jit(solution)/shard_map/concatenate | solution.py:249
  26.6 0.5 collective-permute-start.19
  27.2 2.8 %collective-permute-done.2 = f32[2,2]{1,0:T(2,128)S(1)} collective-permute-done((f32[2,2]{1,0:T(2,128)S(1)}, f32[2,2]{1,0:T(2,128)S(1)}, u32[]{:S(2)}, u32[]{:S(2)}) %collective-permute-start.2) | collective-permute-done | bytes 48 | tf_op jit(solution)/shard_map/ppermute | solution.py:33
  30.2 22.6 %collective-permute-done.1 = f32[2,2]{1,0:T(2,128)S(1)} collective-permute-done((f32[2,2]{1,0:T(2,128)S(1)}, f32[2,2]{1,0:T(2,128)S(1)}, u32[]{:S(2)}, u32[]{:S(2)}) %collective-permute-start.1) | collective-permute-done | bytes 48 | tf_op jit(solution)/shard_map/ppermute | solution.py:33
  53.2 3.4 %collective-permute-done = f32[2,2]{1,0:T(2,128)S(1)} collective-permute-done((f32[2,2]{1,0:T(2,128)}, f32[2,2]{1,0:T(2,128)S(1)}, u32[]{:S(2)}, u32[]{:S(2)}) %collective-permute-start) | collective-permute-done | bytes 48 | tf_op jit(solution)/shard_map/ppermute | solution.py:33
  56.6 1.8 collective-permute-start.4
  58.4 0.7 broadcast_select_fusion.3
  59.1 0.4 collective-permute-start.17
  59.6 0.5 slice_bitcast_fusion.7
  60.1 0.6 rev.15
  60.7 0.7 rev.14
  61.4 1.9 slice.94
  63.3 1.6 collective-permute-start.9
  64.9 0.6 broadcast_select_fusion.1
  65.6 0.6 slice_bitcast_fusion.4
  66.3 1.1 slice.95
  67.4 1.1 slice.98
  68.4 17.1 %collective-permute-done.17.rest_3_ = bf16[1024,512]{1,0:T(8,128)(2,1)} collective-permute-done((bf16[1024,512]{1,0:T(8,128)(2,1)}, bf16[1024,512]{1,0:T(8,128)(2,1)}, u32[]{:S(2)}, u32[]{:S(2)}) %collective-permute-start.17) | collective-permute-done | bytes 1048608 | tf_op jit(solution)/shard_map/ppermute | solution.py:33
  85.6 1.5 collective-permute-start.10
  87.1 1.1 slice.99
  88.2 5.8 %collective-permute-done.9.rest_0_ = bf16[512,512]{1,0:T(8,128)(2,1)} collective-permute-done((bf16[512,512]{1,0:T(8,128)(2,1)}, bf16[512,512]{1,0:T(8,128)(2,1)}, u32[]{:S(2)}, u32[]{:S(2)}) %collective-permute-start.9) | collective-permute-done | bytes 524320 | tf_op jit(solution)/shard_map/ppermute | solution.py:33
  94.3 1.7 collective-permute-start.22
  96.3 1.5 fusion.3
  97.8 1.3 collective-permute-start.13
  99.1 5.7 %collective-permute-done.21.rest_0_.rest_7_ = bf16[512,512]{1,0:T(8,128)(2,1)S(1)} collective-permute-done((bf16[512,512]{1,0:T(8,128)(2,1)S(1)}, bf16[512,512]{1,0:T(8,128)(2,1)S(1)}, u32[]{:S(2)}, u32[]{:S(2)}) %collective-permute-start.21) | collective-permute-done | bytes 524320 | tf_op jit(solution)/shard_map/ppermute | solution.py:33
  104.7 0.7 collective-permute-start.14
  105.4 0.6 collective-permute-done.22.rest_1_.rest_8_
  106.0 0.5 collective-permute-start.12
  106.9 1.3 slice.92.k_ref
  108.7 0.4 collective-permute-start.18
  109.2 11.2 %collective-permute-done.13.c_ref = bf16[768,512]{1,0:T(8,128)(2,1)S(1)} collective-permute-done((bf16[768,512]{1,0:T(8,128)(2,1)S(1)}, bf16[768,512]{1,0:T(8,128)(2,1)S(1)}, u32[]{:S(2)}, u32[]{:S(2)}) %collective-permute-start.13) | collective-permute-done | bytes 786464 | tf_op jit(solution)/shard_map/ppermute | solution.py:261
  120.5 0.5 collective-permute-start.24
  121.0 15.9 %shard_map.64 = f32[8,8,256]{2,1,0:T(8,128)S(1)} custom-call(s32[5]{0:T(128)S(1)} %stack.40.where_ref, f32[6,192,256]{2,1,0:T(8,128)} %slice.92.k_ref, bf16[1536,512]{1,0:T(8,128)(2,1)} %bitcast.32, bf16[1536,512]{1,0:T(8,128)(2,1)} %copy-done.2, bf16[1536,512]{1,0:T(8,128)(2,1)} %collective-permute-done.4.b_ref, ...), custom_call_target="tpu_custom_call" | custom-call | flops 9663676416 | bytes 6291456 | tf_op jit(solution)/shard_map/pallas_call | solution.py:208
  136.9 0.8 copy-done.16
  137.7 1.3 collective-permute-start.25
  139.0 0.8 copy-done.19
  139.8 0.8 collective-permute-start.26
  140.7 1.0 copy-done.11
  141.7 1.0 copy-done.13
  142.8 1.0 copy-done.15
  143.8 6.2 %shard_map.65 = f32[8,8,256]{2,1,0:T(8,128)S(1)} custom-call(s32[5]{0:T(128)S(1)} %stack.40.where_ref, f32[2,192,256]{2,1,0:T(8,128)S(1)} %slice.93.k_ref, bf16[1536,512]{1,0:T(8,128)(2,1)S(1)} %bitcast.35, bf16[1536,512]{1,0:T(8,128)(2,1)S(1)} %copy-done.3, bf16[1536,512]{1,0:T(8,128)(2,1)} %collective-permute-done.4.b_ref, ...), custom_call_target="tpu_custom_call" | custom-call | flops 3221225472 | bytes 2097152 | tf_op jit(solution)/shard_map/pallas_call | solution.py:208
  150.0 3.5 %shard_map.67 = f32[4,8,256]{2,1,0:T(8,128)S(1)} custom-call(s32[5]{0:T(128)S(1)} %stack.40.where_ref, f32[2,192,256]{2,1,0:T(8,128)S(1)} %slice.93.k_ref, bf16[768,512]{1,0:T(8,128)(2,1)S(1)} %bitcast.37, bf16[768,512]{1,0:T(8,128)(2,1)S(1)} %get-tuple-element.9.a_ref, bf16[768,512]{1,0:T(8,128)(2,1)S(1)} %collective-permute-done.13.c_ref, ...), custom_call_target="tpu_custom_call" | custom-call | flops 1610612736 | bytes 2097152 | tf_op jit(solution)/shard_map/pallas_call | solution.py:208
  153.6 10.6 %shard_map.66 = f32[4,8,256]{2,1,0:T(8,128)S(1)} custom-call(s32[5]{0:T(128)S(1)} %stack.40.where_ref, f32[6,192,256]{2,1,0:T(8,128)} %slice.92.k_ref, bf16[768,512]{1,0:T(8,128)(2,1)S(1)} %bitcast.38, bf16[768,512]{1,0:T(8,128)(2,1)S(1)} %get-tuple-element.9.a_ref, bf16[768,512]{1,0:T(8,128)(2,1)S(1)} %collective-permute-done.13.c_ref, ...), custom_call_target="tpu_custom_call" | custom-call | flops 4831838208 | bytes 6291456 | tf_op jit(solution)/shard_map/pallas_call | solution.py:208
  164.3 13.4 %shard_map.68 = f32[4,8,256]{2,1,0:T(8,128)S(1)} custom-call(s32[5]{0:T(128)S(1)} %stack.40.where_ref, f32[8,192,256]{2,1,0:T(8,128)} %copy-done.22, bf16[768,512]{1,0:T(8,128)(2,1)S(1)} %bitcast.36, bf16[768,512]{1,0:T(8,128)(2,1)S(1)} %get-tuple-element.10.a_ref, bf16[768,512]{1,0:T(8,128)(2,1)S(1)} %collective-permute-done.25.c_ref, ...), custom_call_target="tpu_custom_call" | custom-call | flops 6442450944 | bytes 8388608 | tf_op jit(solution)/shard_map/pallas_call | solution.py:208
  177.7 1.1 collective-permute-start.28
  178.8 1.9 collective-permute-start.29
  180.7 0.5 collective-permute-start.27
  181.4 1.9 collective-permute-done.29
  183.3 1.0 collective-permute-done.27
  184.4 6.0 %collective-permute-start.31 = (f32[8,256]{1,0:T(8,128)S(1)}, f32[8,256]{1,0:T(8,128)S(1)}, u32[]{:S(2)}, u32[]{:S(2)}) collective-permute-start(f32[8,256]{1,0:T(8,128)S(1)} %add_add_fusion.1), channel_id=1, source_target_pairs={{0,4},{2,6},{4,0},{6,2},{1,5},{3,7},{5,1},{7,3},{8,12},{10,14},{12... | collective-permute-start | bytes 24584 | tf_op jit(solution)/shard_map/ppermute | solution.py:33
  190.4 2.6 %collective-permute-start.32 = (f32[8,256]{1,0:T(8,128)S(1)}, f32[8,256]{1,0:T(8,128)S(1)}, u32[]{:S(2)}, u32[]{:S(2)}) collective-permute-start(f32[8,256]{1,0:T(8,128)S(1)} %add_add_fusion.1), channel_id=1, source_target_pairs={{0,6},{2,4},{4,2},{6,0},{1,7},{3,5},{5,3},{7,1},{8,14},{10,12},{12... | collective-permute-start | bytes 24584 | tf_op jit(solution)/shard_map/ppermute | solution.py:33
  193.0 2.8 %collective-permute-done.32 = f32[8,256]{1,0:T(8,128)S(1)} collective-permute-done((f32[8,256]{1,0:T(8,128)S(1)}, f32[8,256]{1,0:T(8,128)S(1)}, u32[]{:S(2)}, u32[]{:S(2)}) %collective-permute-start.32) | collective-permute-done | bytes 8224 | tf_op jit(solution)/shard_map/ppermute | solution.py:33
  195.8 0.8 collective-permute-done.30
  196.6 0.6 add_add_fusion
  (112 shorter events, 3.0 us)
Async XLA Ops:
  2.3 8.4 %copy-start.26 = (f32[2]{0:T(128)S(1)}, f32[2]{0:T(128)}, u32[]{:S(2)}) copy-start(f32[2]{0:T(128)} %param.9) | copy-start | bytes 28
  2.3 8.4 %copy-start.27 = (f32[2]{0:T(128)S(1)}, f32[2]{0:T(128)}, u32[]{:S(2)}) copy-start(f32[2]{0:T(128)} %param.8) | copy-start | bytes 28
  2.3 8.9 %copy-start = (bf16[8,192,512]{2,1,0:T(8,128)(2,1)S(1)}, bf16[8,192,512]{2,1,0:T(8,128)(2,1)}, u32[]{:S(2)}) copy-start(bf16[8,192,512]{2,1,0:T(8,128)(2,1)} %param.6) | copy-start | bytes 4718596
  2.3 9.0 %copy-start.33 = (f32[256]{0:T(256)S(1)}, f32[256]{0:T(256)}, u32[]{:S(2)}) copy-start(f32[256]{0:T(256)} %param.10) | copy-start | bytes 3076
  2.3 9.0 %copy-start.34 = (s32[192]{0:T(256)S(1)}, s32[192]{0:T(256)}, u32[]{:S(2)}) copy-start(s32[192]{0:T(256)} %param.11) | copy-start | bytes 2308
  2.4 60.9 %collective-permute-start.5 = (bf16[1024,512]{1,0:T(8,128)(2,1)}, bf16[1024,512]{1,0:T(8,128)(2,1)}, u32[]{:S(2)}, u32[]{:S(2)}) collective-permute-start(bf16[1024,512]{1,0:T(8,128)(2,1)} %dynamic-slice_bitcast_fusion.rest_0_), channel_id=1, source_target_pairs={{0,8},{8,0},{16,24},{24,16},{1,9},{9,1},{17,25},{25,17},{2,10},{10... | collective-permute-start | bytes 3145736 | tf_op jit(solution)/shard_map/ppermute | solution.py:33
  5.4 53.8 %collective-permute-start.7 = (bf16[1024,512]{1,0:T(8,128)(2,1)}, bf16[1024,512]{1,0:T(8,128)(2,1)}, u32[]{:S(2)}, u32[]{:S(2)}) collective-permute-start(bf16[1024,512]{1,0:T(8,128)(2,1)} %dynamic-slice_bitcast_fusion.rest_0_), channel_id=1, source_target_pairs={{0,16},{8,24},{16,0},{24,8},{1,17},{9,25},{17,1},{25,9},{2,18},{10... | collective-permute-start | bytes 3145736 | tf_op jit(solution)/shard_map/ppermute | solution.py:33
  9.1 15.2 %collective-permute-start.15 = (bf16[512,512]{1,0:T(8,128)(2,1)}, bf16[512,512]{1,0:T(8,128)(2,1)}, u32[]{:S(2)}, u32[]{:S(2)}) collective-permute-start(bf16[512,512]{1,0:T(8,128)(2,1)} %get-tuple-element.6), channel_id=1, source_target_pairs={{0,2},{2,0},{4,6},{6,4},{1,3},{3,1},{5,7},{7,5},{8,10},{10,8},{12,... | collective-permute-start | bytes 1572872 | tf_op jit(solution)/shard_map/ppermute | solution.py:243
  10.7 19.2 %copy-start.25 = (f32[2,2]{1,0:T(2,128)}, f32[2,2]{1,0:T(2,128)S(1)}, u32[]{:S(2)}) copy-start(f32[2,2]{1,0:T(2,128)S(1)} %pad_maximum_fusion.1) | copy-start | bytes 52
  10.7 19.2 %collective-permute-start.2 = (f32[2,2]{1,0:T(2,128)S(1)}, f32[2,2]{1,0:T(2,128)S(1)}, u32[]{:S(2)}, u32[]{:S(2)}) collective-permute-start(f32[2,2]{1,0:T(2,128)S(1)} %pad_maximum_fusion.1), channel_id=1, source_target_pairs={{0,24},{8,16},{16,8},{24,0},{1,25},{9,17},{17,9},{25,1},{2,26},{10... | collective-permute-start | bytes 56 | tf_op jit(solution)/shard_map/ppermute | solution.py:33
  11.3 83.1 %collective-permute-start.3 = (bf16[1536,512]{1,0:T(8,128)(2,1)S(1)}, bf16[1536,512]{1,0:T(8,128)(2,1)S(1)}, u32[]{:S(2)}, u32[]{:S(2)}) collective-permute-start(bf16[1536,512]{1,0:T(8,128)(2,1)S(1)} %bitcast.33), channel_id=1, source_target_pairs={{0,2},{2,0},{4,6},{6,4},{1,3},{3,1},{5,7},{7,5},{8,10},{10,8},{12,... | collective-permute-start | bytes 4718600 | tf_op jit(solution)/shard_map/ppermute | solution.py:247
  14.0 13.0 %copy-start.32 = (f32[256]{0:T(256)S(1)}, f32[256]{0:T(256)}, u32[]{:S(2)}) copy-start(f32[256]{0:T(256)} %multiply_add_fusion) | copy-start | bytes 3076
  14.1 44.4 %copy-start.23 = (f32[2,2]{1,0:T(2,128)S(1)}, f32[2,2]{1,0:T(2,128)}, u32[]{:S(2)}) copy-start(f32[2,2]{1,0:T(2,128)} %rev.12) | copy-start | bytes 52
  26.6 39.0 %collective-permute-start.19 = (bf16[1024,512]{1,0:T(8,128)(2,1)}, bf16[1024,512]{1,0:T(8,128)(2,1)}, u32[]{:S(2)}, u32[]{:S(2)}) collective-permute-start(bf16[1024,512]{1,0:T(8,128)(2,1)} %pad_maximum_fusion.rest_0_), channel_id=1, source_target_pairs={{0,16},{8,24},{16,0},{24,8},{1,17},{9,25},{17,1},{25,9},{2,18},{10... | collective-permute-start | bytes 3145736 | tf_op jit(solution)/shard_map/ppermute | solution.py:33
  30.0 22.8 %collective-permute-start.1 = (f32[2,2]{1,0:T(2,128)S(1)}, f32[2,2]{1,0:T(2,128)S(1)}, u32[]{:S(2)}, u32[]{:S(2)}) collective-permute-start(f32[2,2]{1,0:T(2,128)S(1)} %pad_maximum_fusion.1), channel_id=1, source_target_pairs={{0,16},{8,24},{16,0},{24,8},{1,17},{9,25},{17,1},{25,9},{2,18},{10... | collective-permute-start | bytes 56 | tf_op jit(solution)/shard_map/ppermute | solution.py:33
  52.8 10.5 %copy-start.24 = (f32[2,2]{1,0:T(2,128)}, f32[2,2]{1,0:T(2,128)S(1)}, u32[]{:S(2)}) copy-start(f32[2,2]{1,0:T(2,128)S(1)} %collective-permute-done.1) | copy-start | bytes 52
  52.8 3.8 %collective-permute-start = (f32[2,2]{1,0:T(2,128)}, f32[2,2]{1,0:T(2,128)S(1)}, u32[]{:S(2)}, u32[]{:S(2)}) collective-permute-start(f32[2,2]{1,0:T(2,128)} %copy-done.25), channel_id=1, source_target_pairs={{0,8},{8,0},{16,24},{24,16},{1,9},{9,1},{17,25},{25,17},{2,10},{10... | collective-permute-start | bytes 56 | tf_op jit(solution)/shard_map/ppermute | solution.py:33
  56.6 39.6 %collective-permute-start.4 = (bf16[1536,512]{1,0:T(8,128)(2,1)S(1)}, bf16[1536,512]{1,0:T(8,128)(2,1)}, u32[]{:S(2)}, u32[]{:S(2)}) collective-permute-start(bf16[1536,512]{1,0:T(8,128)(2,1)S(1)} %bitcast.34), channel_id=1, source_target_pairs={{2,4},{4,2},{3,5},{5,3},{10,12},{12,10},{11,13},{13,11},{18,20},{2... | collective-permute-start | bytes 4718600 | tf_op jit(solution)/shard_map/ppermute | solution.py:248
  59.1 26.5 %collective-permute-start.17 = (bf16[1024,512]{1,0:T(8,128)(2,1)}, bf16[1024,512]{1,0:T(8,128)(2,1)}, u32[]{:S(2)}, u32[]{:S(2)}) collective-permute-start(bf16[1024,512]{1,0:T(8,128)(2,1)} %pad_maximum_fusion.rest_0_), channel_id=1, source_target_pairs={{0,8},{8,0},{16,24},{24,16},{1,9},{9,1},{17,25},{25,17},{2,10},{10... | collective-permute-start | bytes 3145736 | tf_op jit(solution)/shard_map/ppermute | solution.py:33
  63.3 30.6 %collective-permute-start.9 = (bf16[512,512]{1,0:T(8,128)(2,1)}, bf16[512,512]{1,0:T(8,128)(2,1)}, u32[]{:S(2)}, u32[]{:S(2)}) collective-permute-start(bf16[512,512]{1,0:T(8,128)(2,1)} %slice.94), channel_id=1, source_target_pairs={{0,8},{8,0},{16,24},{24,16},{1,9},{9,1},{17,25},{25,17},{2,10},{10... | collective-permute-start | bytes 1572872 | tf_op jit(solution)/shard_map/ppermute | solution.py:33
  65.6 40.4 %collective-permute-start.6 = (bf16[1024,512]{1,0:T(8,128)(2,1)}, bf16[1024,512]{1,0:T(8,128)(2,1)}, u32[]{:S(2)}, u32[]{:S(2)}) collective-permute-start(bf16[1024,512]{1,0:T(8,128)(2,1)} %collective-permute-done.5.rest_2_), channel_id=1, source_target_pairs={{0,1},{1,0},{2,3},{3,2},{4,5},{5,4},{6,7},{7,6},{8,9},{9,8},{10,11... | collective-permute-start | bytes 3145736 | tf_op jit(solution)/shard_map/ppermute | solution.py:33
  85.6 12.1 %collective-permute-start.10 = (bf16[512,512]{1,0:T(8,128)(2,1)S(1)}, bf16[512,512]{1,0:T(8,128)(2,1)S(1)}, u32[]{:S(2)}, u32[]{:S(2)}) collective-permute-start(bf16[512,512]{1,0:T(8,128)(2,1)S(1)} %slice.95), channel_id=1, source_target_pairs={{0,16},{8,24},{16,0},{24,8},{1,17},{9,25},{17,1},{25,9},{2,18},{10... | collective-permute-start | bytes 1572872 | tf_op jit(solution)/shard_map/ppermute | solution.py:33
  93.9 10.8 %collective-permute-start.21 = (bf16[512,512]{1,0:T(8,128)(2,1)S(1)}, bf16[512,512]{1,0:T(8,128)(2,1)S(1)}, u32[]{:S(2)}, u32[]{:S(2)}) collective-permute-start(bf16[512,512]{1,0:T(8,128)(2,1)S(1)} %slice.98), channel_id=1, source_target_pairs={{0,8},{8,0},{16,24},{24,16},{1,9},{9,1},{17,25},{25,17},{2,10},{10... | collective-permute-start | bytes 1572872 | tf_op jit(solution)/shard_map/ppermute | solution.py:33
  94.3 1.8 copy-start.2
  94.3 11.7 %collective-permute-start.22 = (bf16[512,512]{1,0:T(8,128)(2,1)S(1)}, bf16[512,512]{1,0:T(8,128)(2,1)S(1)}, u32[]{:S(2)}, u32[]{:S(2)}) collective-permute-start(bf16[512,512]{1,0:T(8,128)(2,1)S(1)} %slice.99), channel_id=1, source_target_pairs={{0,16},{8,24},{16,0},{24,8},{1,17},{9,25},{17,1},{25,9},{2,18},{10... | collective-permute-start | bytes 1572872 | tf_op jit(solution)/shard_map/ppermute | solution.py:33
  96.1 10.4 %copy-start.28 = (f32[2]{0:T(128)S(1)}, f32[2]{0:T(128)}, u32[]{:S(2)}) copy-start(f32[2]{0:T(128)} %get-tuple-element.15) | copy-start | bytes 28
  96.1 10.4 %copy-start.29 = (f32[2]{0:T(128)S(1)}, f32[2]{0:T(128)}, u32[]{:S(2)}) copy-start(f32[2]{0:T(128)} %get-tuple-element.16) | copy-start | bytes 28
  96.1 10.4 %copy-start.30 = (f32[2]{0:T(128)S(1)}, f32[2]{0:T(128)}, u32[]{:S(2)}) copy-start(f32[2]{0:T(128)} %get-tuple-element.21) | copy-start | bytes 28
  96.2 10.4 %copy-start.31 = (f32[2]{0:T(128)S(1)}, f32[2]{0:T(128)}, u32[]{:S(2)}) copy-start(f32[2]{0:T(128)} %get-tuple-element.22) | copy-start | bytes 28
  96.2 12.3 %collective-permute-start.8 = (bf16[1024,512]{1,0:T(8,128)(2,1)}, bf16[1024,512]{1,0:T(8,128)(2,1)S(1)}, u32[]{:S(2)}, u32[]{:S(2)}) collective-permute-start(bf16[1024,512]{1,0:T(8,128)(2,1)} %collective-permute-done.7.rest_4_), channel_id=1, source_target_pairs={{0,1},{1,0},{2,3},{3,2},{4,5},{5,4},{6,7},{7,6},{8,9},{9,8},{10,11... | collective-permute-start | bytes 3145736 | tf_op jit(solution)/shard_map/ppermute | solution.py:33
  97.7 10.5 %copy-start.10 = (bf16[512,512]{1,0:T(8,128)(2,1)}, bf16[512,512]{1,0:T(8,128)(2,1)S(1)}, u32[]{:S(2)}) copy-start(bf16[512,512]{1,0:T(8,128)(2,1)S(1)} %collective-permute-done.10.rest_1_) | copy-start | bytes 1572868
  97.8 22.7 %collective-permute-start.13 = (bf16[768,512]{1,0:T(8,128)(2,1)S(1)}, bf16[768,512]{1,0:T(8,128)(2,1)S(1)}, u32[]{:S(2)}, u32[]{:S(2)}) collective-permute-start(bf16[768,512]{1,0:T(8,128)(2,1)S(1)} %get-tuple-element.7), channel_id=1, source_target_pairs={{2,0},{4,6},{3,1},{5,7},{10,8},{12,14},{11,9},{13,15},{18,16},{20,... | collective-permute-start | bytes 2359304 | tf_op jit(solution)/shard_map/ppermute | solution.py:261
  104.7 15.7 %copy-start.6 = (bf16[512,512]{1,0:T(8,128)(2,1)}, bf16[512,512]{1,0:T(8,128)(2,1)S(1)}, u32[]{:S(2)}) copy-start(bf16[512,512]{1,0:T(8,128)(2,1)S(1)} %collective-permute-done.21.rest_0_.rest_7_) | copy-start | bytes 1572868
  104.7 15.7 %collective-permute-start.14 = (bf16[768,512]{1,0:T(8,128)(2,1)S(1)}, bf16[768,512]{1,0:T(8,128)(2,1)S(1)}, u32[]{:S(2)}, u32[]{:S(2)}) collective-permute-start(bf16[768,512]{1,0:T(8,128)(2,1)S(1)} %get-tuple-element.9.a_ref), channel_id=1, source_target_pairs={{2,4},{4,2},{3,5},{5,3},{10,12},{12,10},{11,13},{13,11},{18,20},{2... | collective-permute-start | bytes 2359304 | tf_op jit(solution)/shard_map/ppermute | solution.py:262
  106.0 14.5 %copy-start.8 = (bf16[512,512]{1,0:T(8,128)(2,1)}, bf16[512,512]{1,0:T(8,128)(2,1)S(1)}, u32[]{:S(2)}) copy-start(bf16[512,512]{1,0:T(8,128)(2,1)S(1)} %collective-permute-done.22.rest_1_.rest_8_) | copy-start | bytes 1572868
  106.0 2.7 %collective-permute-start.11 = (bf16[512,512]{1,0:T(8,128)(2,1)}, bf16[512,512]{1,0:T(8,128)(2,1)S(1)}, u32[]{:S(2)}, u32[]{:S(2)}) collective-permute-start(bf16[512,512]{1,0:T(8,128)(2,1)} %collective-permute-done.9.rest_0_), channel_id=1, source_target_pairs={{0,1},{1,0},{2,3},{3,2},{4,5},{5,4},{6,7},{7,6},{8,9},{9,8},{10,11... | collective-permute-start | bytes 1572872 | tf_op jit(solution)/shard_map/ppermute | solution.py:33
  106.0 3.1 %collective-permute-start.12 = (bf16[512,512]{1,0:T(8,128)(2,1)S(1)}, bf16[512,512]{1,0:T(8,128)(2,1)S(1)}, u32[]{:S(2)}, u32[]{:S(2)}) collective-permute-start(bf16[512,512]{1,0:T(8,128)(2,1)S(1)} %collective-permute-done.10.rest_1_), channel_id=1, source_target_pairs={{0,1},{1,0},{2,3},{3,2},{4,5},{5,4},{6,7},{7,6},{8,9},{9,8},{10,11... | collective-permute-start | bytes 1572872 | tf_op jit(solution)/shard_map/ppermute | solution.py:33
  106.9 1.5 copy-start.22
  108.5 32.2 %copy-start.1 = (bf16[8,192,512]{2,1,0:T(8,128)(2,1)S(1)}, bf16[8,192,512]{2,1,0:T(8,128)(2,1)}, u32[]{:S(2)}) copy-start(bf16[8,192,512]{2,1,0:T(8,128)(2,1)} %param.6) | copy-start | bytes 4718596
  108.5 32.2 %copy-start.3 = (bf16[1536,512]{1,0:T(8,128)(2,1)S(1)}, bf16[1536,512]{1,0:T(8,128)(2,1)}, u32[]{:S(2)}) copy-start(bf16[1536,512]{1,0:T(8,128)(2,1)} %copy-done.2) | copy-start | bytes 4718596
  108.5 45.0 %collective-permute-start.16 = (bf16[512,512]{1,0:T(8,128)(2,1)}, bf16[512,512]{1,0:T(8,128)(2,1)}, u32[]{:S(2)}, u32[]{:S(2)}) collective-permute-start(bf16[512,512]{1,0:T(8,128)(2,1)} %collective-permute-done.15), channel_id=1, source_target_pairs={{0,1},{1,0},{2,3},{3,2},{4,5},{5,4},{6,7},{7,6},{8,9},{9,8},{10,11... | collective-permute-start | bytes 1572872 | tf_op jit(solution)/shard_map/ppermute | solution.py:33
  108.7 28.2 %copy-start.12 = (bf16[512,512]{1,0:T(8,128)(2,1)}, bf16[512,512]{1,0:T(8,128)(2,1)S(1)}, u32[]{:S(2)}) copy-start(bf16[512,512]{1,0:T(8,128)(2,1)S(1)} %collective-permute-done.11.rest_2_) | copy-start | bytes 1572868
  108.7 44.9 %collective-permute-start.18 = (bf16[1024,512]{1,0:T(8,128)(2,1)}, bf16[1024,512]{1,0:T(8,128)(2,1)}, u32[]{:S(2)}, u32[]{:S(2)}) collective-permute-start(bf16[1024,512]{1,0:T(8,128)(2,1)} %collective-permute-done.17.rest_3_), channel_id=1, source_target_pairs={{0,1},{1,0},{2,3},{3,2},{4,5},{5,4},{6,7},{7,6},{8,9},{9,8},{10,11... | collective-permute-start | bytes 3145736 | tf_op jit(solution)/shard_map/ppermute | solution.py:33
  109.1 27.7 %copy-start.14 = (bf16[512,512]{1,0:T(8,128)(2,1)}, bf16[512,512]{1,0:T(8,128)(2,1)S(1)}, u32[]{:S(2)}) copy-start(bf16[512,512]{1,0:T(8,128)(2,1)S(1)} %collective-permute-done.12.rest_3_) | copy-start | bytes 1572868
  109.1 44.4 %collective-permute-start.20 = (bf16[1024,512]{1,0:T(8,128)(2,1)}, bf16[1024,512]{1,0:T(8,128)(2,1)}, u32[]{:S(2)}, u32[]{:S(2)}) collective-permute-start(bf16[1024,512]{1,0:T(8,128)(2,1)} %collective-permute-done.19.rest_5_), channel_id=1, source_target_pairs={{0,1},{1,0},{2,3},{3,2},{4,5},{5,4},{6,7},{7,6},{8,9},{9,8},{10,11... | collective-permute-start | bytes 3145736 | tf_op jit(solution)/shard_map/ppermute | solution.py:33
  120.5 16.4 %collective-permute-start.23 = (bf16[512,512]{1,0:T(8,128)(2,1)S(1)}, bf16[512,512]{1,0:T(8,128)(2,1)S(1)}, u32[]{:S(2)}, u32[]{:S(2)}) collective-permute-start(bf16[512,512]{1,0:T(8,128)(2,1)S(1)} %collective-permute-done.21.rest_0_.rest_7_), channel_id=1, source_target_pairs={{0,1},{1,0},{2,3},{3,2},{4,5},{5,4},{6,7},{7,6},{8,9},{9,8},{10,11... | collective-permute-start | bytes 1572872 | tf_op jit(solution)/shard_map/ppermute | solution.py:33
  120.5 18.5 %collective-permute-start.24 = (bf16[512,512]{1,0:T(8,128)(2,1)S(1)}, bf16[512,512]{1,0:T(8,128)(2,1)S(1)}, u32[]{:S(2)}, u32[]{:S(2)}) collective-permute-start(bf16[512,512]{1,0:T(8,128)(2,1)S(1)} %collective-permute-done.22.rest_1_.rest_8_), channel_id=1, source_target_pairs={{0,1},{1,0},{2,3},{3,2},{4,5},{5,4},{6,7},{7,6},{8,9},{9,8},{10,11... | collective-permute-start | bytes 1572872 | tf_op jit(solution)/shard_map/ppermute | solution.py:33
  137.7 26.5 %collective-permute-start.25 = (bf16[768,512]{1,0:T(8,128)(2,1)S(1)}, bf16[768,512]{1,0:T(8,128)(2,1)S(1)}, u32[]{:S(2)}, u32[]{:S(2)}) collective-permute-start(bf16[768,512]{1,0:T(8,128)(2,1)S(1)} %get-tuple-element.8), channel_id=1, source_target_pairs={{2,0},{4,6},{3,1},{5,7},{10,8},{12,14},{11,9},{13,15},{18,16},{20,... | collective-permute-start | bytes 2359304 | tf_op jit(solution)/shard_map/ppermute | solution.py:261
  139.8 10.2 %copy-start.5 = (bf16[4,192,512]{2,1,0:T(8,128)(2,1)S(1)}, bf16[4,192,512]{2,1,0:T(8,128)(2,1)}, u32[]{:S(2)}) copy-start(bf16[4,192,512]{2,1,0:T(8,128)(2,1)} %get-tuple-element.11) | copy-start | bytes 2359300
  139.8 10.2 %copy-start.7 = (bf16[512,512]{1,0:T(8,128)(2,1)S(1)}, bf16[512,512]{1,0:T(8,128)(2,1)}, u32[]{:S(2)}) copy-start(bf16[512,512]{1,0:T(8,128)(2,1)} %copy-done.6) | copy-start | bytes 1572868
  139.8 10.2 %copy-start.9 = (bf16[512,512]{1,0:T(8,128)(2,1)S(1)}, bf16[512,512]{1,0:T(8,128)(2,1)}, u32[]{:S(2)}) copy-start(bf16[512,512]{1,0:T(8,128)(2,1)} %copy-done.8) | copy-start | bytes 1572868
  139.8 24.4 %collective-permute-start.26 = (bf16[768,512]{1,0:T(8,128)(2,1)S(1)}, bf16[768,512]{1,0:T(8,128)(2,1)S(1)}, u32[]{:S(2)}, u32[]{:S(2)}) collective-permute-start(bf16[768,512]{1,0:T(8,128)(2,1)S(1)} %get-tuple-element.10.a_ref), channel_id=1, source_target_pairs={{2,4},{4,2},{3,5},{5,3},{10,12},{12,10},{11,13},{13,11},{18,20},{2... | collective-permute-start | bytes 2359304 | tf_op jit(solution)/shard_map/ppermute | solution.py:262
  140.7 1.0 copy-start.11
  143.8 6.2 %copy-start.17 = (bf16[512,512]{1,0:T(8,128)(2,1)S(1)}, bf16[512,512]{1,0:T(8,128)(2,1)}, u32[]{:S(2)}) copy-start(bf16[512,512]{1,0:T(8,128)(2,1)} %copy-done.16) | copy-start | bytes 1572868
  143.8 6.2 %copy-start.20 = (bf16[512,512]{1,0:T(8,128)(2,1)S(1)}, bf16[512,512]{1,0:T(8,128)(2,1)}, u32[]{:S(2)}) copy-start(bf16[512,512]{1,0:T(8,128)(2,1)} %copy-done.19) | copy-start | bytes 1572868
  153.5 10.7 %copy-start.4 = (bf16[4,192,512]{2,1,0:T(8,128)(2,1)S(1)}, bf16[4,192,512]{2,1,0:T(8,128)(2,1)}, u32[]{:S(2)}) copy-start(bf16[4,192,512]{2,1,0:T(8,128)(2,1)} %get-tuple-element.12) | copy-start | bytes 2359300
  153.5 10.7 %copy-start.18 = (bf16[512,512]{1,0:T(8,128)(2,1)S(1)}, bf16[512,512]{1,0:T(8,128)(2,1)}, u32[]{:S(2)}) copy-start(bf16[512,512]{1,0:T(8,128)(2,1)} %copy-done.16) | copy-start | bytes 1572868
  153.5 10.7 %copy-start.21 = (bf16[512,512]{1,0:T(8,128)(2,1)S(1)}, bf16[512,512]{1,0:T(8,128)(2,1)}, u32[]{:S(2)}) copy-start(bf16[512,512]{1,0:T(8,128)(2,1)} %copy-done.19) | copy-start | bytes 1572868
  177.7 3.7 %collective-permute-start.28 = (f32[8,256]{1,0:T(8,128)S(1)}, f32[8,256]{1,0:T(8,128)S(1)}, u32[]{:S(2)}, u32[]{:S(2)}) collective-permute-start(f32[8,256]{1,0:T(8,128)S(1)} %fusion), channel_id=1, source_target_pairs={{0,16},{8,24},{16,0},{24,8},{1,17},{9,25},{17,1},{25,9},{2,18},{10... | collective-permute-start | bytes 24584 | tf_op jit(solution)/shard_map/ppermute | solution.py:33
  178.8 4.6 %collective-permute-start.29 = (f32[8,256]{1,0:T(8,128)S(1)}, f32[8,256]{1,0:T(8,128)S(1)}, u32[]{:S(2)}, u32[]{:S(2)}) collective-permute-start(f32[8,256]{1,0:T(8,128)S(1)} %fusion), channel_id=1, source_target_pairs={{0,24},{8,16},{16,8},{24,0},{1,25},{9,17},{17,9},{25,1},{2,26},{10... | collective-permute-start | bytes 24584 | tf_op jit(solution)/shard_map/ppermute | solution.py:33
  180.7 3.7 %collective-permute-start.27 = (f32[8,256]{1,0:T(8,128)S(1)}, f32[8,256]{1,0:T(8,128)S(1)}, u32[]{:S(2)}, u32[]{:S(2)}) collective-permute-start(f32[8,256]{1,0:T(8,128)S(1)} %fusion), channel_id=1, source_target_pairs={{0,8},{8,0},{16,24},{24,16},{1,9},{9,1},{17,25},{25,17},{2,10},{10... | collective-permute-start | bytes 24584 | tf_op jit(solution)/shard_map/ppermute | solution.py:33
  184.4 8.6 %collective-permute-start.31 = (f32[8,256]{1,0:T(8,128)S(1)}, f32[8,256]{1,0:T(8,128)S(1)}, u32[]{:S(2)}, u32[]{:S(2)}) collective-permute-start(f32[8,256]{1,0:T(8,128)S(1)} %add_add_fusion.1), channel_id=1, source_target_pairs={{0,4},{2,6},{4,0},{6,2},{1,5},{3,7},{5,1},{7,3},{8,12},{10,14},{12... | collective-permute-start | bytes 24584 | tf_op jit(solution)/shard_map/ppermute | solution.py:33
  190.4 5.4 %collective-permute-start.32 = (f32[8,256]{1,0:T(8,128)S(1)}, f32[8,256]{1,0:T(8,128)S(1)}, u32[]{:S(2)}, u32[]{:S(2)}) collective-permute-start(f32[8,256]{1,0:T(8,128)S(1)} %add_add_fusion.1), channel_id=1, source_target_pairs={{0,6},{2,4},{4,2},{6,0},{1,7},{3,5},{5,3},{7,1},{8,14},{10,12},{12... | collective-permute-start | bytes 24584 | tf_op jit(solution)/shard_map/ppermute | solution.py:33
  193.0 3.7 %collective-permute-start.30 = (f32[8,256]{1,0:T(8,128)S(1)}, f32[8,256]{1,0:T(8,128)S(1)}, u32[]{:S(2)}, u32[]{:S(2)}) collective-permute-start(f32[8,256]{1,0:T(8,128)S(1)} %add_add_fusion.1), channel_id=1, source_target_pairs={{0,2},{2,0},{4,6},{6,4},{1,3},{3,1},{5,7},{7,5},{8,10},{10,8},{12,... | collective-permute-start | bytes 24584 | tf_op jit(solution)/shard_map/ppermute | solution.py:33
  (4 other events, 3.7 us)

commit v2 on v0

v2 whole, which is shorter than its diff:
```python
import functools
import math

import jax
import jax.numpy as jnp
from jax import lax
from jax.experimental import pallas as pl
from jax.experimental.pallas import tpu as pltpu
from jax.sharding import PartitionSpec as P

NW = 256

omega_low = -10.0
omega_span = 20.0


def make_grid(count):
    return omega_low + omega_span * jnp.arange(count, dtype=jnp.float32) / (count - 1)


def lookup(indices, table):
    hit = indices[:, None] == jnp.arange(table.shape[0], dtype=jnp.int32)[None, :]
    return jnp.sum(jnp.where(hit, table[None, :], 0.0), axis=1)


def from_behind(block, axis, distance):
    devices = range(lax.axis_size(axis))
    route = [((i - distance) % len(devices), i) for i in devices]
    return lax.ppermute(block, axis, route)


def flip(block, axis, bits):
    return lax.ppermute(block, axis, [(i, i ^ bits) for i in range(lax.axis_size(axis))])


def contribute(full_rows, panel_rows, w_mat, nu_val, weight_val, energies, omega_grid, n_dev):
    product = jnp.dot(full_rows, w_mat, preferred_element_type=jnp.float32)
    contract = jnp.sum(product * panel_rows.astype(jnp.float32), axis=-1).reshape(n_dev, -1)
    offsets = omega_grid[None, :] - energies[:, None]
    kernel = offsets / (offsets * offsets + nu_val * nu_val)
    return -weight_val / math.pi * jnp.dot(contract, kernel, precision=lax.Precision.HIGHEST)


def general(pair_matrix, screened, imag_freq, quad_weight, band_energy, band_index):
    n_dev, m_dev, g_panel = pair_matrix.shape
    f_dev = screened.shape[0]
    cycle_size = lax.axis_size("freq")
    cycle_pos = lax.axis_index("freq")
    full_pairs = lax.all_gather(pair_matrix, "ga", axis=2, tiled=True)
    g_all = full_pairs.shape[2]
    omega_grid = make_grid(NW)
    sigma_part = jnp.zeros((n_dev, NW), jnp.float32)
    panel_rows = pair_matrix.reshape(n_dev * m_dev, g_panel)
    full_rows = full_pairs.reshape(n_dev * m_dev, g_all)
    energies = lookup(band_index, band_energy)
    nu_all = lax.all_gather(imag_freq, "freq", axis=0, tiled=True)
    weight_all = lax.all_gather(quad_weight, "freq", axis=0, tiled=True)
    w_slab = screened
    for turn_index in range(cycle_size):
        source = jnp.mod(cycle_pos - turn_index, cycle_size)
        nu_vals = lax.dynamic_slice_in_dim(nu_all, source * f_dev, f_dev)
        weight_vals = lax.dynamic_slice_in_dim(weight_all, source * f_dev, f_dev)
        for slot in range(f_dev):
            sigma_part = sigma_part + contribute(
                full_rows, panel_rows, w_slab[slot], nu_vals[slot], weight_vals[slot],
                energies, omega_grid, n_dev,
            )
        if turn_index + 1 < cycle_size:
            w_slab = from_behind(w_slab, "freq", 1)
    return lax.psum(sigma_part, ("freq", "ga"))


def accumulate(contract, weight_ref, slot, out_ref, first, m_dev):
    for k in range(contract.shape[0] // m_dev):
        rows = contract[k * m_dev : (k + 1) * m_dev]
        term = rows * weight_ref[slot]
        out_ref[first + k] += jnp.sum(term.reshape(m_dev // 8, 8, NW), axis=0)


def choose(flag, yes, no):
    @pl.when(flag == 1)
    def _():
        yes.start()

    @pl.when(flag == 0)
    def _():
        no.start()


def near_kernel(tile, m_dev, where_ref, k_ref, own_ref, a_ref, b_ref, w_ref, out_ref, left, own, w_all, k_all, sems, w_sems):
    n_slots, depth, panel = w_all.shape
    end, low = where_ref[0], where_ref[1]
    here = left.at[:, pl.ds(pl.multiple_of((1 - low) * panel, panel), panel)]
    there = left.at[:, pl.ds(pl.multiple_of(low * panel, panel), panel)]
    waits = [
        pltpu.make_async_copy(own_ref, own, sems.at[0]),
        pltpu.make_async_copy(own_ref, here, sems.at[1]),
        pltpu.make_async_copy(k_ref, k_all, sems.at[3]),
    ]
    for c in waits:
        c.start()
    near = pltpu.make_async_copy(a_ref, there, sems.at[2])
    choose(end, near, pltpu.make_async_copy(b_ref, there, sems.at[2]))
    slots = [pltpu.make_async_copy(w_ref.at[s, :depth, :], w_all.at[s], w_sems.at[s]) for s in range(n_slots)]
    for c in slots:
        c.start()
    out_ref[...] = jnp.zeros_like(out_ref)
    for c in waits + [near]:
        c.wait()

    def one(slot, carry):
        pltpu.make_async_copy(w_all.at[slot], w_all.at[slot], w_sems.at[slot]).wait()
        for t in range(own.shape[0] // tile):
            at = slice(t * tile, (t + 1) * tile)
            y = jnp.dot(left[at], w_all[slot], preferred_element_type=jnp.float32)
            c = jnp.sum(y * own[at].astype(jnp.float32), axis=1, keepdims=True)
            accumulate(c, k_all, slot, out_ref, t * (tile // m_dev), m_dev)
        return carry

    lax.fori_loop(0, n_slots, one, 0)


def far_kernel(tile, m_dev, begin, where_ref, k_ref, own_ref, a_ref, c_ref, d_ref, w_ref, out_ref, own, far, other, left, w_all, k_all, sems, w_sems):
    n_slots, _, panel = w_all.shape
    end = where_ref[0]
    mine = own_ref.at[begin : begin + own.shape[0], :]
    theirs = a_ref.at[begin : begin + own.shape[0], :]
    waits = [
        pltpu.make_async_copy(mine, own, sems.at[0]),
        pltpu.make_async_copy(theirs, other, sems.at[1]),
        pltpu.make_async_copy(k_ref, k_all, sems.at[4]),
    ]
    for c in waits:
        c.start()
    far_copy = pltpu.make_async_copy(c_ref, far, sems.at[2])
    choose(end, far_copy, pltpu.make_async_copy(d_ref, far, sems.at[2]))
    left_copy = pltpu.make_async_copy(mine, left, sems.at[3])
    choose(end, left_copy, pltpu.make_async_copy(d_ref, left, sems.at[3]))
    slots = [pltpu.make_async_copy(w_ref.at[s], w_all.at[s], w_sems.at[s]) for s in range(n_slots)]
    for c in slots:
        c.start()
    out_ref[...] = jnp.zeros_like(out_ref)
    for c in waits + [far_copy, left_copy]:
        c.wait()

    def one(slot, carry):
        pltpu.make_async_copy(w_all.at[slot], w_all.at[slot], w_sems.at[slot]).wait()
        for t in range(own.shape[0] // tile):
            at = slice(t * tile, (t + 1) * tile)
            y = jnp.dot(far[at], w_all[slot, :panel], preferred_element_type=jnp.float32)
            z = y * own[at].astype(jnp.float32)
            x = jnp.dot(left[at], w_all[slot, panel:], preferred_element_type=jnp.float32)
            z = z + x * other[at].astype(jnp.float32)
            c = jnp.sum(z, axis=1, keepdims=True)
            accumulate(c, k_all, slot, out_ref, t * (tile // m_dev), m_dev)
        return carry

    lax.fori_loop(0, n_slots, one, 0)


def run_kernel(body, where, k_part, mats, w_set, n_rows, m_dev, n_lefts, wide):
    panel = mats[0].shape[1]
    n_slots, depth = k_part.shape[0], 2 * panel
    n_states = n_rows // m_dev
    scratch = [pltpu.VMEM((n_rows, panel * wide), jnp.bfloat16)]
    scratch += [pltpu.VMEM((n_rows, panel), jnp.bfloat16)] * (n_lefts - 1)
    scratch += [
        pltpu.VMEM((n_slots, depth, panel), jnp.bfloat16),
        pltpu.VMEM(k_part.shape, jnp.float32),
        pltpu.SemaphoreType.DMA((5,)),
        pltpu.SemaphoreType.DMA((n_slots,)),
    ]
    flops = 2 * n_rows * depth * panel * n_slots
    return pl.pallas_call(
        body,
        out_shape=jax.ShapeDtypeStruct((n_states, 8, NW), jnp.float32),
        in_specs=[pl.BlockSpec(memory_space=pltpu.SMEM)]
        + [pl.BlockSpec(memory_space=pl.ANY)] * (2 + len(mats)),
        out_specs=pl.BlockSpec(memory_space=pltpu.VMEM),
        scratch_shapes=scratch,
        cost_estimate=pl.CostEstimate(flops=flops, bytes_accessed=n_slots * depth * panel * 2, transcendentals=0),
        compiler_params=pltpu.CompilerParams(vmem_limit_bytes=48 * 2**20),
    )(where, k_part, *mats, w_set)


def split3(x):
    hi = lax.reduce_precision(x, 8, 7)
    mid = lax.reduce_precision(x - hi, 8, 7)
    return jnp.stack([hi, mid, (x - hi) - mid])


def square_line(pair_matrix, screened, imag_freq, quad_weight, band_energy, band_index):
    n_dev, m_dev, panel = pair_matrix.shape
    ga = lax.axis_index("ga")
    core = lax.axis_index("band")
    rows = n_dev * m_dev
    own = pair_matrix.reshape(rows, panel)
    end = (ga == 0) | (ga == 3)
    low = ga < 2
    near_at = jnp.where(ga == 0, 0, jnp.where(ga == 3, 2, 1)) * panel
    far_at = (ga + 2) % 4 * panel
    give_at = jnp.where(ga % 2 == 0, 3, 0) * panel
    where = jnp.stack([end, low]).astype(jnp.int32)

    outer = [(0, 1), (1, 0), (2, 3), (3, 2)]
    inner = [(1, 2), (2, 1)]
    outward = [(1, 0), (2, 3)]

    def piece(start, count):
        return lax.dynamic_slice(screened, (core, start, 0), (1, count, panel))[0]

    given = lax.ppermute(piece(give_at, panel), "ga", outer)
    node = split3(jnp.stack([imag_freq[core], quad_weight[core]])).reshape(1, 6)
    node = jnp.pad(node, ((0, 15), (0, panel - 6))).astype(jnp.bfloat16)
    near_w = jnp.concatenate([piece(near_at, 2 * panel), node])
    near_all = lax.all_gather(near_w, ("freq", "band"))
    a_rows = lax.ppermute(own, "ga", outer)
    b_rows = lax.ppermute(own, "ga", inner)
    far_w = jnp.concatenate([piece(far_at, panel), given])
    far_all = lax.all_gather(far_w, ("freq", "band"))
    half = rows // 2
    begins = (0, half)
    c_rows = [lax.ppermute(b_rows[i : i + half], "ga", outward) for i in begins]
    d_rows = [lax.ppermute(a_rows[i : i + half], "ga", inner) for i in begins]

    energies = lookup(band_index, band_energy)
    offsets = make_grid(NW)[None, :] - energies[:, None]
    nodes = near_all[:, 2 * panel, :6].astype(jnp.float32).reshape(-1, 3, 2)
    nodes = (nodes[:, 0] + nodes[:, 1]) + nodes[:, 2]
    nu, weight = nodes[:, 0, None, None], nodes[:, 1, None, None]
    k_all = (-weight / math.pi) * (offsets / (offsets * offsets + nu * nu))

    tile = 4 * m_dev
    near = run_kernel(
        functools.partial(near_kernel, tile, m_dev),
        where, k_all, (own, a_rows, b_rows), near_all, rows, m_dev, 2, 2,
    )
    parts = [
        run_kernel(
            functools.partial(far_kernel, tile, m_dev, i),
            where, k_all, (own, a_rows, c_rows[n], d_rows[n]), far_all, half, m_dev, 4, 1,
        )
        for n, i in enumerate(begins)
    ]
    sigma = jnp.sum(near + jnp.concatenate(parts), axis=1)
    for axis in ("freq", "ga"):
        t1, t2, t3 = (flip(sigma, axis, r) for r in (1, 2, 3))
        sigma = (sigma + t1) + (t2 + t3)
    return sigma


def on_device(pair_matrix, screened, *rest):
    sizes = tuple(lax.axis_size(a) for a in ("freq", "ga", "band"))
    fits = sizes == (4, 4, 2) and screened.shape[0] == 2 and pair_matrix.shape[0] % 8 == 0
    return (square_line if fits else general)(pair_matrix, screened, *rest)


def solution(mesh):
    placed = (P("band", "freq", "ga"), P("freq", None, "ga"), P("freq"), P("freq"), P(), P("freq"))
    return jax.shard_map(
        on_device, mesh=mesh, in_specs=placed, out_specs=P("band", None), check_vma=False
    )
```

time: 379 us -> 179 us (0.47)
  blocking collectives: 133 us -> 0 us
  waiting for transfers between devices: 140 us -> 79.4 us
  matrix products: 56.8 us -> 0 us
  Pallas kernels: 0 us -> 41.7 us
  starting transfers between devices: 5.41 us -> 25.7 us
  between operations: 30 us -> 13.6 us
    ppermute x3 -> x13, waiting for transfers between devices: 139 us -> 48 us  [the longest x1 29 us: square_line(): a_rows = lax.ppermute(own, 'ga', outer)]
    unnamed x1 -> x0, blocking collectives: 90.8 us -> none
    dot_general x17 -> x0, matrix products: 56.8 us -> none  [the longest x8 54.3 us: contribute(): product = jnp.dot(full_rows, w_mat, preferred_element_type=jnp.float32)]
    psum x1 -> x0, blocking collectives: 42.2 us -> none  [on_device(): sigma = lax.psum(sigma_part, ('freq', 'ga'))]
    pallas_call x0 -> x3, Pallas kernels: none -> 41.7 us  [run_kernel(): pl.pallas_call(body, out_shape=jax.ShapeDtypeStruct((n_states, 8, NW), jn...]
    all_gather x1 -> x2, waiting for transfers between devices: 0.01 us -> 31.3 us  [the longest x1 31.3 us: square_line(): far_all = lax.all_gather(far_w, ('freq', 'band'))]
    ppermute x3 -> x13, starting transfers between devices: 5.41 us -> 25.7 us  [the longest x6 11.7 us: flip(): lax.ppermute(block, axis, [(i, i ^ bits) for i in range(lax.axis_size(axi...]
  transfers between devices with their start and end apart: 4 -> 15, of which waited for: 2 -> 8; matrix products, arithmetic and copies ran while one was open for 14% -> 4% of each run, Pallas kernels for 0% -> 17%
where the time goes in v2:
time: 179 us
  waiting for transfers between devices  79.4 us (44%)
  Pallas kernels  41.7 us (23%)
  starting transfers between devices  25.7 us (14%)
  between operations  13.6 us (8%)
  local copies, waits for them, and re-layouts  12.8 us (7%)
  other arithmetic  5.58 us (3%)
    pallas_call x3, Pallas kernels, run_kernel(): pl.pallas_call(body, out_shape=jax.ShapeDtypeStruct((n_states, 8, NW), jn...  41.7 us
    all_gather x1, waiting for transfers between devices, square_line(): far_all = lax.all_gather(far_w, ('freq', 'band'))  31.3 us
    ppermute x1, waiting for transfers between devices, square_line(): a_rows = lax.ppermute(own, 'ga', outer)  29 us
    ppermute x1, waiting for transfers between devices, square_line(): given = lax.ppermute(piece(give_at, panel), 'ga', outer)  11.9 us
    ppermute x6, starting transfers between devices, flip(): lax.ppermute(block, axis, [(i, i ^ bits) for i in range(lax.axis_size(axi...  11.7 us
    ppermute x6, waiting for transfers between devices, flip(): lax.ppermute(block, axis, [(i, i ^ bits) for i in range(lax.axis_size(axi...  7.1 us
  transfers between devices with their start and end apart: 15, of which 8 were waited for; matrix products, arithmetic and copies ran while one was open for 4% of the time, Pallas kernels for 17%

profile of v2, /device:TPU:0, one launch (start us, length us, event | category | flops | bytes accessed | tf_op | source)
XLA Modules:
  0.0 178.8 jit_solution(14019444270859218408)
XLA Ops:
  6.5 0.0 all-gather.5.cloned.1.call-start
  6.5 1.2 dynamic_slice.17
  7.8 1.3 dynamic_slice.16
  9.1 1.4 reduce-precision_convert_fusion.1
  10.5 0.1 reshape.174
  10.6 1.3 dynamic-slice_bitcast_fusion
  11.9 1.0 fusion.1
  12.9 0.0 all-gather.5.cloned.1.call-update
  12.9 0.0 all-gather.7.cloned.1.call-start
  13.0 1.3 dynamic-slice_bitcast_fusion.2
  14.3 3.1 %collective-permute-start.4 = (bf16[512,512]{1,0:T(8,128)(2,1)S(1)}, bf16[512,512]{1,0:T(8,128)(2,1)S(1)}, u32[]{:S(2)}, u32[]{:S(2)}) collective-permute-start(bf16[512,512]{1,0:T(8,128)(2,1)S(1)} %get-tuple-element.8), channel_id=1, source_target_pairs={{0,2},{2,0},{4,6},{6,4},{1,3},{3,1},{5,7},{7,5},{8,10},{10,8},{12,... | collective-permute-start | bytes 1572872 | tf_op jit(solution)/shard_map/ppermute | solution.py:212
  17.4 11.9 %collective-permute-done.4 = bf16[512,512]{1,0:T(8,128)(2,1)S(1)} collective-permute-done((bf16[512,512]{1,0:T(8,128)(2,1)S(1)}, bf16[512,512]{1,0:T(8,128)(2,1)S(1)}, u32[]{:S(2)}, u32[]{:S(2)}) %collective-permute-start.4) | collective-permute-done | bytes 524320 | tf_op jit(solution)/shard_map/ppermute | solution.py:212
  29.3 0.0 copy-start.1
  29.3 0.0 copy-start.5
  29.3 0.0 copy-start.6
  29.3 1.1 pad_maximum_fusion
  30.4 0.0 all-gather.7.cloned.1.call-update
  30.4 0.7 copy-done.1
  31.1 1.8 %collective-permute-start.1 = (bf16[1536,512]{1,0:T(8,128)(2,1)S(1)}, bf16[1536,512]{1,0:T(8,128)(2,1)}, u32[]{:S(2)}, u32[]{:S(2)}) collective-permute-start(bf16[1536,512]{1,0:T(8,128)(2,1)S(1)} %bitcast.21), channel_id=1, source_target_pairs={{2,4},{4,2},{3,5},{5,3},{10,12},{12,10},{11,13},{13,11},{18,20},{2... | collective-permute-start | bytes 4718600 | tf_op jit(solution)/shard_map/ppermute | solution.py:218
  32.9 3.5 %collective-permute-start = (bf16[1536,512]{1,0:T(8,128)(2,1)S(1)}, bf16[1536,512]{1,0:T(8,128)(2,1)S(1)}, u32[]{:S(2)}, u32[]{:S(2)}) collective-permute-start(bf16[1536,512]{1,0:T(8,128)(2,1)S(1)} %bitcast.22), channel_id=1, source_target_pairs={{0,2},{2,0},{4,6},{6,4},{1,3},{3,1},{5,7},{7,5},{8,10},{10,8},{12,... | collective-permute-start | bytes 4718600 | tf_op jit(solution)/shard_map/ppermute | solution.py:217
  36.4 0.1 add_convert_fusion.where_ref
  36.5 0.0 copy-done.5
  36.5 0.0 copy-done.6
  36.5 0.2 select_reduce_fusion
  36.7 0.1 broadcast_subtract_fusion
  36.8 0.0 collective-permute-done.1.b_ref
  36.8 2.7 %fusion.7 = (bf16[768,512]{1,0:T(8,128)(2,1)}, bf16[768,512]{1,0:T(8,128)(2,1)}) fusion(bf16[1536,512]{1,0:T(8,128)(2,1)} %collective-permute-done.1.b_ref), kind=kLoop, calls=%fused_computation.32 | loop fusion | bytes 3145728 | tf_op jit(solution)/shard_map/slice | solution.py:223
  39.4 1.3 collective-permute-start.5
  40.7 29.0 %collective-permute-done.a_ref = bf16[1536,512]{1,0:T(8,128)(2,1)S(1)} collective-permute-done((bf16[1536,512]{1,0:T(8,128)(2,1)S(1)}, bf16[1536,512]{1,0:T(8,128)(2,1)S(1)}, u32[]{:S(2)}, u32[]{:S(2)}) %collective-permute-start) | collective-permute-done | bytes 1572896 | tf_op jit(solution)/shard_map/ppermute | solution.py:217
  69.7 0.0 copy-start
  69.7 1.3 fusion.6
  71.1 1.5 collective-permute-start.6
  72.6 1.3 collective-permute-start.2
  73.9 1.6 collective-permute-start.3
  75.5 0.0 all-gather.5.cloned.1.call-done
  75.5 0.7 slice_convert_fusion
  76.2 0.1 copy.10
  76.3 0.3 divide_multiply_fusion.k_ref
  76.6 0.0 copy-done
  76.6 0.0 copy-start.2
  76.6 1.4 copy-done.2
  78.0 17.7 %shard_map.64 = f32[8,8,256]{2,1,0:T(8,128)S(1)} custom-call(s32[2]{0:T(128)S(1)} %add_convert_fusion.where_ref, f32[8,192,256]{2,1,0:T(8,128)S(1)} %divide_multiply_fusion.k_ref, bf16[1536,512]{1,0:T(8,128)(2,1)S(1)} %bitcast.23, bf16[1536,512]{1,0:T(8,128)(2,1)S(1)} %collective-permute-done.a_ref, bf16[1536,512]{1,0:T(8,128)(2,1)} %collective-permute-done.1.b_ref, ...), custom_call_target="tpu_custom_call" | custom-call | flops 12884901888 | bytes 8388608 | tf_op jit(solution)/shard_map/pallas_call | solution.py:174
  95.7 0.0 collective-permute-done.5.c_ref
  95.7 0.0 collective-permute-done.6.d_ref
  95.7 31.3 %all-gather.7.cloned.1.call-done = bf16[8192,512]{1,0:T(8,128)(2,1)} async-done(((bf16[1024,512]{1,0:T(8,128)(2,1)}), bf16[8192,512]{1,0:T(8,128)(2,1)}) %all-gather.7.cloned.1.call-update) | async-done | bytes 8388624 | tf_op jit(solution)/shard_map/all_gather | solution.py:220
  127.1 1.4 copy-done.3
  128.5 12.0 %shard_map.66 = f32[4,8,256]{2,1,0:T(8,128)S(1)} custom-call(s32[2]{0:T(128)S(1)} %add_convert_fusion.where_ref, f32[8,192,256]{2,1,0:T(8,128)S(1)} %divide_multiply_fusion.k_ref, bf16[1536,512]{1,0:T(8,128)(2,1)S(1)} %bitcast.24, bf16[1536,512]{1,0:T(8,128)(2,1)} %copy-done, bf16[768,512]{1,0:T(8,128)(2,1)} %collective-permute-done.5.c_ref, ...), custom_call_target="tpu_custom_call" | custom-call | flops 6442450944 | bytes 8388608 | tf_op jit(solution)/shard_map/pallas_call | solution.py:174
  140.5 0.0 collective-permute-done.2.c_ref
  140.5 0.0 collective-permute-done.3.d_ref
  140.5 0.0 copy-done.4
  140.5 12.0 %shard_map.65 = f32[4,8,256]{2,1,0:T(8,128)S(1)} custom-call(s32[2]{0:T(128)S(1)} %add_convert_fusion.where_ref, f32[8,192,256]{2,1,0:T(8,128)S(1)} %divide_multiply_fusion.k_ref, bf16[1536,512]{1,0:T(8,128)(2,1)S(1)} %bitcast.25, bf16[1536,512]{1,0:T(8,128)(2,1)} %copy-done, bf16[768,512]{1,0:T(8,128)(2,1)} %collective-permute-done.2.c_ref, ...), custom_call_target="tpu_custom_call" | custom-call | flops 6442450944 | bytes 8388608 | tf_op jit(solution)/shard_map/pallas_call | solution.py:174
  152.6 1.2 collective-permute-start.8
  153.8 1.8 %collective-permute-start.9 = (f32[8,256]{1,0:T(8,128)S(1)}, f32[8,256]{1,0:T(8,128)S(1)}, u32[]{:S(2)}, u32[]{:S(2)}) collective-permute-start(f32[8,256]{1,0:T(8,128)S(1)} %fusion.2), channel_id=1, source_target_pairs={{0,24},{8,16},{16,8},{24,0},{1,25},{9,17},{17,9},{25,1},{2,26},{10... | collective-permute-start | bytes 24584 | tf_op jit(solution)/shard_map/ppermute | solution.py:33
  155.6 0.6 collective-permute-start.7
  156.1 0.2 collective-permute-done.8
  156.3 2.0 %collective-permute-done.9 = f32[8,256]{1,0:T(8,128)S(1)} collective-permute-done((f32[8,256]{1,0:T(8,128)S(1)}, f32[8,256]{1,0:T(8,128)S(1)}, u32[]{:S(2)}, u32[]{:S(2)}) %collective-permute-start.9) | collective-permute-done | bytes 8224 | tf_op jit(solution)/shard_map/ppermute | solution.py:33
  158.3 0.9 collective-permute-done.7
  159.2 6.7 %collective-permute-start.11 = (f32[8,256]{1,0:T(8,128)S(1)}, f32[8,256]{1,0:T(8,128)S(1)}, u32[]{:S(2)}, u32[]{:S(2)}) collective-permute-start(f32[8,256]{1,0:T(8,128)S(1)} %add_add_fusion.1), channel_id=1, source_target_pairs={{0,4},{2,6},{4,0},{6,2},{1,5},{3,7},{5,1},{7,3},{8,12},{10,14},{12... | collective-permute-start | bytes 24584 | tf_op jit(solution)/shard_map/ppermute | solution.py:33
  165.9 1.4 collective-permute-start.12
  167.3 0.0 collective-permute-start.10
  167.3 0.2 collective-permute-done.11
  167.5 3.8 %collective-permute-done.12 = f32[8,256]{1,0:T(8,128)S(1)} collective-permute-done((f32[8,256]{1,0:T(8,128)S(1)}, f32[8,256]{1,0:T(8,128)S(1)}, u32[]{:S(2)}, u32[]{:S(2)}) %collective-permute-start.12) | collective-permute-done | bytes 8224 | tf_op jit(solution)/shard_map/ppermute | solution.py:33
  171.3 0.0 collective-permute-done.10
  171.3 0.6 add_add_fusion
  (10 shorter events, 0.1 us)
Async XLA Ops:
  6.5 68.9 %all-gather.5.cloned.1.call-start = ((), (), s32[]{:S(2)}) async-start(), calls=%async_computation | async-start | bytes 9584640 | tf_op jit(solution)/shard_map/all_gather | solution.py:216
  12.9 114.1 %all-gather.7.cloned.1.call-start = ((), (), s32[]{:S(2)}) async-start(), calls=%async_computation.1 | async-start | bytes 9437184 | tf_op jit(solution)/shard_map/all_gather | solution.py:220
  14.3 15.0 %collective-permute-start.4 = (bf16[512,512]{1,0:T(8,128)(2,1)S(1)}, bf16[512,512]{1,0:T(8,128)(2,1)S(1)}, u32[]{:S(2)}, u32[]{:S(2)}) collective-permute-start(bf16[512,512]{1,0:T(8,128)(2,1)S(1)} %get-tuple-element.8), channel_id=1, source_target_pairs={{0,2},{2,0},{4,6},{6,4},{1,3},{3,1},{5,7},{7,5},{8,10},{10,8},{12,... | collective-permute-start | bytes 1572872 | tf_op jit(solution)/shard_map/ppermute | solution.py:212
  29.3 1.8 copy-start.1
  29.3 7.2 %copy-start.5 = (f32[256]{0:T(256)S(1)}, f32[256]{0:T(256)}, u32[]{:S(2)}) copy-start(f32[256]{0:T(256)} %param.10) | copy-start | bytes 3076
  29.3 7.2 %copy-start.6 = (s32[192]{0:T(256)S(1)}, s32[192]{0:T(256)}, u32[]{:S(2)}) copy-start(s32[192]{0:T(256)} %param.11) | copy-start | bytes 2308
  31.1 5.7 %collective-permute-start.1 = (bf16[1536,512]{1,0:T(8,128)(2,1)S(1)}, bf16[1536,512]{1,0:T(8,128)(2,1)}, u32[]{:S(2)}, u32[]{:S(2)}) collective-permute-start(bf16[1536,512]{1,0:T(8,128)(2,1)S(1)} %bitcast.21), channel_id=1, source_target_pairs={{2,4},{4,2},{3,5},{5,3},{10,12},{12,10},{11,13},{13,11},{18,20},{2... | collective-permute-start | bytes 4718600 | tf_op jit(solution)/shard_map/ppermute | solution.py:218
  32.9 36.8 %collective-permute-start = (bf16[1536,512]{1,0:T(8,128)(2,1)S(1)}, bf16[1536,512]{1,0:T(8,128)(2,1)S(1)}, u32[]{:S(2)}, u32[]{:S(2)}) collective-permute-start(bf16[1536,512]{1,0:T(8,128)(2,1)S(1)} %bitcast.22), channel_id=1, source_target_pairs={{0,2},{2,0},{4,6},{6,4},{1,3},{3,1},{5,7},{7,5},{8,10},{10,8},{12,... | collective-permute-start | bytes 4718600 | tf_op jit(solution)/shard_map/ppermute | solution.py:217
  39.4 56.3 %collective-permute-start.5 = (bf16[768,512]{1,0:T(8,128)(2,1)}, bf16[768,512]{1,0:T(8,128)(2,1)}, u32[]{:S(2)}, u32[]{:S(2)}) collective-permute-start(bf16[768,512]{1,0:T(8,128)(2,1)} %get-tuple-element.12), channel_id=1, source_target_pairs={{2,0},{4,6},{3,1},{5,7},{10,8},{12,14},{11,9},{13,15},{18,16},{20,... | collective-permute-start | bytes 2359304 | tf_op jit(solution)/shard_map/ppermute | solution.py:223
  69.7 6.9 %copy-start = (bf16[1536,512]{1,0:T(8,128)(2,1)}, bf16[1536,512]{1,0:T(8,128)(2,1)S(1)}, u32[]{:S(2)}) copy-start(bf16[1536,512]{1,0:T(8,128)(2,1)S(1)} %collective-permute-done.a_ref) | copy-start | bytes 4718596
  71.1 24.6 %collective-permute-start.6 = (bf16[768,512]{1,0:T(8,128)(2,1)}, bf16[768,512]{1,0:T(8,128)(2,1)}, u32[]{:S(2)}, u32[]{:S(2)}) collective-permute-start(bf16[768,512]{1,0:T(8,128)(2,1)} %get-tuple-element.10), channel_id=1, source_target_pairs={{2,4},{4,2},{3,5},{5,3},{10,12},{12,10},{11,13},{13,11},{18,20},{2... | collective-permute-start | bytes 2359304 | tf_op jit(solution)/shard_map/ppermute | solution.py:224
  72.6 67.9 %collective-permute-start.2 = (bf16[768,512]{1,0:T(8,128)(2,1)}, bf16[768,512]{1,0:T(8,128)(2,1)}, u32[]{:S(2)}, u32[]{:S(2)}) collective-permute-start(bf16[768,512]{1,0:T(8,128)(2,1)} %get-tuple-element.11), channel_id=1, source_target_pairs={{2,0},{4,6},{3,1},{5,7},{10,8},{12,14},{11,9},{13,15},{18,16},{20,... | collective-permute-start | bytes 2359304 | tf_op jit(solution)/shard_map/ppermute | solution.py:223
  73.9 66.6 %collective-permute-start.3 = (bf16[768,512]{1,0:T(8,128)(2,1)}, bf16[768,512]{1,0:T(8,128)(2,1)}, u32[]{:S(2)}, u32[]{:S(2)}) collective-permute-start(bf16[768,512]{1,0:T(8,128)(2,1)} %get-tuple-element.9), channel_id=1, source_target_pairs={{2,4},{4,2},{3,5},{5,3},{10,12},{12,10},{11,13},{13,11},{18,20},{2... | collective-permute-start | bytes 2359304 | tf_op jit(solution)/shard_map/ppermute | solution.py:224
  76.6 1.4 copy-start.2
  127.1 1.4 copy-start.3
  128.5 12.0 %copy-start.4 = (bf16[8,192,512]{2,1,0:T(8,128)(2,1)S(1)}, bf16[8,192,512]{2,1,0:T(8,128)(2,1)}, u32[]{:S(2)}) copy-start(bf16[8,192,512]{2,1,0:T(8,128)(2,1)} %param.6) | copy-start | bytes 4718596
  152.6 3.7 %collective-permute-start.8 = (f32[8,256]{1,0:T(8,128)S(1)}, f32[8,256]{1,0:T(8,128)S(1)}, u32[]{:S(2)}, u32[]{:S(2)}) collective-permute-start(f32[8,256]{1,0:T(8,128)S(1)} %fusion.2), channel_id=1, source_target_pairs={{0,16},{8,24},{16,0},{24,8},{1,17},{9,25},{17,1},{25,9},{2,18},{10... | collective-permute-start | bytes 24584 | tf_op jit(solution)/shard_map/ppermute | solution.py:33
  153.8 4.5 %collective-permute-start.9 = (f32[8,256]{1,0:T(8,128)S(1)}, f32[8,256]{1,0:T(8,128)S(1)}, u32[]{:S(2)}, u32[]{:S(2)}) collective-permute-start(f32[8,256]{1,0:T(8,128)S(1)} %fusion.2), channel_id=1, source_target_pairs={{0,24},{8,16},{16,8},{24,0},{1,25},{9,17},{17,9},{25,1},{2,26},{10... | collective-permute-start | bytes 24584 | tf_op jit(solution)/shard_map/ppermute | solution.py:33
  155.6 3.7 %collective-permute-start.7 = (f32[8,256]{1,0:T(8,128)S(1)}, f32[8,256]{1,0:T(8,128)S(1)}, u32[]{:S(2)}, u32[]{:S(2)}) collective-permute-start(f32[8,256]{1,0:T(8,128)S(1)} %fusion.2), channel_id=1, source_target_pairs={{0,8},{8,0},{16,24},{24,16},{1,9},{9,1},{17,25},{25,17},{2,10},{10... | collective-permute-start | bytes 24584 | tf_op jit(solution)/shard_map/ppermute | solution.py:33
  159.2 8.3 %collective-permute-start.11 = (f32[8,256]{1,0:T(8,128)S(1)}, f32[8,256]{1,0:T(8,128)S(1)}, u32[]{:S(2)}, u32[]{:S(2)}) collective-permute-start(f32[8,256]{1,0:T(8,128)S(1)} %add_add_fusion.1), channel_id=1, source_target_pairs={{0,4},{2,6},{4,0},{6,2},{1,5},{3,7},{5,1},{7,3},{8,12},{10,14},{12... | collective-permute-start | bytes 24584 | tf_op jit(solution)/shard_map/ppermute | solution.py:33
  165.9 5.4 %collective-permute-start.12 = (f32[8,256]{1,0:T(8,128)S(1)}, f32[8,256]{1,0:T(8,128)S(1)}, u32[]{:S(2)}, u32[]{:S(2)}) collective-permute-start(f32[8,256]{1,0:T(8,128)S(1)} %add_add_fusion.1), channel_id=1, source_target_pairs={{0,6},{2,4},{4,2},{6,0},{1,7},{3,5},{5,3},{7,1},{8,14},{10,12},{12... | collective-permute-start | bytes 24584 | tf_op jit(solution)/shard_map/ppermute | solution.py:33
  167.3 4.0 %collective-permute-start.10 = (f32[8,256]{1,0:T(8,128)S(1)}, f32[8,256]{1,0:T(8,128)S(1)}, u32[]{:S(2)}, u32[]{:S(2)}) collective-permute-start(f32[8,256]{1,0:T(8,128)S(1)} %add_add_fusion.1), channel_id=1, source_target_pairs={{0,2},{2,0},{4,6},{6,4},{1,3},{3,1},{5,7},{7,5},{8,10},{10,8},{12,... | collective-permute-start | bytes 24584 | tf_op jit(solution)/shard_map/ppermute | solution.py:33
Sparse Core Ops, SparseCore 0:
  13.1 57.6 all-gather.4
  72.6 54.3 all-gather.6

commit v3 on v2

v3 whole, which is shorter than its diff:
```python
import functools
import math

import jax
import jax.numpy as jnp
from jax import lax
from jax.experimental import pallas as pl
from jax.experimental.pallas import tpu as pltpu
from jax.sharding import PartitionSpec as P

NW = 256

omega_low = -10.0
omega_span = 20.0


def make_grid(count):
    return omega_low + omega_span * jnp.arange(count, dtype=jnp.float32) / (count - 1)


def lookup(indices, table):
    hit = indices[:, None] == jnp.arange(table.shape[0], dtype=jnp.int32)[None, :]
    return jnp.sum(jnp.where(hit, table[None, :], 0.0), axis=1)


def from_behind(block, axis, distance):
    devices = range(lax.axis_size(axis))
    route = [((i - distance) % len(devices), i) for i in devices]
    return lax.ppermute(block, axis, route)


def flip(block, axis, bits):
    return lax.ppermute(block, axis, [(i, i ^ bits) for i in range(lax.axis_size(axis))])


def contribute(full_rows, panel_rows, w_mat, nu_val, weight_val, energies, omega_grid, n_dev):
    product = jnp.dot(full_rows, w_mat, preferred_element_type=jnp.float32)
    contract = jnp.sum(product * panel_rows.astype(jnp.float32), axis=-1).reshape(n_dev, -1)
    offsets = omega_grid[None, :] - energies[:, None]
    kernel = offsets / (offsets * offsets + nu_val * nu_val)
    return -weight_val / math.pi * jnp.dot(contract, kernel, precision=lax.Precision.HIGHEST)


def general(pair_matrix, screened, imag_freq, quad_weight, band_energy, band_index):
    n_dev, m_dev, g_panel = pair_matrix.shape
    f_dev = screened.shape[0]
    cycle_size = lax.axis_size("freq")
    cycle_pos = lax.axis_index("freq")
    full_pairs = lax.all_gather(pair_matrix, "ga", axis=2, tiled=True)
    g_all = full_pairs.shape[2]
    omega_grid = make_grid(NW)
    sigma_part = jnp.zeros((n_dev, NW), jnp.float32)
    panel_rows = pair_matrix.reshape(n_dev * m_dev, g_panel)
    full_rows = full_pairs.reshape(n_dev * m_dev, g_all)
    energies = lookup(band_index, band_energy)
    nu_all = lax.all_gather(imag_freq, "freq", axis=0, tiled=True)
    weight_all = lax.all_gather(quad_weight, "freq", axis=0, tiled=True)
    w_slab = screened
    for turn_index in range(cycle_size):
        source = jnp.mod(cycle_pos - turn_index, cycle_size)
        nu_vals = lax.dynamic_slice_in_dim(nu_all, source * f_dev, f_dev)
        weight_vals = lax.dynamic_slice_in_dim(weight_all, source * f_dev, f_dev)
        for slot in range(f_dev):
            sigma_part = sigma_part + contribute(
                full_rows, panel_rows, w_slab[slot], nu_vals[slot], weight_vals[slot],
                energies, omega_grid, n_dev,
            )
        if turn_index + 1 < cycle_size:
            w_slab = from_behind(w_slab, "freq", 1)
    return lax.psum(sigma_part, ("freq", "ga"))


def choose(flag, yes, no):
    @pl.when(flag == 1)
    def _():
        yes.start()

    @pl.when(flag == 0)
    def _():
        no.start()


def reduce_rows(y_ref, right_ref, weight_ref, slot, out_ref, first, m_dev):
    for k in range(y_ref.shape[0] // m_dev):
        at = slice(k * m_dev, (k + 1) * m_dev)
        z = y_ref[at] * right_ref[at].astype(jnp.float32)
        term = jnp.sum(z, axis=1, keepdims=True) * weight_ref[slot]
        out_ref[first + k] += jnp.sum(term.reshape(m_dev // 8, 8, NW), axis=0)


def alternate(n_slots, w_all, w_sems, y0, y1, dot0, dot1, sum0, sum1):
    y1[...] = jnp.zeros_like(y1)

    def one(slot, carry):
        pltpu.make_async_copy(w_all.at[slot], w_all.at[slot], w_sems.at[slot]).wait()
        y0[...] = dot0(slot)
        sum1(y1, jnp.maximum(slot - 1, 0))
        y1[...] = dot1(slot)
        sum0(y0, slot)
        return carry

    lax.fori_loop(0, n_slots, one, 0)
    sum1(y1, n_slots - 1)


def start_slots(where_ref, plan, refs, w_all, w_sems, panel):
    for slot, pieces in enumerate(plan):
        at = 0
        for index, lead, begin, count in pieces:
            if lead is None:
                src = refs[index].at[begin : begin + count, :]
            else:
                src = refs[index].at[where_ref[lead], pl.ds(pl.multiple_of(where_ref[begin], panel), count), :]
            pltpu.make_async_copy(src, w_all.at[slot, at : at + count, :], w_sems.at[slot]).start()
            at += count


def near_kernel(plan, m_dev, where_ref, k_ref, own_ref, a_ref, b_ref, *rest):
    w_refs, (out_ref, left, own, w_all, k_all, y0, y1, sems, w_sems) = rest[:-9], rest[-9:]
    n_slots, depth, panel = w_all.shape
    end, low = where_ref[0], where_ref[1]
    here = left.at[:, pl.ds(pl.multiple_of((1 - low) * panel, panel), panel)]
    there = left.at[:, pl.ds(pl.multiple_of(low * panel, panel), panel)]
    waits = [
        pltpu.make_async_copy(own_ref, own, sems.at[0]),
        pltpu.make_async_copy(own_ref, here, sems.at[1]),
        pltpu.make_async_copy(k_ref, k_all, sems.at[3]),
    ]
    for c in waits:
        c.start()
    near = pltpu.make_async_copy(a_ref, there, sems.at[2])
    choose(end, near, pltpu.make_async_copy(b_ref, there, sems.at[2]))
    start_slots(where_ref, plan, w_refs, w_all, w_sems, panel)
    out_ref[...] = jnp.zeros_like(out_ref)
    for c in waits + [near]:
        c.wait()
    tile = y0.shape[0]
    states = tile // m_dev

    def product(t):
        return lambda s: jnp.dot(left[t * tile : (t + 1) * tile], w_all[s], preferred_element_type=jnp.float32)

    def total(t):
        right = own.at[t * tile : (t + 1) * tile, :]
        return lambda y, s: reduce_rows(y, right, k_all, s, out_ref, t * states, m_dev)

    alternate(n_slots, w_all, w_sems, y0, y1, product(0), product(1), total(0), total(1))


def far_kernel(plan, m_dev, begin, where_ref, k_ref, own_ref, a_ref, c_ref, d_ref, *rest):
    w_refs, (out_ref, far, own, other, left, w_all, k_all, y0, y1, sems, w_sems) = rest[:-11], rest[-11:]
    n_slots, _, panel = w_all.shape
    end = where_ref[0]
    mine = own_ref.at[begin : begin + own.shape[0], :]
    theirs = a_ref.at[begin : begin + own.shape[0], :]
    waits = [
        pltpu.make_async_copy(mine, own, sems.at[0]),
        pltpu.make_async_copy(theirs, other, sems.at[1]),
        pltpu.make_async_copy(k_ref, k_all, sems.at[4]),
    ]
    for c in waits:
        c.start()
    far_copy = pltpu.make_async_copy(c_ref, far, sems.at[2])
    choose(end, far_copy, pltpu.make_async_copy(d_ref, far, sems.at[2]))
    left_copy = pltpu.make_async_copy(mine, left, sems.at[3])
    choose(end, left_copy, pltpu.make_async_copy(d_ref, left, sems.at[3]))
    start_slots(where_ref, plan, w_refs, w_all, w_sems, panel)
    out_ref[...] = jnp.zeros_like(out_ref)
    for c in waits + [far_copy, left_copy]:
        c.wait()
    alternate(
        n_slots, w_all, w_sems, y0, y1,
        lambda s: jnp.dot(far[...], w_all[s, :panel], preferred_element_type=jnp.float32),
        lambda s: jnp.dot(left[...], w_all[s, panel:], preferred_element_type=jnp.float32),
        lambda y, s: reduce_rows(y, own, k_all, s, out_ref, 0, m_dev),
        lambda y, s: reduce_rows(y, other, k_all, s, out_ref, 0, m_dev),
    )


def run_kernel(body, where, k_part, mats, arrays, lefts, tile, n_rows, m_dev):
    panel = mats[0].shape[1]
    n_slots, depth = k_part.shape[0], 2 * panel
    scratch = [pltpu.VMEM((n_rows, width), jnp.bfloat16) for width in lefts]
    scratch += [
        pltpu.VMEM((n_slots, depth, panel), jnp.bfloat16),
        pltpu.VMEM(k_part.shape, jnp.float32),
        pltpu.VMEM((tile, panel), jnp.float32),
        pltpu.VMEM((tile, panel), jnp.float32),
        pltpu.SemaphoreType.DMA((5,)),
        pltpu.SemaphoreType.DMA((n_slots,)),
    ]
    flops = 2 * n_rows * depth * panel * n_slots
    return pl.pallas_call(
        body,
        out_shape=jax.ShapeDtypeStruct((n_rows // m_dev, 8, NW), jnp.float32),
        in_specs=[pl.BlockSpec(memory_space=pltpu.SMEM)]
        + [pl.BlockSpec(memory_space=pl.ANY)] * (1 + len(mats) + len(arrays)),
        out_specs=pl.BlockSpec(memory_space=pltpu.VMEM),
        scratch_shapes=scratch,
        cost_estimate=pl.CostEstimate(flops=flops, bytes_accessed=depth * panel, transcendentals=0),
        compiler_params=pltpu.CompilerParams(vmem_limit_bytes=48 * 2**20),
    )(where, k_part, *mats, *arrays)


def split3(x):
    hi = lax.reduce_precision(x, 8, 7)
    mid = lax.reduce_precision(x - hi, 8, 7)
    return jnp.stack([hi, mid, (x - hi) - mid])


def after(value, *others):
    return lax.optimization_barrier((value,) + others)[0]


def square_line(pair_matrix, screened, imag_freq, quad_weight, band_energy, band_index):
    n_dev, m_dev, panel = pair_matrix.shape
    ga = lax.axis_index("ga")
    core = lax.axis_index("band")
    rows = n_dev * m_dev
    own = pair_matrix.reshape(rows, panel)
    end = (ga == 0) | (ga == 3)
    low = ga < 2
    near_at = jnp.where(ga == 0, 0, jnp.where(ga == 3, 2, 1)) * panel
    far_at = (ga + 2) % 4 * panel
    give_at = jnp.where(ga % 2 == 0, 3, 0) * panel
    where = jnp.stack([end, low, near_at, far_at, core, 1 - core]).astype(jnp.int32)

    outer = [(0, 1), (1, 0), (2, 3), (3, 2)]
    inner = [(1, 2), (2, 1)]
    outward = [(1, 0), (2, 3)]

    def piece(start, count):
        return lax.dynamic_slice(screened, (core, start, 0), (1, count, panel))[0]

    def share(block):
        return flip(block, "band", 1)

    node = split3(jnp.stack([imag_freq[core], quad_weight[core]])).reshape(1, 6)
    node = jnp.pad(node, ((0, 15), (0, panel - 6))).astype(jnp.bfloat16)
    near_w = jnp.concatenate([piece(near_at, 2 * panel), node])

    given = lax.ppermute(piece(give_at, panel), "ga", outer)
    x1 = flip(near_w, "freq", 1)
    y1 = flip(near_w, "freq", 2)
    a_rows = lax.ppermute(after(own, given), "ga", outer)
    b_rows = lax.ppermute(own, "ga", inner)
    far_w = jnp.concatenate([piece(far_at, panel), given])
    d1a = flip(y1[:panel], "freq", 1)
    d1b = flip(x1[panel:], "freq", 2)
    x2 = flip(after(far_w, x1, y1), "freq", 1)
    x1_o, y1_o = share(after(x1, b_rows)), share(after(y1, a_rows))
    given_o = share(given)
    y2 = flip(after(far_w, d1a, d1b), "freq", 2)
    energies = lookup(band_index, band_energy)
    offsets = make_grid(NW)[None, :] - energies[:, None]
    mine = jnp.stack([imag_freq, quad_weight], axis=1)
    mine = jnp.where(core == 0, mine, mine[::-1])

    def weigh(nodes):
        nu, weight = nodes[:, 0, None, None], nodes[:, 1, None, None]
        return (-weight / math.pi) * (offsets / (offsets * offsets + nu * nu))

    def carried(*places):
        terms = jnp.stack([w[row, :6] for w, row in places]).astype(jnp.float32).reshape(-1, 3, 2)
        return (terms[:, 0] + terms[:, 1]) + terms[:, 2]

    k_here = weigh(jnp.concatenate([mine, carried((x1, 2 * panel), (y1, 2 * panel))]))

    whole, one = 2 * panel, panel

    def close(plan, k_part, arrays):
        return run_kernel(
            functools.partial(near_kernel, plan, m_dev), where, k_part,
            (own, a_rows, b_rows), arrays, (whole, one), rows // 2, rows, m_dev,
        )

    near_plan = [[(0, 4 + s, 2, whole)] for s in range(2)]
    near_plan += [[(r, None, 0, whole)] for r in (1, 2)]
    near = close(near_plan, k_here, (screened, x1, y1))
    d1a_o, d1b_o = share(after(d1a, near)), share(after(d1b, near))
    k_there = weigh(carried((x1_o, 2 * panel), (y1_o, 2 * panel), (d1b, panel), (d1b_o, panel)))

    corner_plan = [[(r, None, 0, whole)] for r in (0, 1)]
    corner_plan += [[(r, None, 0, one), (r + 1, None, 0, one)] for r in (2, 4)]
    corner = close(corner_plan, k_there, (x1_o, y1_o, d1a, d1b, d1a_o, d1b_o))
    d2a = flip(y2[:panel], "freq", 1)
    d2b = flip(x2[panel:], "freq", 2)
    x2_o, y2_o, d2a_o, d2b_o = (share(w) for w in (x2, y2, d2a, d2b))
    cuts = ((0, rows // 2), (rows // 2, rows // 4), (3 * rows // 4, rows // 4))
    c_rows, d_rows = [], []
    for n, (i, count) in enumerate(cuts):
        c_gate = ((), (near, *d_rows[:1]), (corner, *d_rows[1:]))[n]
        d_gate = ((), (near, *c_rows[:1]), (corner, *c_rows[1:]))[n]
        c_rows.append(lax.ppermute(after(b_rows[i : i + count], *c_gate), "ga", outward))
        d_rows.append(lax.ppermute(after(a_rows[i : i + count], *d_gate), "ga", inner))
    first = [[(0, 4 + s, 3, one), (1 + s, None, 0, one)] for s in range(2)]
    first += [[(r, None, 0, whole)] for r in (3, 4)]
    first_arrays = (screened, given, given_o, x2, y2)
    last_arrays = (x2_o, y2_o, d2a, d2b, d2a_o, d2b_o)

    def last(r):
        plan = [[(r + s, None, 0, whole)] for s in range(2)]
        return plan + [[(r + s, None, 0, one), (r + s + 1, None, 0, one)] for s in (2, 4)]

    def far(n, plan, k_part, arrays):
        i, count = cuts[n]
        return run_kernel(
            functools.partial(far_kernel, plan, m_dev, i), where, k_part,
            (own, a_rows, c_rows[n], d_rows[n]), arrays, (one,) * 4, count, count, m_dev,
        )

    parts = [far(0, first, k_here, first_arrays) + far(0, last(0), k_there, last_arrays)]
    k_all = jnp.concatenate([k_here, k_there])
    for n in (1, 2):
        parts.append(far(n, first + last(5), k_all, first_arrays + last_arrays))
    sigma = jnp.sum(near + corner + jnp.concatenate(parts), axis=1)
    for axis, bits in (("freq", 1), ("freq", 2), ("ga", 1), ("ga", 2)):
        sigma = sigma + flip(sigma, axis, bits)
    return sigma


def on_device(pair_matrix, screened, *rest):
    sizes = tuple(lax.axis_size(a) for a in ("freq", "ga", "band"))
    fits = sizes == (4, 4, 2) and screened.shape[0] == 2 and pair_matrix.shape[0] % 8 == 0
    return (square_line if fits else general)(pair_matrix, screened, *rest)


def solution(mesh):
    placed = (P("band", "freq", "ga"), P("freq", None, "ga"), P("freq"), P("freq"), P(), P("freq"))
    return jax.shard_map(
        on_device, mesh=mesh, in_specs=placed, out_specs=P("band", None), check_vma=False
    )
```

time: 179 us -> 185 us (1.034)
  waiting for transfers between devices: 79.4 us -> 55.2 us
  starting transfers between devices: 25.7 us -> 41.4 us
  between operations: 13.6 us -> 0.38 us
  local copies, waits for them, and re-layouts: 12.8 us -> 25.8 us
  Pallas kernels: 41.7 us -> 51.3 us
  other arithmetic: 5.58 us -> 10.1 us
    ppermute x6 -> x21, waiting for transfers between devices: 7.1 us -> 43.9 us  [flip(): lax.ppermute(block, axis, [(i, i ^ bits) for i in range(lax.axis_size(axi...]
    all_gather x2 -> x0, waiting for transfers between devices: 31.3 us -> none  [the longest x1 31.3 us: square_line(): far_all = lax.all_gather(far_w, ('freq', 'band'))]
    ppermute x5 -> x7, waiting for transfers between devices: 29 us -> 9.23 us  [the longest x1 6.4 us: square_line(): a_rows = lax.ppermute(after(own, given), 'ga', outer)]
    ppermute x6 -> x21, starting transfers between devices: 11.7 us -> 27.3 us  [flip(): lax.ppermute(block, axis, [(i, i ^ bits) for i in range(lax.axis_size(axi...]
    slice x2 -> x14, local copies, waits for them, and re-layouts: 3.99 us -> 15.2 us  [the longest x6 4.13 us: carried(): w[row, :6]]
    ppermute x1, waiting for transfers between devices: 11.9 us -> 2 us  [square_line(): given = lax.ppermute(piece(give_at, panel), 'ga', outer)]
    pallas_call x3 -> x6, Pallas kernels: 41.7 us -> 51.3 us  [run_kernel(): pl.pallas_call(body, out_shape=jax.ShapeDtypeStruct((n_rows // m_dev, 8,...]
    mul x1 -> x2, other arithmetic: 0.28 us -> 2.3 us  [weigh(): return -weight / math.pi * (offsets / (offsets * offsets + nu * nu))]
  transfers between devices with their start and end apart: 15 -> 30, of which waited for: 8 -> 11; matrix products, arithmetic and copies ran while one was open for 4% -> 15% of each run, Pallas kernels for 17% -> 24%
where the time goes in v3:
time: 185 us; the launch traced here: 184 us
  waiting for transfers between devices  55.2 us (30%)
  Pallas kernels  51.3 us (28%)
  starting transfers between devices  41.4 us (22%)
  local copies, waits for them, and re-layouts  25.8 us (14%)
  other arithmetic  10.1 us (5%)
    pallas_call x6, Pallas kernels, run_kernel(): pl.pallas_call(body, out_shape=jax.ShapeDtypeStruct((n_rows // m_dev, 8,...  51.3 us
    ppermute x21, waiting for transfers between devices, flip(): lax.ppermute(block, axis, [(i, i ^ bits) for i in range(lax.axis_size(axi...  43.9 us
    ppermute x21, starting transfers between devices, flip(): lax.ppermute(block, axis, [(i, i ^ bits) for i in range(lax.axis_size(axi...  27.3 us
    ppermute x1, waiting for transfers between devices, square_line(): a_rows = lax.ppermute(after(own, given), 'ga', outer)  6.4 us
    unnamed x40, local copies, waits for them, and re-layouts  5.22 us
    slice x6, local copies, waits for them, and re-layouts, carried(): w[row, :6]  4.13 us
    ppermute x3, starting transfers between devices, square_line(): lax.ppermute(after(b_rows[i:i + count], *c_gate), 'ga', outward)  3.84 us
  transfers between devices with their start and end apart: 30, of which 11 were waited for; matrix products, arithmetic and copies ran while one was open for 15% of the time, Pallas kernels for 24%

profile of v3, /device:TPU:0, one launch (start us, length us, event | category | flops | bytes accessed | tf_op | source)
XLA Modules:
  0.0 184.2 jit_solution(5542470742400290764)
XLA Ops:
  0.0 2.1 %dynamic-slice_bitcast_fusion.1 = (bf16[512,512]{1,0:T(8,128)(2,1)}, bf16[512,512]{1,0:T(8,128)(2,1)S(1)}) fusion(bf16[2,2048,512]{2,1,0:T(8,128)(2,1)} %rest_0_.7, s32[]{:T(128)S(6)} %select_n.55, s32[]{:T(128)S(6)} %select_n.61, s32[]{:T(128)S(6)} %select_n.60), kind=kLoop, calls=%fused_computation.8 | loop fusion | bytes 2097164 | tf_op jit(solution)/shard_map/squeeze | solution.py:233
  2.1 3.0 %collective-permute-start.2 = (bf16[512,512]{1,0:T(8,128)(2,1)S(1)}, bf16[512,512]{1,0:T(8,128)(2,1)}, u32[]{:S(2)}, u32[]{:S(2)}) collective-permute-start(bf16[512,512]{1,0:T(8,128)(2,1)S(1)} %get-tuple-element.30), channel_id=1, source_target_pairs={{0,2},{2,0},{4,6},{6,4},{1,3},{3,1},{5,7},{7,5},{8,10},{10,8},{12,... | collective-permute-start | bytes 1572872 | tf_op jit(solution)/shard_map/ppermute | solution.py:242
  6.3 1.3 reduce-precision_convert_fusion.1
  7.7 1.3 dynamic-slice_bitcast_fusion
  9.0 1.1 fusion.1
  10.1 1.5 collective-permute-start
  11.6 1.5 collective-permute-start.1
  13.1 1.8 collective-permute-start.4
  15.1 2.0 %collective-permute-done.2.rest_1_ = bf16[512,512]{1,0:T(8,128)(2,1)} collective-permute-done((bf16[512,512]{1,0:T(8,128)(2,1)S(1)}, bf16[512,512]{1,0:T(8,128)(2,1)}, u32[]{:S(2)}, u32[]{:S(2)}) %collective-permute-start.2) | collective-permute-done | bytes 524320 | tf_op jit(solution)/shard_map/ppermute | solution.py:242
  17.1 1.7 collective-permute-start.3
  19.1 0.8 broadcast_subtract_fusion
  19.9 2.3 %pad_maximum_fusion.1 = bf16[1024,512]{1,0:T(8,128)(2,1)} fusion(bf16[512,512]{1,0:T(8,128)(2,1)} %collective-permute-done.2.rest_1_, bf16[512,512]{1,0:T(8,128)(2,1)} %get-tuple-element.29), kind=kLoop, calls=%fused_computation.4 | loop fusion | flops 2097152 | bytes 2097152 | tf_op jit(solution)/shard_map/concatenate | solution.py:247
  22.2 13.2 %collective-permute-done.rest_1_ = bf16[1040,512]{1,0:T(8,128)(2,1)} collective-permute-done((bf16[1040,512]{1,0:T(8,128)(2,1)}, bf16[1040,512]{1,0:T(8,128)(2,1)}, u32[]{:S(2)}, u32[]{:S(2)}) %collective-permute-start) | collective-permute-done | bytes 1064992 | tf_op jit(solution)/shard_map/ppermute | solution.py:33
  35.4 1.9 %slice.108 = bf16[528,512]{1,0:T(8,128)(2,1)} slice(bf16[1040,512]{1,0:T(8,128)(2,1)} %collective-permute-done.rest_1_), slice={[512:1040], [0:512]} | slice | bytes 1081344 | tf_op jit(solution)/shard_map/slice | solution.py:249
  37.3 1.5 collective-permute-start.7
  38.8 0.7 slice_reduce_fusion.4
  39.6 0.7 slice_reduce_fusion.5
  40.5 1.1 slice.114
  41.6 1.6 collective-permute-start.9
  43.7 1.1 divide_multiply_fusion.1.k_ref
  44.9 1.4 slice.115
  46.3 6.4 %collective-permute-done.3.a_ref = bf16[1536,512]{1,0:T(8,128)(2,1)S(1)} collective-permute-done((bf16[1536,512]{1,0:T(8,128)(2,1)S(1)}, bf16[1536,512]{1,0:T(8,128)(2,1)S(1)}, u32[]{:S(2)}, u32[]{:S(2)}) %collective-permute-start.3) | collective-permute-done | bytes 1572896 | tf_op jit(solution)/shard_map/ppermute | solution.py:245
  52.7 1.3 collective-permute-start.11
  54.0 9.8 %shard_map.64 = f32[8,8,256]{2,1,0:T(8,128)S(1)} custom-call(s32[6]{0:T(128)S(1)} %stack.76.where_ref, f32[4,192,256]{2,1,0:T(8,128)S(1)} %divide_multiply_fusion.1.k_ref, bf16[1536,512]{1,0:T(8,128)(2,1)S(1)} %bitcast.35, bf16[1536,512]{1,0:T(8,128)(2,1)S(1)} %collective-permute-done.3.a_ref, bf16[1536,512]{1,0:T(8,128)(2,1)} %collective-permute-done.4.b_ref, ...), custom_call_target="tpu_custom_call" | custom-call | flops 6442450944 | bytes 524288 | tf_op jit(solution)/shard_map/pallas_call | solution.py:193
  64.0 1.4 collective-permute-start.15
  65.4 1.0 slice.116
  66.4 10.0 %collective-permute-done.14.rest_3_ = bf16[1024,512]{1,0:T(8,128)(2,1)} collective-permute-done((bf16[1024,512]{1,0:T(8,128)(2,1)}, bf16[1024,512]{1,0:T(8,128)(2,1)}, u32[]{:S(2)}, u32[]{:S(2)}) %collective-permute-start.14) | collective-permute-done | bytes 1048608 | tf_op jit(solution)/shard_map/ppermute | solution.py:33
  76.4 0.9 copy-done.5
  77.3 1.5 collective-permute-start.12
  78.9 2.1 %fusion.8 = (bf16[384,512]{1,0:T(8,128)(2,1)}, bf16[384,512]{1,0:T(8,128)(2,1)}) fusion(bf16[1536,512]{1,0:T(8,128)(2,1)} %collective-permute-done.4.b_ref), kind=kLoop, calls=%fused_computation.45 | loop fusion | bytes 1572864 | tf_op jit(solution)/shard_map/slice | solution.py:294
  81.5 0.7 slice_reduce_fusion.1
  82.3 0.9 fusion.9
  83.2 1.9 %slice.118 = bf16[512,512]{1,0:T(8,128)(2,1)} slice(bf16[1024,512]{1,0:T(8,128)(2,1)} %collective-permute-done.14.rest_3_), slice={[512:1024], [0:512]} | slice | bytes 1048576 | tf_op jit(solution)/shard_map/slice | solution.py:287
  85.1 0.7 slice_reduce_fusion
  86.0 0.7 slice_reduce_fusion.3
  86.8 3.0 %collective-permute-done.15.rest_4_ = bf16[1024,512]{1,0:T(8,128)(2,1)S(1)} collective-permute-done((bf16[1024,512]{1,0:T(8,128)(2,1)}, bf16[1024,512]{1,0:T(8,128)(2,1)S(1)}, u32[]{:S(2)}, u32[]{:S(2)}) %collective-permute-start.15) | collective-permute-done | bytes 1048608 | tf_op jit(solution)/shard_map/ppermute | solution.py:33
  89.8 1.4 collective-permute-start.19
  91.1 0.8 slice.117
  92.0 1.4 collective-permute-start.23
  93.4 1.1 copy-done.6
  94.5 7.4 %shard_map.66 = f32[4,8,256]{2,1,0:T(8,128)S(1)} custom-call(s32[6]{0:T(128)S(1)} %stack.76.where_ref, f32[4,192,256]{2,1,0:T(8,128)S(1)} %copy-done.3, bf16[1536,512]{1,0:T(8,128)(2,1)} %bitcast.28, bf16[1536,512]{1,0:T(8,128)(2,1)} %copy-done, bf16[768,512]{1,0:T(8,128)(2,1)S(1)} %copy-done.6, bf16[768,512]{1,0:T(8,128)(2,1)} %collective-permute-done.12.d_ref, ...), custom_call_target="tpu_custom_call" | custom-call | flops 3221225472 | bytes 524288 | tf_op jit(solution)/shard_map/pallas_call | solution.py:193
  101.9 1.6 collective-permute-start.18
  103.5 0.7 slice_reduce_fusion.2
  104.6 1.2 divide_multiply_fusion.k_ref
  106.2 1.3 collective-permute-start.22
  107.5 9.1 %collective-permute-done.18.rest_2_.rest_7_ = bf16[512,512]{1,0:T(8,128)(2,1)} collective-permute-done((bf16[512,512]{1,0:T(8,128)(2,1)}, bf16[512,512]{1,0:T(8,128)(2,1)}, u32[]{:S(2)}, u32[]{:S(2)}) %collective-permute-start.18) | collective-permute-done | bytes 524320 | tf_op jit(solution)/shard_map/ppermute | solution.py:33
  116.6 1.0 copy-done.9
  117.7 1.0 copy-done.11
  118.7 11.2 %shard_map.65 = f32[8,8,256]{2,1,0:T(8,128)S(1)} custom-call(s32[6]{0:T(128)S(1)} %stack.76.where_ref, f32[4,192,256]{2,1,0:T(8,128)S(1)} %divide_multiply_fusion.k_ref, bf16[1536,512]{1,0:T(8,128)(2,1)} %bitcast.29, bf16[1536,512]{1,0:T(8,128)(2,1)} %copy-done, bf16[1536,512]{1,0:T(8,128)(2,1)} %collective-permute-done.4.b_ref, ...), custom_call_target="tpu_custom_call" | custom-call | flops 6442450944 | bytes 524288 | tf_op jit(solution)/shard_map/pallas_call | solution.py:193
  129.9 1.3 pad_maximum_fusion.k_ref
  131.2 1.3 collective-permute-start.24
  132.5 0.7 collective-permute-start.25
  133.2 1.0 copy-done.12
  134.3 6.9 %shard_map.67 = f32[4,8,256]{2,1,0:T(8,128)S(1)} custom-call(s32[6]{0:T(128)S(1)} %stack.76.where_ref, f32[4,192,256]{2,1,0:T(8,128)S(1)} %divide_multiply_fusion.k_ref, bf16[1536,512]{1,0:T(8,128)(2,1)} %bitcast.30, bf16[1536,512]{1,0:T(8,128)(2,1)} %copy-done, bf16[768,512]{1,0:T(8,128)(2,1)S(1)} %copy-done.7, ...), custom_call_target="tpu_custom_call" | custom-call | flops 3221225472 | bytes 524288 | tf_op jit(solution)/shard_map/pallas_call | solution.py:193
  141.2 8.6 %shard_map.68 = f32[2,8,256]{2,1,0:T(8,128)S(1)} custom-call(s32[6]{0:T(128)S(1)} %stack.76.where_ref, f32[8,192,256]{2,1,0:T(8,128)} %pad_maximum_fusion.k_ref, bf16[1536,512]{1,0:T(8,128)(2,1)} %bitcast.31, bf16[1536,512]{1,0:T(8,128)(2,1)} %copy-done, bf16[384,512]{1,0:T(8,128)(2,1)S(1)} %collective-permute-done.22.c_ref, ...), custom_call_target="tpu_custom_call" | custom-call | flops 3221225472 | bytes 524288 | tf_op jit(solution)/shard_map/pallas_call | solution.py:193
  149.8 2.8 %collective-permute-done.24.c_ref = bf16[384,512]{1,0:T(8,128)(2,1)S(1)} collective-permute-done((bf16[384,512]{1,0:T(8,128)(2,1)S(1)}, bf16[384,512]{1,0:T(8,128)(2,1)S(1)}, u32[]{:S(2)}, u32[]{:S(2)}) %collective-permute-start.24) | collective-permute-done | bytes 393248 | tf_op jit(solution)/shard_map/ppermute | solution.py:294
  152.6 7.5 %shard_map.69 = f32[2,8,256]{2,1,0:T(8,128)S(1)} custom-call(s32[6]{0:T(128)S(1)} %stack.76.where_ref, f32[8,192,256]{2,1,0:T(8,128)} %pad_maximum_fusion.k_ref, bf16[1536,512]{1,0:T(8,128)(2,1)} %bitcast.32, bf16[1536,512]{1,0:T(8,128)(2,1)} %copy-done, bf16[384,512]{1,0:T(8,128)(2,1)S(1)} %collective-permute-done.24.c_ref, ...), custom_call_target="tpu_custom_call" | custom-call | flops 3221225472 | bytes 524288 | tf_op jit(solution)/shard_map/pallas_call | solution.py:193
  160.1 1.6 collective-permute-start.26
  161.7 2.2 %collective-permute-done.26 = f32[8,256]{1,0:T(8,128)S(1)} collective-permute-done((f32[8,256]{1,0:T(8,128)S(1)}, f32[8,256]{1,0:T(8,128)S(1)}, u32[]{:S(2)}, u32[]{:S(2)}) %collective-permute-start.26) | collective-permute-done | bytes 8224 | tf_op jit(solution)/shard_map/ppermute | solution.py:33
  164.3 3.1 %collective-permute-done.27 = f32[8,256]{1,0:T(8,128)S(1)} collective-permute-done((f32[8,256]{1,0:T(8,128)S(1)}, f32[8,256]{1,0:T(8,128)S(1)}, u32[]{:S(2)}, u32[]{:S(2)}) %collective-permute-start.27) | collective-permute-done | bytes 8224 | tf_op jit(solution)/shard_map/ppermute | solution.py:33
  167.5 9.9 %collective-permute-start.28 = (f32[8,256]{1,0:T(8,128)S(1)}, f32[8,256]{1,0:T(8,128)S(1)}, u32[]{:S(2)}, u32[]{:S(2)}) collective-permute-start(f32[8,256]{1,0:T(8,128)S(1)} %add.127), channel_id=1, source_target_pairs={{0,2},{2,0},{4,6},{6,4},{1,3},{3,1},{5,7},{7,5},{8,10},{10,8},{12,... | collective-permute-start | bytes 24584 | tf_op jit(solution)/shard_map/ppermute | solution.py:33
  177.4 1.6 collective-permute-done.28
  179.0 2.9 %collective-permute-start.29 = (f32[8,256]{1,0:T(8,128)S(1)}, f32[8,256]{1,0:T(8,128)S(1)}, u32[]{:S(2)}, u32[]{:S(2)}) collective-permute-start(f32[8,256]{1,0:T(8,128)S(1)} %add.128), channel_id=1, source_target_pairs={{0,4},{2,6},{4,0},{6,2},{1,5},{3,7},{5,1},{7,3},{8,12},{10,14},{12... | collective-permute-start | bytes 24584 | tf_op jit(solution)/shard_map/ppermute | solution.py:33
  181.9 1.7 collective-permute-done.29
  (95 shorter events, 5.8 us)
Async XLA Ops:
  0.0 5.1 %copy-start.16 = (f32[2]{0:T(128)S(1)}, f32[2]{0:T(128)}, u32[]{:S(2)}) copy-start(f32[2]{0:T(128)} %param.9) | copy-start | bytes 28
  0.0 5.7 %copy-start.17 = (f32[2]{0:T(128)S(1)}, f32[2]{0:T(128)}, u32[]{:S(2)}) copy-start(f32[2]{0:T(128)} %param.8) | copy-start | bytes 28
  2.1 15.0 %collective-permute-start.2 = (bf16[512,512]{1,0:T(8,128)(2,1)S(1)}, bf16[512,512]{1,0:T(8,128)(2,1)}, u32[]{:S(2)}, u32[]{:S(2)}) collective-permute-start(bf16[512,512]{1,0:T(8,128)(2,1)S(1)} %get-tuple-element.30), channel_id=1, source_target_pairs={{0,2},{2,0},{4,6},{6,4},{1,3},{3,1},{5,7},{7,5},{8,10},{10,8},{12,... | collective-permute-start | bytes 1572872 | tf_op jit(solution)/shard_map/ppermute | solution.py:242
  9.0 4.1 %copy-start.1 = (bf16[8,192,512]{2,1,0:T(8,128)(2,1)S(1)}, bf16[8,192,512]{2,1,0:T(8,128)(2,1)}, u32[]{:S(2)}) copy-start(bf16[8,192,512]{2,1,0:T(8,128)(2,1)} %param.6) | copy-start | bytes 4718596
  9.0 6.0 %copy-start.18 = (f32[256]{0:T(256)S(1)}, f32[256]{0:T(256)}, u32[]{:S(2)}) copy-start(f32[256]{0:T(256)} %param.10) | copy-start | bytes 3076
  9.0 6.0 %copy-start.19 = (s32[192]{0:T(256)S(1)}, s32[192]{0:T(256)}, u32[]{:S(2)}) copy-start(s32[192]{0:T(256)} %param.11) | copy-start | bytes 2308
  10.1 25.3 %collective-permute-start = (bf16[1040,512]{1,0:T(8,128)(2,1)}, bf16[1040,512]{1,0:T(8,128)(2,1)}, u32[]{:S(2)}, u32[]{:S(2)}) collective-permute-start(bf16[1040,512]{1,0:T(8,128)(2,1)} %fusion.1), channel_id=1, source_target_pairs={{0,8},{8,0},{16,24},{24,16},{1,9},{9,1},{17,25},{25,17},{2,10},{10... | collective-permute-start | bytes 3194888 | tf_op jit(solution)/shard_map/ppermute | solution.py:33
  11.6 27.2 %collective-permute-start.1 = (bf16[1040,512]{1,0:T(8,128)(2,1)}, bf16[1040,512]{1,0:T(8,128)(2,1)}, u32[]{:S(2)}, u32[]{:S(2)}) collective-permute-start(bf16[1040,512]{1,0:T(8,128)(2,1)} %fusion.1), channel_id=1, source_target_pairs={{0,16},{8,24},{16,0},{24,8},{1,17},{9,25},{17,1},{25,9},{2,18},{10... | collective-permute-start | bytes 3194888 | tf_op jit(solution)/shard_map/ppermute | solution.py:33
  13.1 31.8 %collective-permute-start.4 = (bf16[1536,512]{1,0:T(8,128)(2,1)S(1)}, bf16[1536,512]{1,0:T(8,128)(2,1)}, u32[]{:S(2)}, u32[]{:S(2)}) collective-permute-start(bf16[1536,512]{1,0:T(8,128)(2,1)S(1)} %bitcast.33), channel_id=1, source_target_pairs={{2,4},{4,2},{3,5},{5,3},{10,12},{12,10},{11,13},{13,11},{18,20},{2... | collective-permute-start | bytes 4718600 | tf_op jit(solution)/shard_map/ppermute | solution.py:246
  17.1 35.6 %collective-permute-start.3 = (bf16[1536,512]{1,0:T(8,128)(2,1)S(1)}, bf16[1536,512]{1,0:T(8,128)(2,1)S(1)}, u32[]{:S(2)}, u32[]{:S(2)}) collective-permute-start(bf16[1536,512]{1,0:T(8,128)(2,1)S(1)} %bitcast.34), channel_id=1, source_target_pairs={{0,2},{2,0},{4,6},{6,4},{1,3},{3,1},{5,7},{7,5},{8,10},{10,8},{12,... | collective-permute-start | bytes 4718600 | tf_op jit(solution)/shard_map/ppermute | solution.py:245
  19.9 23.9 %copy-start.13 = (f32[192,256]{1,0:T(8,128)}, f32[192,256]{1,0:T(8,128)S(1)}, u32[]{:S(2)}) copy-start(f32[192,256]{1,0:T(8,128)S(1)} %get-tuple-element.35) | copy-start | bytes 589828
  37.3 26.6 %collective-permute-start.7 = (bf16[528,512]{1,0:T(8,128)(2,1)}, bf16[528,512]{1,0:T(8,128)(2,1)}, u32[]{:S(2)}, u32[]{:S(2)}) collective-permute-start(bf16[528,512]{1,0:T(8,128)(2,1)} %slice.108), channel_id=1, source_target_pairs={{0,16},{8,24},{16,0},{24,8},{1,17},{9,25},{17,1},{25,9},{2,18},{10... | collective-permute-start | bytes 1622024 | tf_op jit(solution)/shard_map/ppermute | solution.py:33
  41.6 22.4 %collective-permute-start.9 = (bf16[512,512]{1,0:T(8,128)(2,1)S(1)}, bf16[512,512]{1,0:T(8,128)(2,1)S(1)}, u32[]{:S(2)}, u32[]{:S(2)}) collective-permute-start(bf16[512,512]{1,0:T(8,128)(2,1)S(1)} %slice.114), channel_id=1, source_target_pairs={{0,8},{8,0},{16,24},{24,16},{1,9},{9,1},{17,25},{25,17},{2,10},{10... | collective-permute-start | bytes 1572872 | tf_op jit(solution)/shard_map/ppermute | solution.py:33
  43.1 33.3 %collective-permute-start.14 = (bf16[1024,512]{1,0:T(8,128)(2,1)}, bf16[1024,512]{1,0:T(8,128)(2,1)}, u32[]{:S(2)}, u32[]{:S(2)}) collective-permute-start(bf16[1024,512]{1,0:T(8,128)(2,1)} %pad_maximum_fusion.1), channel_id=1, source_target_pairs={{0,8},{8,0},{16,24},{24,16},{1,9},{9,1},{17,25},{25,17},{2,10},{10... | collective-permute-start | bytes 3145736 | tf_op jit(solution)/shard_map/ppermute | solution.py:33
  44.8 19.0 %copy-start.2 = (f32[4,192,256]{2,1,0:T(8,128)}, f32[4,192,256]{2,1,0:T(8,128)S(1)}, u32[]{:S(2)}) copy-start(f32[4,192,256]{2,1,0:T(8,128)S(1)} %divide_multiply_fusion.1.k_ref) | copy-start | bytes 2359300
  44.9 41.0 %collective-permute-start.5 = (bf16[1040,512]{1,0:T(8,128)(2,1)}, bf16[1040,512]{1,0:T(8,128)(2,1)}, u32[]{:S(2)}, u32[]{:S(2)}) collective-permute-start(bf16[1040,512]{1,0:T(8,128)(2,1)} %collective-permute-done.rest_1_), channel_id=1, source_target_pairs={{0,1},{1,0},{2,3},{3,2},{4,5},{5,4},{6,7},{7,6},{8,9},{9,8},{10,11... | collective-permute-start | bytes 3194888 | tf_op jit(solution)/shard_map/ppermute | solution.py:33
  52.7 29.5 %copy-start = (bf16[1536,512]{1,0:T(8,128)(2,1)}, bf16[1536,512]{1,0:T(8,128)(2,1)S(1)}, u32[]{:S(2)}) copy-start(bf16[1536,512]{1,0:T(8,128)(2,1)S(1)} %collective-permute-done.3.a_ref) | copy-start | bytes 4718596
  52.7 23.7 %collective-permute-start.11 = (bf16[768,512]{1,0:T(8,128)(2,1)S(1)}, bf16[768,512]{1,0:T(8,128)(2,1)S(1)}, u32[]{:S(2)}, u32[]{:S(2)}) collective-permute-start(bf16[768,512]{1,0:T(8,128)(2,1)S(1)} %slice.115), channel_id=1, source_target_pairs={{2,0},{4,6},{3,1},{5,7},{10,8},{12,14},{11,9},{13,15},{18,16},{20,... | collective-permute-start | bytes 2359304 | tf_op jit(solution)/shard_map/ppermute | solution.py:294
  63.9 17.0 %collective-permute-start.8 = (bf16[528,512]{1,0:T(8,128)(2,1)}, bf16[528,512]{1,0:T(8,128)(2,1)S(1)}, u32[]{:S(2)}, u32[]{:S(2)}) collective-permute-start(bf16[528,512]{1,0:T(8,128)(2,1)} %collective-permute-done.7.rest_3_), channel_id=1, source_target_pairs={{0,1},{1,0},{2,3},{3,2},{4,5},{5,4},{6,7},{7,6},{8,9},{9,8},{10,11... | collective-permute-start | bytes 1622024 | tf_op jit(solution)/shard_map/ppermute | solution.py:33
  64.0 16.9 %copy-start.10 = (bf16[512,512]{1,0:T(8,128)(2,1)}, bf16[512,512]{1,0:T(8,128)(2,1)S(1)}, u32[]{:S(2)}) copy-start(bf16[512,512]{1,0:T(8,128)(2,1)S(1)} %collective-permute-done.9.rest_2_) | copy-start | bytes 1572868
  64.0 25.8 %collective-permute-start.15 = (bf16[1024,512]{1,0:T(8,128)(2,1)}, bf16[1024,512]{1,0:T(8,128)(2,1)S(1)}, u32[]{:S(2)}, u32[]{:S(2)}) collective-permute-start(bf16[1024,512]{1,0:T(8,128)(2,1)} %pad_maximum_fusion.1), channel_id=1, source_target_pairs={{0,16},{8,24},{16,0},{24,8},{1,17},{9,25},{17,1},{25,9},{2,18},{10... | collective-permute-start | bytes 3145736 | tf_op jit(solution)/shard_map/ppermute | solution.py:33
  76.4 25.5 %collective-permute-start.6 = (bf16[1040,512]{1,0:T(8,128)(2,1)}, bf16[1040,512]{1,0:T(8,128)(2,1)}, u32[]{:S(2)}, u32[]{:S(2)}) collective-permute-start(bf16[1040,512]{1,0:T(8,128)(2,1)} %collective-permute-done.1.rest_2_), channel_id=1, source_target_pairs={{0,1},{1,0},{2,3},{3,2},{4,5},{5,4},{6,7},{7,6},{8,9},{9,8},{10,11... | collective-permute-start | bytes 3194888 | tf_op jit(solution)/shard_map/ppermute | solution.py:33
  76.4 0.9 copy-start.5
  77.3 14.7 %collective-permute-start.12 = (bf16[768,512]{1,0:T(8,128)(2,1)}, bf16[768,512]{1,0:T(8,128)(2,1)}, u32[]{:S(2)}, u32[]{:S(2)}) collective-permute-start(bf16[768,512]{1,0:T(8,128)(2,1)} %slice.116), channel_id=1, source_target_pairs={{2,4},{4,2},{3,5},{5,3},{10,12},{12,10},{11,13},{13,11},{18,20},{2... | collective-permute-start | bytes 2359304 | tf_op jit(solution)/shard_map/ppermute | solution.py:295
  80.9 1.3 copy-start.8
  80.9 11.0 %collective-permute-start.13 = (bf16[512,512]{1,0:T(8,128)(2,1)}, bf16[512,512]{1,0:T(8,128)(2,1)}, u32[]{:S(2)}, u32[]{:S(2)}) collective-permute-start(bf16[512,512]{1,0:T(8,128)(2,1)} %collective-permute-done.2.rest_1_), channel_id=1, source_target_pairs={{0,1},{1,0},{2,3},{3,2},{4,5},{5,4},{6,7},{7,6},{8,9},{9,8},{10,11... | collective-permute-start | bytes 1572872 | tf_op jit(solution)/shard_map/ppermute | solution.py:33
  82.3 11.1 %copy-start.3 = (f32[4,192,256]{2,1,0:T(8,128)S(1)}, f32[4,192,256]{2,1,0:T(8,128)}, u32[]{:S(2)}) copy-start(f32[4,192,256]{2,1,0:T(8,128)} %copy-done.2) | copy-start | bytes 2359300
  85.9 18.5 %collective-permute-start.10 = (bf16[512,512]{1,0:T(8,128)(2,1)}, bf16[512,512]{1,0:T(8,128)(2,1)}, u32[]{:S(2)}, u32[]{:S(2)}) collective-permute-start(bf16[512,512]{1,0:T(8,128)(2,1)} %copy-done.10), channel_id=1, source_target_pairs={{0,1},{1,0},{2,3},{3,2},{4,5},{5,4},{6,7},{7,6},{8,9},{9,8},{10,11... | collective-permute-start | bytes 1572872 | tf_op jit(solution)/shard_map/ppermute | solution.py:33
  89.8 16.1 %collective-permute-start.19 = (bf16[512,512]{1,0:T(8,128)(2,1)}, bf16[512,512]{1,0:T(8,128)(2,1)S(1)}, u32[]{:S(2)}, u32[]{:S(2)}) collective-permute-start(bf16[512,512]{1,0:T(8,128)(2,1)} %slice.118), channel_id=1, source_target_pairs={{0,16},{8,24},{16,0},{24,8},{1,17},{9,25},{17,1},{25,9},{2,18},{10... | collective-permute-start | bytes 1572872 | tf_op jit(solution)/shard_map/ppermute | solution.py:33
  92.0 40.5 %collective-permute-start.16 = (bf16[1024,512]{1,0:T(8,128)(2,1)}, bf16[1024,512]{1,0:T(8,128)(2,1)S(1)}, u32[]{:S(2)}, u32[]{:S(2)}) collective-permute-start(bf16[1024,512]{1,0:T(8,128)(2,1)} %collective-permute-done.14.rest_3_), channel_id=1, source_target_pairs={{0,1},{1,0},{2,3},{3,2},{4,5},{5,4},{6,7},{7,6},{8,9},{9,8},{10,11... | collective-permute-start | bytes 3145736 | tf_op jit(solution)/shard_map/ppermute | solution.py:33
  92.0 14.2 %collective-permute-start.23 = (bf16[384,512]{1,0:T(8,128)(2,1)}, bf16[384,512]{1,0:T(8,128)(2,1)}, u32[]{:S(2)}, u32[]{:S(2)}) collective-permute-start(bf16[384,512]{1,0:T(8,128)(2,1)} %get-tuple-element.24), channel_id=1, source_target_pairs={{2,4},{4,2},{3,5},{5,3},{10,12},{12,10},{11,13},{13,11},{18,20},{2... | collective-permute-start | bytes 1179656 | tf_op jit(solution)/shard_map/ppermute | solution.py:295
  93.4 1.1 copy-start.6
  101.9 14.7 %collective-permute-start.18 = (bf16[512,512]{1,0:T(8,128)(2,1)}, bf16[512,512]{1,0:T(8,128)(2,1)}, u32[]{:S(2)}, u32[]{:S(2)}) collective-permute-start(bf16[512,512]{1,0:T(8,128)(2,1)} %slice.117), channel_id=1, source_target_pairs={{0,8},{8,0},{16,24},{24,16},{1,9},{9,1},{17,25},{25,17},{2,10},{10... | collective-permute-start | bytes 1572872 | tf_op jit(solution)/shard_map/ppermute | solution.py:33
  104.3 28.9 %collective-permute-start.17 = (bf16[1024,512]{1,0:T(8,128)(2,1)S(1)}, bf16[1024,512]{1,0:T(8,128)(2,1)S(1)}, u32[]{:S(2)}, u32[]{:S(2)}) collective-permute-start(bf16[1024,512]{1,0:T(8,128)(2,1)S(1)} %collective-permute-done.15.rest_4_), channel_id=1, source_target_pairs={{0,1},{1,0},{2,3},{3,2},{4,5},{5,4},{6,7},{7,6},{8,9},{9,8},{10,11... | collective-permute-start | bytes 3145736 | tf_op jit(solution)/shard_map/ppermute | solution.py:33
  105.8 27.4 %collective-permute-start.21 = (bf16[512,512]{1,0:T(8,128)(2,1)S(1)}, bf16[512,512]{1,0:T(8,128)(2,1)S(1)}, u32[]{:S(2)}, u32[]{:S(2)}) collective-permute-start(bf16[512,512]{1,0:T(8,128)(2,1)S(1)} %collective-permute-done.19.rest_3_.rest_8_), channel_id=1, source_target_pairs={{0,1},{1,0},{2,3},{3,2},{4,5},{5,4},{6,7},{7,6},{8,9},{9,8},{10,11... | collective-permute-start | bytes 1572872 | tf_op jit(solution)/shard_map/ppermute | solution.py:33
  106.2 25.0 %collective-permute-start.22 = (bf16[384,512]{1,0:T(8,128)(2,1)}, bf16[384,512]{1,0:T(8,128)(2,1)S(1)}, u32[]{:S(2)}, u32[]{:S(2)}) collective-permute-start(bf16[384,512]{1,0:T(8,128)(2,1)} %get-tuple-element.23), channel_id=1, source_target_pairs={{2,0},{4,6},{3,1},{5,7},{10,8},{12,14},{11,9},{13,15},{18,16},{20,... | collective-permute-start | bytes 1179656 | tf_op jit(solution)/shard_map/ppermute | solution.py:294
  116.6 16.6 %collective-permute-start.20 = (bf16[512,512]{1,0:T(8,128)(2,1)}, bf16[512,512]{1,0:T(8,128)(2,1)S(1)}, u32[]{:S(2)}, u32[]{:S(2)}) collective-permute-start(bf16[512,512]{1,0:T(8,128)(2,1)} %collective-permute-done.18.rest_2_.rest_7_), channel_id=1, source_target_pairs={{0,1},{1,0},{2,3},{3,2},{4,5},{5,4},{6,7},{7,6},{8,9},{9,8},{10,11... | collective-permute-start | bytes 1572872 | tf_op jit(solution)/shard_map/ppermute | solution.py:33
  116.6 1.0 copy-start.9
  117.7 1.0 copy-start.11
  129.9 1.3 copy-start.14
  129.9 2.6 %copy-start.15 = (bf16[384,512]{1,0:T(8,128)(2,1)S(1)}, bf16[384,512]{1,0:T(8,128)(2,1)}, u32[]{:S(2)}) copy-start(bf16[384,512]{1,0:T(8,128)(2,1)} %get-tuple-element.26) | copy-start | bytes 1179652
  129.9 4.4 %copy-start.7 = (bf16[768,512]{1,0:T(8,128)(2,1)S(1)}, bf16[768,512]{1,0:T(8,128)(2,1)}, u32[]{:S(2)}) copy-start(bf16[768,512]{1,0:T(8,128)(2,1)} %copy-done.5) | copy-start | bytes 2359300
  131.2 21.4 %collective-permute-start.24 = (bf16[384,512]{1,0:T(8,128)(2,1)S(1)}, bf16[384,512]{1,0:T(8,128)(2,1)S(1)}, u32[]{:S(2)}, u32[]{:S(2)}) collective-permute-start(bf16[384,512]{1,0:T(8,128)(2,1)S(1)} %copy-done.14), channel_id=1, source_target_pairs={{2,0},{4,6},{3,1},{5,7},{10,8},{12,14},{11,9},{13,15},{18,16},{20,... | collective-permute-start | bytes 1179656 | tf_op jit(solution)/shard_map/ppermute | solution.py:294
  132.5 8.7 %copy-start.4 = (bf16[1024,512]{1,0:T(8,128)(2,1)}, bf16[1024,512]{1,0:T(8,128)(2,1)S(1)}, u32[]{:S(2)}) copy-start(bf16[1024,512]{1,0:T(8,128)(2,1)S(1)} %collective-permute-done.16.rest_0_.rest_5_) | copy-start | bytes 3145732
  132.5 20.1 %collective-permute-start.25 = (bf16[384,512]{1,0:T(8,128)(2,1)S(1)}, bf16[384,512]{1,0:T(8,128)(2,1)S(1)}, u32[]{:S(2)}, u32[]{:S(2)}) collective-permute-start(bf16[384,512]{1,0:T(8,128)(2,1)S(1)} %copy-done.15), channel_id=1, source_target_pairs={{2,4},{4,2},{3,5},{5,3},{10,12},{12,10},{11,13},{13,11},{18,20},{2... | collective-permute-start | bytes 1179656 | tf_op jit(solution)/shard_map/ppermute | solution.py:295
  133.2 1.0 copy-start.12
  160.1 3.7 %collective-permute-start.26 = (f32[8,256]{1,0:T(8,128)S(1)}, f32[8,256]{1,0:T(8,128)S(1)}, u32[]{:S(2)}, u32[]{:S(2)}) collective-permute-start(f32[8,256]{1,0:T(8,128)S(1)} %fusion.2), channel_id=1, source_target_pairs={{0,8},{8,0},{16,24},{24,16},{1,9},{9,1},{17,25},{25,17},{2,10},{10... | collective-permute-start | bytes 24584 | tf_op jit(solution)/shard_map/ppermute | solution.py:33
  163.8 3.7 %collective-permute-start.27 = (f32[8,256]{1,0:T(8,128)S(1)}, f32[8,256]{1,0:T(8,128)S(1)}, u32[]{:S(2)}, u32[]{:S(2)}) collective-permute-start(f32[8,256]{1,0:T(8,128)S(1)} %add.126), channel_id=1, source_target_pairs={{0,16},{8,24},{16,0},{24,8},{1,17},{9,25},{17,1},{25,9},{2,18},{10... | collective-permute-start | bytes 24584 | tf_op jit(solution)/shard_map/ppermute | solution.py:33
  167.5 11.6 %collective-permute-start.28 = (f32[8,256]{1,0:T(8,128)S(1)}, f32[8,256]{1,0:T(8,128)S(1)}, u32[]{:S(2)}, u32[]{:S(2)}) collective-permute-start(f32[8,256]{1,0:T(8,128)S(1)} %add.127), channel_id=1, source_target_pairs={{0,2},{2,0},{4,6},{6,4},{1,3},{3,1},{5,7},{7,5},{8,10},{10,8},{12,... | collective-permute-start | bytes 24584 | tf_op jit(solution)/shard_map/ppermute | solution.py:33
  179.0 4.5 %collective-permute-start.29 = (f32[8,256]{1,0:T(8,128)S(1)}, f32[8,256]{1,0:T(8,128)S(1)}, u32[]{:S(2)}, u32[]{:S(2)}) collective-permute-start(f32[8,256]{1,0:T(8,128)S(1)} %add.128), channel_id=1, source_target_pairs={{0,4},{2,6},{4,0},{6,2},{1,5},{3,7},{5,1},{7,3},{8,12},{10,14},{12... | collective-permute-start | bytes 24584 | tf_op jit(solution)/shard_map/ppermute | solution.py:33

commit v4 on v3

v4 whole, which is shorter than its diff:
```python
import functools
import math

import jax
import jax.numpy as jnp
from jax import lax
from jax.experimental import pallas as pl
from jax.experimental.pallas import tpu as pltpu
from jax.sharding import PartitionSpec as P

NW = 256

omega_low = -10.0
omega_span = 20.0


def make_grid(count):
    return omega_low + omega_span * jnp.arange(count, dtype=jnp.float32) / (count - 1)


def lookup(indices, table):
    hit = indices[:, None] == jnp.arange(table.shape[0], dtype=jnp.int32)[None, :]
    return jnp.sum(jnp.where(hit, table[None, :], 0.0), axis=1)


def from_behind(block, axis, distance):
    devices = range(lax.axis_size(axis))
    route = [((i - distance) % len(devices), i) for i in devices]
    return lax.ppermute(block, axis, route)


def flip(block, axis, bits):
    return lax.ppermute(block, axis, [(i, i ^ bits) for i in range(lax.axis_size(axis))])


def contribute(full_rows, panel_rows, w_mat, nu_val, weight_val, energies, omega_grid, n_dev):
    product = jnp.dot(full_rows, w_mat, preferred_element_type=jnp.float32)
    contract = jnp.sum(product * panel_rows.astype(jnp.float32), axis=-1).reshape(n_dev, -1)
    offsets = omega_grid[None, :] - energies[:, None]
    kernel = offsets / (offsets * offsets + nu_val * nu_val)
    return -weight_val / math.pi * jnp.dot(contract, kernel, precision=lax.Precision.HIGHEST)


def general(pair_matrix, screened, imag_freq, quad_weight, band_energy, band_index):
    n_dev, m_dev, g_panel = pair_matrix.shape
    f_dev = screened.shape[0]
    cycle_size = lax.axis_size("freq")
    cycle_pos = lax.axis_index("freq")
    full_pairs = lax.all_gather(pair_matrix, "ga", axis=2, tiled=True)
    g_all = full_pairs.shape[2]
    omega_grid = make_grid(NW)
    sigma_part = jnp.zeros((n_dev, NW), jnp.float32)
    panel_rows = pair_matrix.reshape(n_dev * m_dev, g_panel)
    full_rows = full_pairs.reshape(n_dev * m_dev, g_all)
    energies = lookup(band_index, band_energy)
    nu_all = lax.all_gather(imag_freq, "freq", axis=0, tiled=True)
    weight_all = lax.all_gather(quad_weight, "freq", axis=0, tiled=True)
    w_slab = screened
    for turn_index in range(cycle_size):
        source = jnp.mod(cycle_pos - turn_index, cycle_size)
        nu_vals = lax.dynamic_slice_in_dim(nu_all, source * f_dev, f_dev)
        weight_vals = lax.dynamic_slice_in_dim(weight_all, source * f_dev, f_dev)
        for slot in range(f_dev):
            sigma_part = sigma_part + contribute(
                full_rows, panel_rows, w_slab[slot], nu_vals[slot], weight_vals[slot],
                energies, omega_grid, n_dev,
            )
        if turn_index + 1 < cycle_size:
            w_slab = from_behind(w_slab, "freq", 1)
    return lax.psum(sigma_part, ("freq", "ga"))


def choose(flag, yes, no):
    @pl.when(flag == 1)
    def _():
        yes.start()

    @pl.when(flag == 0)
    def _():
        no.start()


def reduce_rows(y_ref, right_ref, weight_ref, slot, out_ref, first, m_dev):
    for k in range(y_ref.shape[0] // m_dev):
        at = slice(k * m_dev, (k + 1) * m_dev)
        z = y_ref[at] * right_ref[at].astype(jnp.float32)
        term = jnp.sum(z, axis=1, keepdims=True) * weight_ref[slot]
        out_ref[first + k] += jnp.sum(term.reshape(m_dev // 8, 8, NW), axis=0)


def alternate(fetch, n_slots, y0, y1, dot0, dot1, sum0, sum1):
    y1[...] = jnp.zeros_like(y1)

    def one(slot, carry):
        fetch(slot + 2)
        fetch.wait(slot)
        y0[...] = dot0(slot)
        sum1(y1, jnp.maximum(slot - 1, 0))
        y1[...] = dot1(slot)
        sum0(y0, slot)
        return carry

    lax.fori_loop(0, n_slots, one, 0)
    sum1(y1, n_slots - 1)


class Fetch:
    def __init__(self, parts, w_all, sems):
        self.parts, self.w_all, self.sems = parts, w_all, sems

    def __call__(self, slot):
        last = self.w_all.shape[0] - 1
        safe = jnp.minimum(slot, last)
        at = 0
        for refs, count in self.parts:
            each = (last + 1) // len(refs)
            for n, ref in enumerate(refs):

                @pl.when((slot >= n * each) & (slot < (n + 1) * each))
                def _():
                    src = ref.at[jnp.clip(slot - n * each, 0, each - 1), :count, :]
                    pltpu.make_async_copy(src, self.w_all.at[safe, at : at + count, :], self.sems.at[safe]).start()

            at += count

    def wait(self, slot):
        pltpu.make_async_copy(self.w_all.at[slot], self.w_all.at[slot], self.sems.at[slot]).wait()


def near_kernel(m_dev, where_ref, k_ref, own_ref, a_ref, b_ref, w_ref, out_ref, left, own, w_all, k_all, y0, y1, sems, w_sems):
    n_slots, depth, panel = w_all.shape
    end, low = where_ref[0], where_ref[1]
    here = left.at[:, pl.ds(pl.multiple_of((1 - low) * panel, panel), panel)]
    there = left.at[:, pl.ds(pl.multiple_of(low * panel, panel), panel)]
    fetch = Fetch([((w_ref,), depth)], w_all, w_sems)
    fetch(0)
    mine = pltpu.make_async_copy(own_ref, here, sems.at[1])
    mine.start()
    near = pltpu.make_async_copy(a_ref, there, sems.at[2])
    choose(end, near, pltpu.make_async_copy(b_ref, there, sems.at[2]))
    late = [
        pltpu.make_async_copy(own_ref, own, sems.at[0]),
        pltpu.make_async_copy(k_ref, k_all, sems.at[3]),
    ]
    for c in late:
        c.start()
    fetch(1)
    out_ref[...] = jnp.zeros_like(out_ref)
    for c in [mine, near] + late:
        c.wait()
    tile = y0.shape[0]
    states = tile // m_dev

    def product(t):
        return lambda s: jnp.dot(left[t * tile : (t + 1) * tile], w_all[s], preferred_element_type=jnp.float32)

    def total(t):
        right = own.at[t * tile : (t + 1) * tile, :]
        return lambda y, s: reduce_rows(y, right, k_all, s, out_ref, t * states, m_dev)

    alternate(fetch, n_slots, y0, y1, product(0), product(1), total(0), total(1))


def far_kernel(m_dev, begin, where_ref, k_ref, own_ref, a_ref, c_ref, d_ref, f_ref, f_other_ref, x_ref, x_other_ref, out_ref, far, own, other, left, w_all, k_all, y0, y1, sems, w_sems):
    n_slots, _, panel = w_all.shape
    end = where_ref[0]
    mine = own_ref.at[begin : begin + own.shape[0], :]
    theirs = a_ref.at[begin : begin + own.shape[0], :]
    fetch = Fetch([((f_ref, f_other_ref), panel), ((x_ref, x_other_ref), panel)], w_all, w_sems)
    fetch(0)
    far_copy = pltpu.make_async_copy(c_ref, far, sems.at[2])
    choose(end, far_copy, pltpu.make_async_copy(d_ref, far, sems.at[2]))
    left_copy = pltpu.make_async_copy(mine, left, sems.at[3])
    choose(end, left_copy, pltpu.make_async_copy(d_ref, left, sems.at[3]))
    late = [
        pltpu.make_async_copy(mine, own, sems.at[0]),
        pltpu.make_async_copy(theirs, other, sems.at[1]),
        pltpu.make_async_copy(k_ref, k_all, sems.at[4]),
    ]
    for c in late:
        c.start()
    fetch(1)
    out_ref[...] = jnp.zeros_like(out_ref)
    for c in [far_copy, left_copy] + late:
        c.wait()
    alternate(
        fetch, n_slots, y0, y1,
        lambda s: jnp.dot(far[...], w_all[s, :panel], preferred_element_type=jnp.float32),
        lambda s: jnp.dot(left[...], w_all[s, panel:], preferred_element_type=jnp.float32),
        lambda y, s: reduce_rows(y, own, k_all, s, out_ref, 0, m_dev),
        lambda y, s: reduce_rows(y, other, k_all, s, out_ref, 0, m_dev),
    )


def run_kernel(body, where, k_part, mats, arrays, lefts, tile, n_rows, m_dev):
    panel = mats[0].shape[1]
    n_slots, depth = k_part.shape[0], 2 * panel
    scratch = [pltpu.VMEM((n_rows, width), jnp.bfloat16) for width in lefts]
    scratch += [
        pltpu.VMEM((n_slots, depth, panel), jnp.bfloat16),
        pltpu.VMEM(k_part.shape, jnp.float32),
        pltpu.VMEM((tile, panel), jnp.float32),
        pltpu.VMEM((tile, panel), jnp.float32),
        pltpu.SemaphoreType.DMA((5,)),
        pltpu.SemaphoreType.DMA((n_slots,)),
    ]
    flops = 2 * n_rows * depth * panel * n_slots
    return pl.pallas_call(
        body,
        out_shape=jax.ShapeDtypeStruct((n_rows // m_dev, 8, NW), jnp.float32),
        in_specs=[pl.BlockSpec(memory_space=pltpu.SMEM)]
        + [pl.BlockSpec(memory_space=pl.ANY)] * (1 + len(mats) + len(arrays)),
        out_specs=pl.BlockSpec(memory_space=pltpu.VMEM),
        scratch_shapes=scratch,
        cost_estimate=pl.CostEstimate(flops=flops, bytes_accessed=depth * panel, transcendentals=0),
        compiler_params=pltpu.CompilerParams(vmem_limit_bytes=48 * 2**20),
    )(where, k_part, *mats, *arrays)


def split3(x):
    hi = lax.reduce_precision(x, 8, 7)
    mid = lax.reduce_precision(x - hi, 8, 7)
    return jnp.stack([hi, mid, (x - hi) - mid])


def after(value, *others):
    return lax.optimization_barrier((value,) + others)[0]


def square_line(pair_matrix, screened, imag_freq, quad_weight, band_energy, band_index):
    n_dev, m_dev, panel = pair_matrix.shape
    ga = lax.axis_index("ga")
    core = lax.axis_index("band")
    rows = n_dev * m_dev
    own = pair_matrix.reshape(rows, panel)
    end = (ga == 0) | (ga == 3)
    low = ga < 2
    near_at = jnp.where(ga == 0, 0, jnp.where(ga == 3, 2, 1)) * panel
    far_at = (ga + 2) % 4 * panel
    give_at = jnp.where(ga % 2 == 0, 3, 0) * panel
    where = jnp.stack([end, low]).astype(jnp.int32)

    outer = [(0, 1), (1, 0), (2, 3), (3, 2)]
    inner = [(1, 2), (2, 1)]
    outward = [(1, 0), (2, 3)]

    def piece(start, count):
        return lax.dynamic_slice(screened, (core, start, 0), (1, count, panel))[0]

    node = split3(jnp.stack([imag_freq[core], quad_weight[core]])).reshape(1, 6)
    node = jnp.pad(node, ((0, 15), (0, panel - 6))).astype(jnp.bfloat16)
    near_w = jnp.concatenate([piece(near_at, 2 * panel), node])
    near_w = lax.all_gather(near_w, "freq")
    a_rows = lax.ppermute(own, "ga", outer)
    b_rows = lax.ppermute(own, "ga", inner)
    given = lax.ppermute(piece(give_at, panel), "ga", outer)
    near_o = flip(after(near_w, a_rows, b_rows, given), "band", 1)

    energies = lookup(band_index, band_energy)
    offsets = make_grid(NW)[None, :] - energies[:, None]

    def weigh(slots):
        nodes = slots[:, 2 * panel, :6].astype(jnp.float32).reshape(-1, 3, 2)
        nodes = (nodes[:, 0] + nodes[:, 1]) + nodes[:, 2]
        nu, weight = nodes[:, 0, None, None], nodes[:, 1, None, None]
        return (-weight / math.pi) * (offsets / (offsets * offsets + nu * nu))

    def close(slots, k_part):
        return run_kernel(
            functools.partial(near_kernel, m_dev), where, k_part,
            (own, a_rows, b_rows), (slots,), (2 * panel, panel), rows // 2, rows, m_dev,
        )

    k_here, k_there = weigh(near_w), weigh(near_o)
    near = close(near_w, k_here)
    near_other = close(near_o, k_there)

    far_w = lax.all_gather(after(piece(far_at, panel), a_rows, b_rows, given), "freq")
    cuts = ((0, rows // 2), (rows // 2, rows // 2))
    c_rows = [lax.ppermute(b_rows[i : i + count], "ga", outward) for i, count in cuts]
    d_rows = [lax.ppermute(a_rows[i : i + count], "ga", inner) for i, count in cuts]
    given_w = lax.all_gather(after(given, near, c_rows[0], d_rows[0]), "freq")
    far_o = flip(after(far_w, near_other, c_rows[0], d_rows[0]), "band", 1)
    given_o = flip(after(given_w, c_rows[1], d_rows[1]), "band", 1)
    k_all = jnp.concatenate([k_here, k_there])
    parts = [
        run_kernel(
            functools.partial(far_kernel, m_dev, i), where, k_all,
            (own, a_rows, c_rows[n], d_rows[n]), (far_w, far_o, given_w, given_o),
            (panel,) * 4, count, count, m_dev,
        )
        for n, (i, count) in enumerate(cuts)
    ]
    sigma = jnp.sum(near + near_other + jnp.concatenate(parts), axis=1)
    for axis in ("freq", "ga"):
        t1, t2, t3 = (flip(sigma, axis, r) for r in (1, 2, 3))
        sigma = (sigma + t1) + (t2 + t3)
    return sigma


def on_device(pair_matrix, screened, *rest):
    sizes = tuple(lax.axis_size(a) for a in ("freq", "ga", "band"))
    fits = sizes == (4, 4, 2) and screened.shape[0] == 2 and pair_matrix.shape[0] % 8 == 0
    return (square_line if fits else general)(pair_matrix, screened, *rest)


def solution(mesh):
    placed = (P("band", "freq", "ga"), P("freq", None, "ga"), P("freq"), P("freq"), P(), P("freq"))
    return jax.shard_map(
        on_device, mesh=mesh, in_specs=placed, out_specs=P("band", None), check_vma=False
    )
```

time: 185 us -> 195 us (1.054)
  waiting for transfers between devices: 55.2 us -> 95.7 us
  starting transfers between devices: 41.4 us -> 21.9 us
  between operations: 0.38 us -> 13.3 us
  local copies, waits for them, and re-layouts: 25.8 us -> 13 us
  Pallas kernels: 51.3 us -> 44 us
  other arithmetic: 10.1 us -> 6.85 us
    ppermute x1, waiting for transfers between devices: 2 us -> 38.8 us  [square_line(): given = lax.ppermute(piece(give_at, panel), 'ga', outer)]
    ppermute x21 -> x9, waiting for transfers between devices: 43.9 us -> 12.5 us  [flip(): lax.ppermute(block, axis, [(i, i ^ bits) for i in range(lax.axis_size(axi...]
    all_gather x0 -> x3, waiting for transfers between devices: none -> 30.3 us  [the longest x1 23.3 us: square_line(): given_w = lax.all_gather(after(given, near, c_rows[0], d_rows[0]), 'freq')]
    ppermute x21 -> x9, starting transfers between devices: 27.3 us -> 8.02 us  [flip(): lax.ppermute(block, axis, [(i, i ^ bits) for i in range(lax.axis_size(axi...]
    slice x10 -> x0, local copies, waits for them, and re-layouts: 9.82 us -> none  [the longest x6 4.13 us: carried(): w[row, :6]]
    pallas_call x6 -> x4, Pallas kernels: 51.3 us -> 44 us  [run_kernel(): pl.pallas_call(body, out_shape=jax.ShapeDtypeStruct((n_rows // m_dev, 8,...]
    ppermute x7 -> x5, waiting for transfers between devices: 9.23 us -> 14 us  [the longest x2 14 us: square_line(): lax.ppermute(b_rows[i:i + count], 'ga', outward)]
    concatenate x2 -> x0, other arithmetic: 2.42 us -> none  [the longest x1 2.35 us: square_line(): far_w = jnp.concatenate([piece(far_at, panel), given])]
  transfers between devices with their start and end apart: 30 -> 19, of which waited for: 11 -> 12; matrix products, arithmetic and copies ran while one was open for 15% -> 4% of each run, Pallas kernels for 24% -> 11%
where the time goes in v4:
time: 195 us
  waiting for transfers between devices  95.7 us (49%)
  Pallas kernels  44 us (23%)
  starting transfers between devices  21.9 us (11%)
  between operations  13.3 us (7%)
  local copies, waits for them, and re-layouts  13 us (7%)
  other arithmetic  6.85 us (4%)
    pallas_call x4, Pallas kernels, run_kernel(): pl.pallas_call(body, out_shape=jax.ShapeDtypeStruct((n_rows // m_dev, 8,...  44 us
    ppermute x1, waiting for transfers between devices, square_line(): given = lax.ppermute(piece(give_at, panel), 'ga', outer)  38.8 us
    all_gather x1, waiting for transfers between devices, square_line(): given_w = lax.all_gather(after(given, near, c_rows[0], d_rows[0]), 'freq')  23.3 us
    ppermute x2, waiting for transfers between devices, square_line(): lax.ppermute(b_rows[i:i + count], 'ga', outward)  14 us
    ppermute x9, waiting for transfers between devices, flip(): lax.ppermute(block, axis, [(i, i ^ bits) for i in range(lax.axis_size(axi...  12.5 us
    ppermute x9, starting transfers between devices, flip(): lax.ppermute(block, axis, [(i, i ^ bits) for i in range(lax.axis_size(axi...  8.02 us
    all_gather x1, waiting for transfers between devices, square_line(): near_w = lax.all_gather(near_w, 'freq')  7 us
    unnamed x14, local copies, waits for them, and re-layouts  4.31 us
  transfers between devices with their start and end apart: 19, of which 12 were waited for; matrix products, arithmetic and copies ran while one was open for 4% of the time, Pallas kernels for 11%

profile of v4, /device:TPU:0, one launch (start us, length us, event | category | flops | bytes accessed | tf_op | source)
XLA Modules:
  0.0 194.8 jit_solution(7314208555800286501)
XLA Ops:
  6.5 1.3 dynamic_slice.16
  7.8 1.2 dynamic_slice.17
  9.0 1.3 reduce-precision_convert_fusion.1
  10.4 0.1 reshape.200
  10.5 1.3 dynamic-slice_bitcast_fusion
  11.8 1.1 fusion.1
  12.8 0.0 all-gather.7.cloned.1.call-update
  12.9 0.0 all-gather.9.cloned.1.call-start
  12.9 3.1 %collective-permute-start = (bf16[1536,512]{1,0:T(8,128)(2,1)}, bf16[1536,512]{1,0:T(8,128)(2,1)S(1)}, u32[]{:S(2)}, u32[]{:S(2)}) collective-permute-start(bf16[1536,512]{1,0:T(8,128)(2,1)} %bitcast.9.own_ref), channel_id=1, source_target_pairs={{0,2},{2,0},{4,6},{6,4},{1,3},{3,1},{5,7},{7,5},{8,10},{10,8},{12,... | collective-permute-start | bytes 4718600 | tf_op jit(solution)/shard_map/ppermute | solution.py:254
  16.0 0.7 collective-permute-start.1
  16.8 2.1 %dynamic-slice_bitcast_fusion.1 = (bf16[512,512]{1,0:T(8,128)(2,1)}, bf16[512,512]{1,0:T(8,128)(2,1)S(1)}) fusion(bf16[2,2048,512]{2,1,0:T(8,128)(2,1)} %param.7, s32[]{:T(128)S(6)} %select_n.42, s32[]{:T(128)S(6)} %select_n.51, s32[]{:T(128)S(6)} %select_n.49), kind=kLoop, calls=%fused_computation.7 | loop fusion | bytes 2097164 | tf_op jit(solution)/shard_map/squeeze | solution.py:248
  18.9 4.3 %collective-permute-start.2 = (bf16[512,512]{1,0:T(8,128)(2,1)S(1)}, bf16[512,512]{1,0:T(8,128)(2,1)}, u32[]{:S(2)}, u32[]{:S(2)}) collective-permute-start(bf16[512,512]{1,0:T(8,128)(2,1)S(1)} %get-tuple-element.18), channel_id=1, source_target_pairs={{0,2},{2,0},{4,6},{6,4},{1,3},{3,1},{5,7},{7,5},{8,10},{10,8},{12,... | collective-permute-start | bytes 1572872 | tf_op jit(solution)/shard_map/ppermute | solution.py:256
  23.2 38.8 %collective-permute-done.2 = bf16[512,512]{1,0:T(8,128)(2,1)} collective-permute-done((bf16[512,512]{1,0:T(8,128)(2,1)S(1)}, bf16[512,512]{1,0:T(8,128)(2,1)}, u32[]{:S(2)}, u32[]{:S(2)}) %collective-permute-start.2) | collective-permute-done | bytes 524320 | tf_op jit(solution)/shard_map/ppermute | solution.py:256
  61.9 0.0 collective-permute-done.a_ref
  61.9 0.0 collective-permute-done.1.b_ref
  62.0 7.0 %all-gather.7.cloned.1.call-done = bf16[4160,512]{1,0:T(8,128)(2,1)} async-done(((bf16[1040,512]{1,0:T(8,128)(2,1)}), bf16[4160,512]{1,0:T(8,128)(2,1)}) %all-gather.7.cloned.1.call-update) | async-done | bytes 4259856 | tf_op jit(solution)/shard_map/all_gather | solution.py:253
  69.0 0.0 collective-permute-start.3
  69.0 0.0 all-gather.9.cloned.1.call-update
  69.0 0.0 all-gather.11.cloned.1.call-start
  69.0 0.1 add_convert_fusion.where_ref
  69.1 0.2 select_reduce_fusion
  69.3 0.8 broadcast_subtract_fusion
  70.1 1.3 fusion.7
  71.4 1.6 collective-permute-start.5
  72.9 1.3 fusion.8
  74.2 1.3 collective-permute-start.4
  75.5 0.7 slice_convert_fusion.1
  76.2 0.1 copy.13
  76.3 0.2 collective-permute-done.3.w_ref
  76.6 0.7 slice_convert_fusion
  77.3 0.1 copy.14
  77.4 1.2 divide_multiply_fusion.1
  78.6 1.5 copy-done.2
  80.2 10.7 %shard_map.64 = f32[8,8,256]{2,1,0:T(8,128)S(1)} custom-call(s32[2]{0:T(128)S(1)} %add_convert_fusion.where_ref, f32[4,192,256]{2,1,0:T(8,128)S(1)} %get-tuple-element.23.k_ref, bf16[1536,512]{1,0:T(8,128)(2,1)} %bitcast.9.own_ref, bf16[1536,512]{1,0:T(8,128)(2,1)S(1)} %collective-permute-done.a_ref, bf16[1536,512]{1,0:T(8,128)(2,1)S(1)} %copy-done.2, ...), custom_call_target="tpu_custom_call" | custom-call | flops 6442450944 | bytes 524288 | tf_op jit(solution)/shard_map/pallas_call | solution.py:208
  90.9 6.1 %collective-permute-done.4.c_ref = bf16[768,512]{1,0:T(8,128)(2,1)} collective-permute-done((bf16[768,512]{1,0:T(8,128)(2,1)}, bf16[768,512]{1,0:T(8,128)(2,1)}, u32[]{:S(2)}, u32[]{:S(2)}) %collective-permute-start.4) | collective-permute-done | bytes 786464 | tf_op jit(solution)/shard_map/ppermute | solution.py:280
  97.1 0.0 all-gather.11.cloned.1.call-update
  97.1 1.6 collective-permute-start.8
  98.6 1.3 collective-permute-start.7
  100.0 1.4 copy-done.3
  101.4 10.7 %shard_map.65 = f32[8,8,256]{2,1,0:T(8,128)S(1)} custom-call(s32[2]{0:T(128)S(1)} %add_convert_fusion.where_ref, f32[4,192,256]{2,1,0:T(8,128)S(1)} %get-tuple-element.24.k_ref, bf16[1536,512]{1,0:T(8,128)(2,1)} %bitcast.9.own_ref, bf16[1536,512]{1,0:T(8,128)(2,1)S(1)} %collective-permute-done.a_ref, bf16[1536,512]{1,0:T(8,128)(2,1)S(1)} %copy-done.3, ...), custom_call_target="tpu_custom_call" | custom-call | flops 6442450944 | bytes 524288 | tf_op jit(solution)/shard_map/pallas_call | solution.py:208
  112.0 0.0 all-gather.9.cloned.1.call-done
  112.1 0.1 collective-permute-start.6
  112.2 7.9 %collective-permute-done.7.c_ref = bf16[768,512]{1,0:T(8,128)(2,1)} collective-permute-done((bf16[768,512]{1,0:T(8,128)(2,1)}, bf16[768,512]{1,0:T(8,128)(2,1)}, u32[]{:S(2)}, u32[]{:S(2)}) %collective-permute-start.7) | collective-permute-done | bytes 786464 | tf_op jit(solution)/shard_map/ppermute | solution.py:280
  120.0 23.3 %all-gather.11.cloned.1.call-done = bf16[2048,512]{1,0:T(8,128)(2,1)} async-done(((bf16[512,512]{1,0:T(8,128)(2,1)}), bf16[2048,512]{1,0:T(8,128)(2,1)}) %all-gather.11.cloned.1.call-update) | async-done | bytes 2097168 | tf_op jit(solution)/shard_map/all_gather | solution.py:282
  143.3 0.0 collective-permute-start.9
  143.4 0.1 pad_maximum_fusion.k_ref
  143.5 0.0 collective-permute-done.6.f_other_ref
  143.5 4.3 %collective-permute-done.9.x_other_ref = bf16[4,512,512]{2,1,0:T(8,128)(2,1)S(1)} collective-permute-done((bf16[4,512,512]{2,1,0:T(8,128)(2,1)}, bf16[4,512,512]{2,1,0:T(8,128)(2,1)S(1)}, u32[]{:S(2)}, u32[]{:S(2)}) %collective-permute-start.9) | collective-permute-done | bytes 2097184 | tf_op jit(solution)/shard_map/ppermute | solution.py:33
  147.7 1.3 copy-done.6
  149.1 11.2 %shard_map.66 = f32[4,8,256]{2,1,0:T(8,128)S(1)} custom-call(s32[2]{0:T(128)S(1)} %add_convert_fusion.where_ref, f32[8,192,256]{2,1,0:T(8,128)S(1)} %pad_maximum_fusion.k_ref, bf16[1536,512]{1,0:T(8,128)(2,1)} %bitcast.9.own_ref, bf16[1536,512]{1,0:T(8,128)(2,1)} %copy-done, bf16[768,512]{1,0:T(8,128)(2,1)} %collective-permute-done.4.c_ref, ...), custom_call_target="tpu_custom_call" | custom-call | flops 6442450944 | bytes 524288 | tf_op jit(solution)/shard_map/pallas_call | solution.py:208
  160.3 11.4 %shard_map.67 = f32[4,8,256]{2,1,0:T(8,128)S(1)} custom-call(s32[2]{0:T(128)S(1)} %add_convert_fusion.where_ref, f32[8,192,256]{2,1,0:T(8,128)S(1)} %pad_maximum_fusion.k_ref, bf16[1536,512]{1,0:T(8,128)(2,1)} %bitcast.9.own_ref, bf16[1536,512]{1,0:T(8,128)(2,1)} %copy-done, bf16[768,512]{1,0:T(8,128)(2,1)} %collective-permute-done.7.c_ref, ...), custom_call_target="tpu_custom_call" | custom-call | flops 6442450944 | bytes 524288 | tf_op jit(solution)/shard_map/pallas_call | solution.py:208
  171.7 1.5 collective-permute-start.10
  173.2 0.6 collective-permute-start.11
  173.8 1.5 collective-permute-start.12
  175.3 0.2 collective-permute-done.10
  175.4 1.5 collective-permute-done.11
  176.9 1.5 collective-permute-done.12
  178.4 1.0 collective-permute-start.13
  179.4 2.9 %collective-permute-start.14 = (f32[8,256]{1,0:T(8,128)S(1)}, f32[8,256]{1,0:T(8,128)S(1)}, u32[]{:S(2)}, u32[]{:S(2)}) collective-permute-start(f32[8,256]{1,0:T(8,128)S(1)} %add_add_fusion.1), channel_id=1, source_target_pairs={{0,4},{2,6},{4,0},{6,2},{1,5},{3,7},{5,1},{7,3},{8,12},{10,14},{12... | collective-permute-start | bytes 24584 | tf_op jit(solution)/shard_map/ppermute | solution.py:33
  182.3 0.5 collective-permute-start.15
  182.8 0.0 collective-permute-done.13
  182.8 1.2 collective-permute-done.14
  183.9 3.8 %collective-permute-done.15 = f32[8,256]{1,0:T(8,128)S(1)} collective-permute-done((f32[8,256]{1,0:T(8,128)S(1)}, f32[8,256]{1,0:T(8,128)S(1)}, u32[]{:S(2)}, u32[]{:S(2)}) %collective-permute-start.15) | collective-permute-done | bytes 8224 | tf_op jit(solution)/shard_map/ppermute | solution.py:33
  187.7 0.6 add_add_fusion
  (24 shorter events, 0.1 us)
Async XLA Ops:
  6.5 62.4 %all-gather.7.cloned.1.call-start = ((), (), s32[]{:S(2)}) async-start(), calls=%async_computation | async-start | bytes 5324800 | tf_op jit(solution)/shard_map/all_gather | solution.py:253
  12.8 56.3 %copy-start.4 = (f32[256]{0:T(256)S(1)}, f32[256]{0:T(256)}, u32[]{:S(2)}) copy-start(f32[256]{0:T(256)} %param.10) | copy-start | bytes 3076
  12.8 56.3 %copy-start.5 = (s32[192]{0:T(256)S(1)}, s32[192]{0:T(256)}, u32[]{:S(2)}) copy-start(s32[192]{0:T(256)} %param.11) | copy-start | bytes 2308
  12.9 99.2 %all-gather.9.cloned.1.call-start = ((), (), s32[]{:S(2)}) async-start(), calls=%async_computation.1 | async-start | bytes 2621440 | tf_op jit(solution)/shard_map/all_gather | solution.py:278
  12.9 49.0 %collective-permute-start = (bf16[1536,512]{1,0:T(8,128)(2,1)}, bf16[1536,512]{1,0:T(8,128)(2,1)S(1)}, u32[]{:S(2)}, u32[]{:S(2)}) collective-permute-start(bf16[1536,512]{1,0:T(8,128)(2,1)} %bitcast.9.own_ref), channel_id=1, source_target_pairs={{0,2},{2,0},{4,6},{6,4},{1,3},{3,1},{5,7},{7,5},{8,10},{10,8},{12,... | collective-permute-start | bytes 4718600 | tf_op jit(solution)/shard_map/ppermute | solution.py:254
  16.0 46.0 %collective-permute-start.1 = (bf16[1536,512]{1,0:T(8,128)(2,1)}, bf16[1536,512]{1,0:T(8,128)(2,1)S(1)}, u32[]{:S(2)}, u32[]{:S(2)}) collective-permute-start(bf16[1536,512]{1,0:T(8,128)(2,1)} %bitcast.9.own_ref), channel_id=1, source_target_pairs={{2,4},{4,2},{3,5},{5,3},{10,12},{12,10},{11,13},{13,11},{18,20},{2... | collective-permute-start | bytes 4718600 | tf_op jit(solution)/shard_map/ppermute | solution.py:255
  18.9 43.1 %collective-permute-start.2 = (bf16[512,512]{1,0:T(8,128)(2,1)S(1)}, bf16[512,512]{1,0:T(8,128)(2,1)}, u32[]{:S(2)}, u32[]{:S(2)}) collective-permute-start(bf16[512,512]{1,0:T(8,128)(2,1)S(1)} %get-tuple-element.18), channel_id=1, source_target_pairs={{0,2},{2,0},{4,6},{6,4},{1,3},{3,1},{5,7},{7,5},{8,10},{10,8},{12,... | collective-permute-start | bytes 1572872 | tf_op jit(solution)/shard_map/ppermute | solution.py:256
  61.9 38.0 %copy-start = (bf16[1536,512]{1,0:T(8,128)(2,1)}, bf16[1536,512]{1,0:T(8,128)(2,1)S(1)}, u32[]{:S(2)}) copy-start(bf16[1536,512]{1,0:T(8,128)(2,1)S(1)} %collective-permute-done.a_ref) | copy-start | bytes 4718596
  62.0 12.3 %copy-start.1 = (bf16[1536,512]{1,0:T(8,128)(2,1)}, bf16[1536,512]{1,0:T(8,128)(2,1)S(1)}, u32[]{:S(2)}) copy-start(bf16[1536,512]{1,0:T(8,128)(2,1)S(1)} %collective-permute-done.1.b_ref) | copy-start | bytes 4718596
  69.0 7.6 %collective-permute-start.3 = (bf16[4,1040,512]{2,1,0:T(8,128)(2,1)}, bf16[4,1040,512]{2,1,0:T(8,128)(2,1)}, u32[]{:S(2)}, u32[]{:S(2)}) collective-permute-start(bf16[4,1040,512]{2,1,0:T(8,128)(2,1)} %bitcast.30), channel_id=1, source_target_pairs={{0,1},{1,0},{2,3},{3,2},{4,5},{5,4},{6,7},{7,6},{8,9},{9,8},{10,11... | collective-permute-start | bytes 12779528 | tf_op jit(solution)/shard_map/ppermute | solution.py:33
  69.0 74.4 %all-gather.11.cloned.1.call-start = ((), (), s32[]{:S(2)}) async-start(), calls=%async_computation.2 | async-start | bytes 2621440 | tf_op jit(solution)/shard_map/all_gather | solution.py:282
  71.4 19.5 %collective-permute-start.5 = (bf16[768,512]{1,0:T(8,128)(2,1)}, bf16[768,512]{1,0:T(8,128)(2,1)}, u32[]{:S(2)}, u32[]{:S(2)}) collective-permute-start(bf16[768,512]{1,0:T(8,128)(2,1)} %get-tuple-element.19), channel_id=1, source_target_pairs={{2,4},{4,2},{3,5},{5,3},{10,12},{12,10},{11,13},{13,11},{18,20},{2... | collective-permute-start | bytes 2359304 | tf_op jit(solution)/shard_map/ppermute | solution.py:281
  74.2 22.8 %collective-permute-start.4 = (bf16[768,512]{1,0:T(8,128)(2,1)}, bf16[768,512]{1,0:T(8,128)(2,1)}, u32[]{:S(2)}, u32[]{:S(2)}) collective-permute-start(bf16[768,512]{1,0:T(8,128)(2,1)} %get-tuple-element.21), channel_id=1, source_target_pairs={{2,0},{4,6},{3,1},{5,7},{10,8},{12,14},{11,9},{13,15},{18,16},{20,... | collective-permute-start | bytes 2359304 | tf_op jit(solution)/shard_map/ppermute | solution.py:280
  78.6 1.6 copy-start.2
  97.1 15.1 %collective-permute-start.8 = (bf16[768,512]{1,0:T(8,128)(2,1)}, bf16[768,512]{1,0:T(8,128)(2,1)}, u32[]{:S(2)}, u32[]{:S(2)}) collective-permute-start(bf16[768,512]{1,0:T(8,128)(2,1)} %get-tuple-element.20), channel_id=1, source_target_pairs={{2,4},{4,2},{3,5},{5,3},{10,12},{12,10},{11,13},{13,11},{18,20},{2... | collective-permute-start | bytes 2359304 | tf_op jit(solution)/shard_map/ppermute | solution.py:281
  98.6 21.4 %collective-permute-start.7 = (bf16[768,512]{1,0:T(8,128)(2,1)}, bf16[768,512]{1,0:T(8,128)(2,1)}, u32[]{:S(2)}, u32[]{:S(2)}) collective-permute-start(bf16[768,512]{1,0:T(8,128)(2,1)} %get-tuple-element.22), channel_id=1, source_target_pairs={{2,0},{4,6},{3,1},{5,7},{10,8},{12,14},{11,9},{13,15},{18,16},{20,... | collective-permute-start | bytes 2359304 | tf_op jit(solution)/shard_map/ppermute | solution.py:280
  99.9 1.4 copy-start.3
  112.1 31.4 %collective-permute-start.6 = (bf16[4,512,512]{2,1,0:T(8,128)(2,1)}, bf16[4,512,512]{2,1,0:T(8,128)(2,1)}, u32[]{:S(2)}, u32[]{:S(2)}) collective-permute-start(bf16[4,512,512]{2,1,0:T(8,128)(2,1)} %bitcast.33), channel_id=1, source_target_pairs={{0,1},{1,0},{2,3},{3,2},{4,5},{5,4},{6,7},{7,6},{8,9},{9,8},{10,11... | collective-permute-start | bytes 6291464 | tf_op jit(solution)/shard_map/ppermute | solution.py:33
  143.3 4.4 %collective-permute-start.9 = (bf16[4,512,512]{2,1,0:T(8,128)(2,1)}, bf16[4,512,512]{2,1,0:T(8,128)(2,1)S(1)}, u32[]{:S(2)}, u32[]{:S(2)}) collective-permute-start(bf16[4,512,512]{2,1,0:T(8,128)(2,1)} %bitcast.36), channel_id=1, source_target_pairs={{0,1},{1,0},{2,3},{3,2},{4,5},{5,4},{6,7},{7,6},{8,9},{9,8},{10,11... | collective-permute-start | bytes 6291464 | tf_op jit(solution)/shard_map/ppermute | solution.py:33
  147.7 1.4 copy-start.6
  171.7 3.7 %collective-permute-start.10 = (f32[8,256]{1,0:T(8,128)S(1)}, f32[8,256]{1,0:T(8,128)S(1)}, u32[]{:S(2)}, u32[]{:S(2)}) collective-permute-start(f32[8,256]{1,0:T(8,128)S(1)} %fusion.2), channel_id=1, source_target_pairs={{0,8},{8,0},{16,24},{24,16},{1,9},{9,1},{17,25},{25,17},{2,10},{10... | collective-permute-start | bytes 24584 | tf_op jit(solution)/shard_map/ppermute | solution.py:33
  173.2 3.7 %collective-permute-start.11 = (f32[8,256]{1,0:T(8,128)S(1)}, f32[8,256]{1,0:T(8,128)S(1)}, u32[]{:S(2)}, u32[]{:S(2)}) collective-permute-start(f32[8,256]{1,0:T(8,128)S(1)} %fusion.2), channel_id=1, source_target_pairs={{0,16},{8,24},{16,0},{24,8},{1,17},{9,25},{17,1},{25,9},{2,18},{10... | collective-permute-start | bytes 24584 | tf_op jit(solution)/shard_map/ppermute | solution.py:33
  173.8 4.5 %collective-permute-start.12 = (f32[8,256]{1,0:T(8,128)S(1)}, f32[8,256]{1,0:T(8,128)S(1)}, u32[]{:S(2)}, u32[]{:S(2)}) collective-permute-start(f32[8,256]{1,0:T(8,128)S(1)} %fusion.2), channel_id=1, source_target_pairs={{0,24},{8,16},{16,8},{24,0},{1,25},{9,17},{17,9},{25,1},{2,26},{10... | collective-permute-start | bytes 24584 | tf_op jit(solution)/shard_map/ppermute | solution.py:33
  178.4 4.4 %collective-permute-start.13 = (f32[8,256]{1,0:T(8,128)S(1)}, f32[8,256]{1,0:T(8,128)S(1)}, u32[]{:S(2)}, u32[]{:S(2)}) collective-permute-start(f32[8,256]{1,0:T(8,128)S(1)} %add_add_fusion.1), channel_id=1, source_target_pairs={{0,2},{2,0},{4,6},{6,4},{1,3},{3,1},{5,7},{7,5},{8,10},{10,8},{12,... | collective-permute-start | bytes 24584 | tf_op jit(solution)/shard_map/ppermute | solution.py:33
  179.4 4.5 %collective-permute-start.14 = (f32[8,256]{1,0:T(8,128)S(1)}, f32[8,256]{1,0:T(8,128)S(1)}, u32[]{:S(2)}, u32[]{:S(2)}) collective-permute-start(f32[8,256]{1,0:T(8,128)S(1)} %add_add_fusion.1), channel_id=1, source_target_pairs={{0,4},{2,6},{4,0},{6,2},{1,5},{3,7},{5,1},{7,3},{8,12},{10,14},{12... | collective-permute-start | bytes 24584 | tf_op jit(solution)/shard_map/ppermute | solution.py:33
  182.3 5.4 %collective-permute-start.15 = (f32[8,256]{1,0:T(8,128)S(1)}, f32[8,256]{1,0:T(8,128)S(1)}, u32[]{:S(2)}, u32[]{:S(2)}) collective-permute-start(f32[8,256]{1,0:T(8,128)S(1)} %add_add_fusion.1), channel_id=1, source_target_pairs={{0,6},{2,4},{4,2},{6,0},{1,7},{3,5},{5,3},{7,1},{8,14},{10,12},{12... | collective-permute-start | bytes 24584 | tf_op jit(solution)/shard_map/ppermute | solution.py:33
Sparse Core Ops, SparseCore 0:
  13.0 55.9 all-gather.6
  70.8 35.3 all-gather.8
  108.0 35.2 all-gather.10

commit v5 on v2

v5 whole, which is shorter than its diff:
```python
import functools
import math

import jax
import jax.numpy as jnp
from jax import lax
from jax.experimental import pallas as pl
from jax.experimental.pallas import tpu as pltpu
from jax.sharding import PartitionSpec as P

NW = 256

omega_low = -10.0
omega_span = 20.0


def make_grid(count):
    return omega_low + omega_span * jnp.arange(count, dtype=jnp.float32) / (count - 1)


def lookup(indices, table):
    hit = indices[:, None] == jnp.arange(table.shape[0], dtype=jnp.int32)[None, :]
    return jnp.sum(jnp.where(hit, table[None, :], 0.0), axis=1)


def from_behind(block, axis, distance):
    devices = range(lax.axis_size(axis))
    route = [((i - distance) % len(devices), i) for i in devices]
    return lax.ppermute(block, axis, route)


def flip(block, axis, bits):
    return lax.ppermute(block, axis, [(i, i ^ bits) for i in range(lax.axis_size(axis))])


def contribute(full_rows, panel_rows, w_mat, nu_val, weight_val, energies, omega_grid, n_dev):
    product = jnp.dot(full_rows, w_mat, preferred_element_type=jnp.float32)
    contract = jnp.sum(product * panel_rows.astype(jnp.float32), axis=-1).reshape(n_dev, -1)
    offsets = omega_grid[None, :] - energies[:, None]
    kernel = offsets / (offsets * offsets + nu_val * nu_val)
    return -weight_val / math.pi * jnp.dot(contract, kernel, precision=lax.Precision.HIGHEST)


def general(pair_matrix, screened, imag_freq, quad_weight, band_energy, band_index):
    n_dev, m_dev, g_panel = pair_matrix.shape
    f_dev = screened.shape[0]
    cycle_size = lax.axis_size("freq")
    cycle_pos = lax.axis_index("freq")
    full_pairs = lax.all_gather(pair_matrix, "ga", axis=2, tiled=True)
    g_all = full_pairs.shape[2]
    omega_grid = make_grid(NW)
    sigma_part = jnp.zeros((n_dev, NW), jnp.float32)
    panel_rows = pair_matrix.reshape(n_dev * m_dev, g_panel)
    full_rows = full_pairs.reshape(n_dev * m_dev, g_all)
    energies = lookup(band_index, band_energy)
    nu_all = lax.all_gather(imag_freq, "freq", axis=0, tiled=True)
    weight_all = lax.all_gather(quad_weight, "freq", axis=0, tiled=True)
    w_slab = screened
    for turn_index in range(cycle_size):
        source = jnp.mod(cycle_pos - turn_index, cycle_size)
        nu_vals = lax.dynamic_slice_in_dim(nu_all, source * f_dev, f_dev)
        weight_vals = lax.dynamic_slice_in_dim(weight_all, source * f_dev, f_dev)
        for slot in range(f_dev):
            sigma_part = sigma_part + contribute(
                full_rows, panel_rows, w_slab[slot], nu_vals[slot], weight_vals[slot],
                energies, omega_grid, n_dev,
            )
        if turn_index + 1 < cycle_size:
            w_slab = from_behind(w_slab, "freq", 1)
    return lax.psum(sigma_part, ("freq", "ga"))


def choose(flag, yes, no):
    @pl.when(flag == 1)
    def _():
        yes.start()

    @pl.when(flag == 0)
    def _():
        no.start()


def start_slot(plan, slot, where_ref, refs, w_all, w_sems):
    at = 0
    for index, lead, begin, count in plan[slot]:
        if lead is None:
            src = refs[index].at[begin : begin + count, :]
        elif begin is None:
            src = refs[index].at[where_ref[5 + lead]]
        else:
            src = refs[index].at[where_ref[lead], pl.ds(pl.multiple_of(where_ref[begin], count // 2), count), :]
        pltpu.make_async_copy(src, w_all.at[slot, at : at + count, :], w_sems.at[slot]).start()
        at += count


def quadratic_kernel(plan, m_dev, tile, kind, where_ref, k_ref, own_ref, a_ref, b_ref, *rest):
    refs = rest[: len(rest) - 7]
    out_ref, left, right, w_all, k_all, sems, w_sems = rest[len(rest) - 7 :]
    n_slots, _, panel = w_all.shape
    end, low = where_ref[0], where_ref[1]
    if kind == "near":
        w_refs = refs
        here = left.at[:, pl.ds(pl.multiple_of((1 - low) * panel, panel), panel)]
        there = left.at[:, pl.ds(pl.multiple_of(low * panel, panel), panel)]
        fixed = [(own_ref, here), (own_ref, right)]
        either = [((a_ref, b_ref), there)]
    else:
        c_ref, w_refs = refs[0], refs[1:]
        fixed = [(a_ref, left.at[:, panel:])]
        either = [((b_ref, own_ref), left.at[:, :panel]), ((own_ref, c_ref), right)]
    start_slot(plan, 0, where_ref, w_refs, w_all, w_sems)
    waits = [pltpu.make_async_copy(src, dst, sems.at[n]) for n, (src, dst) in enumerate(fixed)]
    for c in waits:
        c.start()
    for n, ((yes, no), dst) in enumerate(either):
        sem = sems.at[len(fixed) + n]
        waits.append(pltpu.make_async_copy(yes, dst, sem))
        choose(end, waits[-1], pltpu.make_async_copy(no, dst, sem))
    waits.append(pltpu.make_async_copy(k_ref, k_all, sems.at[4]))
    waits[-1].start()
    for slot in range(1, n_slots):
        start_slot(plan, slot, where_ref, w_refs, w_all, w_sems)
    out_ref[...] = jnp.zeros_like(out_ref)
    for c in waits:
        c.wait()

    def one(slot, carry):
        pltpu.make_async_copy(w_all.at[slot], w_all.at[slot], w_sems.at[slot]).wait()
        for t in range(right.shape[0] // tile):
            at = slice(t * tile, (t + 1) * tile)
            y = jnp.dot(left[at], w_all[slot], preferred_element_type=jnp.float32)
            c = jnp.sum(y * right[at].astype(jnp.float32), axis=1, keepdims=True)
            for k in range(tile // m_dev):
                term = c[k * m_dev : (k + 1) * m_dev] * k_all[slot]
                out_ref[t * (tile // m_dev) + k] += jnp.sum(term.reshape(m_dev // 8, 8, NW), axis=0)
        return carry

    lax.fori_loop(0, n_slots, one, 0)


def turn_kernel(where_ref, far_ref, given_ref, out_ref):
    panel = far_ref.shape[0]

    @pl.when(where_ref[0] == 1)
    def _():
        out_ref[:panel] = far_ref[...]

    @pl.when(where_ref[0] == 0)
    def _():
        out_ref[:panel] = far_ref[...].T

    out_ref[panel:] = given_ref[...].T


def run_kernel(kind, plan, where, k_part, mats, arrays, m_dev):
    n_rows, panel = mats[0].shape
    n_slots, depth = k_part.shape[0], 2 * panel
    scratch = [
        pltpu.VMEM((n_rows, depth), jnp.bfloat16),
        pltpu.VMEM((n_rows, panel), jnp.bfloat16),
        pltpu.VMEM((n_slots, depth, panel), jnp.bfloat16),
        pltpu.VMEM(k_part.shape, jnp.float32),
        pltpu.SemaphoreType.DMA((5,)),
        pltpu.SemaphoreType.DMA((n_slots,)),
    ]
    flops = 2 * n_rows * depth * panel * n_slots
    return pl.pallas_call(
        functools.partial(quadratic_kernel, plan, m_dev, n_rows // 2, kind),
        out_shape=jax.ShapeDtypeStruct((n_rows // m_dev, 8, NW), jnp.float32),
        in_specs=[pl.BlockSpec(memory_space=pltpu.SMEM)]
        + [pl.BlockSpec(memory_space=pl.ANY)] * (1 + len(mats) + len(arrays)),
        out_specs=pl.BlockSpec(memory_space=pltpu.VMEM),
        scratch_shapes=scratch,
        cost_estimate=pl.CostEstimate(flops=flops, bytes_accessed=depth * panel, transcendentals=0),
        compiler_params=pltpu.CompilerParams(vmem_limit_bytes=48 * 2**20),
    )(where, k_part, *mats, *arrays)


def split3(x):
    hi = lax.reduce_precision(x, 8, 7)
    mid = lax.reduce_precision(x - hi, 8, 7)
    return jnp.stack([hi, mid, (x - hi) - mid])


def after(value, *others):
    return lax.optimization_barrier((value,) + others)[0]


def square_line(pair_matrix, screened, imag_freq, quad_weight, band_energy, band_index):
    n_dev, m_dev, panel = pair_matrix.shape
    ga = lax.axis_index("ga")
    core = lax.axis_index("band")
    rows = n_dev * m_dev
    own = pair_matrix.reshape(rows, panel)
    end = (ga == 0) | (ga == 3)
    low = ga < 2
    near_at = jnp.where(ga == 0, 0, jnp.where(ga == 3, 2, 1)) * panel
    far_at = (ga + 2) % 4 * panel
    give_at = jnp.where(ga % 2 == 0, 3, 0) * panel
    where = jnp.stack([end, low, near_at, core, 1 - core]).astype(jnp.int32)

    outer = [(0, 1), (1, 0), (2, 3), (3, 2)]
    inner = [(1, 2), (2, 1)]
    outward = [(1, 0), (2, 3)]

    def piece(start, count):
        return lax.dynamic_slice(screened, (core, start, 0), (1, count, panel))[0]

    def share(block):
        return flip(block, "band", 1)

    given = lax.ppermute(piece(give_at, panel), "ga", outer)
    node = split3(jnp.stack([imag_freq[core], quad_weight[core]])).reshape(1, 6)
    node = jnp.pad(node, ((0, 15), (0, panel - 6))).astype(jnp.bfloat16)
    near_w = jnp.concatenate([piece(near_at, 2 * panel), node])
    x1 = flip(near_w, "freq", 1)
    y1 = flip(near_w, "freq", 2)
    b_rows = lax.ppermute(own, "ga", inner)
    a_rows = lax.ppermute(after(own, given), "ga", outer)
    far_w = pl.pallas_call(
        turn_kernel,
        out_shape=jax.ShapeDtypeStruct((2 * panel, panel), jnp.bfloat16),
        in_specs=[pl.BlockSpec(memory_space=pltpu.SMEM)] + [pl.BlockSpec(memory_space=pltpu.VMEM)] * 2,
        out_specs=pl.BlockSpec(memory_space=pltpu.VMEM),
        cost_estimate=pl.CostEstimate(flops=0, bytes_accessed=4 * panel * panel, transcendentals=0),
    )(where, piece(far_at, panel), given)
    far_all = lax.all_gather(far_w, ("freq", "band"))
    d1a = flip(y1[:panel], "freq", 1)
    d1b = flip(x1[panel:], "freq", 2)
    x1_o, y1_o, d1a_o, d1b_o = share(x1), share(y1), share(d1a), share(d1b)
    c_rows = lax.ppermute(b_rows, "ga", outward)
    d_rows = lax.ppermute(a_rows, "ga", inner)

    energies = lookup(band_index, band_energy)
    offsets = make_grid(NW)[None, :] - energies[:, None]
    mine = jnp.stack([imag_freq, quad_weight], axis=1)
    mine = jnp.where(core == 0, mine, mine[::-1])

    def weigh(nodes):
        nu, weight = nodes[:, 0, None, None], nodes[:, 1, None, None]
        return (-weight / math.pi) * (offsets / (offsets * offsets + nu * nu))

    def carried(*places):
        terms = jnp.stack([w[row, :6] for w, row in places]).astype(jnp.float32).reshape(-1, 3, 2)
        return (terms[:, 0] + terms[:, 1]) + terms[:, 2]

    here = jnp.concatenate([mine, carried((x1, 2 * panel), (y1, 2 * panel))])
    there = carried((x1_o, 2 * panel), (y1_o, 2 * panel), (d1b, panel), (d1b_o, panel))
    k_here, k_there = weigh(here), weigh(there)
    k_all = jnp.concatenate([k_here, k_there])

    whole, one = 2 * panel, panel
    first = [[(0, 3 + s, 2, whole)] for s in range(2)] + [[(r, None, 0, whole)] for r in (1, 2)]
    second = [[(r, None, 0, whole)] for r in (0, 1)]
    second += [[(r, None, 0, one), (r + 1, None, 0, one)] for r in (2, 4)]
    panels = (own, a_rows, b_rows)
    near = run_kernel("near", first, where, k_here, panels, (screened, x1, y1), m_dev)
    near += run_kernel("near", second, where, k_there, panels, (x1_o, y1_o, d1a, d1b, d1a_o, d1b_o), m_dev)

    square = lax.axis_index("freq")
    order = ((0, core), (0, 1 - core), (1, core), (2, core), (1, 1 - core), (2, 1 - core), (3, core), (3, 1 - core))
    ranks = jnp.stack([(square ^ r) * 2 + c for r, c in order]).astype(jnp.int32)
    far = run_kernel(
        "far", [[(0, n, None, whole)] for n in range(8)], jnp.concatenate([where, ranks]), k_all,
        (own, a_rows, c_rows), (d_rows, far_all), m_dev,
    )
    sigma = jnp.sum(near + far, axis=1)
    for axis in ("freq", "ga"):
        t1, t2, t3 = (flip(sigma, axis, r) for r in (1, 2, 3))
        sigma = (sigma + t1) + (t2 + t3)
    return sigma


def on_device(pair_matrix, screened, *rest):
    sizes = tuple(lax.axis_size(a) for a in ("freq", "ga", "band"))
    fits = sizes == (4, 4, 2) and screened.shape[0] == 2 and pair_matrix.shape[0] % 8 == 0
    return (square_line if fits else general)(pair_matrix, screened, *rest)


def solution(mesh):
    placed = (P("band", "freq", "ga"), P("freq", None, "ga"), P("freq"), P("freq"), P(), P("freq"))
    return jax.shard_map(
        on_device, mesh=mesh, in_specs=placed, out_specs=P("band", None), check_vma=False
    )
```

time: 179 us -> 187 us (1.045)
  waiting for transfers between devices: 79.4 us -> 86.2 us
  starting transfers between devices: 25.7 us -> 27.9 us
    ppermute x6 -> x14, waiting for transfers between devices: 7.1 us -> 64.9 us  [flip(): lax.ppermute(block, axis, [(i, i ^ bits) for i in range(lax.axis_size(axi...]
    all_gather x1, waiting for transfers between devices: 31.3 us -> 0.01 us  [square_line(): far_all = lax.all_gather(far_w, ('freq', 'band'))]
    ppermute x5 -> x3, waiting for transfers between devices: 29 us -> 9.96 us  [the longest x1 9.95 us: square_line(): c_rows = lax.ppermute(b_rows, 'ga', outward)]
    ppermute x6 -> x14, starting transfers between devices: 11.7 us -> 16.5 us  [flip(): lax.ppermute(block, axis, [(i, i ^ bits) for i in range(lax.axis_size(axi...]
    ppermute x5 -> x3, starting transfers between devices: 9.14 us -> 6.58 us  [the longest x1 3.47 us: square_line(): a_rows = lax.ppermute(after(own, given), 'ga', outer)]
    pallas_call x3 -> x4, Pallas kernels: 41.7 us -> 43.5 us  [the longest x3 41.1 us: run_kernel(): pl.pallas_call(functools.partial(quadratic_kernel, plan, m_dev, n_rows //...]
    slice x2 -> x8, local copies, waits for them, and re-layouts: 3.99 us -> 3.82 us  [the longest x6 2.1 us: carried(): w[row, :6]]
  transfers between devices with their start and end apart: 15 -> 20, of which waited for: 8 -> 11; matrix products, arithmetic and copies ran while one was open for 4% -> 6% of each run, Pallas kernels for 17% -> 12%
where the time goes in v5:
time: 187 us
  waiting for transfers between devices  86.2 us (46%)
  Pallas kernels  43.5 us (23%)
  starting transfers between devices  27.9 us (15%)
  between operations  13.6 us (7%)
  local copies, waits for them, and re-layouts  11.9 us (6%)
  other arithmetic  3.94 us (2%)
    ppermute x14, waiting for transfers between devices, flip(): lax.ppermute(block, axis, [(i, i ^ bits) for i in range(lax.axis_size(axi...  64.9 us
    pallas_call x3, Pallas kernels, run_kernel(): pl.pallas_call(functools.partial(quadratic_kernel, plan, m_dev, n_rows //...  41.1 us
    ppermute x14, starting transfers between devices, flip(): lax.ppermute(block, axis, [(i, i ^ bits) for i in range(lax.axis_size(axi...  16.5 us
    ppermute x1, waiting for transfers between devices, square_line(): given = lax.ppermute(piece(give_at, panel), 'ga', outer)  11.3 us
    ppermute x1, waiting for transfers between devices, square_line(): c_rows = lax.ppermute(b_rows, 'ga', outward)  9.95 us
  transfers between devices with their start and end apart: 20, of which 11 were waited for; matrix products, arithmetic and copies ran while one was open for 6% of the time, Pallas kernels for 12%

profile of v5, /device:TPU:0, one launch (start us, length us, event | category | flops | bytes accessed | tf_op | source)
XLA Modules:
  0.0 187.1 jit_solution(908436164624213969)
XLA Ops:
  6.5 2.1 %dynamic-slice_bitcast_fusion.1 = (bf16[512,512]{1,0:T(8,128)(2,1)}, bf16[512,512]{1,0:T(8,128)(2,1)S(1)}) fusion(bf16[2,2048,512]{2,1,0:T(8,128)(2,1)} %rest_0_.1, s32[]{:T(128)S(6)} %select_n.54, s32[]{:T(128)S(6)} %select_n.61, s32[]{:T(128)S(6)} %select_n.59), kind=kLoop, calls=%fused_computation.7 | loop fusion | bytes 2097164 | tf_op jit(solution)/shard_map/squeeze | solution.py:207
  8.6 3.0 %collective-permute-start.2 = (bf16[512,512]{1,0:T(8,128)(2,1)S(1)}, bf16[512,512]{1,0:T(8,128)(2,1)S(1)}, u32[]{:S(2)}, u32[]{:S(2)}) collective-permute-start(bf16[512,512]{1,0:T(8,128)(2,1)S(1)} %get-tuple-element.10), channel_id=1, source_target_pairs={{0,2},{2,0},{4,6},{6,4},{1,3},{3,1},{5,7},{7,5},{8,10},{10,8},{12,... | collective-permute-start | bytes 1572872 | tf_op jit(solution)/shard_map/ppermute | solution.py:212
  11.6 0.6 stack.96.where_ref
  12.3 11.3 %collective-permute-done.2.given_ref = bf16[512,512]{1,0:T(8,128)(2,1)S(1)} collective-permute-done((bf16[512,512]{1,0:T(8,128)(2,1)S(1)}, bf16[512,512]{1,0:T(8,128)(2,1)S(1)}, u32[]{:S(2)}, u32[]{:S(2)}) %collective-permute-start.2) | collective-permute-done | bytes 524320 | tf_op jit(solution)/shard_map/ppermute | solution.py:212
  23.6 0.8 copy-done.3
  24.4 2.5 %shard_map.66 = bf16[1024,512]{1,0:T(8,128)(2,1)} custom-call(s32[5]{0:T(128)} %stack.96.where_ref, bf16[512,512]{1,0:T(8,128)(2,1)} %get-tuple-element.9.far_ref, bf16[512,512]{1,0:T(8,128)(2,1)} %copy-done.3), custom_call_target="tpu_custom_call" | custom-call | bytes 1048576 | tf_op jit(solution)/shard_map/pallas_call | solution.py:220
  26.8 0.0 all-gather.3.cloned.1.call-update
  26.9 0.7 dynamic_slice.16
  27.5 0.6 dynamic_slice.17
  28.1 1.3 reduce-precision_convert_fusion.1
  29.5 0.1 reshape.200
  29.5 1.3 dynamic-slice_bitcast_fusion
  30.8 0.0 copy-start.6
  30.9 0.0 copy-start.7
  30.9 1.1 fusion.1
  31.9 1.7 collective-permute-start
  33.6 1.8 collective-permute-start.4
  35.4 1.5 collective-permute-start.1
  36.9 3.5 %collective-permute-start.3 = (bf16[1536,512]{1,0:T(8,128)(2,1)}, bf16[1536,512]{1,0:T(8,128)(2,1)}, u32[]{:S(2)}, u32[]{:S(2)}) collective-permute-start(bf16[1536,512]{1,0:T(8,128)(2,1)} %bitcast.13.own_ref), channel_id=1, source_target_pairs={{0,2},{2,0},{4,6},{6,4},{1,3},{3,1},{5,7},{7,5},{8,10},{10,8},{12,... | collective-permute-start | bytes 4718600 | tf_op jit(solution)/shard_map/ppermute | solution.py:219
  40.4 0.1 rev.3
  40.5 27.6 %collective-permute-done.rest_1_ = bf16[1040,512]{1,0:T(8,128)(2,1)S(1)} collective-permute-done((bf16[1040,512]{1,0:T(8,128)(2,1)}, bf16[1040,512]{1,0:T(8,128)(2,1)S(1)}, u32[]{:S(2)}, u32[]{:S(2)}) %collective-permute-start) | collective-permute-done | bytes 1064992 | tf_op jit(solution)/shard_map/ppermute | solution.py:33
  68.1 6.0 %collective-permute-done.1.rest_2_ = bf16[1040,512]{1,0:T(8,128)(2,1)S(1)} collective-permute-done((bf16[1040,512]{1,0:T(8,128)(2,1)}, bf16[1040,512]{1,0:T(8,128)(2,1)S(1)}, u32[]{:S(2)}, u32[]{:S(2)}) %collective-permute-start.1) | collective-permute-done | bytes 1064992 | tf_op jit(solution)/shard_map/ppermute | solution.py:33
  74.1 0.2 select_reduce_fusion
  74.3 0.1 concatenate.41.where_ref
  74.4 0.9 slice.76
  75.3 2.4 %collective-permute-start.7 = (bf16[528,512]{1,0:T(8,128)(2,1)}, bf16[528,512]{1,0:T(8,128)(2,1)S(1)}, u32[]{:S(2)}, u32[]{:S(2)}) collective-permute-start(bf16[528,512]{1,0:T(8,128)(2,1)} %slice.76), channel_id=1, source_target_pairs={{0,16},{8,24},{16,0},{24,8},{1,17},{9,25},{17,1},{25,9},{2,18},{10... | collective-permute-start | bytes 1622024 | tf_op jit(solution)/shard_map/ppermute | solution.py:33
  77.6 0.1 broadcast_subtract_fusion
  77.7 0.8 slice.82
  78.6 0.1 stack.104
  78.7 0.1 stack.105
  78.8 23.6 %collective-permute-done.7.rest_3_ = bf16[528,512]{1,0:T(8,128)(2,1)S(1)} collective-permute-done((bf16[528,512]{1,0:T(8,128)(2,1)}, bf16[528,512]{1,0:T(8,128)(2,1)S(1)}, u32[]{:S(2)}, u32[]{:S(2)}) %collective-permute-start.7) | collective-permute-done | bytes 540704 | tf_op jit(solution)/shard_map/ppermute | solution.py:33
  102.5 0.1 copy.16
  102.6 0.1 pad_maximum_fusion.4
  102.7 0.1 stack.124
  102.7 0.7 collective-permute-done.9.rest_2_
  103.4 1.3 collective-permute-start.11
  104.7 0.1 collective-permute-start.10
  104.8 1.8 collective-permute-start.12
  106.6 0.6 slice_reduce_fusion.3
  107.3 0.1 stack.122
  107.4 0.7 slice_reduce_fusion.2
  108.1 0.1 stack.123
  108.2 0.7 slice_reduce_fusion
  108.9 0.1 stack.125
  109.0 0.1 maximum_convert_fusion
  109.1 0.3 divide_multiply_fusion.1
  109.4 0.1 pad_maximum_fusion.k_ref
  109.5 1.1 copy-done.1
  110.6 11.1 %shard_map.64 = f32[8,8,256]{2,1,0:T(8,128)S(1)} custom-call(s32[5]{0:T(128)S(1)} %copy-done.2, f32[4,192,256]{2,1,0:T(8,128)S(1)} %get-tuple-element.11.k_ref, bf16[1536,512]{1,0:T(8,128)(2,1)} %bitcast.13.own_ref, bf16[1536,512]{1,0:T(8,128)(2,1)} %collective-permute-done.3.a_ref, bf16[1536,512]{1,0:T(8,128)(2,1)} %collective-permute-done.4.b_ref, ...), custom_call_target="tpu_custom_call" | custom-call | flops 6442450944 | bytes 524288 | tf_op jit(solution)/shard_map/pallas_call | solution.py:167
  121.7 11.7 %shard_map.65 = f32[8,8,256]{2,1,0:T(8,128)S(1)} custom-call(s32[5]{0:T(128)S(1)} %copy-done.2, f32[4,192,256]{2,1,0:T(8,128)S(1)} %get-tuple-element.12.k_ref, bf16[1536,512]{1,0:T(8,128)(2,1)} %bitcast.13.own_ref, bf16[1536,512]{1,0:T(8,128)(2,1)} %collective-permute-done.3.a_ref, bf16[1536,512]{1,0:T(8,128)(2,1)} %collective-permute-done.4.b_ref, ...), custom_call_target="tpu_custom_call" | custom-call | flops 6442450944 | bytes 524288 | tf_op jit(solution)/shard_map/pallas_call | solution.py:167
  133.4 10.0 %collective-permute-done.11.b_ref = bf16[1536,512]{1,0:T(8,128)(2,1)} collective-permute-done((bf16[1536,512]{1,0:T(8,128)(2,1)}, bf16[1536,512]{1,0:T(8,128)(2,1)}, u32[]{:S(2)}, u32[]{:S(2)}) %collective-permute-start.11) | collective-permute-done | bytes 1572896 | tf_op jit(solution)/shard_map/ppermute | solution.py:231
  143.3 18.3 %shard_map.67 = f32[8,8,256]{2,1,0:T(8,128)S(1)} custom-call(s32[13]{0:T(128)S(1)} %concatenate.41.where_ref, f32[8,192,256]{2,1,0:T(8,128)S(1)} %pad_maximum_fusion.k_ref, bf16[1536,512]{1,0:T(8,128)(2,1)} %bitcast.13.own_ref, bf16[1536,512]{1,0:T(8,128)(2,1)} %collective-permute-done.3.a_ref, bf16[1536,512]{1,0:T(8,128)(2,1)} %collective-permute-done.11.b_ref, ...), custom_call_target="tpu_custom_call" | custom-call | flops 12884901888 | bytes 524288 | tf_op jit(solution)/shard_map/pallas_call | solution.py:167
  161.7 0.2 collective-permute-start.13
  161.9 1.9 %collective-permute-start.14 = (f32[8,256]{1,0:T(8,128)S(1)}, f32[8,256]{1,0:T(8,128)S(1)}, u32[]{:S(2)}, u32[]{:S(2)}) collective-permute-start(f32[8,256]{1,0:T(8,128)S(1)} %add_reduce_fusion), channel_id=1, source_target_pairs={{0,16},{8,24},{16,0},{24,8},{1,17},{9,25},{17,1},{25,9},{2,18},{10... | collective-permute-start | bytes 24584 | tf_op jit(solution)/shard_map/ppermute | solution.py:33
  163.8 1.4 collective-permute-start.15
  165.2 0.2 collective-permute-done.13
  165.4 0.2 collective-permute-done.14
  165.6 2.8 %collective-permute-done.15 = f32[8,256]{1,0:T(8,128)S(1)} collective-permute-done((f32[8,256]{1,0:T(8,128)S(1)}, f32[8,256]{1,0:T(8,128)S(1)}, u32[]{:S(2)}, u32[]{:S(2)}) %collective-permute-start.15) | collective-permute-done | bytes 8224 | tf_op jit(solution)/shard_map/ppermute | solution.py:33
  168.3 4.9 %collective-permute-start.16 = (f32[8,256]{1,0:T(8,128)S(1)}, f32[8,256]{1,0:T(8,128)S(1)}, u32[]{:S(2)}, u32[]{:S(2)}) collective-permute-start(f32[8,256]{1,0:T(8,128)S(1)} %add_add_fusion.1), channel_id=1, source_target_pairs={{0,2},{2,0},{4,6},{6,4},{1,3},{3,1},{5,7},{7,5},{8,10},{10,8},{12,... | collective-permute-start | bytes 24584 | tf_op jit(solution)/shard_map/ppermute | solution.py:33
  173.3 0.9 collective-permute-start.17
  174.2 1.5 collective-permute-start.18
  175.7 2.1 %collective-permute-done.17 = f32[8,256]{1,0:T(8,128)S(1)} collective-permute-done((f32[8,256]{1,0:T(8,128)S(1)}, f32[8,256]{1,0:T(8,128)S(1)}, u32[]{:S(2)}, u32[]{:S(2)}) %collective-permute-start.17) | collective-permute-done | bytes 8224 | tf_op jit(solution)/shard_map/ppermute | solution.py:33
  177.8 1.8 collective-permute-done.18
  179.6 0.6 add_add_fusion
  (39 shorter events, 0.2 us)
Async XLA Ops:
  6.5 136.8 %all-gather.3.cloned.1.call-start = ((), (), s32[]{:S(2)}) async-start(), calls=%async_computation | async-start | bytes 9437184 | tf_op jit(solution)/shard_map/all_gather | solution.py:227
  8.6 14.9 %collective-permute-start.2 = (bf16[512,512]{1,0:T(8,128)(2,1)S(1)}, bf16[512,512]{1,0:T(8,128)(2,1)S(1)}, u32[]{:S(2)}, u32[]{:S(2)}) collective-permute-start(bf16[512,512]{1,0:T(8,128)(2,1)S(1)} %get-tuple-element.10), channel_id=1, source_target_pairs={{0,2},{2,0},{4,6},{6,4},{1,3},{3,1},{5,7},{7,5},{8,10},{10,8},{12,... | collective-permute-start | bytes 1572872 | tf_op jit(solution)/shard_map/ppermute | solution.py:212
  23.6 0.8 copy-start.3
  24.4 2.5 %copy-start.5 = (f32[2]{0:T(128)S(1)}, f32[2]{0:T(128)}, u32[]{:S(2)}) copy-start(f32[2]{0:T(128)} %param.8) | copy-start | bytes 28
  24.4 3.2 %copy-start.4 = (f32[2]{0:T(128)S(1)}, f32[2]{0:T(128)}, u32[]{:S(2)}) copy-start(f32[2]{0:T(128)} %param.9) | copy-start | bytes 28
  30.8 43.2 %copy-start.6 = (f32[256]{0:T(256)S(1)}, f32[256]{0:T(256)}, u32[]{:S(2)}) copy-start(f32[256]{0:T(256)} %param.10) | copy-start | bytes 3076
  30.9 43.2 %copy-start.7 = (s32[192]{0:T(256)S(1)}, s32[192]{0:T(256)}, u32[]{:S(2)}) copy-start(s32[192]{0:T(256)} %param.11) | copy-start | bytes 2308
  31.9 36.1 %collective-permute-start = (bf16[1040,512]{1,0:T(8,128)(2,1)}, bf16[1040,512]{1,0:T(8,128)(2,1)S(1)}, u32[]{:S(2)}, u32[]{:S(2)}) collective-permute-start(bf16[1040,512]{1,0:T(8,128)(2,1)} %fusion.1), channel_id=1, source_target_pairs={{0,8},{8,0},{16,24},{24,16},{1,9},{9,1},{17,25},{25,17},{2,10},{10... | collective-permute-start | bytes 3194888 | tf_op jit(solution)/shard_map/ppermute | solution.py:33
  33.6 45.0 %collective-permute-start.4 = (bf16[1536,512]{1,0:T(8,128)(2,1)}, bf16[1536,512]{1,0:T(8,128)(2,1)}, u32[]{:S(2)}, u32[]{:S(2)}) collective-permute-start(bf16[1536,512]{1,0:T(8,128)(2,1)} %bitcast.13.own_ref), channel_id=1, source_target_pairs={{2,4},{4,2},{3,5},{5,3},{10,12},{12,10},{11,13},{13,11},{18,20},{2... | collective-permute-start | bytes 4718600 | tf_op jit(solution)/shard_map/ppermute | solution.py:218
  35.4 38.6 %collective-permute-start.1 = (bf16[1040,512]{1,0:T(8,128)(2,1)}, bf16[1040,512]{1,0:T(8,128)(2,1)S(1)}, u32[]{:S(2)}, u32[]{:S(2)}) collective-permute-start(bf16[1040,512]{1,0:T(8,128)(2,1)} %fusion.1), channel_id=1, source_target_pairs={{0,16},{8,24},{16,0},{24,8},{1,17},{9,25},{17,1},{25,9},{2,18},{10... | collective-permute-start | bytes 3194888 | tf_op jit(solution)/shard_map/ppermute | solution.py:33
  36.9 67.8 %collective-permute-start.3 = (bf16[1536,512]{1,0:T(8,128)(2,1)}, bf16[1536,512]{1,0:T(8,128)(2,1)}, u32[]{:S(2)}, u32[]{:S(2)}) collective-permute-start(bf16[1536,512]{1,0:T(8,128)(2,1)} %bitcast.13.own_ref), channel_id=1, source_target_pairs={{0,2},{2,0},{4,6},{6,4},{1,3},{3,1},{5,7},{7,5},{8,10},{10,8},{12,... | collective-permute-start | bytes 4718600 | tf_op jit(solution)/shard_map/ppermute | solution.py:219
  68.1 36.7 %collective-permute-start.5 = (bf16[1040,512]{1,0:T(8,128)(2,1)S(1)}, bf16[1040,512]{1,0:T(8,128)(2,1)}, u32[]{:S(2)}, u32[]{:S(2)}) collective-permute-start(bf16[1040,512]{1,0:T(8,128)(2,1)S(1)} %collective-permute-done.rest_1_), channel_id=1, source_target_pairs={{0,1},{1,0},{2,3},{3,2},{4,5},{5,4},{6,7},{7,6},{8,9},{9,8},{10,11... | collective-permute-start | bytes 3194888 | tf_op jit(solution)/shard_map/ppermute | solution.py:33
  74.1 35.3 %copy-start = (bf16[1040,512]{1,0:T(8,128)(2,1)}, bf16[1040,512]{1,0:T(8,128)(2,1)S(1)}, u32[]{:S(2)}) copy-start(bf16[1040,512]{1,0:T(8,128)(2,1)S(1)} %collective-permute-done.1.rest_2_) | copy-start | bytes 3194884
  74.1 33.3 %collective-permute-start.6 = (bf16[1040,512]{1,0:T(8,128)(2,1)S(1)}, bf16[1040,512]{1,0:T(8,128)(2,1)}, u32[]{:S(2)}, u32[]{:S(2)}) collective-permute-start(bf16[1040,512]{1,0:T(8,128)(2,1)S(1)} %collective-permute-done.1.rest_2_), channel_id=1, source_target_pairs={{0,1},{1,0},{2,3},{3,2},{4,5},{5,4},{6,7},{7,6},{8,9},{9,8},{10,11... | collective-permute-start | bytes 3194888 | tf_op jit(solution)/shard_map/ppermute | solution.py:33
  75.3 27.2 %collective-permute-start.7 = (bf16[528,512]{1,0:T(8,128)(2,1)}, bf16[528,512]{1,0:T(8,128)(2,1)S(1)}, u32[]{:S(2)}, u32[]{:S(2)}) collective-permute-start(bf16[528,512]{1,0:T(8,128)(2,1)} %slice.76), channel_id=1, source_target_pairs={{0,16},{8,24},{16,0},{24,8},{1,17},{9,25},{17,1},{25,9},{2,18},{10... | collective-permute-start | bytes 1622024 | tf_op jit(solution)/shard_map/ppermute | solution.py:33
  78.6 24.8 %collective-permute-start.9 = (bf16[512,512]{1,0:T(8,128)(2,1)}, bf16[512,512]{1,0:T(8,128)(2,1)}, u32[]{:S(2)}, u32[]{:S(2)}) collective-permute-start(bf16[512,512]{1,0:T(8,128)(2,1)} %slice.82), channel_id=1, source_target_pairs={{0,8},{8,0},{16,24},{24,16},{1,9},{9,1},{17,25},{25,17},{2,10},{10... | collective-permute-start | bytes 1572872 | tf_op jit(solution)/shard_map/ppermute | solution.py:33
  102.4 5.7 %collective-permute-start.8 = (bf16[528,512]{1,0:T(8,128)(2,1)S(1)}, bf16[528,512]{1,0:T(8,128)(2,1)}, u32[]{:S(2)}, u32[]{:S(2)}) collective-permute-start(bf16[528,512]{1,0:T(8,128)(2,1)S(1)} %collective-permute-done.7.rest_3_), channel_id=1, source_target_pairs={{0,1},{1,0},{2,3},{3,2},{4,5},{5,4},{6,7},{7,6},{8,9},{9,8},{10,11... | collective-permute-start | bytes 1622024 | tf_op jit(solution)/shard_map/ppermute | solution.py:33
  103.4 39.9 %collective-permute-start.11 = (bf16[1536,512]{1,0:T(8,128)(2,1)}, bf16[1536,512]{1,0:T(8,128)(2,1)}, u32[]{:S(2)}, u32[]{:S(2)}) collective-permute-start(bf16[1536,512]{1,0:T(8,128)(2,1)} %collective-permute-done.4.b_ref), channel_id=1, source_target_pairs={{2,0},{4,6},{3,1},{5,7},{10,8},{12,14},{11,9},{13,15},{18,16},{20,... | collective-permute-start | bytes 4718600 | tf_op jit(solution)/shard_map/ppermute | solution.py:231
  104.7 17.0 %collective-permute-start.10 = (bf16[512,512]{1,0:T(8,128)(2,1)}, bf16[512,512]{1,0:T(8,128)(2,1)}, u32[]{:S(2)}, u32[]{:S(2)}) collective-permute-start(bf16[512,512]{1,0:T(8,128)(2,1)} %collective-permute-done.9.rest_2_), channel_id=1, source_target_pairs={{0,1},{1,0},{2,3},{3,2},{4,5},{5,4},{6,7},{7,6},{8,9},{9,8},{10,11... | collective-permute-start | bytes 1572872 | tf_op jit(solution)/shard_map/ppermute | solution.py:33
  104.8 38.5 %collective-permute-start.12 = (bf16[1536,512]{1,0:T(8,128)(2,1)}, bf16[1536,512]{1,0:T(8,128)(2,1)}, u32[]{:S(2)}, u32[]{:S(2)}) collective-permute-start(bf16[1536,512]{1,0:T(8,128)(2,1)} %collective-permute-done.3.a_ref), channel_id=1, source_target_pairs={{2,4},{4,2},{3,5},{5,3},{10,12},{12,10},{11,13},{13,11},{18,20},{2... | collective-permute-start | bytes 4718600 | tf_op jit(solution)/shard_map/ppermute | solution.py:232
  109.4 1.2 copy-start.1
  109.4 1.2 copy-start.2
  161.7 3.7 %collective-permute-start.13 = (f32[8,256]{1,0:T(8,128)S(1)}, f32[8,256]{1,0:T(8,128)S(1)}, u32[]{:S(2)}, u32[]{:S(2)}) collective-permute-start(f32[8,256]{1,0:T(8,128)S(1)} %add_reduce_fusion), channel_id=1, source_target_pairs={{0,8},{8,0},{16,24},{24,16},{1,9},{9,1},{17,25},{25,17},{2,10},{10... | collective-permute-start | bytes 24584 | tf_op jit(solution)/shard_map/ppermute | solution.py:33
  161.9 3.7 %collective-permute-start.14 = (f32[8,256]{1,0:T(8,128)S(1)}, f32[8,256]{1,0:T(8,128)S(1)}, u32[]{:S(2)}, u32[]{:S(2)}) collective-permute-start(f32[8,256]{1,0:T(8,128)S(1)} %add_reduce_fusion), channel_id=1, source_target_pairs={{0,16},{8,24},{16,0},{24,8},{1,17},{9,25},{17,1},{25,9},{2,18},{10... | collective-permute-start | bytes 24584 | tf_op jit(solution)/shard_map/ppermute | solution.py:33
  163.8 4.5 %collective-permute-start.15 = (f32[8,256]{1,0:T(8,128)S(1)}, f32[8,256]{1,0:T(8,128)S(1)}, u32[]{:S(2)}, u32[]{:S(2)}) collective-permute-start(f32[8,256]{1,0:T(8,128)S(1)} %add_reduce_fusion), channel_id=1, source_target_pairs={{0,24},{8,16},{16,8},{24,0},{1,25},{9,17},{17,9},{25,1},{2,26},{10... | collective-permute-start | bytes 24584 | tf_op jit(solution)/shard_map/ppermute | solution.py:33
  168.3 7.3 %collective-permute-start.16 = (f32[8,256]{1,0:T(8,128)S(1)}, f32[8,256]{1,0:T(8,128)S(1)}, u32[]{:S(2)}, u32[]{:S(2)}) collective-permute-start(f32[8,256]{1,0:T(8,128)S(1)} %add_add_fusion.1), channel_id=1, source_target_pairs={{0,2},{2,0},{4,6},{6,4},{1,3},{3,1},{5,7},{7,5},{8,10},{10,8},{12,... | collective-permute-start | bytes 24584 | tf_op jit(solution)/shard_map/ppermute | solution.py:33
  173.3 4.5 %collective-permute-start.17 = (f32[8,256]{1,0:T(8,128)S(1)}, f32[8,256]{1,0:T(8,128)S(1)}, u32[]{:S(2)}, u32[]{:S(2)}) collective-permute-start(f32[8,256]{1,0:T(8,128)S(1)} %add_add_fusion.1), channel_id=1, source_target_pairs={{0,4},{2,6},{4,0},{6,2},{1,5},{3,7},{5,1},{7,3},{8,12},{10,14},{12... | collective-permute-start | bytes 24584 | tf_op jit(solution)/shard_map/ppermute | solution.py:33
  174.2 5.4 %collective-permute-start.18 = (f32[8,256]{1,0:T(8,128)S(1)}, f32[8,256]{1,0:T(8,128)S(1)}, u32[]{:S(2)}, u32[]{:S(2)}) collective-permute-start(f32[8,256]{1,0:T(8,128)S(1)} %add_add_fusion.1), channel_id=1, source_target_pairs={{0,6},{2,4},{4,2},{6,0},{1,7},{3,5},{5,3},{7,1},{8,14},{10,12},{12... | collective-permute-start | bytes 24584 | tf_op jit(solution)/shard_map/ppermute | solution.py:33
Sparse Core Ops, SparseCore 0:
  27.0 80.3 all-gather.2

commit v6 on v5

--- a/solution.py
+++ b/solution.py
@@ -83,21 +83,22 @@
 def start_slot(plan, slot, where_ref, refs, w_all, w_sems):
     at = 0
     for index, lead, begin, count in plan[slot]:
-        if lead is None:
-            src = refs[index].at[begin : begin + count, :]
-        elif begin is None:
-            src = refs[index].at[where_ref[5 + lead]]
-        else:
-            src = refs[index].at[where_ref[lead], pl.ds(pl.multiple_of(where_ref[begin], count // 2), count), :]
+        src = refs[index]
+        if lead is not None:
+            src = src.at[where_ref[lead[1]] if isinstance(lead, tuple) else lead]
+        if isinstance(begin, tuple):
+            begin = pl.multiple_of(where_ref[begin[1]], count // 2)
+        src = src.at[pl.ds(begin, count), :]
         pltpu.make_async_copy(src, w_all.at[slot, at : at + count, :], w_sems.at[slot]).start()
         at += count
 
 
-def quadratic_kernel(plan, m_dev, tile, kind, where_ref, k_ref, own_ref, a_ref, b_ref, *rest):
+def quadratic_kernel(plan, m_dev, begin, tile, kind, where_ref, k_ref, own_ref, a_ref, b_ref, *rest):
     refs = rest[: len(rest) - 7]
     out_ref, left, right, w_all, k_all, sems, w_sems = rest[len(rest) - 7 :]
     n_slots, _, panel = w_all.shape
     end, low = where_ref[0], where_ref[1]
+    own_ref, a_ref = (r.at[begin : begin + right.shape[0], :] for r in (own_ref, a_ref))
     if kind == "near":
         w_refs = refs
         here = left.at[:, pl.ds(pl.multiple_of((1 - low) * panel, panel), panel)]
@@ -105,9 +106,9 @@
         fixed = [(own_ref, here), (own_ref, right)]
         either = [((a_ref, b_ref), there)]
     else:
-        c_ref, w_refs = refs[0], refs[1:]
+        c_ref, d_ref, w_refs = refs[0], refs[1], refs[2:]
         fixed = [(a_ref, left.at[:, panel:])]
-        either = [((b_ref, own_ref), left.at[:, :panel]), ((own_ref, c_ref), right)]
+        either = [((c_ref, own_ref), left.at[:, :panel]), ((own_ref, d_ref), right)]
     start_slot(plan, 0, where_ref, w_refs, w_all, w_sems)
     waits = [pltpu.make_async_copy(src, dst, sems.at[n]) for n, (src, dst) in enumerate(fixed)]
     for c in waits:
@@ -116,7 +117,7 @@
         sem = sems.at[len(fixed) + n]
         waits.append(pltpu.make_async_copy(yes, dst, sem))
         choose(end, waits[-1], pltpu.make_async_copy(no, dst, sem))
-    waits.append(pltpu.make_async_copy(k_ref, k_all, sems.at[4]))
+    waits.append(pltpu.make_async_copy(k_ref, k_all, sems.at[5]))
     waits[-1].start()
     for slot in range(1, n_slots):
         start_slot(plan, slot, where_ref, w_refs, w_all, w_sems)
@@ -138,21 +139,24 @@
     lax.fori_loop(0, n_slots, one, 0)
 
 
-def turn_kernel(where_ref, far_ref, given_ref, out_ref):
-    panel = far_ref.shape[0]
-
-    @pl.when(where_ref[0] == 1)
-    def _():
-        out_ref[:panel] = far_ref[...]
-
-    @pl.when(where_ref[0] == 0)
-    def _():
-        out_ref[:panel] = far_ref[...].T
-
-    out_ref[panel:] = given_ref[...].T
-
-
-def run_kernel(kind, plan, where, k_part, mats, arrays, m_dev):
+def turn_kernel(where_ref, blocks_ref, out_ref):
+    for n in range(2):
+        slot = where_ref[3 + n]
+
+        @pl.when(where_ref[0] == 1)
+        def _():
+            out_ref[n] = blocks_ref[slot]
+
+        @pl.when(where_ref[0] == 0)
+        def _():
+            out_ref[n] = blocks_ref[slot].T
+
+
+def transpose_kernel(block_ref, out_ref):
+    out_ref[...] = block_ref[...].T
+
+
+def run_kernel(kind, plan, where, k_part, mats, arrays, m_dev, begin=0):
     n_rows, panel = mats[0].shape
     n_slots, depth = k_part.shape[0], 2 * panel
     scratch = [
@@ -160,12 +164,12 @@
         pltpu.VMEM((n_rows, panel), jnp.bfloat16),
         pltpu.VMEM((n_slots, depth, panel), jnp.bfloat16),
         pltpu.VMEM(k_part.shape, jnp.float32),
-        pltpu.SemaphoreType.DMA((5,)),
+        pltpu.SemaphoreType.DMA((6,)),
         pltpu.SemaphoreType.DMA((n_slots,)),
     ]
-    flops = 2 * n_rows * depth * panel * n_slots
+    flops = 2 * n_rows * depth * panel * n_slots // (16 if kind == "near" else 1)
     return pl.pallas_call(
-        functools.partial(quadratic_kernel, plan, m_dev, n_rows // 2, kind),
+        functools.partial(quadratic_kernel, plan, m_dev, begin, min(n_rows, 4 * m_dev), kind),
         out_shape=jax.ShapeDtypeStruct((n_rows // m_dev, 8, NW), jnp.float32),
         in_specs=[pl.BlockSpec(memory_space=pltpu.SMEM)]
         + [pl.BlockSpec(memory_space=pl.ANY)] * (1 + len(mats) + len(arrays)),
@@ -210,27 +214,30 @@
         return flip(block, "band", 1)
 
     given = lax.ppermute(piece(give_at, panel), "ga", outer)
+    def local(body, shape, *inputs):
+        specs = [pl.BlockSpec(memory_space=pltpu.SMEM if x.dtype == jnp.int32 else pltpu.VMEM) for x in inputs]
+        return pl.pallas_call(
+            body,
+            out_shape=jax.ShapeDtypeStruct(shape, jnp.bfloat16),
+            in_specs=specs,
+            out_specs=pl.BlockSpec(memory_space=pltpu.VMEM),
+            cost_estimate=pl.CostEstimate(flops=0, bytes_accessed=4 * panel * panel, transcendentals=0),
+        )(*inputs)
+
     node = split3(jnp.stack([imag_freq[core], quad_weight[core]])).reshape(1, 6)
     node = jnp.pad(node, ((0, 15), (0, panel - 6))).astype(jnp.bfloat16)
-    near_w = jnp.concatenate([piece(near_at, 2 * panel), node])
-    x1 = flip(near_w, "freq", 1)
-    y1 = flip(near_w, "freq", 2)
+    far_blocks = lax.dynamic_slice(screened, (0, far_at, 0), (2, panel, panel))
+    far_self = local(turn_kernel, (2, panel, panel), where, far_blocks)
+    sent = jnp.concatenate([piece(near_at, 2 * panel), far_self[0], node])
+    cut = 3 * panel // 2
+    x1 = flip(sent, "freq", 1)
+    y1 = flip(sent, "freq", 2)
     b_rows = lax.ppermute(own, "ga", inner)
     a_rows = lax.ppermute(after(own, given), "ga", outer)
-    far_w = pl.pallas_call(
-        turn_kernel,
-        out_shape=jax.ShapeDtypeStruct((2 * panel, panel), jnp.bfloat16),
-        in_specs=[pl.BlockSpec(memory_space=pltpu.SMEM)] + [pl.BlockSpec(memory_space=pltpu.VMEM)] * 2,
-        out_specs=pl.BlockSpec(memory_space=pltpu.VMEM),
-        cost_estimate=pl.CostEstimate(flops=0, bytes_accessed=4 * panel * panel, transcendentals=0),
-    )(where, piece(far_at, panel), given)
-    far_all = lax.all_gather(far_w, ("freq", "band"))
-    d1a = flip(y1[:panel], "freq", 1)
-    d1b = flip(x1[panel:], "freq", 2)
-    x1_o, y1_o, d1a_o, d1b_o = share(x1), share(y1), share(d1a), share(d1b)
-    c_rows = lax.ppermute(b_rows, "ga", outward)
-    d_rows = lax.ppermute(a_rows, "ga", inner)
-
+    turned = local(transpose_kernel, (panel, panel), given)
+    given_all = lax.all_gather(after(turned, x1, y1, b_rows), ("freq", "band"))
+    d1a = flip(y1[:cut], "freq", 1)
+    d1b = flip(x1[cut:], "freq", 2)
     energies = lookup(band_index, band_energy)
     offsets = make_grid(NW)[None, :] - energies[:, None]
     mine = jnp.stack([imag_freq, quad_weight], axis=1)
@@ -244,25 +251,29 @@
         terms = jnp.stack([w[row, :6] for w, row in places]).astype(jnp.float32).reshape(-1, 3, 2)
         return (terms[:, 0] + terms[:, 1]) + terms[:, 2]
 
-    here = jnp.concatenate([mine, carried((x1, 2 * panel), (y1, 2 * panel))])
-    there = carried((x1_o, 2 * panel), (y1_o, 2 * panel), (d1b, panel), (d1b_o, panel))
-    k_here, k_there = weigh(here), weigh(there)
-    k_all = jnp.concatenate([k_here, k_there])
-
-    whole, one = 2 * panel, panel
-    first = [[(0, 3 + s, 2, whole)] for s in range(2)] + [[(r, None, 0, whole)] for r in (1, 2)]
-    second = [[(r, None, 0, whole)] for r in (0, 1)]
-    second += [[(r, None, 0, one), (r + 1, None, 0, one)] for r in (2, 4)]
-    panels = (own, a_rows, b_rows)
-    near = run_kernel("near", first, where, k_here, panels, (screened, x1, y1), m_dev)
-    near += run_kernel("near", second, where, k_there, panels, (x1_o, y1_o, d1a, d1b, d1a_o, d1b_o), m_dev)
+    x1_o, y1_o = share(after(x1, a_rows, b_rows)), share(after(y1, a_rows, b_rows, d1a))
+    d1a_o, d1b_o = share(d1a), share(d1b)
+    c_rows = lax.ppermute(b_rows, "ga", outward)
+    d_rows = lax.ppermute(a_rows, "ga", inner)
+    ends = ((x1, 3 * panel), (y1, 3 * panel), (x1_o, 3 * panel), (y1_o, 3 * panel), (d1b, cut), (d1b_o, cut))
+    k_all = weigh(jnp.concatenate([mine, carried(*ends)]))
+
+    whole = 2 * panel
+    slots = [[(0, ("at", 3 + s), ("at", 2), whole)] for s in range(2)]
+    slots += [[(r, None, 0, whole)] for r in (1, 2, 3, 4)]
+    slots += [[(r, None, 0, cut), (r + 1, None, 0, whole - cut)] for r in (5, 7)]
+    arrays = (screened, x1, y1, x1_o, y1_o, d1a, d1b, d1a_o, d1b_o)
+    near = run_kernel("near", slots, where, k_all, (own, a_rows, b_rows), arrays, m_dev)
 
     square = lax.axis_index("freq")
     order = ((0, core), (0, 1 - core), (1, core), (2, core), (1, 1 - core), (2, 1 - core), (3, core), (3, 1 - core))
     ranks = jnp.stack([(square ^ r) * 2 + c for r, c in order]).astype(jnp.int32)
+    sources = [(1, 0, 0), (1, 1, 0)] + [(r, None, whole) for r in (2, 3, 4, 5)] + [(r, None, whole - cut) for r in (6, 7)]
+    slots = [[(*src, panel), (0, ("at", 5 + n), 0, panel)] for n, src in enumerate(sources)]
+    arrays = (given_all, far_self, x1, y1, x1_o, y1_o, d1b, d1b_o)
     far = run_kernel(
-        "far", [[(0, n, None, whole)] for n in range(8)], jnp.concatenate([where, ranks]), k_all,
-        (own, a_rows, c_rows), (d_rows, far_all), m_dev,
+        "far", slots, jnp.concatenate([where, ranks]), k_all,
+        (own, a_rows, b_rows), (c_rows, d_rows, *arrays), m_dev,
     )
     sigma = jnp.sum(near + far, axis=1)
     for axis in ("freq", "ga"):

time: 187 us -> 183 us (0.979)
  waiting for transfers between devices: 86.2 us -> 75 us
  local copies, waits for them, and re-layouts: 11.9 us -> 16.7 us
  Pallas kernels: 43.5 us -> 40.7 us
  starting transfers between devices: 27.9 us -> 30.4 us
    ppermute x14, waiting for transfers between devices: 64.9 us -> 22.5 us  [flip(): lax.ppermute(block, axis, [(i, i ^ bits) for i in range(lax.axis_size(axi...]
    ppermute x1, waiting for transfers between devices: 0.01 us -> 30.4 us  [square_line(): a_rows = lax.ppermute(after(own, given), 'ga', outer)]
    pallas_call x4, Pallas kernels: 43.5 us -> 40.7 us  [the longest x2 36.4 us: run_kernel(): pl.pallas_call(functools.partial(quadratic_kernel, plan, m_dev, begin, mi...]
    dynamic_slice x0 -> x1, local copies, waits for them, and re-layouts: none -> 2.27 us  [square_line(): far_blocks = lax.dynamic_slice(screened, (0, far_at, 0), (2, panel, panel))]
  transfers between devices with their start and end apart: 20 -> 20, of which waited for: 11 -> 11; matrix products, arithmetic and copies ran while one was open for 6% -> 4% of each run, Pallas kernels for 12% -> 11%
where the time goes in v6:
time: 183 us; the launch traced here: 182 us
  waiting for transfers between devices  75 us (41%)
  Pallas kernels  40.7 us (22%)
  starting transfers between devices  30.4 us (17%)
  local copies, waits for them, and re-layouts  16.7 us (9%)
  between operations  13.7 us (7%)
  other arithmetic  5.6 us (3%)
    pallas_call x2, Pallas kernels, run_kernel(): pl.pallas_call(functools.partial(quadratic_kernel, plan, m_dev, begin, mi...  36.4 us
    ppermute x1, waiting for transfers between devices, square_line(): a_rows = lax.ppermute(after(own, given), 'ga', outer)  30.4 us
    ppermute x14, waiting for transfers between devices, flip(): lax.ppermute(block, axis, [(i, i ^ bits) for i in range(lax.axis_size(axi...  22.5 us
    ppermute x14, starting transfers between devices, flip(): lax.ppermute(block, axis, [(i, i ^ bits) for i in range(lax.axis_size(axi...  17.3 us
    ppermute x1, waiting for transfers between devices, square_line(): given = lax.ppermute(piece(give_at, panel), 'ga', outer)  11.2 us
    ppermute x1, waiting for transfers between devices, square_line(): c_rows = lax.ppermute(b_rows, 'ga', outward)  10.9 us
    ppermute x1, starting transfers between devices, square_line(): a_rows = lax.ppermute(after(own, given), 'ga', outer)  4.52 us
    pallas_call x2, Pallas kernels, local(): pl.pallas_call(body, out_shape=jax.ShapeDtypeStruct(shape, jnp.bfloat16),...  4.33 us
  transfers between devices with their start and end apart: 20, of which 11 were waited for; matrix products, arithmetic and copies ran while one was open for 4% of the time, Pallas kernels for 11%

profile of v6, /device:TPU:0, one launch (start us, length us, event | category | flops | bytes accessed | tf_op | source)
XLA Modules:
  0.0 182.1 jit_solution(9650170204238357619)
XLA Ops:
  6.5 1.3 dynamic_slice.18
  7.8 1.3 dynamic_slice.17
  9.1 1.3 reduce-precision_convert_fusion.1
  10.4 0.1 reshape.177
  10.5 2.3 %constant_dynamic-slice_fusion.blocks_ref = bf16[2,512,512]{2,1,0:T(8,128)(2,1)} fusion(bf16[2,2048,512]{2,1,0:T(8,128)(2,1)} %rest_0_.1, s32[]{:T(128)S(6)} %select_n.56), kind=kLoop, calls=%fused_computation.22 | loop fusion | bytes 2097156 | tf_op jit(solution)/shard_map/dynamic_slice | solution.py:229
  12.8 0.6 stack.93.where_ref
  13.4 2.3 %shard_map.64.rest_3_ = bf16[2,512,512]{2,1,0:T(8,128)(2,1)} custom-call(s32[5]{0:T(128)} %stack.93.where_ref, bf16[2,512,512]{2,1,0:T(8,128)(2,1)} %constant_dynamic-slice_fusion.blocks_ref), custom_call_target="tpu_custom_call" | custom-call | bytes 1048576 | tf_op jit(solution)/shard_map/pallas_call | solution.py:219
  15.7 1.1 slice_bitcast_fusion
  16.8 1.3 dynamic-slice_bitcast_fusion
  18.1 1.3 fusion.1
  19.4 2.9 %collective-permute-start = (bf16[1552,512]{1,0:T(8,128)(2,1)}, bf16[1552,512]{1,0:T(8,128)(2,1)S(1)}, u32[]{:S(2)}, u32[]{:S(2)}) collective-permute-start(bf16[1552,512]{1,0:T(8,128)(2,1)} %fusion.1), channel_id=1, source_target_pairs={{0,8},{8,0},{16,24},{24,16},{1,9},{9,1},{17,25},{25,17},{2,10},{10... | collective-permute-start | bytes 4767752 | tf_op jit(solution)/shard_map/ppermute | solution.py:33
  22.3 1.5 collective-permute-start.1
  23.9 1.8 collective-permute-start.4
  25.7 1.1 dynamic-slice_bitcast_fusion.1
  26.7 3.7 %collective-permute-start.2 = (bf16[512,512]{1,0:T(8,128)(2,1)S(1)}, bf16[512,512]{1,0:T(8,128)(2,1)}, u32[]{:S(2)}, u32[]{:S(2)}) collective-permute-start(bf16[512,512]{1,0:T(8,128)(2,1)S(1)} %dynamic-slice_bitcast_fusion.1), channel_id=1, source_target_pairs={{0,2},{2,0},{4,6},{6,4},{1,3},{3,1},{5,7},{7,5},{8,10},{10,8},{12,... | collective-permute-start | bytes 1572872 | tf_op jit(solution)/shard_map/ppermute | solution.py:216
  30.4 11.2 %collective-permute-done.2.block_ref = bf16[512,512]{1,0:T(8,128)(2,1)} collective-permute-done((bf16[512,512]{1,0:T(8,128)(2,1)S(1)}, bf16[512,512]{1,0:T(8,128)(2,1)}, u32[]{:S(2)}, u32[]{:S(2)}) %collective-permute-start.2) | collective-permute-done | bytes 524320 | tf_op jit(solution)/shard_map/ppermute | solution.py:216
  41.6 2.0 %shard_map.66 = bf16[512,512]{1,0:T(8,128)(2,1)} custom-call(bf16[512,512]{1,0:T(8,128)(2,1)} %collective-permute-done.2.block_ref), custom_call_target="tpu_custom_call" | custom-call | bytes 1048576 | tf_op jit(solution)/shard_map/pallas_call | solution.py:219
  43.6 13.7 %collective-permute-done.rest_1_.rest_4_ = bf16[1552,512]{1,0:T(8,128)(2,1)S(1)} collective-permute-done((bf16[1552,512]{1,0:T(8,128)(2,1)}, bf16[1552,512]{1,0:T(8,128)(2,1)S(1)}, u32[]{:S(2)}, u32[]{:S(2)}) %collective-permute-start) | collective-permute-done | bytes 1589280 | tf_op jit(solution)/shard_map/ppermute | solution.py:33
  57.3 1.6 collective-permute-done.1.rest_2_.rest_5_
  58.9 4.5 %collective-permute-start.3 = (bf16[1536,512]{1,0:T(8,128)(2,1)S(1)}, bf16[1536,512]{1,0:T(8,128)(2,1)}, u32[]{:S(2)}, u32[]{:S(2)}) collective-permute-start(bf16[1536,512]{1,0:T(8,128)(2,1)S(1)} %bitcast.33), channel_id=1, source_target_pairs={{0,2},{2,0},{4,6},{6,4},{1,3},{3,1},{5,7},{7,5},{8,10},{10,8},{12,... | collective-permute-start | bytes 4718600 | tf_op jit(solution)/shard_map/ppermute | solution.py:236
  63.5 1.2 slice.60
  64.6 0.6 collective-permute-start.6
  65.2 0.1 slice.62
  65.3 0.8 collective-permute-start.8
  66.1 30.4 %collective-permute-done.3.a_ref = bf16[1536,512]{1,0:T(8,128)(2,1)} collective-permute-done((bf16[1536,512]{1,0:T(8,128)(2,1)S(1)}, bf16[1536,512]{1,0:T(8,128)(2,1)}, u32[]{:S(2)}, u32[]{:S(2)}) %collective-permute-start.3) | collective-permute-done | bytes 1572896 | tf_op jit(solution)/shard_map/ppermute | solution.py:236
  96.5 0.5 collective-permute-start.7
  97.0 0.2 select_reduce_fusion
  97.2 0.1 collective-permute-start.9
  97.3 0.1 rev.3
  97.4 0.1 concatenate.37.where_ref
  97.5 0.8 broadcast_subtract_fusion
  98.3 1.3 collective-permute-start.11
  99.6 1.8 collective-permute-start.12
  101.4 0.7 slice_reduce_fusion.5
  102.1 0.1 stack.118
  102.2 0.7 slice_reduce_fusion.4
  102.9 0.1 stack.119
  103.0 0.1 stack.122
  103.1 1.0 collective-permute-done.9.rest_8_.rest_9_
  104.1 0.1 collective-permute-start.10
  104.2 0.9 copy-done.3
  105.1 0.1 stack.123
  105.3 0.1 stack.120
  105.4 0.7 slice_reduce_fusion.2
  106.1 0.1 stack.121
  106.2 0.1 stack.107
  106.3 0.1 pad_maximum_fusion.2
  106.4 1.3 divide_multiply_fusion.k_ref
  107.7 18.7 %shard_map.65 = f32[8,8,256]{2,1,0:T(8,128)S(1)} custom-call(s32[5]{0:T(128)S(1)} %copy-done.6, f32[8,192,256]{2,1,0:T(8,128)S(1)} %divide_multiply_fusion.k_ref, bf16[1536,512]{1,0:T(8,128)(2,1)} %bitcast.31, bf16[1536,512]{1,0:T(8,128)(2,1)} %collective-permute-done.3.a_ref, bf16[1536,512]{1,0:T(8,128)(2,1)} %collective-permute-done.4.b_ref, ...), custom_call_target="tpu_custom_call" | custom-call | flops 805306368 | bytes 524288 | tf_op jit(solution)/shard_map/pallas_call | solution.py:171
  126.4 10.9 %collective-permute-done.11.rest_0_ = bf16[1536,512]{1,0:T(8,128)(2,1)} collective-permute-done((bf16[1536,512]{1,0:T(8,128)(2,1)}, bf16[1536,512]{1,0:T(8,128)(2,1)}, u32[]{:S(2)}, u32[]{:S(2)}) %collective-permute-start.11) | collective-permute-done | bytes 1572896 | tf_op jit(solution)/shard_map/ppermute | solution.py:256
  137.3 1.4 copy-done.2
  138.7 1.1 copy-done.5
  139.8 17.7 %shard_map.67 = f32[8,8,256]{2,1,0:T(8,128)S(1)} custom-call(s32[13]{0:T(128)S(1)} %concatenate.37.where_ref, f32[8,192,256]{2,1,0:T(8,128)S(1)} %divide_multiply_fusion.k_ref, bf16[1536,512]{1,0:T(8,128)(2,1)S(1)} %bitcast.34, bf16[1536,512]{1,0:T(8,128)(2,1)} %collective-permute-done.3.a_ref, bf16[1536,512]{1,0:T(8,128)(2,1)} %collective-permute-done.4.b_ref, ...), custom_call_target="tpu_custom_call" | custom-call | flops 12884901888 | bytes 524288 | tf_op jit(solution)/shard_map/pallas_call | solution.py:171
  157.6 0.6 collective-permute-start.14
  158.2 1.5 collective-permute-start.15
  159.7 1.5 collective-permute-start.13
  161.2 0.2 collective-permute-done.14
  161.3 1.4 collective-permute-done.15
  162.7 0.6 collective-permute-done.13
  163.3 5.9 %collective-permute-start.17 = (f32[8,256]{1,0:T(8,128)S(1)}, f32[8,256]{1,0:T(8,128)S(1)}, u32[]{:S(2)}, u32[]{:S(2)}) collective-permute-start(f32[8,256]{1,0:T(8,128)S(1)} %add_add_fusion.1), channel_id=1, source_target_pairs={{0,4},{2,6},{4,0},{6,2},{1,5},{3,7},{5,1},{7,3},{8,12},{10,14},{12... | collective-permute-start | bytes 24584 | tf_op jit(solution)/shard_map/ppermute | solution.py:33
  169.2 1.3 collective-permute-start.18
  170.5 0.3 collective-permute-done.17
  170.8 3.8 %collective-permute-done.18 = f32[8,256]{1,0:T(8,128)S(1)} collective-permute-done((f32[8,256]{1,0:T(8,128)S(1)}, f32[8,256]{1,0:T(8,128)S(1)}, u32[]{:S(2)}, u32[]{:S(2)}) %collective-permute-start.18) | collective-permute-done | bytes 8224 | tf_op jit(solution)/shard_map/ppermute | solution.py:33
  174.6 0.6 add_add_fusion
  (49 shorter events, 0.3 us)
Async XLA Ops:
  6.5 130.7 %all-gather.3.cloned.1.call-start = ((), (), s32[]{:S(2)}) async-start(), calls=%async_computation | async-start | bytes 4718592 | tf_op jit(solution)/shard_map/all_gather | solution.py:238
  18.1 5.8 %copy-start.1 = (bf16[8,192,512]{2,1,0:T(8,128)(2,1)S(1)}, bf16[8,192,512]{2,1,0:T(8,128)(2,1)}, u32[]{:S(2)}) copy-start(bf16[8,192,512]{2,1,0:T(8,128)(2,1)} %param.6) | copy-start | bytes 4718596
  19.4 37.9 %collective-permute-start = (bf16[1552,512]{1,0:T(8,128)(2,1)}, bf16[1552,512]{1,0:T(8,128)(2,1)S(1)}, u32[]{:S(2)}, u32[]{:S(2)}) collective-permute-start(bf16[1552,512]{1,0:T(8,128)(2,1)} %fusion.1), channel_id=1, source_target_pairs={{0,8},{8,0},{16,24},{24,16},{1,9},{9,1},{17,25},{25,17},{2,10},{10... | collective-permute-start | bytes 4767752 | tf_op jit(solution)/shard_map/ppermute | solution.py:33
  22.3 36.5 %collective-permute-start.1 = (bf16[1552,512]{1,0:T(8,128)(2,1)}, bf16[1552,512]{1,0:T(8,128)(2,1)}, u32[]{:S(2)}, u32[]{:S(2)}) collective-permute-start(bf16[1552,512]{1,0:T(8,128)(2,1)} %fusion.1), channel_id=1, source_target_pairs={{0,16},{8,24},{16,0},{24,8},{1,17},{9,25},{17,1},{25,9},{2,18},{10... | collective-permute-start | bytes 4767752 | tf_op jit(solution)/shard_map/ppermute | solution.py:33
  23.9 19.7 %collective-permute-start.4 = (bf16[1536,512]{1,0:T(8,128)(2,1)S(1)}, bf16[1536,512]{1,0:T(8,128)(2,1)}, u32[]{:S(2)}, u32[]{:S(2)}) collective-permute-start(bf16[1536,512]{1,0:T(8,128)(2,1)S(1)} %bitcast.32), channel_id=1, source_target_pairs={{2,4},{4,2},{3,5},{5,3},{10,12},{12,10},{11,13},{13,11},{18,20},{2... | collective-permute-start | bytes 4718600 | tf_op jit(solution)/shard_map/ppermute | solution.py:235
  26.7 14.9 %collective-permute-start.2 = (bf16[512,512]{1,0:T(8,128)(2,1)S(1)}, bf16[512,512]{1,0:T(8,128)(2,1)}, u32[]{:S(2)}, u32[]{:S(2)}) collective-permute-start(bf16[512,512]{1,0:T(8,128)(2,1)S(1)} %dynamic-slice_bitcast_fusion.1), channel_id=1, source_target_pairs={{0,2},{2,0},{4,6},{6,4},{1,3},{3,1},{5,7},{7,5},{8,10},{10,8},{12,... | collective-permute-start | bytes 1572872 | tf_op jit(solution)/shard_map/ppermute | solution.py:216
  57.3 8.0 %copy-start.7 = (bf16[1552,512]{1,0:T(8,128)(2,1)}, bf16[1552,512]{1,0:T(8,128)(2,1)S(1)}, u32[]{:S(2)}) copy-start(bf16[1552,512]{1,0:T(8,128)(2,1)S(1)} %collective-permute-done.rest_1_.rest_4_) | copy-start | bytes 4767748
  58.9 38.1 %copy-start.11 = (f32[256]{0:T(256)S(1)}, f32[256]{0:T(256)}, u32[]{:S(2)}) copy-start(f32[256]{0:T(256)} %param.10) | copy-start | bytes 3076
  58.9 38.1 %copy-start.12 = (s32[192]{0:T(256)S(1)}, s32[192]{0:T(256)}, u32[]{:S(2)}) copy-start(s32[192]{0:T(256)} %param.11) | copy-start | bytes 2308
  58.9 38.4 %copy-start.9 = (f32[2]{0:T(128)S(1)}, f32[2]{0:T(128)}, u32[]{:S(2)}) copy-start(f32[2]{0:T(128)} %param.9) | copy-start | bytes 28
  58.9 38.4 %copy-start.10 = (f32[2]{0:T(128)S(1)}, f32[2]{0:T(128)}, u32[]{:S(2)}) copy-start(f32[2]{0:T(128)} %param.8) | copy-start | bytes 28
  58.9 37.5 %collective-permute-start.3 = (bf16[1536,512]{1,0:T(8,128)(2,1)S(1)}, bf16[1536,512]{1,0:T(8,128)(2,1)}, u32[]{:S(2)}, u32[]{:S(2)}) collective-permute-start(bf16[1536,512]{1,0:T(8,128)(2,1)S(1)} %bitcast.33), channel_id=1, source_target_pairs={{0,2},{2,0},{4,6},{6,4},{1,3},{3,1},{5,7},{7,5},{8,10},{10,8},{12,... | collective-permute-start | bytes 4718600 | tf_op jit(solution)/shard_map/ppermute | solution.py:236
  64.6 31.8 %collective-permute-start.6 = (bf16[768,512]{1,0:T(8,128)(2,1)S(1)}, bf16[768,512]{1,0:T(8,128)(2,1)}, u32[]{:S(2)}, u32[]{:S(2)}) collective-permute-start(bf16[768,512]{1,0:T(8,128)(2,1)S(1)} %slice.60), channel_id=1, source_target_pairs={{0,8},{8,0},{16,24},{24,16},{1,9},{9,1},{17,25},{25,17},{2,10},{10... | collective-permute-start | bytes 2359304 | tf_op jit(solution)/shard_map/ppermute | solution.py:33
  65.3 42.4 %copy-start.6 = (s32[5]{0:T(128)S(1)}, s32[5]{0:T(128)}, u32[]{:S(2)}) copy-start(s32[5]{0:T(128)} %stack.93.where_ref) | copy-start | bytes 64
  65.3 31.9 %collective-permute-start.8 = (bf16[784,512]{1,0:T(8,128)(2,1)S(1)}, bf16[784,512]{1,0:T(8,128)(2,1)S(1)}, u32[]{:S(2)}, u32[]{:S(2)}) collective-permute-start(bf16[784,512]{1,0:T(8,128)(2,1)S(1)} %slice.62), channel_id=1, source_target_pairs={{0,16},{8,24},{16,0},{24,8},{1,17},{9,25},{17,1},{25,9},{2,18},{10... | collective-permute-start | bytes 2408456 | tf_op jit(solution)/shard_map/ppermute | solution.py:33
  96.5 8.8 %collective-permute-start.5 = (bf16[1552,512]{1,0:T(8,128)(2,1)}, bf16[1552,512]{1,0:T(8,128)(2,1)S(1)}, u32[]{:S(2)}, u32[]{:S(2)}) collective-permute-start(bf16[1552,512]{1,0:T(8,128)(2,1)} %copy-done.7), channel_id=1, source_target_pairs={{0,1},{1,0},{2,3},{3,2},{4,5},{5,4},{6,7},{7,6},{8,9},{9,8},{10,11... | collective-permute-start | bytes 4767752 | tf_op jit(solution)/shard_map/ppermute | solution.py:33
  96.5 8.9 %collective-permute-start.7 = (bf16[1552,512]{1,0:T(8,128)(2,1)}, bf16[1552,512]{1,0:T(8,128)(2,1)}, u32[]{:S(2)}, u32[]{:S(2)}) collective-permute-start(bf16[1552,512]{1,0:T(8,128)(2,1)} %collective-permute-done.1.rest_2_.rest_5_), channel_id=1, source_target_pairs={{0,1},{1,0},{2,3},{3,2},{4,5},{5,4},{6,7},{7,6},{8,9},{9,8},{10,11... | collective-permute-start | bytes 4767752 | tf_op jit(solution)/shard_map/ppermute | solution.py:33
  97.2 6.9 %collective-permute-start.9 = (bf16[784,512]{1,0:T(8,128)(2,1)S(1)}, bf16[784,512]{1,0:T(8,128)(2,1)S(1)}, u32[]{:S(2)}, u32[]{:S(2)}) collective-permute-start(bf16[784,512]{1,0:T(8,128)(2,1)S(1)} %collective-permute-done.8.rest_6_.rest_8_), channel_id=1, source_target_pairs={{0,1},{1,0},{2,3},{3,2},{4,5},{5,4},{6,7},{7,6},{8,9},{9,8},{10,11... | collective-permute-start | bytes 2408456 | tf_op jit(solution)/shard_map/ppermute | solution.py:33
  98.3 39.0 %collective-permute-start.11 = (bf16[1536,512]{1,0:T(8,128)(2,1)}, bf16[1536,512]{1,0:T(8,128)(2,1)}, u32[]{:S(2)}, u32[]{:S(2)}) collective-permute-start(bf16[1536,512]{1,0:T(8,128)(2,1)} %collective-permute-done.4.b_ref), channel_id=1, source_target_pairs={{2,0},{4,6},{3,1},{5,7},{10,8},{12,14},{11,9},{13,15},{18,16},{20,... | collective-permute-start | bytes 4718600 | tf_op jit(solution)/shard_map/ppermute | solution.py:256
  99.6 37.7 %collective-permute-start.12 = (bf16[1536,512]{1,0:T(8,128)(2,1)}, bf16[1536,512]{1,0:T(8,128)(2,1)}, u32[]{:S(2)}, u32[]{:S(2)}) collective-permute-start(bf16[1536,512]{1,0:T(8,128)(2,1)} %collective-permute-done.3.a_ref), channel_id=1, source_target_pairs={{2,4},{4,2},{3,5},{5,3},{10,12},{12,10},{11,13},{13,11},{18,20},{2... | collective-permute-start | bytes 4718600 | tf_op jit(solution)/shard_map/ppermute | solution.py:257
  104.1 3.6 %collective-permute-start.10 = (bf16[768,512]{1,0:T(8,128)(2,1)}, bf16[768,512]{1,0:T(8,128)(2,1)}, u32[]{:S(2)}, u32[]{:S(2)}) collective-permute-start(bf16[768,512]{1,0:T(8,128)(2,1)} %collective-permute-done.6.rest_5_), channel_id=1, source_target_pairs={{0,1},{1,0},{2,3},{3,2},{4,5},{5,4},{6,7},{7,6},{8,9},{9,8},{10,11... | collective-permute-start | bytes 2359304 | tf_op jit(solution)/shard_map/ppermute | solution.py:33
  104.2 0.9 copy-start.3
  105.2 1.1 copy-start.8
  106.3 1.4 copy-start.4
  107.6 29.6 %copy-start = (bf16[2,512,512]{2,1,0:T(8,128)(2,1)S(1)}, bf16[2,512,512]{2,1,0:T(8,128)(2,1)}, u32[]{:S(2)}) copy-start(bf16[2,512,512]{2,1,0:T(8,128)(2,1)} %shard_map.64.rest_3_) | copy-start | bytes 3145732
  137.3 1.4 copy-start.2
  138.7 1.1 copy-start.5
  157.6 3.7 %collective-permute-start.14 = (f32[8,256]{1,0:T(8,128)S(1)}, f32[8,256]{1,0:T(8,128)S(1)}, u32[]{:S(2)}, u32[]{:S(2)}) collective-permute-start(f32[8,256]{1,0:T(8,128)S(1)} %add_reduce_fusion), channel_id=1, source_target_pairs={{0,16},{8,24},{16,0},{24,8},{1,17},{9,25},{17,1},{25,9},{2,18},{10... | collective-permute-start | bytes 24584 | tf_op jit(solution)/shard_map/ppermute | solution.py:33
  158.2 4.5 %collective-permute-start.15 = (f32[8,256]{1,0:T(8,128)S(1)}, f32[8,256]{1,0:T(8,128)S(1)}, u32[]{:S(2)}, u32[]{:S(2)}) collective-permute-start(f32[8,256]{1,0:T(8,128)S(1)} %add_reduce_fusion), channel_id=1, source_target_pairs={{0,24},{8,16},{16,8},{24,0},{1,25},{9,17},{17,9},{25,1},{2,26},{10... | collective-permute-start | bytes 24584 | tf_op jit(solution)/shard_map/ppermute | solution.py:33
  159.7 3.7 %collective-permute-start.13 = (f32[8,256]{1,0:T(8,128)S(1)}, f32[8,256]{1,0:T(8,128)S(1)}, u32[]{:S(2)}, u32[]{:S(2)}) collective-permute-start(f32[8,256]{1,0:T(8,128)S(1)} %add_reduce_fusion), channel_id=1, source_target_pairs={{0,8},{8,0},{16,24},{24,16},{1,9},{9,1},{17,25},{25,17},{2,10},{10... | collective-permute-start | bytes 24584 | tf_op jit(solution)/shard_map/ppermute | solution.py:33
  163.3 7.5 %collective-permute-start.17 = (f32[8,256]{1,0:T(8,128)S(1)}, f32[8,256]{1,0:T(8,128)S(1)}, u32[]{:S(2)}, u32[]{:S(2)}) collective-permute-start(f32[8,256]{1,0:T(8,128)S(1)} %add_add_fusion.1), channel_id=1, source_target_pairs={{0,4},{2,6},{4,0},{6,2},{1,5},{3,7},{5,1},{7,3},{8,12},{10,14},{12... | collective-permute-start | bytes 24584 | tf_op jit(solution)/shard_map/ppermute | solution.py:33
  169.2 5.4 %collective-permute-start.18 = (f32[8,256]{1,0:T(8,128)S(1)}, f32[8,256]{1,0:T(8,128)S(1)}, u32[]{:S(2)}, u32[]{:S(2)}) collective-permute-start(f32[8,256]{1,0:T(8,128)S(1)} %add_add_fusion.1), channel_id=1, source_target_pairs={{0,6},{2,4},{4,2},{6,0},{1,7},{3,5},{5,3},{7,1},{8,14},{10,12},{12... | collective-permute-start | bytes 24584 | tf_op jit(solution)/shard_map/ppermute | solution.py:33
  170.5 4.1 %collective-permute-start.16 = (f32[8,256]{1,0:T(8,128)S(1)}, f32[8,256]{1,0:T(8,128)S(1)}, u32[]{:S(2)}, u32[]{:S(2)}) collective-permute-start(f32[8,256]{1,0:T(8,128)S(1)} %add_add_fusion.1), channel_id=1, source_target_pairs={{0,2},{2,0},{4,6},{6,4},{1,3},{3,1},{5,7},{7,5},{8,10},{10,8},{12,... | collective-permute-start | bytes 24584 | tf_op jit(solution)/shard_map/ppermute | solution.py:33
Sparse Core Ops, SparseCore 0:
  59.0 44.7 all-gather.2

commit v7 on v6

--- a/solution.py
+++ b/solution.py
@@ -139,17 +139,51 @@
     lax.fori_loop(0, n_slots, one, 0)
 
 
-def turn_kernel(where_ref, blocks_ref, out_ref):
+def pack_kernel(where_ref, nu_ref, weight_ref, screened_ref, sent_ref, far_ref, blocks, nodes, sems):
+    panel = blocks.shape[1]
+    core = where_ref[3]
+    near_at = pl.multiple_of(where_ref[2], panel)
+    far_at = pl.multiple_of(where_ref[5], panel)
+    loads = [
+        pltpu.make_async_copy(screened_ref.at[where_ref[3 + n], pl.ds(far_at, panel), :], blocks.at[n], sems.at[n])
+        for n in range(2)
+    ]
+    near = pltpu.make_async_copy(
+        screened_ref.at[core, pl.ds(near_at, 2 * panel), :], sent_ref.at[: 2 * panel, :], sems.at[2]
+    )
+    for c in loads:
+        c.start()
+    near.start()
+    lane = lax.broadcasted_iota(jnp.int32, nodes.shape, 1)
+    nu = jnp.full(nodes.shape, nu_ref[core], jnp.float32)
+    weight = jnp.full(nodes.shape, weight_ref[core], jnp.float32)
+    rest = jnp.where(lane % 2 == 0, nu, weight)
+    packed = jnp.zeros(nodes.shape, jnp.float32)
+    for n in range(3):
+        term = rest.astype(jnp.bfloat16).astype(jnp.float32)
+        packed = jnp.where(lane // 2 == n, term, packed)
+        rest = rest - term
+    nodes[...] = packed.astype(jnp.bfloat16)
+    stores = [
+        pltpu.make_async_copy(far_ref.at[0], sent_ref.at[2 * panel : 3 * panel, :], sems.at[3]),
+        pltpu.make_async_copy(nodes, sent_ref.at[3 * panel :, :], sems.at[4]),
+    ]
+    stores[1].start()
     for n in range(2):
-        slot = where_ref[3 + n]
+        loads[n].wait()
 
         @pl.when(where_ref[0] == 1)
         def _():
-            out_ref[n] = blocks_ref[slot]
+            far_ref[n] = blocks[n]
 
         @pl.when(where_ref[0] == 0)
         def _():
-            out_ref[n] = blocks_ref[slot].T
+            far_ref[n] = blocks[n].T
+
+        if n == 0:
+            stores[0].start()
+    for c in stores + [near]:
+        c.wait()
 
 
 def transpose_kernel(block_ref, out_ref):
@@ -180,12 +214,6 @@
     )(where, k_part, *mats, *arrays)
 
 
-def split3(x):
-    hi = lax.reduce_precision(x, 8, 7)
-    mid = lax.reduce_precision(x - hi, 8, 7)
-    return jnp.stack([hi, mid, (x - hi) - mid])
-
-
 def after(value, *others):
     return lax.optimization_barrier((value,) + others)[0]
 
@@ -201,7 +229,7 @@
     near_at = jnp.where(ga == 0, 0, jnp.where(ga == 3, 2, 1)) * panel
     far_at = (ga + 2) % 4 * panel
     give_at = jnp.where(ga % 2 == 0, 3, 0) * panel
-    where = jnp.stack([end, low, near_at, core, 1 - core]).astype(jnp.int32)
+    where = jnp.stack([end, low, near_at, core, 1 - core, far_at]).astype(jnp.int32)
 
     outer = [(0, 1), (1, 0), (2, 3), (3, 2)]
     inner = [(1, 2), (2, 1)]
@@ -224,18 +252,29 @@
             cost_estimate=pl.CostEstimate(flops=0, bytes_accessed=4 * panel * panel, transcendentals=0),
         )(*inputs)
 
-    node = split3(jnp.stack([imag_freq[core], quad_weight[core]])).reshape(1, 6)
-    node = jnp.pad(node, ((0, 15), (0, panel - 6))).astype(jnp.bfloat16)
-    far_blocks = lax.dynamic_slice(screened, (0, far_at, 0), (2, panel, panel))
-    far_self = local(turn_kernel, (2, panel, panel), where, far_blocks)
-    sent = jnp.concatenate([piece(near_at, 2 * panel), far_self[0], node])
+    sent, far_self = pl.pallas_call(
+        pack_kernel,
+        out_shape=(
+            jax.ShapeDtypeStruct((3 * panel + 16, panel), jnp.bfloat16),
+            jax.ShapeDtypeStruct((2, panel, panel), jnp.bfloat16),
+        ),
+        in_specs=[pl.BlockSpec(memory_space=pltpu.SMEM)] * 3 + [pl.BlockSpec(memory_space=pl.ANY)],
+        out_specs=(pl.BlockSpec(memory_space=pl.ANY), pl.BlockSpec(memory_space=pltpu.VMEM)),
+        scratch_shapes=[
+            pltpu.VMEM((2, panel, panel), jnp.bfloat16),
+            pltpu.VMEM((16, panel), jnp.bfloat16),
+            pltpu.SemaphoreType.DMA((5,)),
+        ],
+        cost_estimate=pl.CostEstimate(flops=0, bytes_accessed=8 * panel * panel, transcendentals=0),
+        compiler_params=pltpu.CompilerParams(vmem_limit_bytes=32 * 2**20),
+    )(where, imag_freq, quad_weight, screened)
     cut = 3 * panel // 2
     x1 = flip(sent, "freq", 1)
     y1 = flip(sent, "freq", 2)
     b_rows = lax.ppermute(own, "ga", inner)
     a_rows = lax.ppermute(after(own, given), "ga", outer)
     turned = local(transpose_kernel, (panel, panel), given)
-    given_all = lax.all_gather(after(turned, x1, y1, b_rows), ("freq", "band"))
+    given_all = lax.all_gather(after(turned, x1, y1, a_rows, b_rows), ("freq", "band"))
     d1a = flip(y1[:cut], "freq", 1)
     d1b = flip(x1[cut:], "freq", 2)
     energies = lookup(band_index, band_energy)
@@ -269,7 +308,7 @@
     order = ((0, core), (0, 1 - core), (1, core), (2, core), (1, 1 - core), (2, 1 - core), (3, core), (3, 1 - core))
     ranks = jnp.stack([(square ^ r) * 2 + c for r, c in order]).astype(jnp.int32)
     sources = [(1, 0, 0), (1, 1, 0)] + [(r, None, whole) for r in (2, 3, 4, 5)] + [(r, None, whole - cut) for r in (6, 7)]
-    slots = [[(*src, panel), (0, ("at", 5 + n), 0, panel)] for n, src in enumerate(sources)]
+    slots = [[(*src, panel), (0, ("at", 6 + n), 0, panel)] for n, src in enumerate(sources)]
     arrays = (given_all, far_self, x1, y1, x1_o, y1_o, d1b, d1b_o)
     far = run_kernel(
         "far", slots, jnp.concatenate([where, ranks]), k_all,

time: 183 us -> 173 us (0.945)
  waiting for transfers between devices: 75 us -> 70 us
  other arithmetic: 5.6 us -> 1.32 us
    ppermute x14, waiting for transfers between devices: 22.5 us -> 55.9 us  [flip(): lax.ppermute(block, axis, [(i, i ^ bits) for i in range(lax.axis_size(axi...]
    ppermute x1, waiting for transfers between devices: 30.4 us -> 3.81 us  [square_line(): a_rows = lax.ppermute(after(own, given), 'ga', outer)]
    ppermute x1, waiting for transfers between devices: 11.2 us -> 0.66 us  [square_line(): given = lax.ppermute(piece(give_at, panel), 'ga', outer)]
    unnamed x26 -> x34, local copies, waits for them, and re-layouts: 3.5 us -> 10.8 us
    dynamic_slice x3 -> x0, local copies, waits for them, and re-layouts: 4.83 us -> none  [the longest x2 2.56 us: square_line(): node = split3(jnp.stack([imag_freq[core], quad_weight[core]])).reshape(1, 6)]
    pallas_call x2 -> x1, Pallas kernels: 4.33 us -> 2.03 us  [local(): pl.pallas_call(body, out_shape=jax.ShapeDtypeStruct(shape, jnp.bfloat16),...]
    pallas_call x0 -> x1, Pallas kernels: none -> 1.86 us  [square_line(): pl.pallas_call(pack_kernel, out_shape=(jax.ShapeDtypeStruct((3 * panel +...]
  transfers between devices with their start and end apart: 20 -> 20, of which waited for: 11 -> 11; matrix products, arithmetic and copies ran while one was open for 4% -> 4% of each run, Pallas kernels for 11% -> 13%
where the time goes in v7:
time: 173 us
  waiting for transfers between devices  70 us (40%)
  Pallas kernels  40.9 us (24%)
  starting transfers between devices  28.8 us (17%)
  local copies, waits for them, and re-layouts  18 us (10%)
  between operations  13.6 us (8%)
    ppermute x14, waiting for transfers between devices, flip(): lax.ppermute(block, axis, [(i, i ^ bits) for i in range(lax.axis_size(axi...  55.9 us
    pallas_call x2, Pallas kernels, run_kernel(): pl.pallas_call(functools.partial(quadratic_kernel, plan, m_dev, begin, mi...  37 us
    ppermute x14, starting transfers between devices, flip(): lax.ppermute(block, axis, [(i, i ^ bits) for i in range(lax.axis_size(axi...  18.1 us
    unnamed x34, local copies, waits for them, and re-layouts  10.8 us
    ppermute x1, waiting for transfers between devices, square_line(): c_rows = lax.ppermute(b_rows, 'ga', outward)  9.64 us
    ppermute x1, waiting for transfers between devices, square_line(): a_rows = lax.ppermute(after(own, given), 'ga', outer)  3.81 us
  transfers between devices with their start and end apart: 20, of which 11 were waited for; matrix products, arithmetic and copies ran while one was open for 4% of the time, Pallas kernels for 13%

profile of v7, /device:TPU:0, one launch (start us, length us, event | category | flops | bytes accessed | tf_op | source)
XLA Modules:
  0.0 172.7 jit_solution(13033353970573367445)
XLA Ops:
  6.5 1.1 dynamic-slice_bitcast_fusion
  7.6 3.1 %collective-permute-start.2 = (bf16[512,512]{1,0:T(8,128)(2,1)S(1)}, bf16[512,512]{1,0:T(8,128)(2,1)S(1)}, u32[]{:S(2)}, u32[]{:S(2)}) collective-permute-start(bf16[512,512]{1,0:T(8,128)(2,1)S(1)} %dynamic-slice_bitcast_fusion), channel_id=1, source_target_pairs={{0,2},{2,0},{4,6},{6,4},{1,3},{3,1},{5,7},{7,5},{8,10},{10,8},{12,... | collective-permute-start | bytes 1572872 | tf_op jit(solution)/shard_map/ppermute | solution.py:244
  10.7 0.1 stack.83.where_ref
  10.8 2.2 %copy-done = bf16[2,2048,512]{2,1,0:T(8,128)(2,1)S(1)} copy-done((bf16[2,2048,512]{2,1,0:T(8,128)(2,1)S(1)}, bf16[2,2048,512]{2,1,0:T(8,128)(2,1)}, u32[]{:S(2)}) %copy-start) | copy-done | bytes 4194328
  13.0 0.7 copy-done.9
  13.6 0.7 copy-done.11
  14.3 1.9 %shard_map.64 = (bf16[1552,512]{1,0:T(8,128)(2,1)}, bf16[2,512,512]{2,1,0:T(8,128)(2,1)S(1)}) custom-call(s32[6]{0:T(128)S(1)} %stack.83.where_ref, f32[2]{0:T(128)S(1)} %copy-done.9, f32[2]{0:T(128)S(1)} %copy-done.11, bf16[2,2048,512]{2,1,0:T(8,128)(2,1)S(1)} %copy-done), custom_call_target="tpu_custom_call" | custom-call | bytes 2097152 | tf_op jit(solution)/shard_map/pallas_call | solution.py:255
  16.2 1.0 copy-done.12
  17.2 1.5 collective-permute-start
  18.7 1.5 collective-permute-start.1
  20.2 1.8 %collective-permute-start.4 = (bf16[1536,512]{1,0:T(8,128)(2,1)S(1)}, bf16[1536,512]{1,0:T(8,128)(2,1)}, u32[]{:S(2)}, u32[]{:S(2)}) collective-permute-start(bf16[1536,512]{1,0:T(8,128)(2,1)S(1)} %bitcast.27), channel_id=1, source_target_pairs={{2,4},{4,2},{3,5},{5,3},{10,12},{12,10},{11,13},{13,11},{18,20},{2... | collective-permute-start | bytes 4718600 | tf_op jit(solution)/shard_map/ppermute | solution.py:274
  22.0 0.7 collective-permute-done.2.block_ref
  22.6 2.7 %collective-permute-start.3 = (bf16[1536,512]{1,0:T(8,128)(2,1)S(1)}, bf16[1536,512]{1,0:T(8,128)(2,1)}, u32[]{:S(2)}, u32[]{:S(2)}) collective-permute-start(bf16[1536,512]{1,0:T(8,128)(2,1)S(1)} %bitcast.28), channel_id=1, source_target_pairs={{0,2},{2,0},{4,6},{6,4},{1,3},{3,1},{5,7},{7,5},{8,10},{10,8},{12,... | collective-permute-start | bytes 4718600 | tf_op jit(solution)/shard_map/ppermute | solution.py:275
  25.3 2.0 %shard_map.66 = bf16[512,512]{1,0:T(8,128)(2,1)} custom-call(bf16[512,512]{1,0:T(8,128)(2,1)} %copy-done.14), custom_call_target="tpu_custom_call" | custom-call | bytes 1048576 | tf_op jit(solution)/shard_map/pallas_call | solution.py:247
  27.4 26.3 %collective-permute-done.rest_1_.rest_4_ = bf16[1552,512]{1,0:T(8,128)(2,1)} collective-permute-done((bf16[1552,512]{1,0:T(8,128)(2,1)}, bf16[1552,512]{1,0:T(8,128)(2,1)}, u32[]{:S(2)}, u32[]{:S(2)}) %collective-permute-start) | collective-permute-done | bytes 1589280 | tf_op jit(solution)/shard_map/ppermute | solution.py:33
  53.7 1.2 collective-permute-done.1.rest_2_.rest_5_
  54.9 3.8 %collective-permute-done.3.a_ref = bf16[1536,512]{1,0:T(8,128)(2,1)} collective-permute-done((bf16[1536,512]{1,0:T(8,128)(2,1)S(1)}, bf16[1536,512]{1,0:T(8,128)(2,1)}, u32[]{:S(2)}, u32[]{:S(2)}) %collective-permute-start.3) | collective-permute-done | bytes 1572896 | tf_op jit(solution)/shard_map/ppermute | solution.py:275
  58.7 0.0 all-gather.3.cloned.1.call-update
  58.8 1.2 slice.55
  60.0 1.1 collective-permute-start.6
  61.1 1.2 slice.57
  62.3 1.6 collective-permute-start.8
  63.9 19.4 %collective-permute-done.6.rest_5_ = bf16[768,512]{1,0:T(8,128)(2,1)} collective-permute-done((bf16[768,512]{1,0:T(8,128)(2,1)S(1)}, bf16[768,512]{1,0:T(8,128)(2,1)}, u32[]{:S(2)}, u32[]{:S(2)}) %collective-permute-start.6) | collective-permute-done | bytes 786464 | tf_op jit(solution)/shard_map/ppermute | solution.py:33
  83.3 0.2 select_reduce_fusion
  83.5 2.1 %collective-permute-done.8.rest_6_.rest_8_ = bf16[784,512]{1,0:T(8,128)(2,1)S(1)} collective-permute-done((bf16[784,512]{1,0:T(8,128)(2,1)S(1)}, bf16[784,512]{1,0:T(8,128)(2,1)S(1)}, u32[]{:S(2)}, u32[]{:S(2)}) %collective-permute-start.8) | collective-permute-done | bytes 802848 | tf_op jit(solution)/shard_map/ppermute | solution.py:33
  85.7 0.1 rev.3
  85.8 0.1 concatenate.9.where_ref
  85.9 0.1 broadcast_subtract_fusion
  86.0 1.3 collective-permute-start.11
  87.3 1.8 %collective-permute-start.12 = (bf16[1536,512]{1,0:T(8,128)(2,1)}, bf16[1536,512]{1,0:T(8,128)(2,1)}, u32[]{:S(2)}, u32[]{:S(2)}) collective-permute-start(bf16[1536,512]{1,0:T(8,128)(2,1)} %collective-permute-done.3.a_ref), channel_id=1, source_target_pairs={{2,4},{4,2},{3,5},{5,3},{10,12},{12,10},{11,13},{13,11},{18,20},{2... | collective-permute-start | bytes 4718600 | tf_op jit(solution)/shard_map/ppermute | solution.py:296
  89.1 0.7 slice_reduce_fusion.5
  89.8 0.1 stack.104
  89.9 0.7 slice_reduce_fusion.4
  90.6 0.1 stack.105
  90.7 0.9 copy-done.3
  91.6 0.1 stack.108
  91.7 0.6 collective-permute-start.10
  92.3 0.9 copy-done.6
  93.2 0.1 stack.109
  93.2 0.7 slice_reduce_fusion.3
  94.0 0.1 stack.106
  94.0 0.7 slice_reduce_fusion.2
  94.7 0.1 stack.107
  94.8 0.1 stack.93
  95.0 0.1 pad_maximum_fusion.1
  95.1 0.3 divide_multiply_fusion.k_ref
  95.4 0.7 copy-done.4
  96.1 0.2 copy-done.7
  96.3 19.0 %shard_map.65 = f32[8,8,256]{2,1,0:T(8,128)S(1)} custom-call(s32[6]{0:T(128)S(1)} %stack.83.where_ref, f32[8,192,256]{2,1,0:T(8,128)S(1)} %divide_multiply_fusion.k_ref, bf16[1536,512]{1,0:T(8,128)(2,1)} %bitcast.26, bf16[1536,512]{1,0:T(8,128)(2,1)} %collective-permute-done.3.a_ref, bf16[1536,512]{1,0:T(8,128)(2,1)} %collective-permute-done.4.b_ref, ...), custom_call_target="tpu_custom_call" | custom-call | flops 805306368 | bytes 524288 | tf_op jit(solution)/shard_map/pallas_call | solution.py:205
  115.3 9.6 %collective-permute-done.11.rest_0_ = bf16[1536,512]{1,0:T(8,128)(2,1)} collective-permute-done((bf16[1536,512]{1,0:T(8,128)(2,1)}, bf16[1536,512]{1,0:T(8,128)(2,1)}, u32[]{:S(2)}, u32[]{:S(2)}) %collective-permute-start.11) | collective-permute-done | bytes 1572896 | tf_op jit(solution)/shard_map/ppermute | solution.py:295
  125.0 1.1 copy-done.5
  126.1 1.1 copy-done.8
  127.3 1.2 copy-done.13
  128.5 18.1 %shard_map.67 = f32[8,8,256]{2,1,0:T(8,128)S(1)} custom-call(s32[14]{0:T(128)S(1)} %concatenate.9.where_ref, f32[8,192,256]{2,1,0:T(8,128)S(1)} %divide_multiply_fusion.k_ref, bf16[1536,512]{1,0:T(8,128)(2,1)S(1)} %bitcast.29, bf16[1536,512]{1,0:T(8,128)(2,1)} %collective-permute-done.3.a_ref, bf16[1536,512]{1,0:T(8,128)(2,1)} %collective-permute-done.4.b_ref, ...), custom_call_target="tpu_custom_call" | custom-call | flops 12884901888 | bytes 524288 | tf_op jit(solution)/shard_map/pallas_call | solution.py:205
  146.6 1.6 collective-permute-start.14
  148.2 0.8 collective-permute-start.15
  149.0 1.1 collective-permute-start.13
  150.1 0.2 collective-permute-done.14
  150.3 2.4 %collective-permute-done.15 = f32[8,256]{1,0:T(8,128)S(1)} collective-permute-done((f32[8,256]{1,0:T(8,128)S(1)}, f32[8,256]{1,0:T(8,128)S(1)}, u32[]{:S(2)}, u32[]{:S(2)}) %collective-permute-start.15) | collective-permute-done | bytes 8224 | tf_op jit(solution)/shard_map/ppermute | solution.py:33
  152.7 7.0 %collective-permute-start.17 = (f32[8,256]{1,0:T(8,128)S(1)}, f32[8,256]{1,0:T(8,128)S(1)}, u32[]{:S(2)}, u32[]{:S(2)}) collective-permute-start(f32[8,256]{1,0:T(8,128)S(1)} %add_add_fusion.1), channel_id=1, source_target_pairs={{0,4},{2,6},{4,0},{6,2},{1,5},{3,7},{5,1},{7,3},{8,12},{10,14},{12... | collective-permute-start | bytes 24584 | tf_op jit(solution)/shard_map/ppermute | solution.py:33
  159.8 1.2 collective-permute-start.18
  161.0 0.5 collective-permute-done.17
  161.5 3.7 %collective-permute-done.18 = f32[8,256]{1,0:T(8,128)S(1)} collective-permute-done((f32[8,256]{1,0:T(8,128)S(1)}, f32[8,256]{1,0:T(8,128)S(1)}, u32[]{:S(2)}, u32[]{:S(2)}) %collective-permute-start.18) | collective-permute-done | bytes 8224 | tf_op jit(solution)/shard_map/ppermute | solution.py:33
  165.2 0.6 add_add_fusion
  (47 shorter events, 0.2 us)
Async XLA Ops:
  6.5 118.5 %all-gather.3.cloned.1.call-start = ((), (), s32[]{:S(2)}) async-start(), calls=%async_computation | async-start | bytes 4718592 | tf_op jit(solution)/shard_map/all_gather | solution.py:277
  7.6 15.0 %collective-permute-start.2 = (bf16[512,512]{1,0:T(8,128)(2,1)S(1)}, bf16[512,512]{1,0:T(8,128)(2,1)S(1)}, u32[]{:S(2)}, u32[]{:S(2)}) collective-permute-start(bf16[512,512]{1,0:T(8,128)(2,1)S(1)} %dynamic-slice_bitcast_fusion), channel_id=1, source_target_pairs={{0,2},{2,0},{4,6},{6,4},{1,3},{3,1},{5,7},{7,5},{8,10},{10,8},{12,... | collective-permute-start | bytes 1572872 | tf_op jit(solution)/shard_map/ppermute | solution.py:244
  10.8 2.2 %copy-start = (bf16[2,2048,512]{2,1,0:T(8,128)(2,1)S(1)}, bf16[2,2048,512]{2,1,0:T(8,128)(2,1)}, u32[]{:S(2)}) copy-start(bf16[2,2048,512]{2,1,0:T(8,128)(2,1)} %rest_0_.1) | copy-start | bytes 12582916
  13.0 0.7 copy-start.9
  13.6 0.7 copy-start.11
  14.3 5.9 %copy-start.1 = (bf16[8,192,512]{2,1,0:T(8,128)(2,1)S(1)}, bf16[8,192,512]{2,1,0:T(8,128)(2,1)}, u32[]{:S(2)}) copy-start(bf16[8,192,512]{2,1,0:T(8,128)(2,1)} %param.6) | copy-start | bytes 4718596
  16.2 1.0 copy-start.12
  17.2 36.5 %collective-permute-start = (bf16[1552,512]{1,0:T(8,128)(2,1)}, bf16[1552,512]{1,0:T(8,128)(2,1)}, u32[]{:S(2)}, u32[]{:S(2)}) collective-permute-start(bf16[1552,512]{1,0:T(8,128)(2,1)} %get-tuple-element.11), channel_id=1, source_target_pairs={{0,8},{8,0},{16,24},{24,16},{1,9},{9,1},{17,25},{25,17},{2,10},{10... | collective-permute-start | bytes 4767752 | tf_op jit(solution)/shard_map/ppermute | solution.py:33
  18.7 36.2 %collective-permute-start.1 = (bf16[1552,512]{1,0:T(8,128)(2,1)}, bf16[1552,512]{1,0:T(8,128)(2,1)}, u32[]{:S(2)}, u32[]{:S(2)}) collective-permute-start(bf16[1552,512]{1,0:T(8,128)(2,1)} %get-tuple-element.11), channel_id=1, source_target_pairs={{0,16},{8,24},{16,0},{24,8},{1,17},{9,25},{17,1},{25,9},{2,18},{10... | collective-permute-start | bytes 4767752 | tf_op jit(solution)/shard_map/ppermute | solution.py:33
  20.2 7.2 %collective-permute-start.4 = (bf16[1536,512]{1,0:T(8,128)(2,1)S(1)}, bf16[1536,512]{1,0:T(8,128)(2,1)}, u32[]{:S(2)}, u32[]{:S(2)}) collective-permute-start(bf16[1536,512]{1,0:T(8,128)(2,1)S(1)} %bitcast.27), channel_id=1, source_target_pairs={{2,4},{4,2},{3,5},{5,3},{10,12},{12,10},{11,13},{13,11},{18,20},{2... | collective-permute-start | bytes 4718600 | tf_op jit(solution)/shard_map/ppermute | solution.py:274
  22.6 2.7 %copy-start.14 = (bf16[512,512]{1,0:T(8,128)(2,1)}, bf16[512,512]{1,0:T(8,128)(2,1)S(1)}, u32[]{:S(2)}) copy-start(bf16[512,512]{1,0:T(8,128)(2,1)S(1)} %collective-permute-done.2.block_ref) | copy-start | bytes 1572868
  22.6 36.1 %collective-permute-start.3 = (bf16[1536,512]{1,0:T(8,128)(2,1)S(1)}, bf16[1536,512]{1,0:T(8,128)(2,1)}, u32[]{:S(2)}, u32[]{:S(2)}) collective-permute-start(bf16[1536,512]{1,0:T(8,128)(2,1)S(1)} %bitcast.28), channel_id=1, source_target_pairs={{0,2},{2,0},{4,6},{6,4},{1,3},{3,1},{5,7},{7,5},{8,10},{10,8},{12,... | collective-permute-start | bytes 4718600 | tf_op jit(solution)/shard_map/ppermute | solution.py:275
  58.7 24.6 %copy-start.15 = (f32[256]{0:T(256)S(1)}, f32[256]{0:T(256)}, u32[]{:S(2)}) copy-start(f32[256]{0:T(256)} %param.10) | copy-start | bytes 3076
  58.7 24.6 %copy-start.16 = (s32[192]{0:T(256)S(1)}, s32[192]{0:T(256)}, u32[]{:S(2)}) copy-start(s32[192]{0:T(256)} %param.11) | copy-start | bytes 2308
  58.8 26.9 %copy-start.10 = (f32[2]{0:T(128)S(1)}, f32[2]{0:T(128)}, u32[]{:S(2)}) copy-start(f32[2]{0:T(128)} %nu_ref.1) | copy-start | bytes 28
  60.0 23.3 %collective-permute-start.6 = (bf16[768,512]{1,0:T(8,128)(2,1)S(1)}, bf16[768,512]{1,0:T(8,128)(2,1)}, u32[]{:S(2)}, u32[]{:S(2)}) collective-permute-start(bf16[768,512]{1,0:T(8,128)(2,1)S(1)} %slice.55), channel_id=1, source_target_pairs={{0,8},{8,0},{16,24},{24,16},{1,9},{9,1},{17,25},{25,17},{2,10},{10... | collective-permute-start | bytes 2359304 | tf_op jit(solution)/shard_map/ppermute | solution.py:33
  62.3 23.3 %collective-permute-start.8 = (bf16[784,512]{1,0:T(8,128)(2,1)S(1)}, bf16[784,512]{1,0:T(8,128)(2,1)S(1)}, u32[]{:S(2)}, u32[]{:S(2)}) collective-permute-start(bf16[784,512]{1,0:T(8,128)(2,1)S(1)} %slice.57), channel_id=1, source_target_pairs={{0,16},{8,24},{16,0},{24,8},{1,17},{9,25},{17,1},{25,9},{2,18},{10... | collective-permute-start | bytes 2408456 | tf_op jit(solution)/shard_map/ppermute | solution.py:33
  63.9 29.4 %collective-permute-start.5 = (bf16[1552,512]{1,0:T(8,128)(2,1)}, bf16[1552,512]{1,0:T(8,128)(2,1)}, u32[]{:S(2)}, u32[]{:S(2)}) collective-permute-start(bf16[1552,512]{1,0:T(8,128)(2,1)} %collective-permute-done.rest_1_.rest_4_), channel_id=1, source_target_pairs={{0,1},{1,0},{2,3},{3,2},{4,5},{5,4},{6,7},{7,6},{8,9},{9,8},{10,11... | collective-permute-start | bytes 4767752 | tf_op jit(solution)/shard_map/ppermute | solution.py:33
  83.3 10.8 %collective-permute-start.7 = (bf16[1552,512]{1,0:T(8,128)(2,1)}, bf16[1552,512]{1,0:T(8,128)(2,1)}, u32[]{:S(2)}, u32[]{:S(2)}) collective-permute-start(bf16[1552,512]{1,0:T(8,128)(2,1)} %collective-permute-done.1.rest_2_.rest_5_), channel_id=1, source_target_pairs={{0,1},{1,0},{2,3},{3,2},{4,5},{5,4},{6,7},{7,6},{8,9},{9,8},{10,11... | collective-permute-start | bytes 4767752 | tf_op jit(solution)/shard_map/ppermute | solution.py:33
  85.6 6.0 %collective-permute-start.9 = (bf16[784,512]{1,0:T(8,128)(2,1)S(1)}, bf16[784,512]{1,0:T(8,128)(2,1)S(1)}, u32[]{:S(2)}, u32[]{:S(2)}) collective-permute-start(bf16[784,512]{1,0:T(8,128)(2,1)S(1)} %collective-permute-done.8.rest_6_.rest_8_), channel_id=1, source_target_pairs={{0,1},{1,0},{2,3},{3,2},{4,5},{5,4},{6,7},{7,6},{8,9},{9,8},{10,11... | collective-permute-start | bytes 2408456 | tf_op jit(solution)/shard_map/ppermute | solution.py:33
  86.0 39.0 %collective-permute-start.11 = (bf16[1536,512]{1,0:T(8,128)(2,1)}, bf16[1536,512]{1,0:T(8,128)(2,1)}, u32[]{:S(2)}, u32[]{:S(2)}) collective-permute-start(bf16[1536,512]{1,0:T(8,128)(2,1)} %collective-permute-done.4.b_ref), channel_id=1, source_target_pairs={{2,0},{4,6},{3,1},{5,7},{10,8},{12,14},{11,9},{13,15},{18,16},{20,... | collective-permute-start | bytes 4718600 | tf_op jit(solution)/shard_map/ppermute | solution.py:295
  87.3 37.7 %collective-permute-start.12 = (bf16[1536,512]{1,0:T(8,128)(2,1)}, bf16[1536,512]{1,0:T(8,128)(2,1)}, u32[]{:S(2)}, u32[]{:S(2)}) collective-permute-start(bf16[1536,512]{1,0:T(8,128)(2,1)} %collective-permute-done.3.a_ref), channel_id=1, source_target_pairs={{2,4},{4,2},{3,5},{5,3},{10,12},{12,10},{11,13},{13,11},{18,20},{2... | collective-permute-start | bytes 4718600 | tf_op jit(solution)/shard_map/ppermute | solution.py:296
  90.7 0.9 copy-start.3
  91.7 3.7 %collective-permute-start.10 = (bf16[768,512]{1,0:T(8,128)(2,1)}, bf16[768,512]{1,0:T(8,128)(2,1)}, u32[]{:S(2)}, u32[]{:S(2)}) collective-permute-start(bf16[768,512]{1,0:T(8,128)(2,1)} %collective-permute-done.6.rest_5_), channel_id=1, source_target_pairs={{0,1},{1,0},{2,3},{3,2},{4,5},{5,4},{6,7},{7,6},{8,9},{9,8},{10,11... | collective-permute-start | bytes 2359304 | tf_op jit(solution)/shard_map/ppermute | solution.py:33
  92.3 0.9 copy-start.6
  94.9 1.1 copy-start.4
  95.0 1.4 copy-start.7
  95.4 29.6 %copy-start.2 = (bf16[8,192,512]{2,1,0:T(8,128)(2,1)S(1)}, bf16[8,192,512]{2,1,0:T(8,128)(2,1)}, u32[]{:S(2)}) copy-start(bf16[8,192,512]{2,1,0:T(8,128)(2,1)} %param.6) | copy-start | bytes 4718596
  125.0 1.1 copy-start.5
  126.1 1.1 copy-start.8
  127.3 1.2 copy-start.13
  146.6 3.7 %collective-permute-start.14 = (f32[8,256]{1,0:T(8,128)S(1)}, f32[8,256]{1,0:T(8,128)S(1)}, u32[]{:S(2)}, u32[]{:S(2)}) collective-permute-start(f32[8,256]{1,0:T(8,128)S(1)} %add_reduce_fusion), channel_id=1, source_target_pairs={{0,16},{8,24},{16,0},{24,8},{1,17},{9,25},{17,1},{25,9},{2,18},{10... | collective-permute-start | bytes 24584 | tf_op jit(solution)/shard_map/ppermute | solution.py:33
  148.2 4.5 %collective-permute-start.15 = (f32[8,256]{1,0:T(8,128)S(1)}, f32[8,256]{1,0:T(8,128)S(1)}, u32[]{:S(2)}, u32[]{:S(2)}) collective-permute-start(f32[8,256]{1,0:T(8,128)S(1)} %add_reduce_fusion), channel_id=1, source_target_pairs={{0,24},{8,16},{16,8},{24,0},{1,25},{9,17},{17,9},{25,1},{2,26},{10... | collective-permute-start | bytes 24584 | tf_op jit(solution)/shard_map/ppermute | solution.py:33
  149.0 3.7 %collective-permute-start.13 = (f32[8,256]{1,0:T(8,128)S(1)}, f32[8,256]{1,0:T(8,128)S(1)}, u32[]{:S(2)}, u32[]{:S(2)}) collective-permute-start(f32[8,256]{1,0:T(8,128)S(1)} %add_reduce_fusion), channel_id=1, source_target_pairs={{0,8},{8,0},{16,24},{24,16},{1,9},{9,1},{17,25},{25,17},{2,10},{10... | collective-permute-start | bytes 24584 | tf_op jit(solution)/shard_map/ppermute | solution.py:33
  152.7 8.8 %collective-permute-start.17 = (f32[8,256]{1,0:T(8,128)S(1)}, f32[8,256]{1,0:T(8,128)S(1)}, u32[]{:S(2)}, u32[]{:S(2)}) collective-permute-start(f32[8,256]{1,0:T(8,128)S(1)} %add_add_fusion.1), channel_id=1, source_target_pairs={{0,4},{2,6},{4,0},{6,2},{1,5},{3,7},{5,1},{7,3},{8,12},{10,14},{12... | collective-permute-start | bytes 24584 | tf_op jit(solution)/shard_map/ppermute | solution.py:33
  159.8 5.4 %collective-permute-start.18 = (f32[8,256]{1,0:T(8,128)S(1)}, f32[8,256]{1,0:T(8,128)S(1)}, u32[]{:S(2)}, u32[]{:S(2)}) collective-permute-start(f32[8,256]{1,0:T(8,128)S(1)} %add_add_fusion.1), channel_id=1, source_target_pairs={{0,6},{2,4},{4,2},{6,0},{1,7},{3,5},{5,3},{7,1},{8,14},{10,12},{12... | collective-permute-start | bytes 24584 | tf_op jit(solution)/shard_map/ppermute | solution.py:33
  161.0 4.3 %collective-permute-start.16 = (f32[8,256]{1,0:T(8,128)S(1)}, f32[8,256]{1,0:T(8,128)S(1)}, u32[]{:S(2)}, u32[]{:S(2)}) collective-permute-start(f32[8,256]{1,0:T(8,128)S(1)} %add_add_fusion.1), channel_id=1, source_target_pairs={{0,2},{2,0},{4,6},{6,4},{1,3},{3,1},{5,7},{7,5},{8,10},{10,8},{12,... | collective-permute-start | bytes 24584 | tf_op jit(solution)/shard_map/ppermute | solution.py:33
Sparse Core Ops, SparseCore 0:
  58.8 43.2 all-gather.2

commit v8 on v7

--- a/solution.py
+++ b/solution.py
@@ -106,9 +106,15 @@
         fixed = [(own_ref, here), (own_ref, right)]
         either = [((a_ref, b_ref), there)]
     else:
-        c_ref, d_ref, w_refs = refs[0], refs[1], refs[2:]
+        lower, upper, w_refs = refs[:2], refs[2:4], refs[4:]
+        half = right.shape[0] // 2
         fixed = [(a_ref, left.at[:, panel:])]
-        either = [((c_ref, own_ref), left.at[:, :panel]), ((own_ref, d_ref), right)]
+        either = []
+        for n in range(2):
+            part = slice(n * half, (n + 1) * half)
+            mine = own_ref.at[part, :]
+            either.append(((lower[n], mine), left.at[part, :panel]))
+            either.append(((mine, upper[n]), right.at[part, :]))
     start_slot(plan, 0, where_ref, w_refs, w_all, w_sems)
     waits = [pltpu.make_async_copy(src, dst, sems.at[n]) for n, (src, dst) in enumerate(fixed)]
     for c in waits:
@@ -290,10 +296,12 @@
         terms = jnp.stack([w[row, :6] for w, row in places]).astype(jnp.float32).reshape(-1, 3, 2)
         return (terms[:, 0] + terms[:, 1]) + terms[:, 2]
 
-    x1_o, y1_o = share(after(x1, a_rows, b_rows)), share(after(y1, a_rows, b_rows, d1a))
-    d1a_o, d1b_o = share(d1a), share(d1b)
-    c_rows = lax.ppermute(b_rows, "ga", outward)
-    d_rows = lax.ppermute(a_rows, "ga", inner)
+    half = rows // 2
+    c_rows = [lax.ppermute(b_rows[:half], "ga", outward)]
+    d_rows = [lax.ppermute(a_rows[:half], "ga", inner)]
+    c_rows.append(lax.ppermute(after(b_rows[half:], d_rows[0], d1a, d1b), "ga", outward))
+    d_rows.append(lax.ppermute(after(a_rows[half:], c_rows[0], d1a, d1b), "ga", inner))
+    x1_o, y1_o, d1a_o, d1b_o = (share(after(w, c_rows[0], d_rows[0], d1a, d1b)) for w in (x1, y1, d1a, d1b))
     ends = ((x1, 3 * panel), (y1, 3 * panel), (x1_o, 3 * panel), (y1_o, 3 * panel), (d1b, cut), (d1b_o, cut))
     k_all = weigh(jnp.concatenate([mine, carried(*ends)]))
 
@@ -312,7 +320,7 @@
     arrays = (given_all, far_self, x1, y1, x1_o, y1_o, d1b, d1b_o)
     far = run_kernel(
         "far", slots, jnp.concatenate([where, ranks]), k_all,
-        (own, a_rows, b_rows), (c_rows, d_rows, *arrays), m_dev,
+        (own, a_rows, b_rows), (*c_rows, *d_rows, *arrays), m_dev,
     )
     sigma = jnp.sum(near + far, axis=1)
     for axis in ("freq", "ga"):

time: 173 us -> 170 us (0.983)
  waiting for transfers between devices: 70 us -> 64.7 us
  local copies, waits for them, and re-layouts: 18 us -> 19.9 us
    ppermute x14, waiting for transfers between devices: 55.9 us -> 42.3 us  [flip(): lax.ppermute(block, axis, [(i, i ^ bits) for i in range(lax.axis_size(axi...]
    ppermute x2 -> x4, waiting for transfers between devices: 9.65 us -> 14 us  [the longest x1 9.81 us: square_line(): c_rows = [lax.ppermute(b_rows[:half], 'ga', outward)]]
    slice x0 -> x2, local copies, waits for them, and re-layouts: none -> 3.94 us  [the longest x1 2.46 us: square_line(): a_rows[half:]]
    ppermute x1, waiting for transfers between devices: 3.81 us -> 5.82 us  [square_line(): a_rows = lax.ppermute(after(own, given), 'ga', outer)]
    unnamed x34 -> x28, local copies, waits for them, and re-layouts: 10.8 us -> 8.79 us
    ppermute x1, waiting for transfers between devices: 0.66 us -> 2.55 us  [square_line(): given = lax.ppermute(piece(give_at, panel), 'ga', outer)]
    ppermute x2 -> x4, starting transfers between devices: 3.11 us -> 4.82 us  [the longest x1 1.55 us: square_line(): lax.ppermute(after(a_rows[half:], c_rows[0], d1a, d1b), 'ga', inner)]
  transfers between devices with their start and end apart: 20 -> 22, of which waited for: 11 -> 13; matrix products, arithmetic and copies ran while one was open for 4% -> 6% of each run, Pallas kernels for 13% -> 13%
where the time goes in v8:
time: 170 us
  waiting for transfers between devices  64.7 us (38%)
  Pallas kernels  40.7 us (24%)
  starting transfers between devices  29.2 us (17%)
  local copies, waits for them, and re-layouts  19.9 us (12%)
  between operations  13.7 us (8%)
    ppermute x14, waiting for transfers between devices, flip(): lax.ppermute(block, axis, [(i, i ^ bits) for i in range(lax.axis_size(axi...  42.3 us
    pallas_call x2, Pallas kernels, run_kernel(): pl.pallas_call(functools.partial(quadratic_kernel, plan, m_dev, begin, mi...  37.8 us
    ppermute x14, starting transfers between devices, flip(): lax.ppermute(block, axis, [(i, i ^ bits) for i in range(lax.axis_size(axi...  17.7 us
    ppermute x1, waiting for transfers between devices, square_line(): c_rows = [lax.ppermute(b_rows[:half], 'ga', outward)]  9.81 us
    unnamed x28, local copies, waits for them, and re-layouts  8.79 us
    ppermute x1, waiting for transfers between devices, square_line(): a_rows = lax.ppermute(after(own, given), 'ga', outer)  5.82 us
    ppermute x1, waiting for transfers between devices, square_line(): lax.ppermute(after(b_rows[half:], d_rows[0], d1a, d1b), 'ga', outward)  4.2 us
  transfers between devices with their start and end apart: 22, of which 13 were waited for; matrix products, arithmetic and copies ran while one was open for 6% of the time, Pallas kernels for 13%

profile of v8, /device:TPU:0, one launch (start us, length us, event | category | flops | bytes accessed | tf_op | source)
XLA Modules:
  0.0 169.6 jit_solution(11132434999607820708)
XLA Ops:
  6.5 1.1 dynamic-slice_bitcast_fusion
  7.6 3.1 %collective-permute-start.4 = (bf16[512,512]{1,0:T(8,128)(2,1)S(1)}, bf16[512,512]{1,0:T(8,128)(2,1)}, u32[]{:S(2)}, u32[]{:S(2)}) collective-permute-start(bf16[512,512]{1,0:T(8,128)(2,1)S(1)} %dynamic-slice_bitcast_fusion), channel_id=1, source_target_pairs={{0,2},{2,0},{4,6},{6,4},{1,3},{3,1},{5,7},{7,5},{8,10},{10,8},{12,... | collective-permute-start | bytes 1572872 | tf_op jit(solution)/shard_map/ppermute | solution.py:250
  10.8 2.2 %copy-done = bf16[2,2048,512]{2,1,0:T(8,128)(2,1)S(1)} copy-done((bf16[2,2048,512]{2,1,0:T(8,128)(2,1)S(1)}, bf16[2,2048,512]{2,1,0:T(8,128)(2,1)}, u32[]{:S(2)}) %copy-start) | copy-done | bytes 4194328
  13.0 0.7 copy-done.2
  13.6 0.7 copy-done.4
  14.3 0.9 shard_map.64
  15.2 1.6 collective-permute-start
  16.8 1.5 collective-permute-start.1
  18.3 1.9 %collective-permute-start.2 = (bf16[1536,512]{1,0:T(8,128)(2,1)}, bf16[1536,512]{1,0:T(8,128)(2,1)}, u32[]{:S(2)}, u32[]{:S(2)}) collective-permute-start(bf16[1536,512]{1,0:T(8,128)(2,1)} %bitcast.8.own_ref), channel_id=1, source_target_pairs={{2,4},{4,2},{3,5},{5,3},{10,12},{12,10},{11,13},{13,11},{18,20},{2... | collective-permute-start | bytes 4718600 | tf_op jit(solution)/shard_map/ppermute | solution.py:280
  20.2 2.5 %collective-permute-done.4.block_ref = bf16[512,512]{1,0:T(8,128)(2,1)} collective-permute-done((bf16[512,512]{1,0:T(8,128)(2,1)S(1)}, bf16[512,512]{1,0:T(8,128)(2,1)}, u32[]{:S(2)}, u32[]{:S(2)}) %collective-permute-start.4) | collective-permute-done | bytes 524320 | tf_op jit(solution)/shard_map/ppermute | solution.py:250
  22.7 1.7 %collective-permute-start.5 = (bf16[1536,512]{1,0:T(8,128)(2,1)}, bf16[1536,512]{1,0:T(8,128)(2,1)}, u32[]{:S(2)}, u32[]{:S(2)}) collective-permute-start(bf16[1536,512]{1,0:T(8,128)(2,1)} %bitcast.8.own_ref), channel_id=1, source_target_pairs={{0,2},{2,0},{4,6},{6,4},{1,3},{3,1},{5,7},{7,5},{8,10},{10,8},{12,... | collective-permute-start | bytes 4718600 | tf_op jit(solution)/shard_map/ppermute | solution.py:281
  24.5 2.0 %shard_map.66 = bf16[512,512]{1,0:T(8,128)(2,1)} custom-call(bf16[512,512]{1,0:T(8,128)(2,1)} %collective-permute-done.4.block_ref), custom_call_target="tpu_custom_call" | custom-call | bytes 1048576 | tf_op jit(solution)/shard_map/pallas_call | solution.py:253
  26.5 25.1 %collective-permute-done.rest_1_.rest_6_ = bf16[1552,512]{1,0:T(8,128)(2,1)} collective-permute-done((bf16[1552,512]{1,0:T(8,128)(2,1)S(1)}, bf16[1552,512]{1,0:T(8,128)(2,1)}, u32[]{:S(2)}, u32[]{:S(2)}) %collective-permute-start) | collective-permute-done | bytes 1589280 | tf_op jit(solution)/shard_map/ppermute | solution.py:33
  51.6 1.2 collective-permute-done.1.rest_2_.rest_7_
  52.8 5.8 %collective-permute-done.5.a_ref = bf16[1536,512]{1,0:T(8,128)(2,1)} collective-permute-done((bf16[1536,512]{1,0:T(8,128)(2,1)}, bf16[1536,512]{1,0:T(8,128)(2,1)}, u32[]{:S(2)}, u32[]{:S(2)}) %collective-permute-start.5) | collective-permute-done | bytes 1572896 | tf_op jit(solution)/shard_map/ppermute | solution.py:281
  58.7 1.5 fusion.3
  60.1 1.3 collective-permute-start.3
  61.4 1.2 slice.72
  62.6 1.4 collective-permute-start.7
  64.0 1.2 slice.73
  65.3 1.6 collective-permute-start.8
  66.9 2.5 %fusion.2 = (bf16[768,512]{1,0:T(8,128)(2,1)}, bf16[768,512]{1,0:T(8,128)(2,1)S(1)}) fusion(bf16[1536,512]{1,0:T(8,128)(2,1)} %collective-permute-done.5.a_ref), kind=kLoop, calls=%fused_computation.24 | loop fusion | bytes 3145728 | tf_op jit(solution)/shard_map/slice | solution.py:303
  69.3 0.7 collective-permute-start.6
  70.0 9.8 %collective-permute-done.3.rest_0_ = bf16[768,512]{1,0:T(8,128)(2,1)S(1)} collective-permute-done((bf16[768,512]{1,0:T(8,128)(2,1)S(1)}, bf16[768,512]{1,0:T(8,128)(2,1)S(1)}, u32[]{:S(2)}, u32[]{:S(2)}) %collective-permute-start.3) | collective-permute-done | bytes 786464 | tf_op jit(solution)/shard_map/ppermute | solution.py:300
  79.8 0.9 copy-done.8
  80.7 5.5 %collective-permute-done.7.rest_5_ = bf16[768,512]{1,0:T(8,128)(2,1)} collective-permute-done((bf16[768,512]{1,0:T(8,128)(2,1)S(1)}, bf16[768,512]{1,0:T(8,128)(2,1)}, u32[]{:S(2)}, u32[]{:S(2)}) %collective-permute-start.7) | collective-permute-done | bytes 786464 | tf_op jit(solution)/shard_map/ppermute | solution.py:33
  86.2 2.3 %collective-permute-done.8.rest_6_.rest_10_ = bf16[784,512]{1,0:T(8,128)(2,1)S(1)} collective-permute-done((bf16[784,512]{1,0:T(8,128)(2,1)S(1)}, bf16[784,512]{1,0:T(8,128)(2,1)S(1)}, u32[]{:S(2)}, u32[]{:S(2)}) %collective-permute-start.8) | collective-permute-done | bytes 802848 | tf_op jit(solution)/shard_map/ppermute | solution.py:33
  88.5 0.9 copy-done.10
  89.4 0.5 collective-permute-start.10
  89.9 0.2 select_reduce_fusion
  90.3 0.1 rev.3
  90.3 0.1 concatenate.9.where_ref
  90.5 0.1 broadcast_subtract_fusion
  90.6 0.7 slice_reduce_fusion.5
  91.2 0.1 stack.104
  91.3 0.7 slice_reduce_fusion.4
  92.0 0.1 stack.105
  92.1 0.1 stack.108
  92.2 1.5 collective-permute-start.14
  93.8 0.5 collective-permute-start.12
  94.2 1.3 collective-permute-done.11.rest_8_.rest_11_
  95.5 1.3 collective-permute-start.13
  96.8 0.1 stack.109
  96.9 0.7 slice_reduce_fusion.3
  97.6 0.1 stack.106
  97.7 0.7 slice_reduce_fusion.2
  98.4 0.1 stack.107
  98.5 0.1 stack.93
  98.7 0.3 divide_multiply_fusion.k_ref
  99.0 19.0 %shard_map.65 = f32[8,8,256]{2,1,0:T(8,128)S(1)} custom-call(s32[6]{0:T(128)S(1)} %stack.83.where_ref, f32[8,192,256]{2,1,0:T(8,128)S(1)} %divide_multiply_fusion.k_ref, bf16[1536,512]{1,0:T(8,128)(2,1)} %bitcast.8.own_ref, bf16[1536,512]{1,0:T(8,128)(2,1)} %collective-permute-done.5.a_ref, bf16[1536,512]{1,0:T(8,128)(2,1)} %collective-permute-done.2.b_ref, ...), custom_call_target="tpu_custom_call" | custom-call | flops 805306368 | bytes 524288 | tf_op jit(solution)/shard_map/pallas_call | solution.py:211
  118.1 4.2 %collective-permute-done.13.rest_1_ = bf16[768,512]{1,0:T(8,128)(2,1)} collective-permute-done((bf16[768,512]{1,0:T(8,128)(2,1)S(1)}, bf16[768,512]{1,0:T(8,128)(2,1)}, u32[]{:S(2)}, u32[]{:S(2)}) %collective-permute-start.13) | collective-permute-done | bytes 786464 | tf_op jit(solution)/shard_map/ppermute | solution.py:302
  122.3 1.2 copy-done.7
  123.5 1.1 copy-done.9
  124.6 1.1 copy-done.11
  125.8 18.8 %shard_map.67 = f32[8,8,256]{2,1,0:T(8,128)S(1)} custom-call(s32[14]{0:T(128)S(1)} %concatenate.9.where_ref, f32[8,192,256]{2,1,0:T(8,128)} %copy-done.1, bf16[1536,512]{1,0:T(8,128)(2,1)} %bitcast.8.own_ref, bf16[1536,512]{1,0:T(8,128)(2,1)} %collective-permute-done.5.a_ref, bf16[1536,512]{1,0:T(8,128)(2,1)} %collective-permute-done.2.b_ref, ...), custom_call_target="tpu_custom_call" | custom-call | flops 12884901888 | bytes 524288 | tf_op jit(solution)/shard_map/pallas_call | solution.py:211
  144.6 2.6 %collective-permute-start.16 = (f32[8,256]{1,0:T(8,128)S(1)}, f32[8,256]{1,0:T(8,128)S(1)}, u32[]{:S(2)}, u32[]{:S(2)}) collective-permute-start(f32[8,256]{1,0:T(8,128)S(1)} %add_reduce_fusion), channel_id=1, source_target_pairs={{0,16},{8,24},{16,0},{24,8},{1,17},{9,25},{17,1},{25,9},{2,18},{10... | collective-permute-start | bytes 24584 | tf_op jit(solution)/shard_map/ppermute | solution.py:33
  147.1 1.5 collective-permute-start.15
  148.7 0.1 collective-permute-done.16
  148.8 2.9 %collective-permute-done.17 = f32[8,256]{1,0:T(8,128)S(1)} collective-permute-done((f32[8,256]{1,0:T(8,128)S(1)}, f32[8,256]{1,0:T(8,128)S(1)}, u32[]{:S(2)}, u32[]{:S(2)}) %collective-permute-start.17) | collective-permute-done | bytes 8224 | tf_op jit(solution)/shard_map/ppermute | solution.py:33
  151.7 5.0 %collective-permute-start.19 = (f32[8,256]{1,0:T(8,128)S(1)}, f32[8,256]{1,0:T(8,128)S(1)}, u32[]{:S(2)}, u32[]{:S(2)}) collective-permute-start(f32[8,256]{1,0:T(8,128)S(1)} %add_add_fusion.1), channel_id=1, source_target_pairs={{0,4},{2,6},{4,0},{6,2},{1,5},{3,7},{5,1},{7,3},{8,12},{10,14},{12... | collective-permute-start | bytes 24584 | tf_op jit(solution)/shard_map/ppermute | solution.py:33
  156.7 1.5 collective-permute-start.20
  158.2 0.1 collective-permute-done.19
  158.3 3.8 %collective-permute-done.20 = f32[8,256]{1,0:T(8,128)S(1)} collective-permute-done((f32[8,256]{1,0:T(8,128)S(1)}, f32[8,256]{1,0:T(8,128)S(1)}, u32[]{:S(2)}, u32[]{:S(2)}) %collective-permute-start.20) | collective-permute-done | bytes 8224 | tf_op jit(solution)/shard_map/ppermute | solution.py:33
  162.1 0.6 add_add_fusion
  (47 shorter events, 0.5 us)
Async XLA Ops:
  6.5 115.7 %all-gather.3.cloned.1.call-start = ((), (), s32[]{:S(2)}) async-start(), calls=%async_computation | async-start | bytes 4718592 | tf_op jit(solution)/shard_map/all_gather | solution.py:283
  7.6 15.1 %collective-permute-start.4 = (bf16[512,512]{1,0:T(8,128)(2,1)S(1)}, bf16[512,512]{1,0:T(8,128)(2,1)}, u32[]{:S(2)}, u32[]{:S(2)}) collective-permute-start(bf16[512,512]{1,0:T(8,128)(2,1)S(1)} %dynamic-slice_bitcast_fusion), channel_id=1, source_target_pairs={{0,2},{2,0},{4,6},{6,4},{1,3},{3,1},{5,7},{7,5},{8,10},{10,8},{12,... | collective-permute-start | bytes 1572872 | tf_op jit(solution)/shard_map/ppermute | solution.py:250
  10.8 2.2 %copy-start = (bf16[2,2048,512]{2,1,0:T(8,128)(2,1)S(1)}, bf16[2,2048,512]{2,1,0:T(8,128)(2,1)}, u32[]{:S(2)}) copy-start(bf16[2,2048,512]{2,1,0:T(8,128)(2,1)} %rest_0_.1) | copy-start | bytes 12582916
  13.0 0.7 copy-start.2
  13.6 0.7 copy-start.4
  15.2 44.9 %copy-start.6 = (bf16[2,512,512]{2,1,0:T(8,128)(2,1)}, bf16[2,512,512]{2,1,0:T(8,128)(2,1)S(1)}, u32[]{:S(2)}) copy-start(bf16[2,512,512]{2,1,0:T(8,128)(2,1)S(1)} %get-tuple-element.24.rest_5_) | copy-start | bytes 3145732
  15.2 36.4 %collective-permute-start = (bf16[1552,512]{1,0:T(8,128)(2,1)S(1)}, bf16[1552,512]{1,0:T(8,128)(2,1)}, u32[]{:S(2)}, u32[]{:S(2)}) collective-permute-start(bf16[1552,512]{1,0:T(8,128)(2,1)S(1)} %get-tuple-element.15), channel_id=1, source_target_pairs={{0,8},{8,0},{16,24},{24,16},{1,9},{9,1},{17,25},{25,17},{2,10},{10... | collective-permute-start | bytes 4767752 | tf_op jit(solution)/shard_map/ppermute | solution.py:33
  16.8 36.0 %collective-permute-start.1 = (bf16[1552,512]{1,0:T(8,128)(2,1)S(1)}, bf16[1552,512]{1,0:T(8,128)(2,1)}, u32[]{:S(2)}, u32[]{:S(2)}) collective-permute-start(bf16[1552,512]{1,0:T(8,128)(2,1)S(1)} %get-tuple-element.15), channel_id=1, source_target_pairs={{0,16},{8,24},{16,0},{24,8},{1,17},{9,25},{17,1},{25,9},{2,18},{10... | collective-permute-start | bytes 4767752 | tf_op jit(solution)/shard_map/ppermute | solution.py:33
  18.3 8.2 %collective-permute-start.2 = (bf16[1536,512]{1,0:T(8,128)(2,1)}, bf16[1536,512]{1,0:T(8,128)(2,1)}, u32[]{:S(2)}, u32[]{:S(2)}) collective-permute-start(bf16[1536,512]{1,0:T(8,128)(2,1)} %bitcast.8.own_ref), channel_id=1, source_target_pairs={{2,4},{4,2},{3,5},{5,3},{10,12},{12,10},{11,13},{13,11},{18,20},{2... | collective-permute-start | bytes 4718600 | tf_op jit(solution)/shard_map/ppermute | solution.py:280
  22.7 35.9 %collective-permute-start.5 = (bf16[1536,512]{1,0:T(8,128)(2,1)}, bf16[1536,512]{1,0:T(8,128)(2,1)}, u32[]{:S(2)}, u32[]{:S(2)}) collective-permute-start(bf16[1536,512]{1,0:T(8,128)(2,1)} %bitcast.8.own_ref), channel_id=1, source_target_pairs={{0,2},{2,0},{4,6},{6,4},{1,3},{3,1},{5,7},{7,5},{8,10},{10,8},{12,... | collective-permute-start | bytes 4718600 | tf_op jit(solution)/shard_map/ppermute | solution.py:281
  60.1 19.7 %collective-permute-start.3 = (bf16[768,512]{1,0:T(8,128)(2,1)S(1)}, bf16[768,512]{1,0:T(8,128)(2,1)S(1)}, u32[]{:S(2)}, u32[]{:S(2)}) collective-permute-start(bf16[768,512]{1,0:T(8,128)(2,1)S(1)} %get-tuple-element.28), channel_id=1, source_target_pairs={{2,0},{4,6},{3,1},{5,7},{10,8},{12,14},{11,9},{13,15},{18,16},{20,... | collective-permute-start | bytes 2359304 | tf_op jit(solution)/shard_map/ppermute | solution.py:300
  62.6 23.6 %collective-permute-start.7 = (bf16[768,512]{1,0:T(8,128)(2,1)S(1)}, bf16[768,512]{1,0:T(8,128)(2,1)}, u32[]{:S(2)}, u32[]{:S(2)}) collective-permute-start(bf16[768,512]{1,0:T(8,128)(2,1)S(1)} %slice.72), channel_id=1, source_target_pairs={{0,8},{8,0},{16,24},{24,16},{1,9},{9,1},{17,25},{25,17},{2,10},{10... | collective-permute-start | bytes 2359304 | tf_op jit(solution)/shard_map/ppermute | solution.py:33
  65.2 24.7 %copy-start.12 = (f32[256]{0:T(256)S(1)}, f32[256]{0:T(256)}, u32[]{:S(2)}) copy-start(f32[256]{0:T(256)} %param.10) | copy-start | bytes 3076
  65.2 24.7 %copy-start.13 = (s32[192]{0:T(256)S(1)}, s32[192]{0:T(256)}, u32[]{:S(2)}) copy-start(s32[192]{0:T(256)} %param.11) | copy-start | bytes 2308
  65.3 25.0 %copy-start.3 = (f32[2]{0:T(128)S(1)}, f32[2]{0:T(128)}, u32[]{:S(2)}) copy-start(f32[2]{0:T(128)} %nu_ref.1) | copy-start | bytes 28
  65.3 24.9 %copy-start.5 = (f32[2]{0:T(128)S(1)}, f32[2]{0:T(128)}, u32[]{:S(2)}) copy-start(f32[2]{0:T(128)} %weight_ref.1) | copy-start | bytes 28
  65.3 23.2 %collective-permute-start.8 = (bf16[784,512]{1,0:T(8,128)(2,1)S(1)}, bf16[784,512]{1,0:T(8,128)(2,1)S(1)}, u32[]{:S(2)}, u32[]{:S(2)}) collective-permute-start(bf16[784,512]{1,0:T(8,128)(2,1)S(1)} %slice.73), channel_id=1, source_target_pairs={{0,16},{8,24},{16,0},{24,8},{1,17},{9,25},{17,1},{25,9},{2,18},{10... | collective-permute-start | bytes 2408456 | tf_op jit(solution)/shard_map/ppermute | solution.py:33
  69.3 19.2 %collective-permute-start.6 = (bf16[768,512]{1,0:T(8,128)(2,1)S(1)}, bf16[768,512]{1,0:T(8,128)(2,1)S(1)}, u32[]{:S(2)}, u32[]{:S(2)}) collective-permute-start(bf16[768,512]{1,0:T(8,128)(2,1)S(1)} %get-tuple-element.26), channel_id=1, source_target_pairs={{2,4},{4,2},{3,5},{5,3},{10,12},{12,10},{11,13},{13,11},{18,20},{2... | collective-permute-start | bytes 2359304 | tf_op jit(solution)/shard_map/ppermute | solution.py:301
  79.8 0.9 copy-start.8
  88.5 0.9 copy-start.10
  89.4 7.5 %collective-permute-start.9 = (bf16[1552,512]{1,0:T(8,128)(2,1)}, bf16[1552,512]{1,0:T(8,128)(2,1)}, u32[]{:S(2)}, u32[]{:S(2)}) collective-permute-start(bf16[1552,512]{1,0:T(8,128)(2,1)} %collective-permute-done.rest_1_.rest_6_), channel_id=1, source_target_pairs={{0,1},{1,0},{2,3},{3,2},{4,5},{5,4},{6,7},{7,6},{8,9},{9,8},{10,11... | collective-permute-start | bytes 4767752 | tf_op jit(solution)/shard_map/ppermute | solution.py:33
  89.4 8.3 %collective-permute-start.10 = (bf16[1552,512]{1,0:T(8,128)(2,1)}, bf16[1552,512]{1,0:T(8,128)(2,1)}, u32[]{:S(2)}, u32[]{:S(2)}) collective-permute-start(bf16[1552,512]{1,0:T(8,128)(2,1)} %collective-permute-done.1.rest_2_.rest_7_), channel_id=1, source_target_pairs={{0,1},{1,0},{2,3},{3,2},{4,5},{5,4},{6,7},{7,6},{8,9},{9,8},{10,11... | collective-permute-start | bytes 4767752 | tf_op jit(solution)/shard_map/ppermute | solution.py:33
  90.1 5.4 %collective-permute-start.11 = (bf16[784,512]{1,0:T(8,128)(2,1)S(1)}, bf16[784,512]{1,0:T(8,128)(2,1)S(1)}, u32[]{:S(2)}, u32[]{:S(2)}) collective-permute-start(bf16[784,512]{1,0:T(8,128)(2,1)S(1)} %collective-permute-done.8.rest_6_.rest_10_), channel_id=1, source_target_pairs={{0,1},{1,0},{2,3},{3,2},{4,5},{5,4},{6,7},{7,6},{8,9},{9,8},{10,11... | collective-permute-start | bytes 2408456 | tf_op jit(solution)/shard_map/ppermute | solution.py:33
  92.2 25.8 %collective-permute-start.14 = (bf16[768,512]{1,0:T(8,128)(2,1)}, bf16[768,512]{1,0:T(8,128)(2,1)}, u32[]{:S(2)}, u32[]{:S(2)}) collective-permute-start(bf16[768,512]{1,0:T(8,128)(2,1)} %get-tuple-element.22), channel_id=1, source_target_pairs={{2,4},{4,2},{3,5},{5,3},{10,12},{12,10},{11,13},{13,11},{18,20},{2... | collective-permute-start | bytes 2359304 | tf_op jit(solution)/shard_map/ppermute | solution.py:303
  93.8 5.3 %collective-permute-start.12 = (bf16[768,512]{1,0:T(8,128)(2,1)}, bf16[768,512]{1,0:T(8,128)(2,1)}, u32[]{:S(2)}, u32[]{:S(2)}) collective-permute-start(bf16[768,512]{1,0:T(8,128)(2,1)} %collective-permute-done.7.rest_5_), channel_id=1, source_target_pairs={{0,1},{1,0},{2,3},{3,2},{4,5},{5,4},{6,7},{7,6},{8,9},{9,8},{10,11... | collective-permute-start | bytes 2359304 | tf_op jit(solution)/shard_map/ppermute | solution.py:33
  95.5 26.7 %collective-permute-start.13 = (bf16[768,512]{1,0:T(8,128)(2,1)S(1)}, bf16[768,512]{1,0:T(8,128)(2,1)}, u32[]{:S(2)}, u32[]{:S(2)}) collective-permute-start(bf16[768,512]{1,0:T(8,128)(2,1)S(1)} %get-tuple-element.21), channel_id=1, source_target_pairs={{2,0},{4,6},{3,1},{5,7},{10,8},{12,14},{11,9},{13,15},{18,16},{20,... | collective-permute-start | bytes 2359304 | tf_op jit(solution)/shard_map/ppermute | solution.py:302
  99.0 19.0 %copy-start.1 = (f32[8,192,256]{2,1,0:T(8,128)}, f32[8,192,256]{2,1,0:T(8,128)S(1)}, u32[]{:S(2)}) copy-start(f32[8,192,256]{2,1,0:T(8,128)S(1)} %divide_multiply_fusion.k_ref) | copy-start | bytes 4718596
  122.3 1.2 copy-start.7
  123.5 1.1 copy-start.9
  124.6 1.1 copy-start.11
  144.6 4.2 %collective-permute-start.16 = (f32[8,256]{1,0:T(8,128)S(1)}, f32[8,256]{1,0:T(8,128)S(1)}, u32[]{:S(2)}, u32[]{:S(2)}) collective-permute-start(f32[8,256]{1,0:T(8,128)S(1)} %add_reduce_fusion), channel_id=1, source_target_pairs={{0,16},{8,24},{16,0},{24,8},{1,17},{9,25},{17,1},{25,9},{2,18},{10... | collective-permute-start | bytes 24584 | tf_op jit(solution)/shard_map/ppermute | solution.py:33
  147.1 4.5 %collective-permute-start.17 = (f32[8,256]{1,0:T(8,128)S(1)}, f32[8,256]{1,0:T(8,128)S(1)}, u32[]{:S(2)}, u32[]{:S(2)}) collective-permute-start(f32[8,256]{1,0:T(8,128)S(1)} %add_reduce_fusion), channel_id=1, source_target_pairs={{0,24},{8,16},{16,8},{24,0},{1,25},{9,17},{17,9},{25,1},{2,26},{10... | collective-permute-start | bytes 24584 | tf_op jit(solution)/shard_map/ppermute | solution.py:33
  147.1 4.5 %collective-permute-start.15 = (f32[8,256]{1,0:T(8,128)S(1)}, f32[8,256]{1,0:T(8,128)S(1)}, u32[]{:S(2)}, u32[]{:S(2)}) collective-permute-start(f32[8,256]{1,0:T(8,128)S(1)} %add_reduce_fusion), channel_id=1, source_target_pairs={{0,8},{8,0},{16,24},{24,16},{1,9},{9,1},{17,25},{25,17},{2,10},{10... | collective-permute-start | bytes 24584 | tf_op jit(solution)/shard_map/ppermute | solution.py:33
  151.7 6.6 %collective-permute-start.19 = (f32[8,256]{1,0:T(8,128)S(1)}, f32[8,256]{1,0:T(8,128)S(1)}, u32[]{:S(2)}, u32[]{:S(2)}) collective-permute-start(f32[8,256]{1,0:T(8,128)S(1)} %add_add_fusion.1), channel_id=1, source_target_pairs={{0,4},{2,6},{4,0},{6,2},{1,5},{3,7},{5,1},{7,3},{8,12},{10,14},{12... | collective-permute-start | bytes 24584 | tf_op jit(solution)/shard_map/ppermute | solution.py:33
  156.7 5.4 %collective-permute-start.20 = (f32[8,256]{1,0:T(8,128)S(1)}, f32[8,256]{1,0:T(8,128)S(1)}, u32[]{:S(2)}, u32[]{:S(2)}) collective-permute-start(f32[8,256]{1,0:T(8,128)S(1)} %add_add_fusion.1), channel_id=1, source_target_pairs={{0,6},{2,4},{4,2},{6,0},{1,7},{3,5},{5,3},{7,1},{8,14},{10,12},{12... | collective-permute-start | bytes 24584 | tf_op jit(solution)/shard_map/ppermute | solution.py:33
  158.2 3.9 %collective-permute-start.18 = (f32[8,256]{1,0:T(8,128)S(1)}, f32[8,256]{1,0:T(8,128)S(1)}, u32[]{:S(2)}, u32[]{:S(2)}) collective-permute-start(f32[8,256]{1,0:T(8,128)S(1)} %add_add_fusion.1), channel_id=1, source_target_pairs={{0,2},{2,0},{4,6},{6,4},{1,3},{3,1},{5,7},{7,5},{8,10},{10,8},{12,... | collective-permute-start | bytes 24584 | tf_op jit(solution)/shard_map/ppermute | solution.py:33
Sparse Core Ops, SparseCore 0:
  58.8 43.5 all-gather.2

commit v9 on v7

--- a/solution.py
+++ b/solution.py
@@ -290,19 +290,22 @@
         terms = jnp.stack([w[row, :6] for w, row in places]).astype(jnp.float32).reshape(-1, 3, 2)
         return (terms[:, 0] + terms[:, 1]) + terms[:, 2]
 
-    x1_o, y1_o = share(after(x1, a_rows, b_rows)), share(after(y1, a_rows, b_rows, d1a))
-    d1a_o, d1b_o = share(d1a), share(d1b)
+    whole = 2 * panel
+    panels = (own, a_rows, b_rows)
+    slots = [[(0, ("at", 3 + s), ("at", 2), whole)] for s in range(2)]
+    slots += [[(r, None, 0, whole)] for r in (1, 2)]
+    k_here = weigh(jnp.concatenate([mine, carried((x1, 3 * panel), (y1, 3 * panel))]))
+    near = run_kernel("near", slots, where, k_here, panels, (screened, x1, y1), m_dev)
+
     c_rows = lax.ppermute(b_rows, "ga", outward)
     d_rows = lax.ppermute(a_rows, "ga", inner)
-    ends = ((x1, 3 * panel), (y1, 3 * panel), (x1_o, 3 * panel), (y1_o, 3 * panel), (d1b, cut), (d1b_o, cut))
-    k_all = weigh(jnp.concatenate([mine, carried(*ends)]))
-
-    whole = 2 * panel
-    slots = [[(0, ("at", 3 + s), ("at", 2), whole)] for s in range(2)]
-    slots += [[(r, None, 0, whole)] for r in (1, 2, 3, 4)]
-    slots += [[(r, None, 0, cut), (r + 1, None, 0, whole - cut)] for r in (5, 7)]
-    arrays = (screened, x1, y1, x1_o, y1_o, d1a, d1b, d1a_o, d1b_o)
-    near = run_kernel("near", slots, where, k_all, (own, a_rows, b_rows), arrays, m_dev)
+    x1_o, y1_o = share(after(x1, d1a, d1b, near)), share(after(y1, d1a, d1b, near))
+    d1a_o, d1b_o = share(after(d1a, c_rows, d_rows)), share(after(d1b, c_rows, d_rows))
+    slots = [[(r, None, 0, whole)] for r in (0, 1)]
+    slots += [[(r, None, 0, cut), (r + 1, None, 0, whole - cut)] for r in (2, 4)]
+    k_there = weigh(carried((x1_o, 3 * panel), (y1_o, 3 * panel), (d1b, cut), (d1b_o, cut)))
+    corner = run_kernel("near", slots, where, k_there, panels, (x1_o, y1_o, d1a, d1b, d1a_o, d1b_o), m_dev)
+    k_all = jnp.concatenate([k_here, k_there])
 
     square = lax.axis_index("freq")
     order = ((0, core), (0, 1 - core), (1, core), (2, core), (1, 1 - core), (2, 1 - core), (3, core), (3, 1 - core))
@@ -314,7 +317,7 @@
         "far", slots, jnp.concatenate([where, ranks]), k_all,
         (own, a_rows, b_rows), (c_rows, d_rows, *arrays), m_dev,
     )
-    sigma = jnp.sum(near + far, axis=1)
+    sigma = jnp.sum(near + corner + far, axis=1)
     for axis in ("freq", "ga"):
         t1, t2, t3 = (flip(sigma, axis, r) for r in (1, 2, 3))
         sigma = (sigma + t1) + (t2 + t3)

time: 173 us -> 167 us (0.965)
  waiting for transfers between devices: 70 us -> 54.3 us
  starting transfers between devices: 28.8 us -> 34.6 us
  other arithmetic: 1.32 us -> 5.27 us
    ppermute x14, waiting for transfers between devices: 55.9 us -> 45.4 us  [flip(): lax.ppermute(block, axis, [(i, i ^ bits) for i in range(lax.axis_size(axi...]
    ppermute x14, starting transfers between devices: 18.1 us -> 24 us  [flip(): lax.ppermute(block, axis, [(i, i ^ bits) for i in range(lax.axis_size(axi...]
    ppermute x1, waiting for transfers between devices: 9.64 us -> 4.34 us  [square_line(): c_rows = lax.ppermute(b_rows, 'ga', outward)]
    unnamed x34 -> x22, local copies, waits for them, and re-layouts: 10.8 us -> 7.14 us
    mul x1 -> x2, other arithmetic: 0.28 us -> 2.21 us  [weigh(): return -weight / math.pi * (offsets / (offsets * offsets + nu * nu))]
    pallas_call x2 -> x3, Pallas kernels: 37 us -> 38.2 us  [run_kernel(): pl.pallas_call(functools.partial(quadratic_kernel, plan, m_dev, begin, mi...]
  transfers between devices with their start and end apart: 20 -> 20, of which waited for: 11 -> 13; matrix products, arithmetic and copies ran while one was open for 4% -> 8% of each run, Pallas kernels for 13% -> 14%
where the time goes in v9:
time: 167 us
  waiting for transfers between devices  54.3 us (33%)
  Pallas kernels  42.1 us (25%)
  starting transfers between devices  34.6 us (21%)
  local copies, waits for them, and re-layouts  16.7 us (10%)
  between operations  13.5 us (8%)
  other arithmetic  5.27 us (3%)
    ppermute x14, waiting for transfers between devices, flip(): lax.ppermute(block, axis, [(i, i ^ bits) for i in range(lax.axis_size(axi...  45.4 us
    pallas_call x3, Pallas kernels, run_kernel(): pl.pallas_call(functools.partial(quadratic_kernel, plan, m_dev, begin, mi...  38.2 us
    ppermute x14, starting transfers between devices, flip(): lax.ppermute(block, axis, [(i, i ^ bits) for i in range(lax.axis_size(axi...  24 us
    unnamed x22, local copies, waits for them, and re-layouts  7.14 us
    ppermute x1, waiting for transfers between devices, square_line(): c_rows = lax.ppermute(b_rows, 'ga', outward)  4.34 us
    ppermute x1, waiting for transfers between devices, square_line(): a_rows = lax.ppermute(after(own, given), 'ga', outer)  3.81 us
    slice x6, local copies, waits for them, and re-layouts, carried(): w[row, :6]  3.47 us
  transfers between devices with their start and end apart: 20, of which 13 were waited for; matrix products, arithmetic and copies ran while one was open for 8% of the time, Pallas kernels for 14%

profile of v9, /device:TPU:0, one launch (start us, length us, event | category | flops | bytes accessed | tf_op | source)
XLA Modules:
  0.0 166.5 jit_solution(62731346823486361)
XLA Ops:
  6.5 1.1 dynamic-slice_bitcast_fusion
  7.6 3.1 %collective-permute-start.2 = (bf16[512,512]{1,0:T(8,128)(2,1)S(1)}, bf16[512,512]{1,0:T(8,128)(2,1)S(1)}, u32[]{:S(2)}, u32[]{:S(2)}) collective-permute-start(bf16[512,512]{1,0:T(8,128)(2,1)S(1)} %dynamic-slice_bitcast_fusion), channel_id=1, source_target_pairs={{0,2},{2,0},{4,6},{6,4},{1,3},{3,1},{5,7},{7,5},{8,10},{10,8},{12,... | collective-permute-start | bytes 1572872 | tf_op jit(solution)/shard_map/ppermute | solution.py:244
  10.7 0.1 stack.86.where_ref
  10.8 2.2 %copy-done = bf16[2,2048,512]{2,1,0:T(8,128)(2,1)S(1)} copy-done((bf16[2,2048,512]{2,1,0:T(8,128)(2,1)S(1)}, bf16[2,2048,512]{2,1,0:T(8,128)(2,1)}, u32[]{:S(2)}) %copy-start) | copy-done | bytes 4194328
  13.0 0.7 copy-done.3
  13.6 0.7 copy-done.5
  14.3 1.8 %shard_map.64 = (bf16[1552,512]{1,0:T(8,128)(2,1)}, bf16[2,512,512]{2,1,0:T(8,128)(2,1)S(1)}) custom-call(s32[6]{0:T(128)S(1)} %stack.86.where_ref, f32[2]{0:T(128)S(1)} %copy-done.3, f32[2]{0:T(128)S(1)} %copy-done.5, bf16[2,2048,512]{2,1,0:T(8,128)(2,1)S(1)} %copy-done), custom_call_target="tpu_custom_call" | custom-call | bytes 2097152 | tf_op jit(solution)/shard_map/pallas_call | solution.py:255
  16.1 1.0 copy-done.6
  17.1 1.5 collective-permute-start
  18.6 1.5 collective-permute-start.1
  20.2 1.8 %collective-permute-start.4 = (bf16[1536,512]{1,0:T(8,128)(2,1)S(1)}, bf16[1536,512]{1,0:T(8,128)(2,1)}, u32[]{:S(2)}, u32[]{:S(2)}) collective-permute-start(bf16[1536,512]{1,0:T(8,128)(2,1)S(1)} %bitcast.31), channel_id=1, source_target_pairs={{2,4},{4,2},{3,5},{5,3},{10,12},{12,10},{11,13},{13,11},{18,20},{2... | collective-permute-start | bytes 4718600 | tf_op jit(solution)/shard_map/ppermute | solution.py:274
  22.0 0.7 collective-permute-done.2.block_ref
  22.6 2.7 %collective-permute-start.3 = (bf16[1536,512]{1,0:T(8,128)(2,1)S(1)}, bf16[1536,512]{1,0:T(8,128)(2,1)}, u32[]{:S(2)}, u32[]{:S(2)}) collective-permute-start(bf16[1536,512]{1,0:T(8,128)(2,1)S(1)} %bitcast.32), channel_id=1, source_target_pairs={{0,2},{2,0},{4,6},{6,4},{1,3},{3,1},{5,7},{7,5},{8,10},{10,8},{12,... | collective-permute-start | bytes 4718600 | tf_op jit(solution)/shard_map/ppermute | solution.py:275
  25.3 2.0 %shard_map.67 = bf16[512,512]{1,0:T(8,128)(2,1)} custom-call(bf16[512,512]{1,0:T(8,128)(2,1)} %copy-done.8), custom_call_target="tpu_custom_call" | custom-call | bytes 1048576 | tf_op jit(solution)/shard_map/pallas_call | solution.py:247
  27.3 26.3 %collective-permute-done.rest_1_.rest_4_ = bf16[1552,512]{1,0:T(8,128)(2,1)} collective-permute-done((bf16[1552,512]{1,0:T(8,128)(2,1)}, bf16[1552,512]{1,0:T(8,128)(2,1)}, u32[]{:S(2)}, u32[]{:S(2)}) %collective-permute-start) | collective-permute-done | bytes 1589280 | tf_op jit(solution)/shard_map/ppermute | solution.py:33
  53.7 1.2 collective-permute-done.1.rest_2_.rest_5_
  54.9 3.8 %collective-permute-done.3.a_ref = bf16[1536,512]{1,0:T(8,128)(2,1)} collective-permute-done((bf16[1536,512]{1,0:T(8,128)(2,1)S(1)}, bf16[1536,512]{1,0:T(8,128)(2,1)}, u32[]{:S(2)}, u32[]{:S(2)}) %collective-permute-start.3) | collective-permute-done | bytes 1572896 | tf_op jit(solution)/shard_map/ppermute | solution.py:275
  58.7 0.1 rev.3
  58.8 0.2 select_reduce_fusion
  59.0 0.8 broadcast_subtract_fusion
  59.8 1.3 collective-permute-start.9
  61.1 2.1 %slice.75 = bf16[784,512]{1,0:T(8,128)(2,1)} slice(bf16[1552,512]{1,0:T(8,128)(2,1)} %collective-permute-done.rest_1_.rest_4_), slice={[768:1552], [0:512]} | slice | bytes 1605632 | tf_op jit(solution)/shard_map/slice | solution.py:279
  63.2 1.1 collective-permute-start.6
  64.3 2.1 %slice.74 = bf16[768,512]{1,0:T(8,128)(2,1)} slice(bf16[1552,512]{1,0:T(8,128)(2,1)} %collective-permute-done.1.rest_2_.rest_5_), slice={[0:768], [0:512]} | slice | bytes 1572864 | tf_op jit(solution)/shard_map/slice | solution.py:278
  66.4 1.5 collective-permute-start.5
  67.9 0.7 slice_reduce_fusion.5
  68.6 0.7 slice_reduce_fusion.4
  69.3 0.1 stack.90
  69.3 0.1 stack.91
  69.4 0.1 copy.16
  69.5 1.8 %collective-permute-start.10 = (bf16[1536,512]{1,0:T(8,128)(2,1)}, bf16[1536,512]{1,0:T(8,128)(2,1)}, u32[]{:S(2)}, u32[]{:S(2)}) collective-permute-start(bf16[1536,512]{1,0:T(8,128)(2,1)} %collective-permute-done.3.a_ref), channel_id=1, source_target_pairs={{2,4},{4,2},{3,5},{5,3},{10,12},{12,10},{11,13},{13,11},{18,20},{2... | collective-permute-start | bytes 4718600 | tf_op jit(solution)/shard_map/ppermute | solution.py:301
  71.4 1.1 divide_multiply_fusion.1.k_ref
  72.6 10.1 %shard_map.65 = f32[8,8,256]{2,1,0:T(8,128)S(1)} custom-call(s32[6]{0:T(128)S(1)} %stack.86.where_ref, f32[4,192,256]{2,1,0:T(8,128)S(1)} %divide_multiply_fusion.1.k_ref, bf16[1536,512]{1,0:T(8,128)(2,1)S(1)} %bitcast.33, bf16[1536,512]{1,0:T(8,128)(2,1)} %collective-permute-done.3.a_ref, bf16[1536,512]{1,0:T(8,128)(2,1)} %collective-permute-done.4.b_ref, ...), custom_call_target="tpu_custom_call" | custom-call | flops 402653184 | bytes 524288 | tf_op jit(solution)/shard_map/pallas_call | solution.py:205
  82.7 8.9 %collective-permute-done.5.rest_2_ = bf16[768,512]{1,0:T(8,128)(2,1)} collective-permute-done((bf16[768,512]{1,0:T(8,128)(2,1)}, bf16[768,512]{1,0:T(8,128)(2,1)}, u32[]{:S(2)}, u32[]{:S(2)}) %collective-permute-start.5) | collective-permute-done | bytes 786464 | tf_op jit(solution)/shard_map/ppermute | solution.py:33
  91.5 0.5 collective-permute-start.8
  92.0 4.3 %collective-permute-done.9.rest_0_ = bf16[1536,512]{1,0:T(8,128)(2,1)} collective-permute-done((bf16[1536,512]{1,0:T(8,128)(2,1)}, bf16[1536,512]{1,0:T(8,128)(2,1)}, u32[]{:S(2)}, u32[]{:S(2)}) %collective-permute-start.9) | collective-permute-done | bytes 1572896 | tf_op jit(solution)/shard_map/ppermute | solution.py:300
  96.4 0.1 concatenate.13.where_ref
  96.5 0.1 stack.110
  96.6 0.5 collective-permute-start.12
  97.1 0.7 slice_reduce_fusion.3
  97.8 0.1 stack.108
  98.0 0.7 slice_reduce_fusion.2
  98.6 0.1 stack.109
  98.7 1.9 %collective-permute-done.11.rest_5_.rest_9_ = bf16[784,512]{1,0:T(8,128)(2,1)} collective-permute-done((bf16[784,512]{1,0:T(8,128)(2,1)S(1)}, bf16[784,512]{1,0:T(8,128)(2,1)}, u32[]{:S(2)}, u32[]{:S(2)}) %collective-permute-start.11) | collective-permute-done | bytes 802848 | tf_op jit(solution)/shard_map/ppermute | solution.py:33
  100.6 0.7 slice_reduce_fusion
  101.3 0.1 stack.111
  101.4 0.1 maximum_convert_fusion
  101.5 1.1 divide_multiply_fusion.k_ref
  102.6 10.1 %shard_map.66 = f32[8,8,256]{2,1,0:T(8,128)S(1)} custom-call(s32[6]{0:T(128)S(1)} %stack.86.where_ref, f32[4,192,256]{2,1,0:T(8,128)S(1)} %divide_multiply_fusion.k_ref, bf16[1536,512]{1,0:T(8,128)(2,1)S(1)} %bitcast.34, bf16[1536,512]{1,0:T(8,128)(2,1)} %collective-permute-done.3.a_ref, bf16[1536,512]{1,0:T(8,128)(2,1)} %collective-permute-done.4.b_ref, ...), custom_call_target="tpu_custom_call" | custom-call | flops 402653184 | bytes 524288 | tf_op jit(solution)/shard_map/pallas_call | solution.py:205
  112.7 1.3 pad_maximum_fusion.k_ref
  114.0 1.4 copy-done.2
  115.4 1.2 copy-done.7
  116.6 18.0 %shard_map.68 = f32[8,8,256]{2,1,0:T(8,128)S(1)} custom-call(s32[14]{0:T(128)S(1)} %concatenate.13.where_ref, f32[8,192,256]{2,1,0:T(8,128)S(1)} %copy-done.2, bf16[1536,512]{1,0:T(8,128)(2,1)S(1)} %bitcast.35, bf16[1536,512]{1,0:T(8,128)(2,1)} %collective-permute-done.3.a_ref, bf16[1536,512]{1,0:T(8,128)(2,1)} %collective-permute-done.4.b_ref, ...), custom_call_target="tpu_custom_call" | custom-call | flops 12884901888 | bytes 524288 | tf_op jit(solution)/shard_map/pallas_call | solution.py:205
  134.7 2.3 %collective-permute-start.13 = (f32[8,256]{1,0:T(8,128)S(1)}, f32[8,256]{1,0:T(8,128)S(1)}, u32[]{:S(2)}, u32[]{:S(2)}) collective-permute-start(f32[8,256]{1,0:T(8,128)S(1)} %add_reduce_fusion), channel_id=1, source_target_pairs={{0,8},{8,0},{16,24},{24,16},{1,9},{9,1},{17,25},{25,17},{2,10},{10... | collective-permute-start | bytes 24584 | tf_op jit(solution)/shard_map/ppermute | solution.py:33
  137.0 1.5 collective-permute-start.15
  138.6 0.1 collective-permute-done.13
  138.7 2.1 %collective-permute-done.14 = f32[8,256]{1,0:T(8,128)S(1)} collective-permute-done((f32[8,256]{1,0:T(8,128)S(1)}, f32[8,256]{1,0:T(8,128)S(1)}, u32[]{:S(2)}, u32[]{:S(2)}) %collective-permute-start.14) | collective-permute-done | bytes 8224 | tf_op jit(solution)/shard_map/ppermute | solution.py:33
  140.7 0.9 collective-permute-done.15
  141.6 10.8 %collective-permute-start.16 = (f32[8,256]{1,0:T(8,128)S(1)}, f32[8,256]{1,0:T(8,128)S(1)}, u32[]{:S(2)}, u32[]{:S(2)}) collective-permute-start(f32[8,256]{1,0:T(8,128)S(1)} %add_add_fusion.1), channel_id=1, source_target_pairs={{0,2},{2,0},{4,6},{6,4},{1,3},{3,1},{5,7},{7,5},{8,10},{10,8},{12,... | collective-permute-start | bytes 24584 | tf_op jit(solution)/shard_map/ppermute | solution.py:33
  152.4 1.2 collective-permute-start.17
  153.6 1.4 collective-permute-start.18
  155.0 1.9 %collective-permute-done.17 = f32[8,256]{1,0:T(8,128)S(1)} collective-permute-done((f32[8,256]{1,0:T(8,128)S(1)}, f32[8,256]{1,0:T(8,128)S(1)}, u32[]{:S(2)}, u32[]{:S(2)}) %collective-permute-start.17) | collective-permute-done | bytes 8224 | tf_op jit(solution)/shard_map/ppermute | solution.py:33
  156.9 2.1 %collective-permute-done.18 = f32[8,256]{1,0:T(8,128)S(1)} collective-permute-done((f32[8,256]{1,0:T(8,128)S(1)}, f32[8,256]{1,0:T(8,128)S(1)}, u32[]{:S(2)}, u32[]{:S(2)}) %collective-permute-start.18) | collective-permute-done | bytes 8224 | tf_op jit(solution)/shard_map/ppermute | solution.py:33
  159.1 0.6 add_add_fusion
  (40 shorter events, 0.3 us)
Async XLA Ops:
  6.5 107.4 %all-gather.3.cloned.1.call-start = ((), (), s32[]{:S(2)}) async-start(), calls=%async_computation | async-start | bytes 4718592 | tf_op jit(solution)/shard_map/all_gather | solution.py:277
  7.6 15.0 %collective-permute-start.2 = (bf16[512,512]{1,0:T(8,128)(2,1)S(1)}, bf16[512,512]{1,0:T(8,128)(2,1)S(1)}, u32[]{:S(2)}, u32[]{:S(2)}) collective-permute-start(bf16[512,512]{1,0:T(8,128)(2,1)S(1)} %dynamic-slice_bitcast_fusion), channel_id=1, source_target_pairs={{0,2},{2,0},{4,6},{6,4},{1,3},{3,1},{5,7},{7,5},{8,10},{10,8},{12,... | collective-permute-start | bytes 1572872 | tf_op jit(solution)/shard_map/ppermute | solution.py:244
  10.8 2.2 %copy-start = (bf16[2,2048,512]{2,1,0:T(8,128)(2,1)S(1)}, bf16[2,2048,512]{2,1,0:T(8,128)(2,1)}, u32[]{:S(2)}) copy-start(bf16[2,2048,512]{2,1,0:T(8,128)(2,1)} %rest_0_.1) | copy-start | bytes 12582916
  13.0 0.7 copy-start.3
  13.6 0.7 copy-start.5
  14.3 5.9 %copy-start.1 = (bf16[8,192,512]{2,1,0:T(8,128)(2,1)S(1)}, bf16[8,192,512]{2,1,0:T(8,128)(2,1)}, u32[]{:S(2)}) copy-start(bf16[8,192,512]{2,1,0:T(8,128)(2,1)} %param.6) | copy-start | bytes 4718596
  14.3 44.4 %copy-start.4 = (f32[2]{0:T(128)S(1)}, f32[2]{0:T(128)}, u32[]{:S(2)}) copy-start(f32[2]{0:T(128)} %nu_ref.1) | copy-start | bytes 28
  16.1 1.0 copy-start.6
  17.1 41.7 %copy-start.9 = (f32[256]{0:T(256)S(1)}, f32[256]{0:T(256)}, u32[]{:S(2)}) copy-start(f32[256]{0:T(256)} %param.10) | copy-start | bytes 3076
  17.1 41.7 %copy-start.10 = (s32[192]{0:T(256)S(1)}, s32[192]{0:T(256)}, u32[]{:S(2)}) copy-start(s32[192]{0:T(256)} %param.11) | copy-start | bytes 2308
  17.1 36.5 %collective-permute-start = (bf16[1552,512]{1,0:T(8,128)(2,1)}, bf16[1552,512]{1,0:T(8,128)(2,1)}, u32[]{:S(2)}, u32[]{:S(2)}) collective-permute-start(bf16[1552,512]{1,0:T(8,128)(2,1)} %get-tuple-element.13), channel_id=1, source_target_pairs={{0,8},{8,0},{16,24},{24,16},{1,9},{9,1},{17,25},{25,17},{2,10},{10... | collective-permute-start | bytes 4767752 | tf_op jit(solution)/shard_map/ppermute | solution.py:33
  18.6 36.2 %collective-permute-start.1 = (bf16[1552,512]{1,0:T(8,128)(2,1)}, bf16[1552,512]{1,0:T(8,128)(2,1)}, u32[]{:S(2)}, u32[]{:S(2)}) collective-permute-start(bf16[1552,512]{1,0:T(8,128)(2,1)} %get-tuple-element.13), channel_id=1, source_target_pairs={{0,16},{8,24},{16,0},{24,8},{1,17},{9,25},{17,1},{25,9},{2,18},{10... | collective-permute-start | bytes 4767752 | tf_op jit(solution)/shard_map/ppermute | solution.py:33
  20.2 7.2 %collective-permute-start.4 = (bf16[1536,512]{1,0:T(8,128)(2,1)S(1)}, bf16[1536,512]{1,0:T(8,128)(2,1)}, u32[]{:S(2)}, u32[]{:S(2)}) collective-permute-start(bf16[1536,512]{1,0:T(8,128)(2,1)S(1)} %bitcast.31), channel_id=1, source_target_pairs={{2,4},{4,2},{3,5},{5,3},{10,12},{12,10},{11,13},{13,11},{18,20},{2... | collective-permute-start | bytes 4718600 | tf_op jit(solution)/shard_map/ppermute | solution.py:274
  22.6 2.7 %copy-start.8 = (bf16[512,512]{1,0:T(8,128)(2,1)}, bf16[512,512]{1,0:T(8,128)(2,1)S(1)}, u32[]{:S(2)}) copy-start(bf16[512,512]{1,0:T(8,128)(2,1)S(1)} %collective-permute-done.2.block_ref) | copy-start | bytes 1572868
  22.6 36.0 %collective-permute-start.3 = (bf16[1536,512]{1,0:T(8,128)(2,1)S(1)}, bf16[1536,512]{1,0:T(8,128)(2,1)}, u32[]{:S(2)}, u32[]{:S(2)}) collective-permute-start(bf16[1536,512]{1,0:T(8,128)(2,1)S(1)} %bitcast.32), channel_id=1, source_target_pairs={{0,2},{2,0},{4,6},{6,4},{1,3},{3,1},{5,7},{7,5},{8,10},{10,8},{12,... | collective-permute-start | bytes 4718600 | tf_op jit(solution)/shard_map/ppermute | solution.py:275
  59.8 36.6 %collective-permute-start.9 = (bf16[1536,512]{1,0:T(8,128)(2,1)}, bf16[1536,512]{1,0:T(8,128)(2,1)}, u32[]{:S(2)}, u32[]{:S(2)}) collective-permute-start(bf16[1536,512]{1,0:T(8,128)(2,1)} %collective-permute-done.4.b_ref), channel_id=1, source_target_pairs={{2,0},{4,6},{3,1},{5,7},{10,8},{12,14},{11,9},{13,15},{18,16},{20,... | collective-permute-start | bytes 4718600 | tf_op jit(solution)/shard_map/ppermute | solution.py:300
  63.2 28.3 %collective-permute-start.6 = (bf16[784,512]{1,0:T(8,128)(2,1)}, bf16[784,512]{1,0:T(8,128)(2,1)S(1)}, u32[]{:S(2)}, u32[]{:S(2)}) collective-permute-start(bf16[784,512]{1,0:T(8,128)(2,1)} %slice.75), channel_id=1, source_target_pairs={{0,16},{8,24},{16,0},{24,8},{1,17},{9,25},{17,1},{25,9},{2,18},{10... | collective-permute-start | bytes 2408456 | tf_op jit(solution)/shard_map/ppermute | solution.py:33
  66.4 25.1 %collective-permute-start.5 = (bf16[768,512]{1,0:T(8,128)(2,1)}, bf16[768,512]{1,0:T(8,128)(2,1)}, u32[]{:S(2)}, u32[]{:S(2)}) collective-permute-start(bf16[768,512]{1,0:T(8,128)(2,1)} %slice.74), channel_id=1, source_target_pairs={{0,8},{8,0},{16,24},{24,16},{1,9},{9,1},{17,25},{25,17},{2,10},{10... | collective-permute-start | bytes 2359304 | tf_op jit(solution)/shard_map/ppermute | solution.py:33
  69.5 26.8 %collective-permute-start.10 = (bf16[1536,512]{1,0:T(8,128)(2,1)}, bf16[1536,512]{1,0:T(8,128)(2,1)}, u32[]{:S(2)}, u32[]{:S(2)}) collective-permute-start(bf16[1536,512]{1,0:T(8,128)(2,1)} %collective-permute-done.3.a_ref), channel_id=1, source_target_pairs={{2,4},{4,2},{3,5},{5,3},{10,12},{12,10},{11,13},{13,11},{18,20},{2... | collective-permute-start | bytes 4718600 | tf_op jit(solution)/shard_map/ppermute | solution.py:301
  91.5 5.6 %collective-permute-start.7 = (bf16[1552,512]{1,0:T(8,128)(2,1)}, bf16[1552,512]{1,0:T(8,128)(2,1)}, u32[]{:S(2)}, u32[]{:S(2)}) collective-permute-start(bf16[1552,512]{1,0:T(8,128)(2,1)} %collective-permute-done.rest_1_.rest_4_), channel_id=1, source_target_pairs={{0,1},{1,0},{2,3},{3,2},{4,5},{5,4},{6,7},{7,6},{8,9},{9,8},{10,11... | collective-permute-start | bytes 4767752 | tf_op jit(solution)/shard_map/ppermute | solution.py:33
  91.5 6.4 %collective-permute-start.8 = (bf16[1552,512]{1,0:T(8,128)(2,1)}, bf16[1552,512]{1,0:T(8,128)(2,1)}, u32[]{:S(2)}, u32[]{:S(2)}) collective-permute-start(bf16[1552,512]{1,0:T(8,128)(2,1)} %collective-permute-done.1.rest_2_.rest_5_), channel_id=1, source_target_pairs={{0,1},{1,0},{2,3},{3,2},{4,5},{5,4},{6,7},{7,6},{8,9},{9,8},{10,11... | collective-permute-start | bytes 4767752 | tf_op jit(solution)/shard_map/ppermute | solution.py:33
  96.4 4.2 %collective-permute-start.11 = (bf16[784,512]{1,0:T(8,128)(2,1)S(1)}, bf16[784,512]{1,0:T(8,128)(2,1)}, u32[]{:S(2)}, u32[]{:S(2)}) collective-permute-start(bf16[784,512]{1,0:T(8,128)(2,1)S(1)} %collective-permute-done.6.rest_3_.rest_8_), channel_id=1, source_target_pairs={{0,1},{1,0},{2,3},{3,2},{4,5},{5,4},{6,7},{7,6},{8,9},{9,8},{10,11... | collective-permute-start | bytes 2408456 | tf_op jit(solution)/shard_map/ppermute | solution.py:33
  96.6 6.0 %collective-permute-start.12 = (bf16[768,512]{1,0:T(8,128)(2,1)}, bf16[768,512]{1,0:T(8,128)(2,1)}, u32[]{:S(2)}, u32[]{:S(2)}) collective-permute-start(bf16[768,512]{1,0:T(8,128)(2,1)} %collective-permute-done.5.rest_2_), channel_id=1, source_target_pairs={{0,1},{1,0},{2,3},{3,2},{4,5},{5,4},{6,7},{7,6},{8,9},{9,8},{10,11... | collective-permute-start | bytes 2359304 | tf_op jit(solution)/shard_map/ppermute | solution.py:33
  114.0 1.4 copy-start.2
  115.4 1.2 copy-start.7
  134.7 4.0 %collective-permute-start.13 = (f32[8,256]{1,0:T(8,128)S(1)}, f32[8,256]{1,0:T(8,128)S(1)}, u32[]{:S(2)}, u32[]{:S(2)}) collective-permute-start(f32[8,256]{1,0:T(8,128)S(1)} %add_reduce_fusion), channel_id=1, source_target_pairs={{0,8},{8,0},{16,24},{24,16},{1,9},{9,1},{17,25},{25,17},{2,10},{10... | collective-permute-start | bytes 24584 | tf_op jit(solution)/shard_map/ppermute | solution.py:33
  137.0 3.7 %collective-permute-start.14 = (f32[8,256]{1,0:T(8,128)S(1)}, f32[8,256]{1,0:T(8,128)S(1)}, u32[]{:S(2)}, u32[]{:S(2)}) collective-permute-start(f32[8,256]{1,0:T(8,128)S(1)} %add_reduce_fusion), channel_id=1, source_target_pairs={{0,16},{8,24},{16,0},{24,8},{1,17},{9,25},{17,1},{25,9},{2,18},{10... | collective-permute-start | bytes 24584 | tf_op jit(solution)/shard_map/ppermute | solution.py:33
  137.0 4.5 %collective-permute-start.15 = (f32[8,256]{1,0:T(8,128)S(1)}, f32[8,256]{1,0:T(8,128)S(1)}, u32[]{:S(2)}, u32[]{:S(2)}) collective-permute-start(f32[8,256]{1,0:T(8,128)S(1)} %add_reduce_fusion), channel_id=1, source_target_pairs={{0,24},{8,16},{16,8},{24,0},{1,25},{9,17},{17,9},{25,1},{2,26},{10... | collective-permute-start | bytes 24584 | tf_op jit(solution)/shard_map/ppermute | solution.py:33
  141.6 13.5 %collective-permute-start.16 = (f32[8,256]{1,0:T(8,128)S(1)}, f32[8,256]{1,0:T(8,128)S(1)}, u32[]{:S(2)}, u32[]{:S(2)}) collective-permute-start(f32[8,256]{1,0:T(8,128)S(1)} %add_add_fusion.1), channel_id=1, source_target_pairs={{0,2},{2,0},{4,6},{6,4},{1,3},{3,1},{5,7},{7,5},{8,10},{10,8},{12,... | collective-permute-start | bytes 24584 | tf_op jit(solution)/shard_map/ppermute | solution.py:33
  152.4 4.5 %collective-permute-start.17 = (f32[8,256]{1,0:T(8,128)S(1)}, f32[8,256]{1,0:T(8,128)S(1)}, u32[]{:S(2)}, u32[]{:S(2)}) collective-permute-start(f32[8,256]{1,0:T(8,128)S(1)} %add_add_fusion.1), channel_id=1, source_target_pairs={{0,4},{2,6},{4,0},{6,2},{1,5},{3,7},{5,1},{7,3},{8,12},{10,14},{12... | collective-permute-start | bytes 24584 | tf_op jit(solution)/shard_map/ppermute | solution.py:33
  153.6 5.4 %collective-permute-start.18 = (f32[8,256]{1,0:T(8,128)S(1)}, f32[8,256]{1,0:T(8,128)S(1)}, u32[]{:S(2)}, u32[]{:S(2)}) collective-permute-start(f32[8,256]{1,0:T(8,128)S(1)} %add_add_fusion.1), channel_id=1, source_target_pairs={{0,6},{2,4},{4,2},{6,0},{1,7},{3,5},{5,3},{7,1},{8,14},{10,12},{12... | collective-permute-start | bytes 24584 | tf_op jit(solution)/shard_map/ppermute | solution.py:33
Sparse Core Ops, SparseCore 0:
  58.8 43.4 all-gather.2

commit v10 on v9

--- a/solution.py
+++ b/solution.py
@@ -93,12 +93,11 @@
         at += count
 
 
-def quadratic_kernel(plan, m_dev, begin, tile, kind, where_ref, k_ref, own_ref, a_ref, b_ref, *rest):
+def quadratic_kernel(plan, m_dev, skip, tile, kind, where_ref, k_ref, own_ref, a_ref, b_ref, *rest):
     refs = rest[: len(rest) - 7]
     out_ref, left, right, w_all, k_all, sems, w_sems = rest[len(rest) - 7 :]
     n_slots, _, panel = w_all.shape
     end, low = where_ref[0], where_ref[1]
-    own_ref, a_ref = (r.at[begin : begin + right.shape[0], :] for r in (own_ref, a_ref))
     if kind == "near":
         w_refs = refs
         here = left.at[:, pl.ds(pl.multiple_of((1 - low) * panel, panel), panel)]
@@ -117,7 +116,7 @@
         sem = sems.at[len(fixed) + n]
         waits.append(pltpu.make_async_copy(yes, dst, sem))
         choose(end, waits[-1], pltpu.make_async_copy(no, dst, sem))
-    waits.append(pltpu.make_async_copy(k_ref, k_all, sems.at[5]))
+    waits.append(pltpu.make_async_copy(k_ref.at[skip : skip + n_slots], k_all, sems.at[5]))
     waits[-1].start()
     for slot in range(1, n_slots):
         start_slot(plan, slot, where_ref, w_refs, w_all, w_sems)
@@ -190,20 +189,20 @@
     out_ref[...] = block_ref[...].T
 
 
-def run_kernel(kind, plan, where, k_part, mats, arrays, m_dev, begin=0):
+def run_kernel(kind, plan, where, k_part, mats, arrays, m_dev, skip=0):
     n_rows, panel = mats[0].shape
-    n_slots, depth = k_part.shape[0], 2 * panel
+    n_slots, depth = len(plan), 2 * panel
     scratch = [
         pltpu.VMEM((n_rows, depth), jnp.bfloat16),
         pltpu.VMEM((n_rows, panel), jnp.bfloat16),
         pltpu.VMEM((n_slots, depth, panel), jnp.bfloat16),
-        pltpu.VMEM(k_part.shape, jnp.float32),
+        pltpu.VMEM((n_slots, *k_part.shape[1:]), jnp.float32),
         pltpu.SemaphoreType.DMA((6,)),
         pltpu.SemaphoreType.DMA((n_slots,)),
     ]
     flops = 2 * n_rows * depth * panel * n_slots // (16 if kind == "near" else 1)
     return pl.pallas_call(
-        functools.partial(quadratic_kernel, plan, m_dev, begin, min(n_rows, 4 * m_dev), kind),
+        functools.partial(quadratic_kernel, plan, m_dev, skip, min(n_rows, 4 * m_dev), kind),
         out_shape=jax.ShapeDtypeStruct((n_rows // m_dev, 8, NW), jnp.float32),
         in_specs=[pl.BlockSpec(memory_space=pltpu.SMEM)]
         + [pl.BlockSpec(memory_space=pl.ANY)] * (1 + len(mats) + len(arrays)),
@@ -294,7 +293,8 @@
     panels = (own, a_rows, b_rows)
     slots = [[(0, ("at", 3 + s), ("at", 2), whole)] for s in range(2)]
     slots += [[(r, None, 0, whole)] for r in (1, 2)]
-    k_here = weigh(jnp.concatenate([mine, carried((x1, 3 * panel), (y1, 3 * panel))]))
+    here = jnp.concatenate([mine, carried((x1, 3 * panel), (y1, 3 * panel))])
+    k_here = weigh(here)
     near = run_kernel("near", slots, where, k_here, panels, (screened, x1, y1), m_dev)
 
     c_rows = lax.ppermute(b_rows, "ga", outward)
@@ -303,9 +303,9 @@
     d1a_o, d1b_o = share(after(d1a, c_rows, d_rows)), share(after(d1b, c_rows, d_rows))
     slots = [[(r, None, 0, whole)] for r in (0, 1)]
     slots += [[(r, None, 0, cut), (r + 1, None, 0, whole - cut)] for r in (2, 4)]
-    k_there = weigh(carried((x1_o, 3 * panel), (y1_o, 3 * panel), (d1b, cut), (d1b_o, cut)))
-    corner = run_kernel("near", slots, where, k_there, panels, (x1_o, y1_o, d1a, d1b, d1a_o, d1b_o), m_dev)
-    k_all = jnp.concatenate([k_here, k_there])
+    there = carried((x1_o, 3 * panel), (y1_o, 3 * panel), (d1b, cut), (d1b_o, cut))
+    k_all = weigh(jnp.concatenate([here, there]))
+    corner = run_kernel("near", slots, where, k_all, panels, (x1_o, y1_o, d1a, d1b, d1a_o, d1b_o), m_dev, 4)
 
     square = lax.axis_index("freq")
     order = ((0, core), (0, 1 - core), (1, core), (2, core), (1, 1 - core), (2, 1 - core), (3, core), (3, 1 - core))

time: 167 us -> 169 us (1.012)
    unnamed x22 -> x30, local copies, waits for them, and re-layouts: 7.14 us -> 7.76 us
  transfers between devices with their start and end apart: 20 -> 20, of which waited for: 13 -> 12; matrix products, arithmetic and copies ran while one was open for 8% -> 7% of each run, Pallas kernels for 14% -> 15%
where the time goes in v10:
time: 169 us; the launch traced here: 168 us
  waiting for transfers between devices  54.4 us (32%)
  Pallas kernels  43.2 us (26%)
  starting transfers between devices  34.4 us (20%)
  local copies, waits for them, and re-layouts  18.1 us (11%)
  between operations  13.6 us (8%)
  other arithmetic  4.28 us (3%)
    ppermute x14, waiting for transfers between devices, flip(): lax.ppermute(block, axis, [(i, i ^ bits) for i in range(lax.axis_size(axi...  44.4 us
    pallas_call x3, Pallas kernels, run_kernel(): pl.pallas_call(functools.partial(quadratic_kernel, plan, m_dev, skip, min...  39.4 us
    ppermute x14, starting transfers between devices, flip(): lax.ppermute(block, axis, [(i, i ^ bits) for i in range(lax.axis_size(axi...  25.1 us
    unnamed x30, local copies, waits for them, and re-layouts  7.76 us
    ppermute x1, waiting for transfers between devices, square_line(): c_rows = lax.ppermute(b_rows, 'ga', outward)  4.2 us
    ppermute x1, waiting for transfers between devices, square_line(): a_rows = lax.ppermute(after(own, given), 'ga', outer)  3.79 us
  transfers between devices with their start and end apart: 20, of which 12 were waited for; matrix products, arithmetic and copies ran while one was open for 7% of the time, Pallas kernels for 15%

profile of v10, /device:TPU:0, one launch (start us, length us, event | category | flops | bytes accessed | tf_op | source)
XLA Modules:
  0.0 168.1 jit_solution(13016469200577924632)
XLA Ops:
  6.5 1.9 %dynamic-slice_bitcast_fusion = bf16[512,512]{1,0:T(8,128)(2,1)} fusion(bf16[2,2048,512]{2,1,0:T(8,128)(2,1)} %rest_0_.1, s32[]{:T(128)S(6)} %select_n.46, s32[]{:T(128)S(6)} %select_n.49), kind=kLoop, calls=%fused_computation.2 | loop fusion | bytes 1048584 | tf_op jit(solution)/shard_map/squeeze | solution.py:238
  8.4 3.0 %collective-permute-start.2 = (bf16[512,512]{1,0:T(8,128)(2,1)}, bf16[512,512]{1,0:T(8,128)(2,1)}, u32[]{:S(2)}, u32[]{:S(2)}) collective-permute-start(bf16[512,512]{1,0:T(8,128)(2,1)} %dynamic-slice_bitcast_fusion), channel_id=1, source_target_pairs={{0,2},{2,0},{4,6},{6,4},{1,3},{3,1},{5,7},{7,5},{8,10},{10,8},{12,... | collective-permute-start | bytes 1572872 | tf_op jit(solution)/shard_map/ppermute | solution.py:243
  11.4 0.1 stack.86.where_ref
  11.5 2.2 %copy-done = bf16[2,2048,512]{2,1,0:T(8,128)(2,1)S(1)} copy-done((bf16[2,2048,512]{2,1,0:T(8,128)(2,1)S(1)}, bf16[2,2048,512]{2,1,0:T(8,128)(2,1)}, u32[]{:S(2)}) %copy-start) | copy-done | bytes 4194328
  13.7 0.7 copy-done.7
  14.4 0.7 copy-done.9
  15.0 1.9 %shard_map.64 = (bf16[1552,512]{1,0:T(8,128)(2,1)}, bf16[2,512,512]{2,1,0:T(8,128)(2,1)S(1)}) custom-call(s32[6]{0:T(128)S(1)} %stack.86.where_ref, f32[2]{0:T(128)S(1)} %copy-done.7, f32[2]{0:T(128)S(1)} %copy-done.9, bf16[2,2048,512]{2,1,0:T(8,128)(2,1)S(1)} %copy-done), custom_call_target="tpu_custom_call" | custom-call | bytes 2097152 | tf_op jit(solution)/shard_map/pallas_call | solution.py:254
  16.9 1.0 copy-done.11
  17.9 1.6 collective-permute-start
  19.4 1.5 collective-permute-start.1
  21.0 0.8 collective-permute-start.4
  21.7 2.0 %collective-permute-done.2.block_ref = bf16[512,512]{1,0:T(8,128)(2,1)} collective-permute-done((bf16[512,512]{1,0:T(8,128)(2,1)}, bf16[512,512]{1,0:T(8,128)(2,1)}, u32[]{:S(2)}, u32[]{:S(2)}) %collective-permute-start.2) | collective-permute-done | bytes 524320 | tf_op jit(solution)/shard_map/ppermute | solution.py:243
  23.7 2.4 %collective-permute-start.3 = (bf16[1536,512]{1,0:T(8,128)(2,1)S(1)}, bf16[1536,512]{1,0:T(8,128)(2,1)}, u32[]{:S(2)}, u32[]{:S(2)}) collective-permute-start(bf16[1536,512]{1,0:T(8,128)(2,1)S(1)} %bitcast.33), channel_id=1, source_target_pairs={{0,2},{2,0},{4,6},{6,4},{1,3},{3,1},{5,7},{7,5},{8,10},{10,8},{12,... | collective-permute-start | bytes 4718600 | tf_op jit(solution)/shard_map/ppermute | solution.py:274
  26.1 2.0 %shard_map.67 = bf16[512,512]{1,0:T(8,128)(2,1)} custom-call(bf16[512,512]{1,0:T(8,128)(2,1)} %collective-permute-done.2.block_ref), custom_call_target="tpu_custom_call" | custom-call | bytes 1048576 | tf_op jit(solution)/shard_map/pallas_call | solution.py:246
  28.1 26.3 %collective-permute-done.rest_1_.rest_4_ = bf16[1552,512]{1,0:T(8,128)(2,1)} collective-permute-done((bf16[1552,512]{1,0:T(8,128)(2,1)}, bf16[1552,512]{1,0:T(8,128)(2,1)}, u32[]{:S(2)}, u32[]{:S(2)}) %collective-permute-start) | collective-permute-done | bytes 1589280 | tf_op jit(solution)/shard_map/ppermute | solution.py:33
  54.5 1.2 collective-permute-done.1.rest_2_.rest_5_
  55.7 3.8 %collective-permute-done.3.a_ref = bf16[1536,512]{1,0:T(8,128)(2,1)} collective-permute-done((bf16[1536,512]{1,0:T(8,128)(2,1)S(1)}, bf16[1536,512]{1,0:T(8,128)(2,1)}, u32[]{:S(2)}, u32[]{:S(2)}) %collective-permute-start.3) | collective-permute-done | bytes 1572896 | tf_op jit(solution)/shard_map/ppermute | solution.py:274
  59.5 0.1 rev.3
  59.7 0.2 select_reduce_fusion
  59.9 0.8 broadcast_subtract_fusion
  60.6 1.3 collective-permute-start.9
  61.9 2.1 %slice.75 = bf16[784,512]{1,0:T(8,128)(2,1)} slice(bf16[1552,512]{1,0:T(8,128)(2,1)} %collective-permute-done.rest_1_.rest_4_), slice={[768:1552], [0:512]} | slice | bytes 1605632 | tf_op jit(solution)/shard_map/slice | solution.py:278
  64.0 1.3 collective-permute-start.6
  65.3 2.1 %slice.74 = bf16[768,512]{1,0:T(8,128)(2,1)} slice(bf16[1552,512]{1,0:T(8,128)(2,1)} %collective-permute-done.1.rest_2_.rest_5_), slice={[0:768], [0:512]} | slice | bytes 1572864 | tf_op jit(solution)/shard_map/slice | solution.py:277
  67.4 1.5 collective-permute-start.5
  68.9 0.7 slice_reduce_fusion.5
  69.6 0.7 slice_reduce_fusion.4
  70.2 0.1 stack.90
  70.3 0.1 stack.91
  70.4 0.1 copy.19
  70.5 1.8 %collective-permute-start.10 = (bf16[1536,512]{1,0:T(8,128)(2,1)}, bf16[1536,512]{1,0:T(8,128)(2,1)}, u32[]{:S(2)}, u32[]{:S(2)}) collective-permute-start(bf16[1536,512]{1,0:T(8,128)(2,1)} %collective-permute-done.3.a_ref), channel_id=1, source_target_pairs={{2,4},{4,2},{3,5},{5,3},{10,12},{12,10},{11,13},{13,11},{18,20},{2... | collective-permute-start | bytes 4718600 | tf_op jit(solution)/shard_map/ppermute | solution.py:301
  72.4 1.1 divide_multiply_fusion.1.k_ref
  73.5 10.0 %shard_map.65 = f32[8,8,256]{2,1,0:T(8,128)S(1)} custom-call(s32[6]{0:T(128)S(1)} %stack.86.where_ref, f32[4,192,256]{2,1,0:T(8,128)S(1)} %divide_multiply_fusion.1.k_ref, bf16[1536,512]{1,0:T(8,128)(2,1)S(1)} %bitcast.34, bf16[1536,512]{1,0:T(8,128)(2,1)} %collective-permute-done.3.a_ref, bf16[1536,512]{1,0:T(8,128)(2,1)S(1)} %collective-permute-done.4.b_ref, ...), custom_call_target="tpu_custom_call" | custom-call | flops 402653184 | bytes 524288 | tf_op jit(solution)/shard_map/pallas_call | solution.py:204
  83.5 8.8 %collective-permute-done.5.rest_2_ = bf16[768,512]{1,0:T(8,128)(2,1)} collective-permute-done((bf16[768,512]{1,0:T(8,128)(2,1)}, bf16[768,512]{1,0:T(8,128)(2,1)}, u32[]{:S(2)}, u32[]{:S(2)}) %collective-permute-start.5) | collective-permute-done | bytes 786464 | tf_op jit(solution)/shard_map/ppermute | solution.py:33
  92.3 0.5 collective-permute-start.8
  92.8 4.2 %collective-permute-done.9.rest_0_ = bf16[1536,512]{1,0:T(8,128)(2,1)} collective-permute-done((bf16[1536,512]{1,0:T(8,128)(2,1)S(1)}, bf16[1536,512]{1,0:T(8,128)(2,1)}, u32[]{:S(2)}, u32[]{:S(2)}) %collective-permute-start.9) | collective-permute-done | bytes 1572896 | tf_op jit(solution)/shard_map/ppermute | solution.py:300
  97.0 0.1 concatenate.15.where_ref
  97.1 0.7 slice_reduce_fusion.1
  97.8 0.1 stack.110
  97.9 0.5 collective-permute-start.12
  98.4 0.6 slice_reduce_fusion.3
  99.0 0.1 stack.108
  99.1 0.6 slice_reduce_fusion.2
  99.8 0.1 stack.109
  99.9 1.1 collective-permute-done.11.rest_5_.rest_9_
  100.9 0.9 copy-done.4
  101.8 0.1 stack.111
  101.9 0.1 maximum_convert_fusion
  102.1 1.3 divide_multiply_fusion.k_ref
  103.4 11.7 %shard_map.66 = f32[8,8,256]{2,1,0:T(8,128)S(1)} custom-call(s32[6]{0:T(128)S(1)} %stack.86.where_ref, f32[8,192,256]{2,1,0:T(8,128)S(1)} %divide_multiply_fusion.k_ref, bf16[1536,512]{1,0:T(8,128)(2,1)} %bitcast.31, bf16[1536,512]{1,0:T(8,128)(2,1)} %collective-permute-done.3.a_ref, bf16[1536,512]{1,0:T(8,128)(2,1)} %copy-done.3, ...), custom_call_target="tpu_custom_call" | custom-call | flops 402653184 | bytes 524288 | tf_op jit(solution)/shard_map/pallas_call | solution.py:204
  115.2 1.1 copy-done.6
  116.3 1.2 copy-done.12
  117.5 17.7 %shard_map.68 = f32[8,8,256]{2,1,0:T(8,128)S(1)} custom-call(s32[14]{0:T(128)S(1)} %concatenate.15.where_ref, f32[8,192,256]{2,1,0:T(8,128)S(1)} %divide_multiply_fusion.k_ref, bf16[1536,512]{1,0:T(8,128)(2,1)S(1)} %bitcast.35, bf16[1536,512]{1,0:T(8,128)(2,1)} %collective-permute-done.3.a_ref, bf16[1536,512]{1,0:T(8,128)(2,1)} %copy-done.3, ...), custom_call_target="tpu_custom_call" | custom-call | flops 12884901888 | bytes 524288 | tf_op jit(solution)/shard_map/pallas_call | solution.py:204
  135.3 2.9 %collective-permute-start.13 = (f32[8,256]{1,0:T(8,128)S(1)}, f32[8,256]{1,0:T(8,128)S(1)}, u32[]{:S(2)}, u32[]{:S(2)}) collective-permute-start(f32[8,256]{1,0:T(8,128)S(1)} %add_reduce_fusion), channel_id=1, source_target_pairs={{0,8},{8,0},{16,24},{24,16},{1,9},{9,1},{17,25},{25,17},{2,10},{10... | collective-permute-start | bytes 24584 | tf_op jit(solution)/shard_map/ppermute | solution.py:33
  138.1 1.5 collective-permute-start.15
  139.7 0.1 collective-permute-done.13
  139.8 2.0 %collective-permute-done.14 = f32[8,256]{1,0:T(8,128)S(1)} collective-permute-done((f32[8,256]{1,0:T(8,128)S(1)}, f32[8,256]{1,0:T(8,128)S(1)}, u32[]{:S(2)}, u32[]{:S(2)}) %collective-permute-start.14) | collective-permute-done | bytes 8224 | tf_op jit(solution)/shard_map/ppermute | solution.py:33
  141.8 0.9 collective-permute-done.15
  142.7 11.2 %collective-permute-start.16 = (f32[8,256]{1,0:T(8,128)S(1)}, f32[8,256]{1,0:T(8,128)S(1)}, u32[]{:S(2)}, u32[]{:S(2)}) collective-permute-start(f32[8,256]{1,0:T(8,128)S(1)} %add_add_fusion.1), channel_id=1, source_target_pairs={{0,2},{2,0},{4,6},{6,4},{1,3},{3,1},{5,7},{7,5},{8,10},{10,8},{12,... | collective-permute-start | bytes 24584 | tf_op jit(solution)/shard_map/ppermute | solution.py:33
  153.9 1.2 collective-permute-start.17
  155.2 1.4 collective-permute-start.18
  156.6 1.9 %collective-permute-done.17 = f32[8,256]{1,0:T(8,128)S(1)} collective-permute-done((f32[8,256]{1,0:T(8,128)S(1)}, f32[8,256]{1,0:T(8,128)S(1)}, u32[]{:S(2)}, u32[]{:S(2)}) %collective-permute-start.17) | collective-permute-done | bytes 8224 | tf_op jit(solution)/shard_map/ppermute | solution.py:33
  158.5 2.1 %collective-permute-done.18 = f32[8,256]{1,0:T(8,128)S(1)} collective-permute-done((f32[8,256]{1,0:T(8,128)S(1)}, f32[8,256]{1,0:T(8,128)S(1)}, u32[]{:S(2)}, u32[]{:S(2)}) %collective-permute-start.18) | collective-permute-done | bytes 8224 | tf_op jit(solution)/shard_map/ppermute | solution.py:33
  160.6 0.6 add_add_fusion
  (48 shorter events, 0.4 us)
Async XLA Ops:
  6.5 108.6 %all-gather.3.cloned.1.call-start = ((), (), s32[]{:S(2)}) async-start(), calls=%async_computation | async-start | bytes 4718592 | tf_op jit(solution)/shard_map/all_gather | solution.py:276
  8.4 15.3 %collective-permute-start.2 = (bf16[512,512]{1,0:T(8,128)(2,1)}, bf16[512,512]{1,0:T(8,128)(2,1)}, u32[]{:S(2)}, u32[]{:S(2)}) collective-permute-start(bf16[512,512]{1,0:T(8,128)(2,1)} %dynamic-slice_bitcast_fusion), channel_id=1, source_target_pairs={{0,2},{2,0},{4,6},{6,4},{1,3},{3,1},{5,7},{7,5},{8,10},{10,8},{12,... | collective-permute-start | bytes 1572872 | tf_op jit(solution)/shard_map/ppermute | solution.py:243
  11.5 2.2 %copy-start = (bf16[2,2048,512]{2,1,0:T(8,128)(2,1)S(1)}, bf16[2,2048,512]{2,1,0:T(8,128)(2,1)}, u32[]{:S(2)}) copy-start(bf16[2,2048,512]{2,1,0:T(8,128)(2,1)} %rest_0_.1) | copy-start | bytes 12582916
  13.7 0.7 copy-start.7
  14.4 0.7 copy-start.9
  15.0 5.9 %copy-start.1 = (bf16[8,192,512]{2,1,0:T(8,128)(2,1)S(1)}, bf16[8,192,512]{2,1,0:T(8,128)(2,1)}, u32[]{:S(2)}) copy-start(bf16[8,192,512]{2,1,0:T(8,128)(2,1)} %param.6) | copy-start | bytes 4718596
  16.9 1.0 copy-start.11
  17.9 41.6 %copy-start.8 = (f32[2]{0:T(128)S(1)}, f32[2]{0:T(128)}, u32[]{:S(2)}) copy-start(f32[2]{0:T(128)} %nu_ref.1) | copy-start | bytes 28
  17.9 41.6 %copy-start.10 = (f32[2]{0:T(128)S(1)}, f32[2]{0:T(128)}, u32[]{:S(2)}) copy-start(f32[2]{0:T(128)} %weight_ref.1) | copy-start | bytes 28
  17.9 41.8 %copy-start.13 = (f32[256]{0:T(256)S(1)}, f32[256]{0:T(256)}, u32[]{:S(2)}) copy-start(f32[256]{0:T(256)} %param.10) | copy-start | bytes 3076
  17.9 41.8 %copy-start.14 = (s32[192]{0:T(256)S(1)}, s32[192]{0:T(256)}, u32[]{:S(2)}) copy-start(s32[192]{0:T(256)} %param.11) | copy-start | bytes 2308
  17.9 36.6 %collective-permute-start = (bf16[1552,512]{1,0:T(8,128)(2,1)}, bf16[1552,512]{1,0:T(8,128)(2,1)}, u32[]{:S(2)}, u32[]{:S(2)}) collective-permute-start(bf16[1552,512]{1,0:T(8,128)(2,1)} %get-tuple-element.13), channel_id=1, source_target_pairs={{0,8},{8,0},{16,24},{24,16},{1,9},{9,1},{17,25},{25,17},{2,10},{10... | collective-permute-start | bytes 4767752 | tf_op jit(solution)/shard_map/ppermute | solution.py:33
  19.4 36.2 %collective-permute-start.1 = (bf16[1552,512]{1,0:T(8,128)(2,1)}, bf16[1552,512]{1,0:T(8,128)(2,1)}, u32[]{:S(2)}, u32[]{:S(2)}) collective-permute-start(bf16[1552,512]{1,0:T(8,128)(2,1)} %get-tuple-element.13), channel_id=1, source_target_pairs={{0,16},{8,24},{16,0},{24,8},{1,17},{9,25},{17,1},{25,9},{2,18},{10... | collective-permute-start | bytes 4767752 | tf_op jit(solution)/shard_map/ppermute | solution.py:33
  21.0 7.2 %collective-permute-start.4 = (bf16[1536,512]{1,0:T(8,128)(2,1)S(1)}, bf16[1536,512]{1,0:T(8,128)(2,1)S(1)}, u32[]{:S(2)}, u32[]{:S(2)}) collective-permute-start(bf16[1536,512]{1,0:T(8,128)(2,1)S(1)} %bitcast.32), channel_id=1, source_target_pairs={{2,4},{4,2},{3,5},{5,3},{10,12},{12,10},{11,13},{13,11},{18,20},{2... | collective-permute-start | bytes 4718600 | tf_op jit(solution)/shard_map/ppermute | solution.py:273
  23.7 35.8 %collective-permute-start.3 = (bf16[1536,512]{1,0:T(8,128)(2,1)S(1)}, bf16[1536,512]{1,0:T(8,128)(2,1)}, u32[]{:S(2)}, u32[]{:S(2)}) collective-permute-start(bf16[1536,512]{1,0:T(8,128)(2,1)S(1)} %bitcast.33), channel_id=1, source_target_pairs={{0,2},{2,0},{4,6},{6,4},{1,3},{3,1},{5,7},{7,5},{8,10},{10,8},{12,... | collective-permute-start | bytes 4718600 | tf_op jit(solution)/shard_map/ppermute | solution.py:274
  28.1 45.4 %copy-start.3 = (bf16[1536,512]{1,0:T(8,128)(2,1)}, bf16[1536,512]{1,0:T(8,128)(2,1)S(1)}, u32[]{:S(2)}) copy-start(bf16[1536,512]{1,0:T(8,128)(2,1)S(1)} %collective-permute-done.4.b_ref) | copy-start | bytes 4718596
  60.6 36.4 %collective-permute-start.9 = (bf16[1536,512]{1,0:T(8,128)(2,1)S(1)}, bf16[1536,512]{1,0:T(8,128)(2,1)}, u32[]{:S(2)}, u32[]{:S(2)}) collective-permute-start(bf16[1536,512]{1,0:T(8,128)(2,1)S(1)} %collective-permute-done.4.b_ref), channel_id=1, source_target_pairs={{2,0},{4,6},{3,1},{5,7},{10,8},{12,14},{11,9},{13,15},{18,16},{20,... | collective-permute-start | bytes 4718600 | tf_op jit(solution)/shard_map/ppermute | solution.py:300
  64.0 28.2 %collective-permute-start.6 = (bf16[784,512]{1,0:T(8,128)(2,1)}, bf16[784,512]{1,0:T(8,128)(2,1)}, u32[]{:S(2)}, u32[]{:S(2)}) collective-permute-start(bf16[784,512]{1,0:T(8,128)(2,1)} %slice.75), channel_id=1, source_target_pairs={{0,16},{8,24},{16,0},{24,8},{1,17},{9,25},{17,1},{25,9},{2,18},{10... | collective-permute-start | bytes 2408456 | tf_op jit(solution)/shard_map/ppermute | solution.py:33
  67.4 24.9 %collective-permute-start.5 = (bf16[768,512]{1,0:T(8,128)(2,1)}, bf16[768,512]{1,0:T(8,128)(2,1)}, u32[]{:S(2)}, u32[]{:S(2)}) collective-permute-start(bf16[768,512]{1,0:T(8,128)(2,1)} %slice.74), channel_id=1, source_target_pairs={{0,8},{8,0},{16,24},{24,16},{1,9},{9,1},{17,25},{25,17},{2,10},{10... | collective-permute-start | bytes 2359304 | tf_op jit(solution)/shard_map/ppermute | solution.py:33
  70.5 26.5 %collective-permute-start.10 = (bf16[1536,512]{1,0:T(8,128)(2,1)}, bf16[1536,512]{1,0:T(8,128)(2,1)}, u32[]{:S(2)}, u32[]{:S(2)}) collective-permute-start(bf16[1536,512]{1,0:T(8,128)(2,1)} %collective-permute-done.3.a_ref), channel_id=1, source_target_pairs={{2,4},{4,2},{3,5},{5,3},{10,12},{12,10},{11,13},{13,11},{18,20},{2... | collective-permute-start | bytes 4718600 | tf_op jit(solution)/shard_map/ppermute | solution.py:301
  92.3 6.1 %collective-permute-start.7 = (bf16[1552,512]{1,0:T(8,128)(2,1)}, bf16[1552,512]{1,0:T(8,128)(2,1)}, u32[]{:S(2)}, u32[]{:S(2)}) collective-permute-start(bf16[1552,512]{1,0:T(8,128)(2,1)} %collective-permute-done.rest_1_.rest_4_), channel_id=1, source_target_pairs={{0,1},{1,0},{2,3},{3,2},{4,5},{5,4},{6,7},{7,6},{8,9},{9,8},{10,11... | collective-permute-start | bytes 4767752 | tf_op jit(solution)/shard_map/ppermute | solution.py:33
  92.3 6.8 %collective-permute-start.8 = (bf16[1552,512]{1,0:T(8,128)(2,1)}, bf16[1552,512]{1,0:T(8,128)(2,1)}, u32[]{:S(2)}, u32[]{:S(2)}) collective-permute-start(bf16[1552,512]{1,0:T(8,128)(2,1)} %collective-permute-done.1.rest_2_.rest_5_), channel_id=1, source_target_pairs={{0,1},{1,0},{2,3},{3,2},{4,5},{5,4},{6,7},{7,6},{8,9},{9,8},{10,11... | collective-permute-start | bytes 4767752 | tf_op jit(solution)/shard_map/ppermute | solution.py:33
  97.0 3.9 %collective-permute-start.11 = (bf16[784,512]{1,0:T(8,128)(2,1)}, bf16[784,512]{1,0:T(8,128)(2,1)S(1)}, u32[]{:S(2)}, u32[]{:S(2)}) collective-permute-start(bf16[784,512]{1,0:T(8,128)(2,1)} %collective-permute-done.6.rest_3_.rest_8_), channel_id=1, source_target_pairs={{0,1},{1,0},{2,3},{3,2},{4,5},{5,4},{6,7},{7,6},{8,9},{9,8},{10,11... | collective-permute-start | bytes 2408456 | tf_op jit(solution)/shard_map/ppermute | solution.py:33
  97.9 5.5 %collective-permute-start.12 = (bf16[768,512]{1,0:T(8,128)(2,1)}, bf16[768,512]{1,0:T(8,128)(2,1)}, u32[]{:S(2)}, u32[]{:S(2)}) collective-permute-start(bf16[768,512]{1,0:T(8,128)(2,1)} %collective-permute-done.5.rest_2_), channel_id=1, source_target_pairs={{0,1},{1,0},{2,3},{3,2},{4,5},{5,4},{6,7},{7,6},{8,9},{9,8},{10,11... | collective-permute-start | bytes 2359304 | tf_op jit(solution)/shard_map/ppermute | solution.py:33
  100.9 0.9 copy-start.4
  101.9 1.5 copy-start.5
  103.4 11.7 %copy-start.2 = (bf16[8,192,512]{2,1,0:T(8,128)(2,1)S(1)}, bf16[8,192,512]{2,1,0:T(8,128)(2,1)}, u32[]{:S(2)}) copy-start(bf16[8,192,512]{2,1,0:T(8,128)(2,1)} %param.6) | copy-start | bytes 4718596
  115.1 1.1 copy-start.6
  116.3 1.2 copy-start.12
  135.3 4.5 %collective-permute-start.13 = (f32[8,256]{1,0:T(8,128)S(1)}, f32[8,256]{1,0:T(8,128)S(1)}, u32[]{:S(2)}, u32[]{:S(2)}) collective-permute-start(f32[8,256]{1,0:T(8,128)S(1)} %add_reduce_fusion), channel_id=1, source_target_pairs={{0,8},{8,0},{16,24},{24,16},{1,9},{9,1},{17,25},{25,17},{2,10},{10... | collective-permute-start | bytes 24584 | tf_op jit(solution)/shard_map/ppermute | solution.py:33
  138.1 3.7 %collective-permute-start.14 = (f32[8,256]{1,0:T(8,128)S(1)}, f32[8,256]{1,0:T(8,128)S(1)}, u32[]{:S(2)}, u32[]{:S(2)}) collective-permute-start(f32[8,256]{1,0:T(8,128)S(1)} %add_reduce_fusion), channel_id=1, source_target_pairs={{0,16},{8,24},{16,0},{24,8},{1,17},{9,25},{17,1},{25,9},{2,18},{10... | collective-permute-start | bytes 24584 | tf_op jit(solution)/shard_map/ppermute | solution.py:33
  138.1 4.5 %collective-permute-start.15 = (f32[8,256]{1,0:T(8,128)S(1)}, f32[8,256]{1,0:T(8,128)S(1)}, u32[]{:S(2)}, u32[]{:S(2)}) collective-permute-start(f32[8,256]{1,0:T(8,128)S(1)} %add_reduce_fusion), channel_id=1, source_target_pairs={{0,24},{8,16},{16,8},{24,0},{1,25},{9,17},{17,9},{25,1},{2,26},{10... | collective-permute-start | bytes 24584 | tf_op jit(solution)/shard_map/ppermute | solution.py:33
  142.7 13.9 %collective-permute-start.16 = (f32[8,256]{1,0:T(8,128)S(1)}, f32[8,256]{1,0:T(8,128)S(1)}, u32[]{:S(2)}, u32[]{:S(2)}) collective-permute-start(f32[8,256]{1,0:T(8,128)S(1)} %add_add_fusion.1), channel_id=1, source_target_pairs={{0,2},{2,0},{4,6},{6,4},{1,3},{3,1},{5,7},{7,5},{8,10},{10,8},{12,... | collective-permute-start | bytes 24584 | tf_op jit(solution)/shard_map/ppermute | solution.py:33
  153.9 4.5 %collective-permute-start.17 = (f32[8,256]{1,0:T(8,128)S(1)}, f32[8,256]{1,0:T(8,128)S(1)}, u32[]{:S(2)}, u32[]{:S(2)}) collective-permute-start(f32[8,256]{1,0:T(8,128)S(1)} %add_add_fusion.1), channel_id=1, source_target_pairs={{0,4},{2,6},{4,0},{6,2},{1,5},{3,7},{5,1},{7,3},{8,12},{10,14},{12... | collective-permute-start | bytes 24584 | tf_op jit(solution)/shard_map/ppermute | solution.py:33
  155.2 5.4 %collective-permute-start.18 = (f32[8,256]{1,0:T(8,128)S(1)}, f32[8,256]{1,0:T(8,128)S(1)}, u32[]{:S(2)}, u32[]{:S(2)}) collective-permute-start(f32[8,256]{1,0:T(8,128)S(1)} %add_add_fusion.1), channel_id=1, source_target_pairs={{0,6},{2,4},{4,2},{6,0},{1,7},{3,5},{5,3},{7,1},{8,14},{10,12},{12... | collective-permute-start | bytes 24584 | tf_op jit(solution)/shard_map/ppermute | solution.py:33
Sparse Core Ops, SparseCore 0:
  59.6 43.5 all-gather.2
